TPU v7x, 32 devices: a whole 2x2x4 slice. The times are simulated.
32 devices in a mesh: dp: 16 (over z, y, core), tensor: 2 (over x).
Axes of the slice: x: 2, y: 2, z: 4, core: 2. Of those that a mesh axis runs over, the one named last changes fastest.
Arguments:
- tokens: bfloat16 [32768, 1024], P('dp'), may hold values from -6 to 6
- cotangent: bfloat16 [32768, 1024], P('dp'), may hold values from -6 to 6
- segments: int32 [32768], P('dp'), may hold values from 0 to 2, as said below
- routes: int32 [32768, 8], P('dp'), may hold values from 0 to 31, as said below
- slot_index: int32 [32768, 8], P('dp'), may hold values from 0 to 256, as said below
- w_query: bfloat16 [1024, 1024], P(None, 'tensor'), may hold values from -0.1875 to 0.1875
- w_key: bfloat16 [1024, 512], P(None, 'tensor'), may hold values from -0.1875 to 0.1875
- w_value: bfloat16 [1024, 512], P(None, 'tensor'), may hold values from -0.1875 to 0.1875
- w_output: bfloat16 [1024, 1024], P('tensor'), may hold values from -1.5 to 1.5
- norm_attn: bfloat16 [1024], replicated, may hold values from 0.5 to 1.5
- norm_ffn: bfloat16 [1024], replicated, may hold values from 0.5 to 1.5
- w_router: bfloat16 [1024, 32], replicated, may hold values from -0.09375 to 0.09375
- w_gate: bfloat16 [4, 1024, 512], P(None, None, 'tensor'), may hold values from -0.1875 to 0.1875
- w_up: bfloat16 [4, 1024, 512], P(None, None, 'tensor'), may hold values from -0.1875 to 0.1875
- w_down: bfloat16 [4, 512, 1024], P(None, 'tensor'), may hold values from -1.5 to 1.5
Outputs:
- block_output: bfloat16 [32768, 1024], P('dp')
- token_grad: float32 [32768, 1024], P('dp')
- grad_query: float32 [1024, 1024], P(None, 'tensor')
- grad_key: float32 [1024, 512], P(None, 'tensor')
- grad_value: float32 [1024, 512], P(None, 'tensor')
- grad_output: float32 [1024, 1024], P('tensor')
- grad_norm_attn: float32 [1024], replicated
- grad_norm_ffn: float32 [1024], replicated
- grad_router: float32 [1024, 32], replicated
- grad_gate: float32 [4, 1024, 512], P(None, None, 'tensor')
- grad_up: float32 [4, 1024, 512], P(None, None, 'tensor')
- grad_down: float32 [4, 512, 1024], P(None, 'tensor')
Inputs may be any that keep to these rules, and one draw needn't show every extreme that they name: `routes`: each token names 8 different experts. In every draw one expert below 4 is named by every token. slot_index[t, k] counts the routes to the same expert that come before (t, k) among the tokens of t's sequence of 1024 tokens, in token order and then route order; it is 256 where that count is 256 or more, and where routes[t, k] is 4 or more. `segments`: within each sequence of 1024 tokens the numbers start at 0 and never fall; every document has 256 tokens or more.
All inputs are finite; a program needn't handle non-finite values.
Results may differ from a plain program's by a relative error of at most 0.011.
The roundings to bfloat16 on the way count: a program that leaves them out, or rounds other values in their place, can miss the bound.
Values may be sent and summed in bfloat16 or wider, within the bound.
No kernel may reach another device: no remote copies, remote signals or barrier semaphores. Data moves between devices by JAX's collectives and lax.ppermute only.
A program may use at most 256 MiB of HBM per device.

v0:
```python
from functools import partial

import jax
import jax.numpy as jnp
from jax import lax
from jax.sharding import PartitionSpec as P

HEAD_DIM = 64
SEQ_LEN = 1024
CAP = 256


EPS = 1e-06
THETA = 10000.0
NEG = -1e30


def rmsnorm(values, gain_row):
    return values * lax.rsqrt(jnp.mean(values * values, axis=-1, keepdims=True) + EPS) * gain_row


def rotary_tables(segments, head_size):
    earlier = jnp.sum((segments[None, :] < segments[:, None]).astype(jnp.int32), axis=1)
    positions = (jnp.arange(segments.shape[0], dtype=jnp.int32) - earlier).astype(jnp.float32)
    half_dim = head_size // 2
    frequency = THETA ** (-(2.0 * jnp.arange(half_dim, dtype=jnp.float32)) / head_size)
    angles = positions[:, None] * frequency[None, :]
    angles = jnp.concatenate([angles, angles], axis=1)
    return (jnp.cos(angles)[:, None, :], jnp.sin(angles)[:, None, :])


def rotate(values, cosine, sine):
    half_dim = values.shape[-1] // 2
    turned = jnp.concatenate([-values[..., half_dim:], values[..., :half_dim]], axis=-1)
    return values * cosine + turned * sine


def rotate_back(upward, cosine, sine):
    half_dim = upward.shape[-1] // 2
    scaled = upward * sine
    turned = jnp.concatenate([scaled[..., half_dim:], -scaled[..., :half_dim]], axis=-1)
    return upward * cosine + turned


def gate_weights(route_onehot, logits):
    chosen = jnp.einsum("tke,te->tk", route_onehot, logits, precision=lax.Precision.HIGHEST)
    return jax.nn.softmax(chosen, axis=-1)


def swiglu_mix(gate_pre, up_pre):
    return jax.nn.silu(gate_pre) * up_pre


def allowed_pairs(segs):
    places = jnp.arange(segs.shape[0])
    return (places[None, :] <= places[:, None]) & (segs[None, :] == segs[:, None])


def attend_forward(pieces):
    queries, keys, values, segs = pieces
    seq_rows = queries.shape[0]
    score_scale = queries.shape[-1] ** (-0.5)
    allowed = allowed_pairs(segs)
    raw_scores = jnp.einsum("qkgd,skd->kgqs", queries, keys, preferred_element_type=jnp.float32)
    scores = jnp.where(allowed, raw_scores * score_scale, NEG)
    row_max = jnp.max(scores, axis=-1, keepdims=True)
    weights = jnp.exp(scores - row_max)
    row_total = jnp.sum(weights, axis=-1, keepdims=True)
    log_total = row_max + jnp.log(row_total)
    probs_low = (weights / row_total).astype(jnp.bfloat16)
    attended = jnp.einsum("kgqs,skd->qkgd", probs_low, values, preferred_element_type=jnp.float32)
    return (attended.reshape(seq_rows, -1).astype(jnp.bfloat16), log_total)


def attend_backward(pieces):
    queries, keys, values, segs, upward, log_total = pieces
    score_scale = queries.shape[-1] ** (-0.5)
    allowed = allowed_pairs(segs)
    again_scores = jnp.einsum("qkgd,skd->kgqs", queries, keys, preferred_element_type=jnp.float32)
    again_scores = jnp.where(allowed, again_scores * score_scale, NEG)
    probs_full = jnp.exp(again_scores - log_total)
    probs_again = probs_full.astype(jnp.bfloat16)
    prob_grad = jnp.einsum("qkgd,skd->kgqs", upward, values, preferred_element_type=jnp.float32)
    row_delta = jnp.sum(probs_full * prob_grad, axis=-1, keepdims=True)
    raw_grad = (probs_full * (prob_grad - row_delta) * score_scale).astype(jnp.bfloat16)
    query_grad = jnp.einsum("kgqs,skd->qkgd", raw_grad, keys, preferred_element_type=jnp.float32)
    key_grad = jnp.einsum("kgqs,qkgd->skd", raw_grad, queries, preferred_element_type=jnp.float32)
    value_grad = jnp.einsum(
        "kgqs,qkgd->skd", probs_again, upward, preferred_element_type=jnp.float32
    )
    return (query_grad, key_grad, value_grad)


def per_device(
    tokens,
    cotangent,
    segments,
    routes,
    slot_index,
    w_query,
    w_key,
    w_value,
    w_output,
    norm_attn,
    norm_ffn,
    w_router,
    w_gate,
    w_up,
    w_down,
):
    f32 = jnp.float32
    bf16 = jnp.bfloat16
    length, model_width = tokens.shape
    seq_rows = SEQ_LEN
    seq_count = length // seq_rows
    q_heads = w_query.shape[1] // HEAD_DIM
    kv_heads = w_key.shape[1] // HEAD_DIM
    groups = q_heads // kv_heads
    window = w_gate.shape[0]
    capacity = CAP
    slots_all = seq_count * capacity
    route_width = routes.shape[1]
    inputs = tokens.astype(f32)
    normed_one, norm_one_back = jax.vjp(rmsnorm, inputs, norm_attn.astype(f32))
    first = normed_one.astype(bf16)
    seg_rows = segments.reshape(seq_count, seq_rows)
    cosine, sine = jax.vmap(partial(rotary_tables, head_size=HEAD_DIM))(seg_rows)
    cosine = cosine.reshape(length, 1, HEAD_DIM)
    sine = sine.reshape(length, 1, HEAD_DIM)
    query_raw = jnp.dot(first, w_query, preferred_element_type=f32).reshape(
        length, q_heads, HEAD_DIM
    )
    key_raw = jnp.dot(first, w_key, preferred_element_type=f32).reshape(length, kv_heads, HEAD_DIM)
    value_raw = jnp.dot(first, w_value, preferred_element_type=f32)
    query_heads = (
        rotate(query_raw, cosine, sine)
        .astype(bf16)
        .reshape(seq_count, seq_rows, kv_heads, groups, HEAD_DIM)
    )
    key_heads = (
        rotate(key_raw, cosine, sine).astype(bf16).reshape(seq_count, seq_rows, kv_heads, HEAD_DIM)
    )
    value_heads = value_raw.astype(bf16).reshape(seq_count, seq_rows, kv_heads, HEAD_DIM)
    attended_seq, log_totals = lax.map(
        attend_forward, (query_heads, key_heads, value_heads, seg_rows)
    )
    attended = attended_seq.reshape(length, q_heads * HEAD_DIM)
    attn_part = jnp.dot(attended, w_output, preferred_element_type=f32)
    attn_full = lax.psum(attn_part, "tensor")
    resid = inputs + attn_full
    normed_two, norm_two_back = jax.vjp(rmsnorm, resid, norm_ffn.astype(f32))
    second = normed_two.astype(bf16)
    logits = jnp.dot(second, w_router, preferred_element_type=f32)
    route_onehot = (
        routes[:, :, None] == jnp.arange(w_router.shape[1], dtype=jnp.int32)[None, None, :]
    ).astype(f32)
    gate_values, gate_back = jax.vjp(partial(gate_weights, route_onehot), logits)
    in_window = (routes < window) & (slot_index < capacity)
    seq_of = (jnp.arange(length, dtype=jnp.int32) // seq_rows)[:, None]
    target = jnp.where(
        in_window, routes * slots_all + seq_of * capacity + slot_index, window * slots_all
    ).reshape(-1)
    route_count = length * route_width
    route_of = (
        jnp.full((window * slots_all + 1,), route_count, jnp.int32)
        .at[target]
        .set(jnp.arange(route_count, dtype=jnp.int32))[: window * slots_all]
    )
    token_of = route_of // route_width
    gate_flat = jnp.concatenate(
        [(gate_values * in_window.astype(f32)).reshape(-1), jnp.zeros((1,), f32)]
    )
    gate_slot = gate_flat[route_of]
    padded_two = jnp.concatenate([second, jnp.zeros((1, model_width), bf16)], axis=0)
    expert_in = padded_two[token_of].reshape(window, slots_all, model_width)
    gate_pre = jnp.einsum("ecd,edf->ecf", expert_in, w_gate, preferred_element_type=f32)
    up_pre = jnp.einsum("ecd,edf->ecf", expert_in, w_up, preferred_element_type=f32)
    hidden_full, mix_back = jax.vjp(swiglu_mix, gate_pre, up_pre)
    hidden = hidden_full.astype(bf16)
    expert_out = jnp.einsum("ecf,efd->ecd", hidden, w_down, preferred_element_type=f32).reshape(
        window * slots_all, model_width
    )
    moe_part = jax.ops.segment_sum(
        gate_slot[:, None] * expert_out, token_of, num_segments=length + 1
    )[:length]
    moe_full = lax.psum(moe_part.astype(jnp.bfloat16), "tensor").astype(jnp.float32)
    block_output = (resid + moe_full).astype(bf16)
    upstream = cotangent.astype(f32)
    padded_grad = jnp.concatenate([upstream, jnp.zeros((1, model_width), f32)], axis=0)
    slot_grad = padded_grad[token_of]
    out_grad = (gate_slot[:, None] * slot_grad).astype(bf16).reshape(window, slots_all, model_width)
    slot_gate_grad = jnp.sum(expert_out * slot_grad, axis=-1)
    gate_grad_part = jax.ops.segment_sum(slot_gate_grad, route_of, num_segments=route_count + 1)[
        :route_count
    ].reshape(length, route_width)
    grad_down = jnp.einsum("ecf,ecd->efd", hidden, out_grad, preferred_element_type=f32)
    hidden_grad = jnp.einsum("ecd,efd->ecf", out_grad, w_down, preferred_element_type=f32)
    gate_pre_grad, up_pre_grad = mix_back(hidden_grad)
    gate_pre_low = gate_pre_grad.astype(bf16)
    up_pre_low = up_pre_grad.astype(bf16)
    grad_gate = jnp.einsum("ecd,ecf->edf", expert_in, gate_pre_low, preferred_element_type=f32)
    grad_up = jnp.einsum("ecd,ecf->edf", expert_in, up_pre_low, preferred_element_type=f32)
    slot_input_grad = jnp.einsum("ecf,edf->ecd", gate_pre_low, w_gate, preferred_element_type=f32)
    slot_input_grad = slot_input_grad + jnp.einsum(
        "ecf,edf->ecd", up_pre_low, w_up, preferred_element_type=f32
    )
    second_grad_part = jax.ops.segment_sum(
        slot_input_grad.reshape(window * slots_all, model_width), token_of, num_segments=length + 1
    )[:length]
    second_grad, gate_grad = lax.psum((second_grad_part, gate_grad_part), "tensor")
    logit_grad = gate_back(gate_grad)[0]
    second_wide = second.astype(f32)
    grad_router = jnp.einsum("td,te->de", second_wide, logit_grad, precision=lax.Precision.HIGHEST)
    second_grad = second_grad + jnp.einsum(
        "te,de->td", logit_grad, w_router.astype(f32), precision=lax.Precision.HIGHEST
    )
    resid_grad, grad_norm_two = norm_two_back(second_grad)
    resid_grad = resid_grad + upstream
    resid_low = resid_grad.astype(bf16)
    grad_output = jnp.einsum("ti,td->id", attended, resid_low, preferred_element_type=f32)
    attended_grad = jnp.einsum("td,id->ti", resid_low, w_output, preferred_element_type=f32)
    attended_grad = attended_grad.astype(bf16).reshape(
        seq_count, seq_rows, kv_heads, groups, HEAD_DIM
    )
    query_grad, key_grad, value_grad = lax.map(
        attend_backward, (query_heads, key_heads, value_heads, seg_rows, attended_grad, log_totals)
    )
    query_back = (
        rotate_back(query_grad.reshape(length, q_heads, HEAD_DIM), cosine, sine)
        .reshape(length, q_heads * HEAD_DIM)
        .astype(bf16)
    )
    key_back = (
        rotate_back(key_grad.reshape(length, kv_heads, HEAD_DIM), cosine, sine)
        .reshape(length, kv_heads * HEAD_DIM)
        .astype(bf16)
    )
    value_back = value_grad.reshape(length, kv_heads * HEAD_DIM).astype(bf16)
    grad_query = jnp.einsum("td,ti->di", first, query_back, preferred_element_type=f32)
    grad_key = jnp.einsum("td,ti->di", first, key_back, preferred_element_type=f32)
    grad_value = jnp.einsum("td,ti->di", first, value_back, preferred_element_type=f32)
    first_grad_part = jnp.einsum("ti,di->td", query_back, w_query, preferred_element_type=f32)
    first_grad_part = first_grad_part + jnp.einsum(
        "ti,di->td", key_back, w_key, preferred_element_type=f32
    )
    first_grad_part = first_grad_part + jnp.einsum(
        "ti,di->td", value_back, w_value, preferred_element_type=f32
    )
    first_grad = lax.psum(first_grad_part, "tensor")
    input_norm_grad, grad_norm_one = norm_one_back(first_grad)
    token_grad = resid_grad + input_norm_grad
    (
        part_query,
        part_key,
        part_value,
        part_output,
        part_first,
        part_gate,
        part_up,
        part_down,
        part_router,
        part_norm,
    ) = (
        lax.psum_scatter(grad_query, "dp", scatter_dimension=0, tiled=True),
        lax.psum_scatter(grad_key, "dp", scatter_dimension=0, tiled=True),
        lax.psum_scatter(grad_value, "dp", scatter_dimension=0, tiled=True),
        lax.psum_scatter(grad_output, "dp", scatter_dimension=1, tiled=True),
        lax.psum_scatter(grad_norm_one, "dp", scatter_dimension=0, tiled=True),
        lax.psum_scatter(grad_gate, "dp", scatter_dimension=1, tiled=True),
        lax.psum_scatter(grad_up, "dp", scatter_dimension=1, tiled=True),
        lax.psum_scatter(grad_down, "dp", scatter_dimension=2, tiled=True),
        lax.psum_scatter(grad_router, "dp", scatter_dimension=0, tiled=True),
        lax.psum_scatter(grad_norm_two, "dp", scatter_dimension=0, tiled=True),
    )
    (
        sum_query,
        sum_key,
        sum_value,
        sum_output,
        sum_norm_one,
        sum_gate,
        sum_up,
        sum_down,
        sum_router,
        sum_norm_two,
    ) = (
        lax.all_gather(part_query, "dp", axis=0, tiled=True),
        lax.all_gather(part_key, "dp", axis=0, tiled=True),
        lax.all_gather(part_value, "dp", axis=0, tiled=True),
        lax.all_gather(part_output, "dp", axis=1, tiled=True),
        lax.all_gather(part_first, "dp", axis=0, tiled=True),
        lax.all_gather(part_gate, "dp", axis=1, tiled=True),
        lax.all_gather(part_up, "dp", axis=1, tiled=True),
        lax.all_gather(part_down, "dp", axis=2, tiled=True),
        lax.all_gather(part_router, "dp", axis=0, tiled=True),
        lax.all_gather(part_norm, "dp", axis=0, tiled=True),
    )
    return (
        block_output,
        token_grad,
        sum_query,
        sum_key,
        sum_value,
        sum_output,
        sum_norm_one,
        sum_norm_two,
        sum_router,
        sum_gate,
        sum_up,
        sum_down,
    )


def solution(mesh):
    placed = (
        P("dp", None),
        P("dp", None),
        P("dp"),
        P("dp", None),
        P("dp", None),
        P(None, "tensor"),
        P(None, "tensor"),
        P(None, "tensor"),
        P("tensor", None),
        P(),
        P(),
        P(),
        P(None, None, "tensor"),
        P(None, None, "tensor"),
        P(None, "tensor", None),
    )
    return jax.shard_map(
        per_device,
        mesh=mesh,
        in_specs=placed,
        out_specs=(
            P("dp", None),
            P("dp", None),
            P(None, "tensor"),
            P(None, "tensor"),
            P(None, "tensor"),
            P("tensor", None),
            P(),
            P(),
            P(),
            P(None, None, "tensor"),
            P(None, None, "tensor"),
            P(None, "tensor", None),
        ),
        check_vma=False,
    )
```

profile of v0, /device:TPU:0, one launch (start us, length us, event | category | flops | bytes accessed | tf_op | source)
XLA Modules:
  0.0 2416.6 jit_solution(16218269791367514079)
XLA Ops:
  14.0 7.5 fusion.102
  62.9 6.6 reshape.307
  89.7 97.5 %while.26 = (s32[]{:T(128)}, bf16[2,1024,512]{2,1,0:T(8,128)(2,1)}, f32[2,4,2,1024,1]{3,2,1,4,0:T(2,128)S(1)}, bf16[2,1024,4,64]{1,3,2,0:T(8,128)(2,1)}, s32[2,1...) while((s32[]{:T(128)}, bf16[2,1024,512]{2,1,0:T(8,128)(2,1)}, ...), condition=%wide.region_5.6_spmd, body=%wide.region_2.5_spmd.sunk | while | flops 2251808768 | bytes 112473192 | solution.py:144
  90.8 14.9 fusion.203
  105.7 14.2 fusion.204
  119.9 16.2 fusion.205
  139.3 14.9 fusion.203
  154.2 14.2 fusion.204
  168.5 16.2 fusion.205
  187.3 7.6 fusion.125
  196.7 6.6 concatenate.59
  203.4 60.3 %scatter_custom_fusion = s32[2049]{0:T(1024)S(1)} fusion(s32[16384]{0:T(1024)S(1)} %bitcast.346, s32[16384]{0:T(1024)S(1)} %iota.44, s32[]{:T(128)} %constant.116.clone.1), kind=kCustom, calls=%fused_computation.200 | custom fusion | bytes 8200 | tf_op jit(solution)/shard_map/scatter | solution.py:167
  264.3 15.6 gather_fusion.2
  279.9 115.9 %all-reduce.14.cloned.1.call-done = f32[2048,1024]{1,0:T(8,128)} async-done(((f32[2048,1024]{1,0:T(8,128)}), f32[2048,1024]{1,0:T(8,128)}) %all-reduce.14.cloned.1.call-update) | async-done | bytes 8388624 | tf_op jit(solution)/shard_map/psum | solution.py:149
  409.4 11.9 gather_fusion
  426.6 13.7 gather_fusion.1
  455.7 15.0 scatter_custom_fusion.3
  480.9 22.8 scatter_custom_fusion.2
  503.7 8.3 slice.61
  512.7 7.7 bitcast_multiply_fusion.9
  520.4 22.8 scatter_custom_fusion.1
  553.1 159.4 %all-reduce.20.cloned.1.call-done = (f32[2048,1024]{1,0:T(8,128)}, f32[2048,8]{0,1:T(8,128)}) async-done(((f32[2048,1024]{1,0:T(8,128)}, f32[2048,8]{0,1:T(8,128)}), (f32[2048,1024]{1,0:T(8,128)}, f32[2048,8]{0,1:T(8,128)})) %all-reduce.20.cloned.1.call-update) | async-done | bytes 8454160 | tf_op jit(solution)/shard_map/psum | solution.py:210
  714.5 11.8 multiply_reduce_fusion
  726.3 97.1 %all-reduce.16.cloned.1.call-done = bf16[2048,1024]{1,0:T(8,128)(2,1)} async-done(((bf16[2048,1024]{1,0:T(8,128)(2,1)}), bf16[2048,1024]{1,0:T(8,128)(2,1)}) %all-reduce.16.cloned.1.call-update) | async-done | bytes 4194320 | tf_op jit(solution)/shard_map/psum | solution.py:186
  823.4 11.7 fusion.75
  844.6 10.6 copy.156
  855.2 406.4 %while.27 = (s32[]{:T(128)}, f32[2,1024,4,2,64]{1,0,4,3,2:T(2,128)}, f32[2,1024,4,64]{1,0,3,2:T(2,128)}, bf16[2,1024,4,64]{1,3,2,0:T(8,128)(2,1)S(1)}, bf16[2,10...) while((s32[]{:T(128)}, ...), condition=%wide.region_22.23_spmd, body=%wide.region_20.22_spmd.sunk | while | flops 5589977088 | bytes 410762432 | solution.py:225
  856.0 17.0 fusion.215
  873.0 15.1 fusion.219
  888.1 17.4 fusion.214
  905.5 46.6 %fusion.218 = f32[1,1024,4,64]{1,3,2,0:T(8,128)} fusion(f32[4,1024,1024,2]{2,1,3,0:T(8,128)} %fusion.214, f32[4,1024,1024,2]{2,1,3,0:T(8,128)} %fusion.215, f32[4,2,1024]{2,1,0:T(2,128)S(1)} %dynamic-slice_bitcast_fusion.2, pred[1024,1024]{0,1:T(8,128)(4,1)S(1)} %fusion.216, bf16[2,1024,4,2,64]{1,4,3,2,0:T(8,128)(2,1)} %get-tuple-element.492, ...), kind=kOutput, calls=%fused_computation.48.clone.1 | convolution fusion | flops 1166025728 | bytes 138477568 | tf_op jit(solution)/shard_map/while/body/eval_jaxpr/kgqs,qkgd->skd/dot_general | solution.py:87
  952.1 46.1 %fusion.217 = f32[1,1024,4,2,64]{1,4,3,2,0:T(8,128)} fusion(f32[4,1024,1024,2]{2,1,3,0:T(8,128)} %fusion.214, f32[4,1024,1024,2]{2,1,3,0:T(8,128)} %fusion.215, f32[4,2,1024]{2,1,0:T(2,128)S(1)} %dynamic-slice_bitcast_fusion.2, pred[1024,1024]{0,1:T(8,128)(4,1)S(1)} %fusion.216, bf16[2,1024,4,64]{1,3,2,0:T(8,128)(2,1)} %get-tuple-element.490, ...), kind=kOutput, calls=%fused_computation.47.clone.1 | convolution fusion | flops 1166025728 | bytes 139001856 | tf_op jit(solution)/shard_map/while/body/eval_jaxpr/kgqs,skd->qkgd/dot_general | solution.py:86
  1003.1 18.7 dynamic_update_slice.31
  1021.8 36.4 %dynamic_update_slice.30 = f32[2,1024,4,2,64]{1,0,4,3,2:T(2,128)} dynamic-update-slice(f32[2,1024,4,2,64]{1,0,4,3,2:T(2,128)} %get-tuple-element.475, f32[1,1024,4,2,64]{1,0,4,3,2:T(1,128)S(1)} %copy.228, s32[]{:T(128)S(6)} %copy.252, s32[]{:T(128)} %constant.69.clone.1..sunk, s32[]{:T(128)} %constant.69.clone.1..sunk, s32[]{:T(128)} %constant.69.clone.1..sunk, s32[]{:T(128)} %constant.69.clone.1..sunk) | dynamic-update-slice | bytes 4194308 | tf_op jit(solution)/shard_map/while/body/jit(dynamic_update_index_in_dim)/dynamic_update_slice | solution.py:225
  1058.9 17.0 fusion.215
  1075.9 15.1 fusion.219
  1091.0 17.4 fusion.214
  1108.4 46.6 %fusion.218 = f32[1,1024,4,64]{1,3,2,0:T(8,128)} fusion(f32[4,1024,1024,2]{2,1,3,0:T(8,128)} %fusion.214, f32[4,1024,1024,2]{2,1,3,0:T(8,128)} %fusion.215, f32[4,2,1024]{2,1,0:T(2,128)S(1)} %dynamic-slice_bitcast_fusion.2, pred[1024,1024]{0,1:T(8,128)(4,1)S(1)} %fusion.216, bf16[2,1024,4,2,64]{1,4,3,2,0:T(8,128)(2,1)} %get-tuple-element.492, ...), kind=kOutput, calls=%fused_computation.48.clone.1 | convolution fusion | flops 1166025728 | bytes 138477568 | tf_op jit(solution)/shard_map/while/body/eval_jaxpr/kgqs,qkgd->skd/dot_general | solution.py:87
  1155.0 46.1 %fusion.217 = f32[1,1024,4,2,64]{1,4,3,2,0:T(8,128)} fusion(f32[4,1024,1024,2]{2,1,3,0:T(8,128)} %fusion.214, f32[4,1024,1024,2]{2,1,3,0:T(8,128)} %fusion.215, f32[4,2,1024]{2,1,0:T(2,128)S(1)} %dynamic-slice_bitcast_fusion.2, pred[1024,1024]{0,1:T(8,128)(4,1)S(1)} %fusion.216, bf16[2,1024,4,64]{1,3,2,0:T(8,128)(2,1)} %get-tuple-element.490, ...), kind=kOutput, calls=%fused_computation.47.clone.1 | convolution fusion | flops 1166025728 | bytes 139001856 | tf_op jit(solution)/shard_map/while/body/eval_jaxpr/kgqs,skd->qkgd/dot_general | solution.py:86
  1206.0 18.7 dynamic_update_slice.31
  1224.7 36.4 %dynamic_update_slice.30 = f32[2,1024,4,2,64]{1,0,4,3,2:T(2,128)} dynamic-update-slice(f32[2,1024,4,2,64]{1,0,4,3,2:T(2,128)} %get-tuple-element.475, f32[1,1024,4,2,64]{1,0,4,3,2:T(1,128)S(1)} %copy.228, s32[]{:T(128)S(6)} %copy.252, s32[]{:T(128)} %constant.69.clone.1..sunk, s32[]{:T(128)} %constant.69.clone.1..sunk, s32[]{:T(128)} %constant.69.clone.1..sunk, s32[]{:T(128)} %constant.69.clone.1..sunk) | dynamic-update-slice | bytes 4194308 | tf_op jit(solution)/shard_map/while/body/jit(dynamic_update_index_in_dim)/dynamic_update_slice | solution.py:225
  1275.7 7.3 fusion.97
  1298.8 7.1 fusion.92
  1305.9 6.6 reshape.318
  1325.7 7.4 fusion.135
  1333.8 50.5 %reduce-scatter.13.cloned.1.call-done = f32[64,256]{1,0:T(8,128)} async-done(((f32[1024,256]{1,0:T(8,128)}), f32[64,256]{1,0:T(8,128)}) %reduce-scatter.13.cloned.1.call-update) | async-done | bytes 65552 | tf_op jit(solution)/shard_map/reduce_scatter | solution.py:265
  1384.3 75.7 %reduce-scatter.23.cloned.1.call-done = f32[4,256,64]{1,2,0:T(8,128)} async-done(((f32[4,256,1024]{1,2,0:T(8,128)}), f32[4,256,64]{1,2,0:T(8,128)}) %reduce-scatter.23.cloned.1.call-update) | async-done | bytes 262160 | tf_op jit(solution)/shard_map/reduce_scatter | solution.py:271
  1460.1 75.6 %reduce-scatter.19.cloned.1.call-done = f32[4,64,256]{2,1,0:T(8,128)} async-done(((f32[4,1024,256]{2,1,0:T(8,128)}), f32[4,64,256]{2,1,0:T(8,128)}) %reduce-scatter.19.cloned.1.call-update) | async-done | bytes 262160 | tf_op jit(solution)/shard_map/reduce_scatter | solution.py:269
  1535.8 75.9 %reduce-scatter.21.cloned.1.call-done = f32[4,64,256]{2,1,0:T(8,128)} async-done(((f32[4,1024,256]{2,1,0:T(8,128)}), f32[4,64,256]{2,1,0:T(8,128)}) %reduce-scatter.21.cloned.1.call-update) | async-done | bytes 262160 | tf_op jit(solution)/shard_map/reduce_scatter | solution.py:270
  1611.8 64.3 %reduce-scatter.17.cloned.1.call-done = f32[512,64]{0,1:T(8,128)} async-done(((f32[512,1024]{0,1:T(8,128)}), f32[512,64]{0,1:T(8,128)}) %reduce-scatter.17.cloned.1.call-update) | async-done | bytes 131088 | tf_op jit(solution)/shard_map/reduce_scatter | solution.py:267
  1676.2 65.1 %reduce-scatter.11.cloned.1.call-done = f32[64,512]{1,0:T(8,128)} async-done(((f32[1024,512]{1,0:T(8,128)}), f32[64,512]{1,0:T(8,128)}) %reduce-scatter.11.cloned.1.call-update) | async-done | bytes 131088 | tf_op jit(solution)/shard_map/reduce_scatter | solution.py:264
  1753.0 47.2 %reduce-scatter.25.cloned.1.call-done = f32[64,32]{1,0:T(8,128)} async-done(((f32[1024,32]{1,0:T(8,128)}), f32[64,32]{1,0:T(8,128)}) %reduce-scatter.25.cloned.1.call-update) | async-done | bytes 8208
  1801.0 20.6 all-gather
  1822.5 17.0 all-gather.13.cloned.1.call-done
  1839.5 39.3 %all-gather.11.cloned.1.call-done = f32[1024,256]{1,0:T(8,128)} async-done(((f32[64,256]{1,0:T(8,128)}), f32[1024,256]{1,0:T(8,128)}) %all-gather.11.cloned.1.call-update) | async-done | bytes 1048592 | tf_op jit(solution)/shard_map/all_gather | solution.py:288
  1878.8 51.8 %all-gather.21.cloned.1.call-done = f32[4,256,1024]{1,2,0:T(8,128)} async-done(((f32[4,256,64]{1,2,0:T(8,128)}), f32[4,256,1024]{1,2,0:T(8,128)}) %all-gather.21.cloned.1.call-update) | async-done | bytes 4194320 | tf_op jit(solution)/shard_map/all_gather | solution.py:294
  1935.9 46.0 %all-gather.17.cloned.1.call-done = f32[4,1024,256]{2,1,0:T(8,128)} async-done(((f32[4,64,256]{2,1,0:T(8,128)}), f32[4,1024,256]{2,1,0:T(8,128)}) %all-gather.17.cloned.1.call-update) | async-done | bytes 4194320 | tf_op jit(solution)/shard_map/all_gather | solution.py:292
  1982.0 51.4 %all-gather.19.cloned.1.call-done = f32[4,1024,256]{2,1,0:T(8,128)} async-done(((f32[4,64,256]{2,1,0:T(8,128)}), f32[4,1024,256]{2,1,0:T(8,128)}) %all-gather.19.cloned.1.call-update) | async-done | bytes 4194320 | tf_op jit(solution)/shard_map/all_gather | solution.py:293
  2033.3 42.2 %all-gather.15.cloned.1.call-done = f32[512,1024]{0,1:T(8,128)} async-done(((f32[512,64]{0,1:T(8,128)}), f32[512,1024]{0,1:T(8,128)}) %all-gather.15.cloned.1.call-update) | async-done | bytes 2097168 | tf_op jit(solution)/shard_map/all_gather | solution.py:290
  2078.4 39.6 %all-gather.9.cloned.1.call-done = f32[1024,512]{1,0:T(8,128)} async-done(((f32[64,512]{1,0:T(8,128)}), f32[1024,512]{1,0:T(8,128)}) %all-gather.9.cloned.1.call-update) | async-done | bytes 2097168 | tf_op jit(solution)/shard_map/all_gather | solution.py:287
  2117.9 199.4 %all-reduce.18.cloned.1.call-done = f32[2048,1024]{1,0:T(8,128)} async-done(((f32[2048,1024]{1,0:T(8,128)}), f32[2048,1024]{1,0:T(8,128)}) %all-reduce.18.cloned.1.call-update) | async-done | bytes 8388624 | tf_op jit(solution)/shard_map/psum | solution.py:249
  2323.4 33.7 %all-reduce.7 = (f32[1024]{0:T(1024)S(1)}, f32[1024]{0:T(1024)S(1)}) all-reduce(f32[1024]{0:T(1024)S(1)} %get-tuple-element.256, f32[1024]{0:T(1024)S(1)} %copy-done.69), channel_id=6, replica_groups=mesh['dp'=16,'tensor'=2] {'dp'}, use_global_device_ids=true, to_apply=%region_30.31.clone | all-reduce | flops 2048 | bytes 16384
  2357.5 30.6 %all-reduce.6 = (f32[1024]{0:T(1024)}, f32[1024]{0:T(1024)}) all-reduce(f32[1024]{0:T(1024)S(1)} %dynamic-slice_dynamic-update-slice_fusion.1, f32[1024]{0:T(1024)S(1)} %dynamic-slice_dynamic-update-slice_fusion), channel_id=1, replica_groups=mesh['dp'=16,'tensor'=2] {'dp'}, use_global_device_ids=true, to_apply=%add.2 | all-reduce | flops 2048 | bytes 16384
  2388.0 11.7 fusion.76
  (337 shorter events, 234.9 us)
Async XLA Ops:
  7.2 439.1 %copy-start = (bf16[4,256,1024]{2,1,0:T(8,128)(2,1)S(1)}, bf16[4,256,1024]{2,1,0:T(8,128)(2,1)}, u32[]{:S(2)}) copy-start(bf16[4,256,1024]{2,1,0:T(8,128)(2,1)} %param.33) | copy-start | bytes 6291460
  7.2 388.6 %all-reduce.14.cloned.1.call-start = ((), (), s32[]{:S(2)}) async-start(), calls=%async_computation.8 | async-start | bytes 16777216 | tf_op jit(solution)/shard_map/psum | solution.py:149
  7.3 15.4 copy-start.70
  8.1 14.5 copy-start.64
  8.8 12.6 copy-start.3
  12.0 10.6 copy-start.58
  12.1 10.6 copy-start.54
  21.5 3.2 copy-start.44
  53.5 4.9 copy-start.26
  53.5 4.9 copy-start.76
  194.9 517.6 %all-reduce.20.cloned.1.call-start = ((), (), s32[]{:S(2)}) async-start(), calls=%async_computation.26 | async-start | bytes 16908288 | tf_op jit(solution)/shard_map/psum | solution.py:210
  264.3 15.6 copy-start.56
  401.5 3.4 copy-start.2
  421.9 24.3 %copy-start.66 = (f32[4,512]{1,0:T(4,128)}, f32[4,512]{1,0:T(4,128)S(1)}, u32[]{:S(2)}) copy-start(f32[4,512]{1,0:T(4,128)S(1)} %mul.364) | copy-start | bytes 24580
  421.9 4.6 copy-start.57
  440.2 4.3 copy-start.5
  440.2 4.7 copy-start.15
  440.2 6.0 slice-start
  451.0 4.7 copy-start.21
  451.0 23.4 copy-start.11
  455.7 18.7 copy-start.16
  512.0 311.4 %all-reduce.16.cloned.1.call-start = ((), (), s32[]{:S(2)}) async-start(), calls=%async_computation.9 | async-start | bytes 8388608 | tf_op jit(solution)/shard_map/psum | solution.py:186
  549.6 3.5 copy-start.53
  549.6 162.9 %copy-start.49 = (f32[2048]{0:T(1024)S(1)}, f32[2048]{0:T(1024)}, u32[]{:S(2)}) copy-start(f32[2048]{0:T(1024)} %copy-done.48) | copy-start | bytes 24580
  549.6 164.9 %copy-start.51 = (f32[2048]{0:T(1024)S(1)}, f32[2048]{0:T(1024)}, u32[]{:S(2)}) copy-start(f32[2048]{0:T(1024)} %copy-done.50) | copy-start | bytes 24580
  549.7 783.5 %reduce-scatter.15.cloned.1.call-start = ((), (), s32[]{:S(2)}) async-start(), calls=%async_computation.15 | async-start | bytes 1114112 | tf_op jit(solution)/shard_map/reduce_scatter | solution.py:266
  714.5 11.8 copy-start.32
  714.5 11.8 copy-start.61
  823.4 15.1 copy-start.75
  835.1 3.4 copy-start.6
  888.1 17.4 copy-start.40
  998.2 3.8 copy-start.7
  1021.8 36.5 %copy-start.41 = (bf16[2,1024,4,64]{1,3,2,0:T(8,128)(2,1)S(1)}, bf16[2,1024,4,64]{1,3,2,0:T(8,128)(2,1)}, u32[]{:S(2)}) copy-start(bf16[2,1024,4,64]{1,3,2,0:T(8,128)(2,1)} %copy-done.40) | copy-start | bytes 3145732 | tf_op jit(solution)/shard_map/while
  1091.0 17.4 copy-start.40
  1201.1 3.8 copy-start.7
  1224.7 36.5 %copy-start.41 = (bf16[2,1024,4,64]{1,3,2,0:T(8,128)(2,1)S(1)}, bf16[2,1024,4,64]{1,3,2,0:T(8,128)(2,1)}, u32[]{:S(2)}) copy-start(bf16[2,1024,4,64]{1,3,2,0:T(8,128)(2,1)} %copy-done.40) | copy-start | bytes 3145732 | tf_op jit(solution)/shard_map/while
  1266.2 118.0 %reduce-scatter.13.cloned.1.call-start = ((), (), s32[]{:S(2)}) async-start(), calls=%async_computation.13 | async-start | bytes 1114112 | tf_op jit(solution)/shard_map/reduce_scatter | solution.py:265
  1266.3 3.7 copy-start.13
  1275.7 184.4 %reduce-scatter.23.cloned.1.call-start = ((), (), s32[]{:S(2)}) async-start(), calls=%async_computation.23 | async-start | bytes 4456448 | tf_op jit(solution)/shard_map/reduce_scatter | solution.py:271
  1283.1 252.7 %reduce-scatter.19.cloned.1.call-start = ((), (), s32[]{:S(2)}) async-start(), calls=%async_computation.19 | async-start | bytes 4456448 | tf_op jit(solution)/shard_map/reduce_scatter | solution.py:269
  1290.1 321.6 %reduce-scatter.21.cloned.1.call-start = ((), (), s32[]{:S(2)}) async-start(), calls=%async_computation.21 | async-start | bytes 4456448 | tf_op jit(solution)/shard_map/reduce_scatter | solution.py:270
  1297.2 378.9 %reduce-scatter.17.cloned.1.call-start = ((), (), s32[]{:S(2)}) async-start(), calls=%async_computation.17 | async-start | bytes 2228224 | tf_op jit(solution)/shard_map/reduce_scatter | solution.py:267
  1305.9 435.4 %reduce-scatter.11.cloned.1.call-start = ((), (), s32[]{:S(2)}) async-start(), calls=%async_computation.11 | async-start | bytes 2228224 | tf_op jit(solution)/shard_map/reduce_scatter | solution.py:264
  1312.6 4.3 copy-start.8
  1312.6 4.3 copy-start.14
  1321.7 4.0 copy-start.33
  1325.4 416.0 %copy-start.43 = (bf16[1024,256]{1,0:T(8,128)(2,1)S(1)}, bf16[1024,256]{1,0:T(8,128)(2,1)}, u32[]{:S(2)}) copy-start(bf16[1024,256]{1,0:T(8,128)(2,1)} %param.25) | copy-start | bytes 1572868
  1325.4 474.8 %reduce-scatter.25.cloned.1.call-start = ((), (), s32[]{:S(2)}) async-start(), calls=%async_computation.25 | async-start | bytes 557056
  1333.1 506.4 %all-gather.13.cloned.1.call-start = ((), (), s32[]{:S(2)}) async-start(), calls=%async_computation.16 | async-start | bytes 1114112 | tf_op jit(solution)/shard_map/all_gather | solution.py:289
  1333.7 545.1 %all-gather.11.cloned.1.call-start = ((), (), s32[]{:S(2)}) async-start(), calls=%async_computation.14 | async-start | bytes 1114112 | tf_op jit(solution)/shard_map/all_gather | solution.py:288
  1384.3 546.3 %all-gather.21.cloned.1.call-start = ((), (), s32[]{:S(2)}) async-start(), calls=%async_computation.24 | async-start | bytes 4456448 | tf_op jit(solution)/shard_map/all_gather | solution.py:294
  1460.1 521.9 %all-gather.17.cloned.1.call-start = ((), (), s32[]{:S(2)}) async-start(), calls=%async_computation.20 | async-start | bytes 4456448 | tf_op jit(solution)/shard_map/all_gather | solution.py:292
  1535.8 497.6 %all-gather.19.cloned.1.call-start = ((), (), s32[]{:S(2)}) async-start(), calls=%async_computation.22 | async-start | bytes 4456448 | tf_op jit(solution)/shard_map/all_gather | solution.py:293
  1611.7 463.8 %all-gather.15.cloned.1.call-start = ((), (), s32[]{:S(2)}) async-start(), calls=%async_computation.18 | async-start | bytes 2228224 | tf_op jit(solution)/shard_map/all_gather | solution.py:290
  1676.1 441.8 %all-gather.9.cloned.1.call-start = ((), (), s32[]{:S(2)}) async-start(), calls=%async_computation.12 | async-start | bytes 2228224 | tf_op jit(solution)/shard_map/all_gather | solution.py:287
  1741.3 576.0 %all-reduce.18.cloned.1.call-start = ((), (), s32[]{:S(2)}) async-start(), calls=%async_computation.10 | async-start | bytes 16777216 | tf_op jit(solution)/shard_map/psum | solution.py:249
  1935.9 381.4 %copy-start.55 = (f32[2048]{0:T(1024)S(1)}, f32[2048]{0:T(1024)}, u32[]{:S(2)}) copy-start(f32[2048]{0:T(1024)} %copy-done.54) | copy-start | bytes 24580
  1935.9 381.4 %copy-start.65 = (f32[1024]{0:T(1024)S(1)}, f32[1024]{0:T(1024)}, u32[]{:S(2)}) copy-start(f32[1024]{0:T(1024)} %copy-done.64) | copy-start | bytes 12292
  2078.4 245.0 %copy-start.59 = (f32[2048]{0:T(1024)S(1)}, f32[2048]{0:T(1024)}, u32[]{:S(2)}) copy-start(f32[2048]{0:T(1024)} %copy-done.58) | copy-start | bytes 24580
  2078.4 245.1 %copy-start.69 = (f32[1024]{0:T(1024)S(1)}, f32[1024]{0:T(1024)}, u32[]{:S(2)}) copy-start(f32[1024]{0:T(1024)} %get-tuple-element.254) | copy-start | bytes 12292
  2388.0 11.7 copy-start.35
  2399.8 4.2 copy-start.30
  2403.9 3.7 copy-start.31
  2403.9 5.7 copy-start.1
  (38 other events, 58.5 us)
Sparse Core Ops, SparseCore 0:
  195.0 200.6 all-reduce.13
  512.2 200.2 all-reduce.19
  715.5 107.8 all-reduce.15
  1266.4 57.4 reduce-scatter.14
  1327.9 56.3 reduce-scatter.12
  1388.5 71.5 reduce-scatter.22
  1463.9 71.7 reduce-scatter.18
  1540.1 71.5 reduce-scatter.20
  1615.4 60.6 reduce-scatter.16
  1680.7 60.5 reduce-scatter.10
  1745.4 54.6 reduce-scatter.24
  1802.4 37.0 all-gather.12
  1841.9 36.8 all-gather.10
  1881.1 49.4 all-gather.20
  1932.9 49.0 all-gather.16
  1984.2 49.0 all-gather.18
  2035.6 39.8 all-gather.14
  2077.7 40.1 all-gather.8
  2120.5 196.7 all-reduce.17
where the time goes:
time: 2430 us; the launch traced here: 2420 us
  waiting for transfers between devices  1310 us (54%)
  matrix products  451 us (19%)
  local copies, waits for them, and re-layouts  371 us (15%)
  other arithmetic  176 us (7%)
  blocking collectives  84.8 us (3%)
    psum x1, waiting for transfers between devices, per_device(): first_grad = lax.psum(first_grad_part, 'tensor')  199 us
    psum x1, waiting for transfers between devices, per_device(): lax.psum((second_grad_part, gate_grad_part), 'tensor')  159 us
    dynamic_update_slice x8, local copies, waits for them, and re-layouts, per_device(): lax.map(attend_backward, (query_heads, key_heads, value_heads, seg_rows,...  120 us
    psum x1, waiting for transfers between devices, per_device(): attn_full = lax.psum(attn_part, 'tensor')  116 us
    psum x1, waiting for transfers between devices, per_device(): lax.psum(moe_part.astype(jnp.bfloat16), 'tensor').astype(jnp.float32)  97.1 us
    dot_general x2, matrix products, attend_backward(): jnp.einsum('kgqs,qkgd->skd', raw_grad, queries, preferred_element_type=jn...  93.2 us
    dot_general x2, matrix products, attend_backward(): jnp.einsum('kgqs,skd->qkgd', raw_grad, keys, preferred_element_type=jnp.f...  92.2 us
    reduce_scatter x1, waiting for transfers between devices, per_device(): lax.psum_scatter(grad_up, 'dp', scatter_dimension=1, tiled=True)  75.9 us
  transfers between devices with their start and end apart: 19, of which 18 were waited for; matrix products, arithmetic and copies ran while one was open for 9% of the time, Pallas kernels for 0%

commit v1 on v0

v1 whole, which is shorter than its diff:
```python
from functools import partial

import jax
import jax.numpy as jnp
from jax import lax
from jax.experimental import pallas as pl
from jax.experimental.pallas import tpu as pltpu
from jax.sharding import PartitionSpec as P

HEAD_DIM = 64
SEQ_LEN = 1024
CAP = 256
EPS = 1e-06
THETA = 10000.0
NEG = -1e30
BLOCK = 256
LANES = 128
GROUP = 4 * HEAD_DIM

f32 = jnp.float32
bf16 = jnp.bfloat16


def nn(left, right):
    return lax.dot_general(left, right, (((1,), (0,)), ((), ())), preferred_element_type=f32)


def nt(left, right):
    return lax.dot_general(left, right, (((1,), (1,)), ((), ())), preferred_element_type=f32)


def tn(left, right):
    return lax.dot_general(left, right, (((0,), (0,)), ((), ())), preferred_element_type=f32)


def params(count=1):
    return pltpu.CompilerParams(
        dimension_semantics=("arbitrary",) * count, vmem_limit_bytes=56 * 1024 * 1024
    )


def whole(shape):
    return pl.BlockSpec(shape, lambda *_: (0,) * len(shape))


def lane_iota(rows, lanes=LANES):
    return lax.broadcasted_iota(jnp.int32, (rows, lanes), 1)


def prologue_kernel(x_ref, gain_ref, seg_ref, freq_ref, first_ref, first_t_ref, cos_ref, up_ref, down_ref):
    rows = x_ref.shape[0]
    values = x_ref[...].astype(f32)
    scale = lax.rsqrt(jnp.mean(values * values, axis=-1, keepdims=True) + EPS)
    normed = values * scale * gain_ref[...].astype(f32)
    first_ref[...] = normed.astype(bf16)
    first_t_ref[...] = normed.astype(bf16).T
    seg = seg_ref[...]
    zeros = jnp.sum((seg == 0).astype(f32), axis=1, keepdims=True)
    ones = jnp.sum((seg == 1).astype(f32), axis=1, keepdims=True)
    places = lax.broadcasted_iota(jnp.int32, (1, rows), 1).astype(f32)
    places = places - jnp.where(seg >= 1, zeros, 0.0) - jnp.where(seg >= 2, ones, 0.0)
    angles = freq_ref[:, 0:1] * places
    cosine = jnp.cos(angles)
    sine = jnp.sin(angles)
    cosine = jnp.concatenate([cosine] * 4, axis=0).T
    sine = jnp.concatenate([sine] * 4, axis=0).T
    lower = (lane_iota(rows) % HEAD_DIM) < HEAD_DIM // 2
    cos_ref[...] = cosine
    up_ref[...] = jnp.where(lower, -sine, 0.0)
    down_ref[...] = jnp.where(lower, 0.0, sine)


def prologue(x, gain, seg_row, freq):
    rows, width = x.shape
    table = jax.ShapeDtypeStruct((rows, LANES), f32)
    return pl.pallas_call(
        prologue_kernel,
        out_shape=(
            jax.ShapeDtypeStruct((rows, width), bf16),
            jax.ShapeDtypeStruct((width, rows), bf16),
            table,
            table,
            table,
        ),
        compiler_params=pltpu.CompilerParams(vmem_limit_bytes=56 * 1024 * 1024),
        name="prologue",
    )(x, gain, seg_row, freq)


def rotate(values, cosine, up, down):
    return (
        values * cosine
        + pltpu.roll(values, LANES - 32, 1) * up
        + pltpu.roll(values, 32, 1) * down
    )


def rotate_back(values, cosine, up, down):
    return (
        values * cosine
        - pltpu.roll(values, LANES - 32, 1) * up
        - pltpu.roll(values, 32, 1) * down
    )


def doubled(values):
    turned = pltpu.roll(values, HEAD_DIM, 1)
    left = lane_iota(values.shape[0]) < HEAD_DIM
    return (
        jnp.where(left, values, turned).astype(bf16),
        jnp.where(left, turned, values).astype(bf16),
    )


def halves_mask():
    left = (lane_iota(1) < HEAD_DIM).astype(f32)
    return left.astype(bf16), (1.0 - left).astype(bf16)


def attend_kernel(
    first_ref, wq_ref, wk_ref, wv_ref, cos_ref, up_ref, down_ref, segc_ref, segr_ref,
    q_ref, k_ref, v_ref, att_ref, lse_ref, bias_ref,
):
    rows = first_ref.shape[0]

    @pl.when(pl.program_id(0) == 0)
    def _():
        for start in range(0, rows, BLOCK):
            at_row = lax.broadcasted_iota(jnp.int32, (BLOCK, rows), 0) + start
            at_col = lax.broadcasted_iota(jnp.int32, (BLOCK, rows), 1)
            allowed = (at_col <= at_row) & (segc_ref[start : start + BLOCK, :] == segr_ref[...])
            bias_ref[start : start + BLOCK, :] = jnp.where(allowed, 0.0, NEG)

    first = first_ref[...]
    cosine, up, down = cos_ref[...], up_ref[...], down_ref[...]
    for tile in range(2):
        part = slice(tile * LANES, (tile + 1) * LANES)
        raw = nn(first, wq_ref[:, part])
        q_ref[:, part] = (rotate(raw, cosine, up, down) * HEAD_DIM**-0.5).astype(bf16)
    key = rotate(nn(first, wk_ref[...]), cosine, up, down)
    value = nn(first, wv_ref[...])
    k_ref[...] = key.astype(bf16)
    v_ref[...] = value.astype(bf16)
    keys, values = doubled(key), doubled(value)
    low, high = halves_mask()
    for start in range(0, rows, BLOCK):
        width = start + BLOCK
        mine = slice(start, width)
        bias = bias_ref[mine, :width]
        bias = jnp.concatenate([bias, bias], axis=0)
        logs = jnp.zeros((BLOCK, LANES), f32)
        lanes = lane_iota(BLOCK)
        for kv in range(2):
            part = slice(kv * LANES, (kv + 1) * LANES)
            query = q_ref[mine, part]
            query = jnp.concatenate([query * low, query * high], axis=0)
            scores = nt(query, keys[kv][:width]) + bias
            row_max = jnp.max(scores, axis=-1, keepdims=True)
            weights = jnp.exp(scores - row_max)
            total = jnp.sum(weights, axis=-1, keepdims=True)
            probs = (weights * (1.0 / total)).astype(bf16)
            out = nn(probs, values[kv][:width])
            att_ref[mine, part] = jnp.where(lanes < HEAD_DIM, out[:BLOCK], out[BLOCK:]).astype(bf16)
            log_total = row_max + jnp.log(total)
            logs = jnp.where(lanes == 2 * kv, log_total[:BLOCK], logs)
            logs = jnp.where(lanes == 2 * kv + 1, log_total[BLOCK:], logs)
        lse_ref[0, :, mine] = logs.T[:8]


def attend(first, wq, wk, wv, tables, seg_col, seg_row):
    rows, width = first.shape
    groups = wq.shape[1] // GROUP
    table = whole((rows, LANES))
    return pl.pallas_call(
        attend_kernel,
        grid=(groups,),
        in_specs=[
            whole((rows, width)),
            pl.BlockSpec((width, GROUP), lambda g: (0, g)),
            pl.BlockSpec((width, LANES), lambda g: (0, g)),
            pl.BlockSpec((width, LANES), lambda g: (0, g)),
            table,
            table,
            table,
            whole((rows, 1)),
            whole((1, rows)),
        ],
        out_specs=[
            pl.BlockSpec((rows, GROUP), lambda g: (0, g)),
            pl.BlockSpec((rows, LANES), lambda g: (0, g)),
            pl.BlockSpec((rows, LANES), lambda g: (0, g)),
            pl.BlockSpec((rows, GROUP), lambda g: (0, g)),
            pl.BlockSpec((1, 8, rows), lambda g: (g, 0, 0)),
        ],
        out_shape=(
            jax.ShapeDtypeStruct((rows, groups * GROUP), bf16),
            jax.ShapeDtypeStruct((rows, groups * LANES), bf16),
            jax.ShapeDtypeStruct((rows, groups * LANES), bf16),
            jax.ShapeDtypeStruct((rows, groups * GROUP), bf16),
            jax.ShapeDtypeStruct((groups, 8, rows), f32),
        ),
        scratch_shapes=[pltpu.VMEM((rows, rows), f32)],
        compiler_params=params(),
        name="attend",
    )(first, wq, wk, wv, *tables, seg_col, seg_row)


def router_kernel(
    x_ref, att_a_ref, att_b_ref, wo_a_ref, wo_b_ref, gain_ref, wr_ref, routes_ref, slots_ref,
    resid_ref, second_ref, gates_ref, places_ref,
):
    resid = x_ref[...].astype(f32) + (nn(att_a_ref[...], wo_a_ref[...]) + nn(att_b_ref[...], wo_b_ref[...]))
    resid_ref[...] = resid
    scale = lax.rsqrt(jnp.mean(resid * resid, axis=-1, keepdims=True) + EPS)
    second = (resid * scale * gain_ref[...].astype(f32)).astype(bf16)
    second_ref[...] = second
    logits = nt(wr_ref[...], second)
    experts, rows = logits.shape
    routes, slots = routes_ref[...], slots_ref[...]
    number = lax.broadcasted_iota(jnp.int32, (experts, rows), 0)
    chosen = jnp.zeros((experts, rows), f32)
    place = jnp.zeros((8, rows), jnp.int32)
    taken = jnp.zeros((8, rows), jnp.int32)
    for k in range(routes.shape[0]):
        hit = number == routes[k : k + 1, :]
        chosen = jnp.where(hit, 1.0, chosen)
        hit = number[:8] == routes[k : k + 1, :]
        place = jnp.where(hit, slots[k : k + 1, :], place)
        taken = jnp.where(hit, 1, taken)
    places_ref[...] = jnp.where(taken > 0, place, CAP)
    top = jnp.max(jnp.where(chosen > 0, logits, NEG), axis=0, keepdims=True)
    weights = jnp.where(chosen > 0, jnp.exp(logits - top), 0.0)
    gates_ref[...] = weights / jnp.sum(weights, axis=0, keepdims=True)


def router(x, att_a, att_b, wo_a, wo_b, gain, wr_t, routes_t, slots_t):
    rows, width = x.shape
    return pl.pallas_call(
        router_kernel,
        out_shape=(
            jax.ShapeDtypeStruct((rows, width), f32),
            jax.ShapeDtypeStruct((rows, width), bf16),
            jax.ShapeDtypeStruct((wr_t.shape[0], rows), f32),
            jax.ShapeDtypeStruct((8, rows), jnp.int32),
        ),
        compiler_params=pltpu.CompilerParams(vmem_limit_bytes=56 * 1024 * 1024),
        name="router",
    )(x, att_a, att_b, wo_a, wo_b, gain, wr_t, routes_t, slots_t)


def split_three(values):
    first = values.astype(bf16)
    rest = values - first.astype(f32)
    second = rest.astype(bf16)
    return first, second, (rest - second.astype(f32)).astype(bf16)


def experts_kernel(
    second_ref, cot_ref, resid_ref, gates_ref, places_ref, gain_ref, wr_ref,
    wg_a_ref, wg_b_ref, wu_a_ref, wu_b_ref, wd_a_ref, wd_b_ref,
    out_ref, low_ref, grad_ref, small_ref,
    gg_a_ref, gg_b_ref, gu_a_ref, gu_b_ref, gd_a_ref, gd_b_ref,
    moe_ref, back_ref, slot_grads_ref,
):
    e = pl.program_id(0)
    rows = second_ref.shape[0]
    second = second_ref[...]
    slots = lax.broadcasted_iota(jnp.int32, (CAP, rows), 0)
    hit = slots == places_ref[pl.ds(e, 1), :]
    gate_slot = jnp.sum(jnp.where(hit, gates_ref[pl.ds(e, 1), :], 0.0), axis=1, keepdims=True)
    onehot = jnp.where(hit, 1.0, 0.0).astype(bf16)
    expert_in = nn(onehot, second).astype(bf16)
    slot_grad = nn(onehot, cot_ref[...])
    out_grad = (gate_slot * slot_grad).astype(bf16)
    expert_out = None
    back = None
    for wg_ref, wu_ref, wd_ref, gg_ref, gu_ref, gd_ref in (
        (wg_a_ref, wu_a_ref, wd_a_ref, gg_a_ref, gu_a_ref, gd_a_ref),
        (wg_b_ref, wu_b_ref, wd_b_ref, gg_b_ref, gu_b_ref, gd_b_ref),
    ):
        wg, wu, wd = wg_ref[0], wu_ref[0], wd_ref[0]
        gate_pre = nn(expert_in, wg)
        up_pre = nn(expert_in, wu)
        sig = 1.0 / (1.0 + jnp.exp(-gate_pre))
        silu = gate_pre * sig
        hidden = (silu * up_pre).astype(bf16)
        part = nn(hidden, wd)
        expert_out = part if expert_out is None else expert_out + part
        hidden_grad = nt(out_grad, wd)
        gd_ref[0] = tn(hidden, out_grad).astype(bf16)
        gate_low = (hidden_grad * up_pre * sig * (1.0 + gate_pre * (1.0 - sig))).astype(bf16)
        up_low = (hidden_grad * silu).astype(bf16)
        gg_ref[0] = tn(expert_in, gate_low).astype(bf16)
        gu_ref[0] = tn(expert_in, up_low).astype(bf16)
        part = nt(gate_low, wg) + nt(up_low, wu)
        back = part if back is None else back + part
    slot_gate = jnp.sum(expert_out * slot_grad, axis=1, keepdims=True)
    gate_row = jnp.sum(jnp.where(hit, slot_gate, 0.0), axis=0, keepdims=True)
    moe = tn(onehot, (gate_slot * expert_out).astype(bf16))
    second_back = tn(onehot, back.astype(bf16))

    @pl.when(e == 0)
    def _():
        moe_ref[...] = moe
        back_ref[...] = second_back
        slot_grads_ref[...] = jnp.zeros_like(slot_grads_ref)

    @pl.when(e > 0)
    def _():
        moe_ref[...] += moe
        back_ref[...] += second_back

    slot_grads_ref[pl.ds(e, 1), :] = gate_row

    @pl.when(e == pl.num_programs(0) - 1)
    def _():
        gates = gates_ref[...]
        resid = resid_ref[...]
        out_ref[...] = (resid + moe_ref[...]).astype(bf16)
        gate_grad = slot_grads_ref[...]
        logit_grad = gates * (gate_grad - jnp.sum(gates * gate_grad, axis=0, keepdims=True))
        router_grad = None
        second_grad = back_ref[...]
        for piece in split_three(logit_grad):
            part = nn(piece, second)
            router_grad = part if router_grad is None else router_grad + part
            second_grad = second_grad + tn(piece, wr_ref[...])
        experts = gates.shape[0]
        small_ref[0:experts, :] = router_grad
        gain = gain_ref[...].astype(f32)
        scale = lax.rsqrt(jnp.mean(resid * resid, axis=-1, keepdims=True) + EPS)
        norm_grad = jnp.sum(second_grad * resid * scale, axis=0, keepdims=True)
        small_ref[experts : experts + 8, :] = jnp.where(
            lax.broadcasted_iota(jnp.int32, (8, resid.shape[1]), 0) == 0, norm_grad, 0.0
        )
        inner = jnp.mean(gain * second_grad * resid, axis=-1, keepdims=True)
        grad = scale * gain * second_grad - resid * (scale * scale * scale) * inner
        grad = grad + cot_ref[...].astype(f32)
        grad_ref[...] = grad
        low_ref[...] = grad.astype(bf16)


def experts_layer(second, cot, resid, gates, places, gain, wr_t, weights):
    rows, width = second.shape
    experts = gates.shape[0]
    window, _, hidden = weights[0].shape
    wide = pl.BlockSpec((1, width, hidden), lambda e: (e, 0, 0))
    tall = pl.BlockSpec((1, hidden, width), lambda e: (e, 0, 0))
    wide_out = jax.ShapeDtypeStruct((window, width, hidden), bf16)
    tall_out = jax.ShapeDtypeStruct((window, hidden, width), bf16)
    return pl.pallas_call(
        experts_kernel,
        grid=(window,),
        in_specs=[
            whole((rows, width)),
            whole((rows, width)),
            whole((rows, width)),
            whole((experts, rows)),
            whole((8, rows)),
            whole((1, width)),
            whole((experts, width)),
            wide,
            wide,
            wide,
            wide,
            tall,
            tall,
        ],
        out_specs=[
            whole((rows, width)),
            whole((rows, width)),
            whole((rows, width)),
            whole((experts + 8, width)),
            wide,
            wide,
            wide,
            wide,
            tall,
            tall,
        ],
        out_shape=(
            jax.ShapeDtypeStruct((rows, width), bf16),
            jax.ShapeDtypeStruct((rows, width), bf16),
            jax.ShapeDtypeStruct((rows, width), f32),
            jax.ShapeDtypeStruct((experts + 8, width), f32),
            wide_out,
            wide_out,
            wide_out,
            wide_out,
            tall_out,
            tall_out,
        ),
        scratch_shapes=[
            pltpu.VMEM((rows, width), f32),
            pltpu.VMEM((rows, width), f32),
            pltpu.VMEM((experts, rows), f32),
        ],
        compiler_params=params(),
        name="experts",
    )(second, cot, resid, gates, places, gain, wr_t, *weights)


def attend_back_kernel(
    final,
    q_ref, k_ref, v_ref, att_ref, lse_ref, cos_ref, up_ref, down_ref, segc_ref, segr_ref,
    low_ref, wo_ref, first_t_ref, wq_ref, wk_ref, wv_ref, *rest,
):
    if final:
        (before_ref, x_ref, gain_ref, grad_ref, gq_ref, gk_ref, gv_ref, go_ref, token_ref, norm_ref,
         bias_ref, sum_ref, dq_ref, dk_ref, dv_ref) = rest
    else:
        gq_ref, gk_ref, gv_ref, go_ref, sum_ref, bias_ref, dq_ref, dk_ref, dv_ref = rest
    rows = q_ref.shape[0]
    g = pl.program_id(0)

    @pl.when(g == 0)
    def _():
        for start in range(0, rows, BLOCK):
            at_key = lax.broadcasted_iota(jnp.int32, (BLOCK, rows), 0) + start
            at_query = lax.broadcasted_iota(jnp.int32, (BLOCK, rows), 1)
            allowed = (at_key <= at_query) & (segc_ref[start : start + BLOCK, :] == segr_ref[...])
            bias_ref[start : start + BLOCK, :] = jnp.where(allowed, 0.0, NEG)
        if final:
            sum_ref[...] = before_ref[...]
        else:
            sum_ref[...] = jnp.zeros_like(sum_ref)

    low_grad = low_ref[...]
    go_ref[...] = tn(att_ref[...], low_grad).astype(bf16)
    upward = nt(low_grad, wo_ref[...]).astype(bf16)
    keys = doubled(k_ref[...].astype(f32))
    values = doubled(v_ref[...].astype(f32))
    low, high = halves_mask()
    dk_ref[...] = jnp.zeros_like(dk_ref)
    dv_ref[...] = jnp.zeros_like(dv_ref)
    lanes = lane_iota(BLOCK)
    for start in range(0, rows, BLOCK):
        width = start + BLOCK
        mine = slice(start, width)
        bias = bias_ref[:width, mine]
        bias = jnp.concatenate([bias, bias], axis=1)
        for kv in range(2):
            part = slice(kv * LANES, (kv + 1) * LANES)
            query = q_ref[mine, part]
            query = jnp.concatenate([query * low, query * high], axis=0)
            upper = upward[mine, part]
            upper = jnp.concatenate([upper * low, upper * high], axis=0)
            logs = jnp.concatenate(
                [lse_ref[0, 2 * kv : 2 * kv + 1, mine], lse_ref[0, 2 * kv + 1 : 2 * kv + 2, mine]], axis=1
            )
            key = keys[kv][:width]
            probs = jnp.exp(nt(key, query) + bias - logs)
            prob_grad = nt(values[kv][:width], upper)
            product = probs * prob_grad
            delta = jnp.sum(product, axis=0, keepdims=True)
            raw = (product - probs * delta).astype(bf16)
            dv_ref[kv, :width, :] += nn(probs.astype(bf16), upper)
            dk_ref[kv, :width, :] += nn(raw, query)
            back = tn(raw, key)
            dq_ref[mine, part] = jnp.where(lanes < HEAD_DIM, back[:BLOCK], back[BLOCK:])
    cosine, up, down = cos_ref[...], up_ref[...], down_ref[...]
    left = lane_iota(rows) < HEAD_DIM

    def both(ref):
        one, two = ref[0], ref[1]
        one = one + pltpu.roll(one, HEAD_DIM, 1)
        two = two + pltpu.roll(two, HEAD_DIM, 1)
        return jnp.where(left, one, two)

    first_t = first_t_ref[...]
    key_back = rotate_back(both(dk_ref), cosine, up, down).astype(bf16)
    value_back = both(dv_ref).astype(bf16)
    query_back = jnp.concatenate(
        [
            (rotate_back(dq_ref[:, :LANES], cosine, up, down) * HEAD_DIM**-0.5).astype(bf16),
            (rotate_back(dq_ref[:, LANES:], cosine, up, down) * HEAD_DIM**-0.5).astype(bf16),
        ],
        axis=1,
    )
    gq_ref[...] = nn(first_t, query_back).astype(bf16)
    gk_ref[...] = nn(first_t, key_back).astype(bf16)
    gv_ref[...] = nn(first_t, value_back).astype(bf16)
    sum_ref[...] += nt(query_back, wq_ref[...]) + nt(key_back, wk_ref[...]) + nt(value_back, wv_ref[...])

    if final:

        @pl.when(g == pl.num_programs(0) - 1)
        def _():
            values = x_ref[...].astype(f32)
            first_grad = sum_ref[...]
            gain = gain_ref[...].astype(f32)
            scale = lax.rsqrt(jnp.mean(values * values, axis=-1, keepdims=True) + EPS)
            norm_ref[...] = jnp.broadcast_to(
                jnp.sum(first_grad * values * scale, axis=0, keepdims=True), norm_ref.shape
            )
            inner = jnp.mean(gain * first_grad * values, axis=-1, keepdims=True)
            grad = scale * gain * first_grad - values * (scale * scale * scale) * inner
            token_ref[...] = (grad + grad_ref[...]).astype(bf16)


def attend_back(saved, tables, seg_col, seg_row, low_grad, wo, first_t, wq, wk, wv, final=None):
    query, key, value, att, logs = saved
    rows = query.shape[0]
    width = wq.shape[0]
    groups = query.shape[1] // GROUP
    table = whole((rows, LANES))
    wide = pl.BlockSpec((rows, GROUP), lambda g: (0, g))
    thin = pl.BlockSpec((rows, LANES), lambda g: (0, g))
    wide_w = pl.BlockSpec((width, GROUP), lambda g: (0, g))
    thin_w = pl.BlockSpec((width, LANES), lambda g: (0, g))
    tall_w = pl.BlockSpec((GROUP, width), lambda g: (g, 0))
    square = whole((rows, width))
    in_specs = [
        wide, thin, thin, wide, pl.BlockSpec((1, 8, rows), lambda g: (g, 0, 0)),
        table, table, table, whole((rows, 1)), whole((1, rows)),
        square, tall_w, whole((width, rows)), wide_w, thin_w, thin_w,
    ]
    out_specs = [wide_w, thin_w, thin_w, tall_w]
    out_shape = [
        jax.ShapeDtypeStruct((width, groups * GROUP), bf16),
        jax.ShapeDtypeStruct((width, groups * LANES), bf16),
        jax.ShapeDtypeStruct((width, groups * LANES), bf16),
        jax.ShapeDtypeStruct((groups * GROUP, width), bf16),
    ]
    scratch = [pltpu.VMEM((rows, rows), f32)]
    extra = ()
    if final is None:
        out_specs.append(square)
        out_shape.append(jax.ShapeDtypeStruct((rows, width), f32))
    else:
        extra = final
        in_specs += [square, square, whole((1, width)), square]
        out_specs += [square, whole((8, width))]
        out_shape += [
            jax.ShapeDtypeStruct((rows, width), bf16),
            jax.ShapeDtypeStruct((8, width), f32),
        ]
        scratch.append(pltpu.VMEM((rows, width), f32))
    scratch += [
        pltpu.VMEM((rows, GROUP), f32),
        pltpu.VMEM((2, rows, LANES), f32),
        pltpu.VMEM((2, rows, LANES), f32),
    ]
    return pl.pallas_call(
        partial(attend_back_kernel, final is not None),
        grid=(groups,),
        in_specs=in_specs,
        out_specs=out_specs,
        out_shape=tuple(out_shape),
        scratch_shapes=scratch,
        compiler_params=params(),
        name="attend_back_final" if final is not None else "attend_back",
    )(query, key, value, att, logs, *tables, seg_col, seg_row, low_grad, wo, first_t, wq, wk, wv, *extra)


def swap_tensor(values):
    return lax.ppermute(values, "tensor", [(0, 1), (1, 0)])


def swap_dp(values, bit):
    count = lax.axis_size("dp")
    return lax.ppermute(values, "dp", [(i, i ^ bit) for i in range(count)])


def after(values, earlier):
    return lax.optimization_barrier((values, earlier))[0]


def fetch_half(weights, core):
    pieces = [
        lax.dynamic_slice_in_dim(w, core * (w.shape[0] // 2), w.shape[0] // 2, 0) for w in weights
    ]
    got = [swap_tensor(p) for p in pieces]
    return got


def join_cores(got, core):
    other = [swap_dp(p, 1) for p in got]
    return [
        jnp.where(core == 0, jnp.concatenate([a, b], 0), jnp.concatenate([b, a], 0))
        for a, b in zip(got, other)
    ]


def per_device(
    tokens, cotangent, segments, routes, slot_index,
    w_query, w_key, w_value, w_output, norm_attn, norm_ffn, w_router, w_gate, w_up, w_down,
):
    length, width = tokens.shape
    side = lax.axis_index("tensor")
    core = lax.axis_index("dp") % 2
    rows = SEQ_LEN

    def own(values):
        return lax.dynamic_slice_in_dim(values, side * rows, rows, 0)

    got_one = fetch_half((w_query, w_key, w_value), core)
    r_query, r_key, r_value = join_cores(got_one, core)
    got_two = fetch_half(after((w_output,), got_one[0]), core)
    (r_output,) = join_cores(got_two, core)
    got_three = fetch_half(after((w_gate, w_up, w_down), got_two[0]), core)
    r_gate, r_up, r_down = join_cores(got_three, core)

    x = own(tokens)
    cot = own(cotangent)
    seg = own(segments)
    seg_row, seg_col = seg[None, :], seg[:, None]
    routes_t = own(routes).T
    slots_t = own(slot_index).T
    wr_t = w_router.T
    gain_one, gain_two = norm_attn[None, :], norm_ffn[None, :]
    half_dim = HEAD_DIM // 2
    frequency = THETA ** (-(2.0 * jnp.arange(half_dim, dtype=f32)) / HEAD_DIM)
    freq = jnp.broadcast_to(frequency[:, None], (half_dim, LANES))

    first, first_t, *tables = prologue(x, gain_one, seg_row, freq)
    saved_a = attend(first, w_query, w_key, w_value, tables, seg_col, seg_row)
    saved_b = attend(first, r_query, r_key, r_value, tables, seg_col, seg_row)
    resid, second, gates, places = router(
        x, saved_a[3], saved_b[3], w_output, r_output, gain_two, wr_t, routes_t, slots_t
    )
    (out, low_grad, resid_grad, small, gg_a, gg_b, gu_a, gu_b, gd_a, gd_b) = experts_layer(
        second, cot, resid, gates, places, gain_two, wr_t,
        (w_gate, r_gate, w_up, r_up, w_down, r_down),
    )

    def finish(mine, theirs):
        total = mine.astype(f32) + swap_tensor(theirs).astype(f32)
        return lax.psum(total.astype(bf16), "dp").astype(f32)

    grad_gate = finish(gg_a, gg_b)
    grad_up = finish(gu_a, gu_b)
    grad_down = finish(gd_a, gd_b)
    out_other = swap_tensor(out)

    gq_b, gk_b, gv_b, go_b, partial_sum = attend_back(
        saved_b, tables, seg_col, seg_row, low_grad, r_output, first_t, r_query, r_key, r_value
    )
    gq_a, gk_a, gv_a, go_a, token, norm_one = attend_back(
        saved_a, tables, seg_col, seg_row, low_grad, w_output, first_t, w_query, w_key, w_value,
        final=(partial_sum, x, gain_one, resid_grad),
    )
    token_other = swap_tensor(token)
    grad_query = finish(gq_a, gq_b)
    grad_key = finish(gk_a, gk_b)
    grad_value = finish(gv_a, gv_b)
    grad_output = finish(go_a, go_b)
    packed = lax.psum(jnp.concatenate([small, norm_one], 0), ("dp", "tensor"))
    experts = w_router.shape[1]
    grad_router = packed[:experts].T
    grad_norm_ffn = packed[experts]
    grad_norm_attn = packed[experts + 8]

    def both(mine, other):
        return jnp.where(side == 0, jnp.concatenate([mine, other], 0), jnp.concatenate([other, mine], 0))

    return (
        both(out, out_other),
        both(token, token_other).astype(f32),
        grad_query,
        grad_key,
        grad_value,
        grad_output,
        grad_norm_attn,
        grad_norm_ffn,
        grad_router,
        grad_gate,
        grad_up,
        grad_down,
    )


def solution(mesh):
    placed = (
        P("dp", None), P("dp", None), P("dp"), P("dp", None), P("dp", None),
        P(None, "tensor"), P(None, "tensor"), P(None, "tensor"), P("tensor", None),
        P(), P(), P(),
        P(None, None, "tensor"), P(None, None, "tensor"), P(None, "tensor", None),
    )
    return jax.shard_map(
        per_device,
        mesh=mesh,
        in_specs=placed,
        out_specs=(
            P("dp", None), P("dp", None),
            P(None, "tensor"), P(None, "tensor"), P(None, "tensor"), P("tensor", None),
            P(), P(), P(),
            P(None, None, "tensor"), P(None, None, "tensor"), P(None, "tensor", None),
        ),
        check_vma=False,
    )
```

time: 2430 us -> 698 us (0.29)
  waiting for transfers between devices: 1310 us -> 410 us
  matrix products: 451 us -> 0 us
  local copies, waits for them, and re-layouts: 371 us -> 18.6 us
  Pallas kernels: 0 us -> 166 us
  other arithmetic: 176 us -> 62.1 us
  blocking collectives: 84.8 us -> 0 us
    dot_general x37 -> x0, matrix products: 444 us -> none  [the longest x2 93.2 us: attend_backward(): jnp.einsum('kgqs,qkgd->skd', raw_grad, queries, preferred_element_type=jn...]
    psum x4 -> x2, waiting for transfers between devices: 572 us -> 147 us  [the longest x1 122 us: finish(): return lax.psum(total.astype(bf16), 'dp').astype(f32)]
    reduce_scatter x7 -> x0, waiting for transfers between devices: 407 us -> none  [the longest x1 75.9 us: per_device(): lax.psum_scatter(grad_up, 'dp', scatter_dimension=1, tiled=True)]
    all_gather x7 -> x0, waiting for transfers between devices: 287 us -> none  [the longest x1 51.8 us: per_device(): lax.all_gather(part_down, 'dp', axis=2, tiled=True)]
    ppermute x0 -> x23, waiting for transfers between devices: none -> 263 us  [the longest x16 263 us: swap_tensor(): return lax.ppermute(values, 'tensor', [(0, 1), (1, 0)])]
    pallas_call x0 -> x7, Pallas kernels: none -> 166 us  [the longest x2 73.3 us: attend_back(): pl.pallas_call(partial(attend_back_kernel, final is not None), grid=(grou...]
    dynamic_update_slice x12 -> x0, local copies, waits for them, and re-layouts: 125 us -> none  [the longest x8 120 us: per_device(): lax.map(attend_backward, (query_heads, key_heads, value_heads, seg_rows,...]
    unnamed x2 -> x0, blocking collectives: 64.2 us -> none
  transfers between devices with their start and end apart: 19 -> 25, of which waited for: 18 -> 13; matrix products, arithmetic and copies ran while one was open for 9% -> 9% of each run, Pallas kernels for 0% -> 18%
where the time goes in v1:
time: 698 us; the launch traced here: 693 us
  waiting for transfers between devices  410 us (59%)
  Pallas kernels  166 us (24%)
  other arithmetic  62.1 us (9%)
  starting transfers between devices  21.8 us (3%)
  local copies, waits for them, and re-layouts  18.6 us (3%)
  between operations  14.7 us (2%)
    ppermute x16, waiting for transfers between devices, swap_tensor(): return lax.ppermute(values, 'tensor', [(0, 1), (1, 0)])  263 us
    psum x1, waiting for transfers between devices, finish(): return lax.psum(total.astype(bf16), 'dp').astype(f32)  122 us
    pallas_call x2, Pallas kernels, attend_back(): pl.pallas_call(partial(attend_back_kernel, final is not None), grid=(grou...  73.3 us
    pallas_call x2, Pallas kernels, attend(): pl.pallas_call(attend_kernel, grid=(groups,), in_specs=[whole((rows, widt...  40.3 us
    pallas_call x1, Pallas kernels, experts_layer(): pl.pallas_call(experts_kernel, grid=(window,), in_specs=[whole((rows, wid...  39.2 us
    convert_element_type x14, other arithmetic, finish(): return lax.psum(total.astype(bf16), 'dp').astype(f32)  31.3 us
    psum x1, waiting for transfers between devices, per_device(): packed = lax.psum(jnp.concatenate([small, norm_one], 0), ('dp', 'tensor'))  24.4 us
    ppermute x16, starting transfers between devices, swap_tensor(): return lax.ppermute(values, 'tensor', [(0, 1), (1, 0)])  20.1 us
  transfers between devices with their start and end apart: 25, of which 13 were waited for; matrix products, arithmetic and copies ran while one was open for 9% of the time, Pallas kernels for 18%

profile of v1, /device:TPU:0, one launch (start us, length us, event | category | flops | bytes accessed | tf_op | source)
XLA Modules:
  0.0 693.3 jit_solution(4129962520341569740)
XLA Ops:
  7.3 1.2 constant_dynamic-slice_fusion.7
  8.5 3.0 collective-permute-start
  11.5 11.9 %collective-permute-done = bf16[512,512]{1,0:T(8,128)(2,1)S(1)} collective-permute-done((bf16[512,512]{1,0:T(8,128)(2,1)S(1)}, bf16[512,512]{1,0:T(8,128)(2,1)S(1)}, u32[]{:S(2)}, u32[]{:S(2)}) %collective-permute-start) | collective-permute-done | bytes 524320 | tf_op jit(solution)/shard_map/ppermute | solution.py:557
  23.4 1.3 constant_dynamic-slice_fusion.4
  24.7 1.8 collective-permute-start.6
  26.5 11.5 %collective-permute-done.6 = bf16[256,1024]{1,0:T(8,128)(2,1)} collective-permute-done((bf16[256,1024]{1,0:T(8,128)(2,1)S(1)}, bf16[256,1024]{1,0:T(8,128)(2,1)}, u32[]{:S(2)}, u32[]{:S(2)}) %collective-permute-start.6) | collective-permute-done | bytes 524320 | tf_op jit(solution)/shard_map/ppermute | solution.py:557
  38.0 2.3 constant_dynamic-slice_fusion
  40.2 1.4 collective-permute-start.12
  41.7 1.0 constant_dynamic-slice_fusion.1
  43.3 1.0 constant_dynamic-slice_fusion.2
  44.3 1.4 collective-permute-start.8
  46.5 1.5 collective-permute-start.2
  48.0 69.2 %collective-permute-done.4 = bf16[512,256]{1,0:T(8,128)(2,1)} collective-permute-done((bf16[512,256]{1,0:T(8,128)(2,1)S(1)}, bf16[512,256]{1,0:T(8,128)(2,1)}, u32[]{:S(2)}, u32[]{:S(2)}) %collective-permute-start.4) | collective-permute-done | bytes 262176 | tf_op jit(solution)/shard_map/ppermute | solution.py:557
  117.2 2.9 collective-permute-done.2
  120.7 3.1 constant_dynamic-slice_fusion.8.x_ref.rest_1_
  124.3 1.5 constant_dynamic-slice_fusion.3.cot_ref
  128.9 5.2 prologue.1
  134.1 20.1 %attend.2 = (bf16[1024,512]{1,0:T(8,128)(2,1)}, bf16[1024,256]{1,0:T(8,128)(2,1)}, bf16[1024,256]{1,0:T(8,128)(2,1)}, bf16[1024,512]{1,0:T(8,128)(2,1)}, f32[2,8,1024]{2,1,0:T(8,128)}) custom-call(bf16[1024,1024]{1,0:T(8,128)(2,1)} %get-tuple-element.56.first_ref, bf16[1024,512]{1,0:T(8,128)(2,1)} %wq_ref.3, bf16[1024,256]{1,0:T(8,128)(2,1)} %wk_ref.3, ...), custom_call_target="tpu_custom_call" | custom-call | tf_op jit(solution)/shard_map/attend/pallas_call | solution.py:174
  155.4 2.1 maximum_select_fusion.8.wv_ref
  157.5 2.1 maximum_select_fusion.7.wk_ref
  159.6 2.6 maximum_select_fusion.5.wq_ref
  162.2 20.2 %attend.3 = (bf16[1024,512]{1,0:T(8,128)(2,1)}, bf16[1024,256]{1,0:T(8,128)(2,1)}, bf16[1024,256]{1,0:T(8,128)(2,1)}, bf16[1024,512]{1,0:T(8,128)(2,1)}, f32[2,8,1024]{2,1,0:T(8,128)}) custom-call(bf16[1024,1024]{1,0:T(8,128)(2,1)} %get-tuple-element.56.first_ref, bf16[1024,512]{1,0:T(8,128)(2,1)} %maximum_select_fusion.5.wq_ref, ...), custom_call_target="tpu_custom_call" | custom-call | tf_op jit(solution)/shard_map/attend/pallas_call | solution.py:174
  182.4 3.1 maximum_select_fusion.6.wo_b_ref.wo_ref
  185.5 8.1 %router.1 = (f32[1024,1024]{1,0:T(8,128)}, bf16[1024,1024]{1,0:T(8,128)(2,1)}, f32[32,1024]{1,0:T(8,128)}, s32[8,1024]{1,0:T(8,128)}) custom-call(bf16[1024,1024]{1,0:T(8,128)(2,1)} %constant_dynamic-slice_fusion.8.x_ref.rest_1_, bf16[1024,512]{1,0:T(8,128)(2,1)} %get-tuple-element.60.att_a_ref.att_ref, ...), custom_call_target="tpu_custom_call" | custom-call | tf_op jit(solution)/shard_map/router/pallas_call | solution.py:238
  193.6 3.2 maximum_select_fusion.4.wd_b_ref
  196.8 3.3 maximum_select_fusion.3.wu_b_ref
  200.1 1.6 maximum_select_fusion.2.wg_b_ref
  201.8 39.2 %experts.1 = (bf16[1024,1024]{1,0:T(8,128)(2,1)}, bf16[1024,1024]{1,0:T(8,128)(2,1)}, f32[1024,1024]{1,0:T(8,128)}, f32[40,1024]{1,0:T(8,128)}, bf16[4,1024,256]...) custom-call(bf16[1024,1024]{1,0:T(8,128)(2,1)} %get-tuple-element.63, ...), custom_call_target="tpu_custom_call" | custom-call | tf_op jit(solution)/shard_map/experts/pallas_call | solution.py:351
  240.9 1.2 collective-permute-start.20
  242.1 34.0 %attend_back.1 = (bf16[1024,512]{1,0:T(8,128)(2,1)}, bf16[1024,256]{1,0:T(8,128)(2,1)}, bf16[1024,256]{1,0:T(8,128)(2,1)}, bf16[512,1024]{1,0:T(8,128)(2,1)}, f32[1024,1024]{1,0:T(8,128)}) custom-call(bf16[1024,512]{1,0:T(8,128)(2,1)} %get-tuple-element.77.q_ref, bf16[1024,256]{1,0:T(8,128)(2,1)} %get-tuple-element.78.k_ref, ...), custom_call_target="tpu_custom_call" | custom-call | tf_op jit(solution)/shard_map/attend_back/pallas_call | solution.py:544
  277.1 1.1 collective-permute-start.18
  279.1 1.1 collective-permute-start.16
  280.2 20.8 %collective-permute-done.17 = bf16[1024,256]{1,0:T(8,128)(2,1)} collective-permute-done((bf16[1024,256]{1,0:T(8,128)(2,1)}, bf16[1024,256]{1,0:T(8,128)(2,1)}, u32[]{:S(2)}, u32[]{:S(2)}) %collective-permute-start.17) | collective-permute-done | bytes 524320 | tf_op jit(solution)/shard_map/ppermute | solution.py:557
  301.0 1.1 collective-permute-start.19
  302.2 10.1 %collective-permute-done.18 = bf16[1024,256]{1,0:T(8,128)(2,1)} collective-permute-done((bf16[1024,256]{1,0:T(8,128)(2,1)}, bf16[1024,256]{1,0:T(8,128)(2,1)}, u32[]{:S(2)}, u32[]{:S(2)}) %collective-permute-start.18) | collective-permute-done | bytes 524320 | tf_op jit(solution)/shard_map/ppermute | solution.py:557
  312.3 1.1 collective-permute-start.22
  313.4 39.3 %attend_back_final.1 = (bf16[1024,512]{1,0:T(8,128)(2,1)}, bf16[1024,256]{1,0:T(8,128)(2,1)}, bf16[1024,256]{1,0:T(8,128)(2,1)}, bf16[512,1024]{1,0:T(8,128)(2,1...) custom-call(bf16[1024,512]{1,0:T(8,128)(2,1)} %get-tuple-element.71.q_ref, bf16[1024,256]{1,0:T(8,128)(2,1)} %get-tuple-element.72.k_ref, ...), custom_call_target="tpu_custom_call" | custom-call | tf_op jit(solution)/shard_map/attend_back_final/pallas_call | solution.py:544
  352.7 1.4 pad_maximum_fusion
  354.3 2.2 add_convert_fusion.6
  356.5 2.2 add_convert_fusion.5
  358.7 21.4 %collective-permute-done.16 = bf16[1024,512]{1,0:T(8,128)(2,1)S(1)} collective-permute-done((bf16[1024,512]{1,0:T(8,128)(2,1)}, bf16[1024,512]{1,0:T(8,128)(2,1)S(1)}, u32[]{:S(2)}, u32[]{:S(2)}) %collective-permute-start.16) | collective-permute-done | bytes 1048608 | tf_op jit(solution)/shard_map/ppermute | solution.py:557
  380.1 1.3 add_convert_fusion.4
  381.4 21.5 %collective-permute-done.19 = bf16[512,1024]{1,0:T(8,128)(2,1)} collective-permute-done((bf16[512,1024]{1,0:T(8,128)(2,1)}, bf16[512,1024]{1,0:T(8,128)(2,1)}, u32[]{:S(2)}, u32[]{:S(2)}) %collective-permute-start.19) | collective-permute-done | bytes 1048608 | tf_op jit(solution)/shard_map/ppermute | solution.py:557
  402.9 2.6 add_convert_fusion.3
  405.5 1.8 add_convert_fusion.2
  407.4 3.5 add_convert_fusion.1
  410.9 36.5 %collective-permute-done.22 = bf16[4,256,1024]{2,1,0:T(8,128)(2,1)} collective-permute-done((bf16[4,256,1024]{2,1,0:T(8,128)(2,1)}, bf16[4,256,1024]{2,1,0:T(8,128)(2,1)}, u32[]{:S(2)}, u32[]{:S(2)}) %collective-permute-start.22) | collective-permute-done | bytes 2097184 | tf_op jit(solution)/shard_map/ppermute | solution.py:557
  447.4 3.9 add_convert_fusion
  451.3 1.1 collective-permute-start.14
  453.9 24.4 %all-reduce.4.cloned.1.call-done = f32[48,1024]{1,0:T(8,128)} async-done(((f32[48,1024]{1,0:T(8,128)}), f32[48,1024]{1,0:T(8,128)}) %all-reduce.4.cloned.1.call-update) | async-done | bytes 196624 | tf_op jit(solution)/shard_map/psum | solution.py:648
  478.2 1.4 fusion.1
  479.6 1.6 slice_bitcast_fusion
  481.2 19.5 %collective-permute-done.14 = bf16[1024,1024]{1,0:T(8,128)(2,1)} collective-permute-done((bf16[1024,1024]{1,0:T(8,128)(2,1)}, bf16[1024,1024]{1,0:T(8,128)(2,1)}, u32[]{:S(2)}, u32[]{:S(2)}) %collective-permute-start.14) | collective-permute-done | bytes 2097184 | tf_op jit(solution)/shard_map/ppermute | solution.py:557
  500.7 5.5 maximum_select_fusion
  506.1 37.7 %collective-permute-done.15 = bf16[1024,1024]{1,0:T(8,128)(2,1)} collective-permute-done((bf16[1024,1024]{1,0:T(8,128)(2,1)S(1)}, bf16[1024,1024]{1,0:T(8,128)(2,1)}, u32[]{:S(2)}, u32[]{:S(2)}) %collective-permute-start.15) | collective-permute-done | bytes 2097184 | tf_op jit(solution)/shard_map/ppermute | solution.py:557
  543.9 5.8 fusion
  549.7 122.4 %all-reduce.6.cloned.1.call-done = (bf16[1024,512]{1,0:T(8,128)(2,1)}, bf16[1024,256]{1,0:T(8,128)(2,1)}, bf16[1024,256]{1,0:T(8,128)(2,1)}, bf16[512,1024]{1,0:...) async-done(((bf16[1024,512]{1,0:T(8,128)(2,1)}, bf16[1024,256]{1,0:T(8,128)(2,1)}, ...) | async-done | bytes 9437200 | tf_op jit(solution)/shard_map/psum | solution.py:629
  672.1 2.9 convert_element_type.91
  675.1 1.0 convert_element_type.95
  676.1 1.0 convert_element_type.99
  677.2 1.6 convert_element_type.103
  678.7 2.4 convert_element_type.107
  681.1 2.4 convert_element_type.111
  683.5 2.5 convert_element_type.115
  (89 shorter events, 10.2 us)
Async XLA Ops:
  7.2 471.1 %all-reduce.4.cloned.1.call-start = ((), (), s32[]{:S(2)}) async-start(), calls=%async_computation | async-start | bytes 393216 | tf_op jit(solution)/shard_map/psum | solution.py:648
  7.2 34.4 %copy-start.1 = (bf16[4,1024,256]{2,1,0:T(8,128)(2,1)S(1)}, bf16[4,1024,256]{2,1,0:T(8,128)(2,1)}, u32[]{:S(2)}) copy-start(bf16[4,1024,256]{2,1,0:T(8,128)(2,1)} %wu_a_ref.1) | copy-start | bytes 6291460
  8.5 14.9 %collective-permute-start = (bf16[512,512]{1,0:T(8,128)(2,1)S(1)}, bf16[512,512]{1,0:T(8,128)(2,1)S(1)}, u32[]{:S(2)}, u32[]{:S(2)}) collective-permute-start(bf16[512,512]{1,0:T(8,128)(2,1)S(1)} %constant_dynamic-slice_fusion.7), channel_id=1, source_target_pairs={{0,1},{1,0},{2,3},{3,2},{4,5},{5,4},{6,7},{7,6},{8,9},{9,8},{10,11... | collective-permute-start | bytes 1572872 | tf_op jit(solution)/shard_map/ppermute | solution.py:557
  23.4 14.6 %copy-start.15 = (bf16[512,512]{1,0:T(8,128)(2,1)}, bf16[512,512]{1,0:T(8,128)(2,1)S(1)}, u32[]{:S(2)}) copy-start(bf16[512,512]{1,0:T(8,128)(2,1)S(1)} %collective-permute-done) | copy-start | bytes 1572868
  24.7 13.3 %collective-permute-start.6 = (bf16[256,1024]{1,0:T(8,128)(2,1)S(1)}, bf16[256,1024]{1,0:T(8,128)(2,1)}, u32[]{:S(2)}, u32[]{:S(2)}) collective-permute-start(bf16[256,1024]{1,0:T(8,128)(2,1)S(1)} %constant_dynamic-slice_fusion.4), channel_id=1, source_target_pairs={{0,1},{1,0},{2,3},{3,2},{4,5},{5,4},{6,7},{7,6},{8,9},{9,8},{10,11... | collective-permute-start | bytes 1572872 | tf_op jit(solution)/shard_map/ppermute | solution.py:557
  26.5 16.8 %copy-start = (bf16[4,1024,256]{2,1,0:T(8,128)(2,1)S(1)}, bf16[4,1024,256]{2,1,0:T(8,128)(2,1)}, u32[]{:S(2)}) copy-start(bf16[4,1024,256]{2,1,0:T(8,128)(2,1)} %wg_a_ref.1) | copy-start | bytes 6291460
  40.2 5.6 copy-start.3
  40.2 6.2 copy-start.2
  40.2 79.9 %collective-permute-start.12 = (bf16[2,256,1024]{2,1,0:T(8,128)(2,1)}, bf16[2,256,1024]{2,1,0:T(8,128)(2,1)S(1)}, u32[]{:S(2)}, u32[]{:S(2)}) collective-permute-start(bf16[2,256,1024]{2,1,0:T(8,128)(2,1)} %constant_dynamic-slice_fusion), channel_id=1, source_target_pairs={{0,1},{1,0},{2,3},{3,2},{4,5},{5,4},{6,7},{7,6},{8,9},{9,8},{10,11... | collective-permute-start | bytes 3145736 | tf_op jit(solution)/shard_map/ppermute | solution.py:557
  42.7 81.1 %collective-permute-start.10 = (bf16[2,1024,256]{2,1,0:T(8,128)(2,1)}, bf16[2,1024,256]{2,1,0:T(8,128)(2,1)S(1)}, u32[]{:S(2)}, u32[]{:S(2)}) collective-permute-start(bf16[2,1024,256]{2,1,0:T(8,128)(2,1)} %constant_dynamic-slice_fusion.1), channel_id=1, source_target_pairs={{0,1},{1,0},{2,3},{3,2},{4,5},{5,4},{6,7},{7,6},{8,9},{9,8},{10,11... | collective-permute-start | bytes 3145736 | tf_op jit(solution)/shard_map/ppermute | solution.py:557
  44.3 109.9 %collective-permute-start.8 = (bf16[2,1024,256]{2,1,0:T(8,128)(2,1)}, bf16[2,1024,256]{2,1,0:T(8,128)(2,1)S(1)}, u32[]{:S(2)}, u32[]{:S(2)}) collective-permute-start(bf16[2,1024,256]{2,1,0:T(8,128)(2,1)} %constant_dynamic-slice_fusion.2), channel_id=1, source_target_pairs={{0,1},{1,0},{2,3},{3,2},{4,5},{5,4},{6,7},{7,6},{8,9},{9,8},{10,11... | collective-permute-start | bytes 3145736 | tf_op jit(solution)/shard_map/ppermute | solution.py:557
  45.8 71.4 %collective-permute-start.4 = (bf16[512,256]{1,0:T(8,128)(2,1)S(1)}, bf16[512,256]{1,0:T(8,128)(2,1)}, u32[]{:S(2)}, u32[]{:S(2)}) collective-permute-start(bf16[512,256]{1,0:T(8,128)(2,1)S(1)} %constant_dynamic-slice_fusion.5), channel_id=1, source_target_pairs={{0,1},{1,0},{2,3},{3,2},{4,5},{5,4},{6,7},{7,6},{8,9},{9,8},{10,11... | collective-permute-start | bytes 786440 | tf_op jit(solution)/shard_map/ppermute | solution.py:557
  46.5 73.7 %collective-permute-start.2 = (bf16[512,256]{1,0:T(8,128)(2,1)S(1)}, bf16[512,256]{1,0:T(8,128)(2,1)}, u32[]{:S(2)}, u32[]{:S(2)}) collective-permute-start(bf16[512,256]{1,0:T(8,128)(2,1)S(1)} %constant_dynamic-slice_fusion.6), channel_id=1, source_target_pairs={{0,1},{1,0},{2,3},{3,2},{4,5},{5,4},{6,7},{7,6},{8,9},{9,8},{10,11... | collective-permute-start | bytes 786440 | tf_op jit(solution)/shard_map/ppermute | solution.py:557
  117.2 6.5 collective-permute-start.5
  117.2 7.1 %copy-start.14 = (bf16[2048,1024]{1,0:T(8,128)(2,1)S(1)}, bf16[2048,1024]{1,0:T(8,128)(2,1)}, u32[]{:S(2)}) copy-start(bf16[2048,1024]{1,0:T(8,128)(2,1)} %param.16) | copy-start | bytes 12582916
  120.2 5.7 collective-permute-start.3
  120.2 73.5 %collective-permute-start.13 = (bf16[2,256,1024]{2,1,0:T(8,128)(2,1)S(1)}, bf16[2,256,1024]{2,1,0:T(8,128)(2,1)}, u32[]{:S(2)}, u32[]{:S(2)}) collective-permute-start(bf16[2,256,1024]{2,1,0:T(8,128)(2,1)S(1)} %collective-permute-done.12), channel_id=1, source_target_pairs={{0,2},{2,0},{4,6},{6,4},{8,10},{10,8},{12,14},{14,12},{16,18},{18,... | collective-permute-start | bytes 3145736 | tf_op jit(solution)/shard_map/ppermute | solution.py:562
  123.7 2.2 copy-start.25
  123.7 2.2 copy-start.23
  123.7 2.8 copy-start.24
  123.8 35.9 %collective-permute-start.1 = (bf16[512,512]{1,0:T(8,128)(2,1)}, bf16[512,512]{1,0:T(8,128)(2,1)}, u32[]{:S(2)}, u32[]{:S(2)}) collective-permute-start(bf16[512,512]{1,0:T(8,128)(2,1)} %copy-done.15), channel_id=1, source_target_pairs={{0,2},{2,0},{4,6},{6,4},{8,10},{10,8},{12,14},{14,12},{16,18},{18,... | collective-permute-start | bytes 1572872 | tf_op jit(solution)/shard_map/ppermute | solution.py:562
  123.8 73.0 %collective-permute-start.11 = (bf16[2,1024,256]{2,1,0:T(8,128)(2,1)S(1)}, bf16[2,1024,256]{2,1,0:T(8,128)(2,1)}, u32[]{:S(2)}, u32[]{:S(2)}) collective-permute-start(bf16[2,1024,256]{2,1,0:T(8,128)(2,1)S(1)} %collective-permute-done.10), channel_id=1, source_target_pairs={{0,2},{2,0},{4,6},{6,4},{8,10},{10,8},{12,14},{14,12},{16,18},{18,... | collective-permute-start | bytes 3145736 | tf_op jit(solution)/shard_map/ppermute | solution.py:562
  125.8 56.6 %collective-permute-start.7 = (bf16[256,1024]{1,0:T(8,128)(2,1)}, bf16[256,1024]{1,0:T(8,128)(2,1)}, u32[]{:S(2)}, u32[]{:S(2)}) collective-permute-start(bf16[256,1024]{1,0:T(8,128)(2,1)} %collective-permute-done.6), channel_id=1, source_target_pairs={{0,2},{2,0},{4,6},{6,4},{8,10},{10,8},{12,14},{14,12},{16,18},{18,... | collective-permute-start | bytes 1572872 | tf_op jit(solution)/shard_map/ppermute | solution.py:562
  126.0 2.9 copy-start.19
  134.1 20.6 %copy-start.21 = (s32[2048,8]{0,1:T(8,128)S(1)}, s32[2048,8]{0,1:T(8,128)}, u32[]{:S(2)}) copy-start(s32[2048,8]{0,1:T(8,128)} %param.19) | copy-start | bytes 196612
  134.1 20.6 %copy-start.22 = (s32[2048,8]{0,1:T(8,128)S(1)}, s32[2048,8]{0,1:T(8,128)}, u32[]{:S(2)}) copy-start(s32[2048,8]{0,1:T(8,128)} %param.18) | copy-start | bytes 196612
  154.3 5.3 copy-start.16
  154.3 45.8 %collective-permute-start.9 = (bf16[2,1024,256]{2,1,0:T(8,128)(2,1)S(1)}, bf16[2,1024,256]{2,1,0:T(8,128)(2,1)S(1)}, u32[]{:S(2)}, u32[]{:S(2)}) collective-permute-start(bf16[2,1024,256]{2,1,0:T(8,128)(2,1)S(1)} %collective-permute-done.8), channel_id=1, source_target_pairs={{0,2},{2,0},{4,6},{6,4},{8,10},{10,8},{12,14},{14,12},{16,18},{18,... | collective-permute-start | bytes 3145736 | tf_op jit(solution)/shard_map/ppermute | solution.py:562
  240.9 164.5 %collective-permute-start.20 = (bf16[4,1024,256]{2,1,0:T(8,128)(2,1)}, bf16[4,1024,256]{2,1,0:T(8,128)(2,1)S(1)}, u32[]{:S(2)}, u32[]{:S(2)}) collective-permute-start(bf16[4,1024,256]{2,1,0:T(8,128)(2,1)} %get-tuple-element.95), channel_id=1, source_target_pairs={{0,1},{1,0},{2,3},{3,2},{4,5},{5,4},{6,7},{7,6},{8,9},{9,8},{10,11... | collective-permute-start | bytes 6291464 | tf_op jit(solution)/shard_map/ppermute | solution.py:557
  276.1 24.9 %collective-permute-start.17 = (bf16[1024,256]{1,0:T(8,128)(2,1)}, bf16[1024,256]{1,0:T(8,128)(2,1)}, u32[]{:S(2)}, u32[]{:S(2)}) collective-permute-start(bf16[1024,256]{1,0:T(8,128)(2,1)} %get-tuple-element.87), channel_id=1, source_target_pairs={{0,1},{1,0},{2,3},{3,2},{4,5},{5,4},{6,7},{7,6},{8,9},{9,8},{10,11... | collective-permute-start | bytes 1572872 | tf_op jit(solution)/shard_map/ppermute | solution.py:557
  277.1 35.2 %collective-permute-start.18 = (bf16[1024,256]{1,0:T(8,128)(2,1)}, bf16[1024,256]{1,0:T(8,128)(2,1)}, u32[]{:S(2)}, u32[]{:S(2)}) collective-permute-start(bf16[1024,256]{1,0:T(8,128)(2,1)} %get-tuple-element.89), channel_id=1, source_target_pairs={{0,1},{1,0},{2,3},{3,2},{4,5},{5,4},{6,7},{7,6},{8,9},{9,8},{10,11... | collective-permute-start | bytes 1572872 | tf_op jit(solution)/shard_map/ppermute | solution.py:557
  278.2 129.1 %collective-permute-start.21 = (bf16[4,1024,256]{2,1,0:T(8,128)(2,1)}, bf16[4,1024,256]{2,1,0:T(8,128)(2,1)}, u32[]{:S(2)}, u32[]{:S(2)}) collective-permute-start(bf16[4,1024,256]{2,1,0:T(8,128)(2,1)} %get-tuple-element.97), channel_id=1, source_target_pairs={{0,1},{1,0},{2,3},{3,2},{4,5},{5,4},{6,7},{7,6},{8,9},{9,8},{10,11... | collective-permute-start | bytes 6291464 | tf_op jit(solution)/shard_map/ppermute | solution.py:557
  279.1 101.0 %collective-permute-start.16 = (bf16[1024,512]{1,0:T(8,128)(2,1)}, bf16[1024,512]{1,0:T(8,128)(2,1)S(1)}, u32[]{:S(2)}, u32[]{:S(2)}) collective-permute-start(bf16[1024,512]{1,0:T(8,128)(2,1)} %get-tuple-element.85), channel_id=1, source_target_pairs={{0,1},{1,0},{2,3},{3,2},{4,5},{5,4},{6,7},{7,6},{8,9},{9,8},{10,11... | collective-permute-start | bytes 3145736 | tf_op jit(solution)/shard_map/ppermute | solution.py:557
  301.0 101.8 %collective-permute-start.19 = (bf16[512,1024]{1,0:T(8,128)(2,1)}, bf16[512,1024]{1,0:T(8,128)(2,1)}, u32[]{:S(2)}, u32[]{:S(2)}) collective-permute-start(bf16[512,1024]{1,0:T(8,128)(2,1)} %get-tuple-element.91), channel_id=1, source_target_pairs={{0,1},{1,0},{2,3},{3,2},{4,5},{5,4},{6,7},{7,6},{8,9},{9,8},{10,11... | collective-permute-start | bytes 3145736 | tf_op jit(solution)/shard_map/ppermute | solution.py:557
  312.3 135.1 %collective-permute-start.22 = (bf16[4,256,1024]{2,1,0:T(8,128)(2,1)}, bf16[4,256,1024]{2,1,0:T(8,128)(2,1)}, u32[]{:S(2)}, u32[]{:S(2)}) collective-permute-start(bf16[4,256,1024]{2,1,0:T(8,128)(2,1)} %get-tuple-element.99), channel_id=1, source_target_pairs={{0,1},{1,0},{2,3},{3,2},{4,5},{5,4},{6,7},{7,6},{8,9},{9,8},{10,11... | collective-permute-start | bytes 6291464 | tf_op jit(solution)/shard_map/ppermute | solution.py:557
  313.4 39.3 %copy-start.20 = (f32[40,1024]{1,0:T(8,128)S(1)}, f32[40,1024]{1,0:T(8,128)}, u32[]{:S(2)}) copy-start(f32[40,1024]{1,0:T(8,128)} %get-tuple-element.92) | copy-start | bytes 491524
  354.2 317.9 %all-reduce.6.cloned.1.call-start = ((), (), s32[]{:S(2)}) async-start(), calls=%async_computation.1 | async-start | bytes 18874368 | tf_op jit(solution)/shard_map/psum | solution.py:629
  354.3 25.9 %copy-start.13 = (bf16[1024,512]{1,0:T(8,128)(2,1)S(1)}, bf16[1024,512]{1,0:T(8,128)(2,1)}, u32[]{:S(2)}) copy-start(bf16[1024,512]{1,0:T(8,128)(2,1)} %get-tuple-element.84) | copy-start | bytes 3145732
  356.5 46.4 %copy-start.12 = (bf16[512,1024]{1,0:T(8,128)(2,1)S(1)}, bf16[512,1024]{1,0:T(8,128)(2,1)}, u32[]{:S(2)}) copy-start(bf16[512,1024]{1,0:T(8,128)(2,1)} %get-tuple-element.90) | copy-start | bytes 3145732
  381.4 24.1 %copy-start.6 = (bf16[4,1024,256]{2,1,0:T(8,128)(2,1)S(1)}, bf16[4,1024,256]{2,1,0:T(8,128)(2,1)}, u32[]{:S(2)}) copy-start(bf16[4,1024,256]{2,1,0:T(8,128)(2,1)} %get-tuple-element.94) | copy-start | bytes 6291460
  405.5 1.9 copy-start.5
  407.4 40.0 %copy-start.4 = (bf16[4,256,1024]{2,1,0:T(8,128)(2,1)S(1)}, bf16[4,256,1024]{2,1,0:T(8,128)(2,1)}, u32[]{:S(2)}) copy-start(bf16[4,256,1024]{2,1,0:T(8,128)(2,1)} %get-tuple-element.98) | copy-start | bytes 6291460
  451.3 1.6 copy-start.7
  451.3 49.4 %collective-permute-start.14 = (bf16[1024,1024]{1,0:T(8,128)(2,1)}, bf16[1024,1024]{1,0:T(8,128)(2,1)}, u32[]{:S(2)}, u32[]{:S(2)}) collective-permute-start(bf16[1024,1024]{1,0:T(8,128)(2,1)} %get-tuple-element.70), channel_id=1, source_target_pairs={{0,1},{1,0},{2,3},{3,2},{4,5},{5,4},{6,7},{7,6},{8,9},{9,8},{10,11... | collective-permute-start | bytes 6291464 | tf_op jit(solution)/shard_map/ppermute | solution.py:557
  452.9 91.0 %collective-permute-start.15 = (bf16[1024,1024]{1,0:T(8,128)(2,1)S(1)}, bf16[1024,1024]{1,0:T(8,128)(2,1)}, u32[]{:S(2)}, u32[]{:S(2)}) collective-permute-start(bf16[1024,1024]{1,0:T(8,128)(2,1)S(1)} %copy-done.7), channel_id=1, source_target_pairs={{0,1},{1,0},{2,3},{3,2},{4,5},{5,4},{6,7},{7,6},{8,9},{9,8},{10,11... | collective-permute-start | bytes 6291464 | tf_op jit(solution)/shard_map/ppermute | solution.py:557
  672.1 2.9 copy-start.18
  672.1 4.0 copy-start.17
  675.1 2.1 copy-start.11
  676.1 2.6 copy-start.10
  678.7 2.4 copy-start.9
  681.1 2.4 copy-start.8
Sparse Core Ops, SparseCore 0:
  354.3 123.8 all-reduce.3
  484.0 188.0 all-reduce.5

commit v2 on v1

--- a/solution.py
+++ b/solution.py
@@ -35,8 +35,13 @@
 
 def params(count=1):
     return pltpu.CompilerParams(
-        dimension_semantics=("arbitrary",) * count, vmem_limit_bytes=56 * 1024 * 1024
-    )
+        dimension_semantics=("arbitrary",) * count if count else None,
+        vmem_limit_bytes=56 * 1024 * 1024,
+    )
+
+
+def cost(micros):
+    return pl.CostEstimate(flops=int(micros * 1.1e9), bytes_accessed=1 << 20, transcendentals=0)
 
 
 def whole(shape):
@@ -82,7 +87,8 @@
             table,
             table,
         ),
-        compiler_params=pltpu.CompilerParams(vmem_limit_bytes=56 * 1024 * 1024),
+        compiler_params=params(0),
+        cost_estimate=cost(5),
         name="prologue",
     )(x, gain, seg_row, freq)
 
@@ -201,15 +207,19 @@
         ),
         scratch_shapes=[pltpu.VMEM((rows, rows), f32)],
         compiler_params=params(),
+        cost_estimate=cost(10 * groups),
         name="attend",
     )(first, wq, wk, wv, *tables, seg_col, seg_row)
 
 
 def router_kernel(
-    x_ref, att_a_ref, att_b_ref, wo_a_ref, wo_b_ref, gain_ref, wr_ref, routes_ref, slots_ref,
+    x_ref, att_a_ref, att_b_ref, att_c_ref, wo_a_ref, wo_b_ref, wo_c_ref, gain_ref, wr_ref, routes_ref, slots_ref,
     resid_ref, second_ref, gates_ref, places_ref,
 ):
-    resid = x_ref[...].astype(f32) + (nn(att_a_ref[...], wo_a_ref[...]) + nn(att_b_ref[...], wo_b_ref[...]))
+    mixed = nn(att_a_ref[...], wo_a_ref[...])
+    mixed = mixed + nn(att_b_ref[...], wo_b_ref[...])
+    mixed = mixed + nn(att_c_ref[...], wo_c_ref[...])
+    resid = x_ref[...].astype(f32) + mixed
     resid_ref[...] = resid
     scale = lax.rsqrt(jnp.mean(resid * resid, axis=-1, keepdims=True) + EPS)
     second = (resid * scale * gain_ref[...].astype(f32)).astype(bf16)
@@ -233,7 +243,7 @@
     gates_ref[...] = weights / jnp.sum(weights, axis=0, keepdims=True)
 
 
-def router(x, att_a, att_b, wo_a, wo_b, gain, wr_t, routes_t, slots_t):
+def router(x, attended, outputs, gain, wr_t, routes_t, slots_t):
     rows, width = x.shape
     return pl.pallas_call(
         router_kernel,
@@ -243,9 +253,10 @@
             jax.ShapeDtypeStruct((wr_t.shape[0], rows), f32),
             jax.ShapeDtypeStruct((8, rows), jnp.int32),
         ),
-        compiler_params=pltpu.CompilerParams(vmem_limit_bytes=56 * 1024 * 1024),
+        compiler_params=params(0),
+        cost_estimate=cost(8),
         name="router",
-    )(x, att_a, att_b, wo_a, wo_b, gain, wr_t, routes_t, slots_t)
+    )(x, *attended, *outputs, gain, wr_t, routes_t, slots_t)
 
 
 def split_three(values):
@@ -256,13 +267,14 @@
 
 
 def experts_kernel(
-    second_ref, cot_ref, resid_ref, gates_ref, places_ref, gain_ref, wr_ref,
+    order_ref, second_ref, cot_ref, resid_ref, gates_ref, places_ref, gain_ref, wr_ref,
     wg_a_ref, wg_b_ref, wu_a_ref, wu_b_ref, wd_a_ref, wd_b_ref,
     out_ref, low_ref, grad_ref, small_ref,
     gg_a_ref, gg_b_ref, gu_a_ref, gu_b_ref, gd_a_ref, gd_b_ref,
     moe_ref, back_ref, slot_grads_ref,
 ):
-    e = pl.program_id(0)
+    step = pl.program_id(0)
+    e = step ^ order_ref[0]
     rows = second_ref.shape[0]
     second = second_ref[...]
     slots = lax.broadcasted_iota(jnp.int32, (CAP, rows), 0)
@@ -299,20 +311,20 @@
     moe = tn(onehot, (gate_slot * expert_out).astype(bf16))
     second_back = tn(onehot, back.astype(bf16))
 
-    @pl.when(e == 0)
+    @pl.when(step == 0)
     def _():
         moe_ref[...] = moe
         back_ref[...] = second_back
         slot_grads_ref[...] = jnp.zeros_like(slot_grads_ref)
 
-    @pl.when(e > 0)
+    @pl.when(step > 0)
     def _():
         moe_ref[...] += moe
         back_ref[...] += second_back
 
     slot_grads_ref[pl.ds(e, 1), :] = gate_row
 
-    @pl.when(e == pl.num_programs(0) - 1)
+    @pl.when(step == pl.num_programs(0) - 1)
     def _():
         gates = gates_ref[...]
         resid = resid_ref[...]
@@ -340,16 +352,20 @@
         low_ref[...] = grad.astype(bf16)
 
 
-def experts_layer(second, cot, resid, gates, places, gain, wr_t, weights):
+def experts_layer(order, second, cot, resid, gates, places, gain, wr_t, weights):
     rows, width = second.shape
     experts = gates.shape[0]
     window, _, hidden = weights[0].shape
-    wide = pl.BlockSpec((1, width, hidden), lambda e: (e, 0, 0))
-    tall = pl.BlockSpec((1, hidden, width), lambda e: (e, 0, 0))
+    wide = pl.BlockSpec((1, width, hidden), lambda i, o: (i ^ o[0], 0, 0))
+    tall = pl.BlockSpec((1, hidden, width), lambda i, o: (i ^ o[0], 0, 0))
+    wide_rel = pl.BlockSpec((1, width, hidden), lambda i, o: (i, 0, 0))
+    tall_rel = pl.BlockSpec((1, hidden, width), lambda i, o: (i, 0, 0))
     wide_out = jax.ShapeDtypeStruct((window, width, hidden), bf16)
     tall_out = jax.ShapeDtypeStruct((window, hidden, width), bf16)
     return pl.pallas_call(
         experts_kernel,
+        grid_spec=pltpu.PrefetchScalarGridSpec(
+        num_scalar_prefetch=1,
         grid=(window,),
         in_specs=[
             whole((rows, width)),
@@ -360,11 +376,11 @@
             whole((1, width)),
             whole((experts, width)),
             wide,
+            wide_rel,
             wide,
-            wide,
-            wide,
+            wide_rel,
             tall,
-            tall,
+            tall_rel,
         ],
         out_specs=[
             whole((rows, width)),
@@ -378,6 +394,12 @@
             tall,
             tall,
         ],
+        scratch_shapes=[
+            pltpu.VMEM((rows, width), f32),
+            pltpu.VMEM((rows, width), f32),
+            pltpu.VMEM((experts, rows), f32),
+        ],
+        ),
         out_shape=(
             jax.ShapeDtypeStruct((rows, width), bf16),
             jax.ShapeDtypeStruct((rows, width), bf16),
@@ -390,44 +412,23 @@
             tall_out,
             tall_out,
         ),
-        scratch_shapes=[
-            pltpu.VMEM((rows, width), f32),
-            pltpu.VMEM((rows, width), f32),
-            pltpu.VMEM((experts, rows), f32),
-        ],
         compiler_params=params(),
+        cost_estimate=cost(39),
         name="experts",
-    )(second, cot, resid, gates, places, gain, wr_t, *weights)
+    )(order, second, cot, resid, gates, places, gain, wr_t, *weights)
 
 
 def attend_back_kernel(
-    final,
-    q_ref, k_ref, v_ref, att_ref, lse_ref, cos_ref, up_ref, down_ref, segc_ref, segr_ref,
-    low_ref, wo_ref, first_t_ref, wq_ref, wk_ref, wv_ref, *rest,
+    sel_ref, q_ref, k_ref, v_ref, lse_ref, cos_ref, up_ref, down_ref, segc_ref, segr_ref, low_ref, wo_ref,
+    back_ref, bias_ref, dq_ref, dk_ref, dv_ref,
 ):
-    if final:
-        (before_ref, x_ref, gain_ref, grad_ref, gq_ref, gk_ref, gv_ref, go_ref, token_ref, norm_ref,
-         bias_ref, sum_ref, dq_ref, dk_ref, dv_ref) = rest
-    else:
-        gq_ref, gk_ref, gv_ref, go_ref, sum_ref, bias_ref, dq_ref, dk_ref, dv_ref = rest
     rows = q_ref.shape[0]
-    g = pl.program_id(0)
-
-    @pl.when(g == 0)
-    def _():
-        for start in range(0, rows, BLOCK):
-            at_key = lax.broadcasted_iota(jnp.int32, (BLOCK, rows), 0) + start
-            at_query = lax.broadcasted_iota(jnp.int32, (BLOCK, rows), 1)
-            allowed = (at_key <= at_query) & (segc_ref[start : start + BLOCK, :] == segr_ref[...])
-            bias_ref[start : start + BLOCK, :] = jnp.where(allowed, 0.0, NEG)
-        if final:
-            sum_ref[...] = before_ref[...]
-        else:
-            sum_ref[...] = jnp.zeros_like(sum_ref)
-
-    low_grad = low_ref[...]
-    go_ref[...] = tn(att_ref[...], low_grad).astype(bf16)
-    upward = nt(low_grad, wo_ref[...]).astype(bf16)
+    for start in range(0, rows, BLOCK):
+        at_key = lax.broadcasted_iota(jnp.int32, (BLOCK, rows), 0) + start
+        at_query = lax.broadcasted_iota(jnp.int32, (BLOCK, rows), 1)
+        allowed = (at_key <= at_query) & (segc_ref[start : start + BLOCK, :] == segr_ref[...])
+        bias_ref[start : start + BLOCK, :] = jnp.where(allowed, 0.0, NEG)
+    upward = nt(low_ref[...], wo_ref[...]).astype(bf16)
     keys = doubled(k_ref[...].astype(f32))
     values = doubled(v_ref[...].astype(f32))
     low, high = halves_mask()
@@ -467,90 +468,201 @@
         two = two + pltpu.roll(two, HEAD_DIM, 1)
         return jnp.where(left, one, two)
 
-    first_t = first_t_ref[...]
-    key_back = rotate_back(both(dk_ref), cosine, up, down).astype(bf16)
-    value_back = both(dv_ref).astype(bf16)
-    query_back = jnp.concatenate(
-        [
-            (rotate_back(dq_ref[:, :LANES], cosine, up, down) * HEAD_DIM**-0.5).astype(bf16),
-            (rotate_back(dq_ref[:, LANES:], cosine, up, down) * HEAD_DIM**-0.5).astype(bf16),
-        ],
-        axis=1,
-    )
-    gq_ref[...] = nn(first_t, query_back).astype(bf16)
-    gk_ref[...] = nn(first_t, key_back).astype(bf16)
-    gv_ref[...] = nn(first_t, value_back).astype(bf16)
-    sum_ref[...] += nt(query_back, wq_ref[...]) + nt(key_back, wk_ref[...]) + nt(value_back, wv_ref[...])
-
+    back_ref[:, 2 * LANES : 3 * LANES] = rotate_back(both(dk_ref), cosine, up, down).astype(bf16)
+    back_ref[:, 3 * LANES :] = both(dv_ref).astype(bf16)
+    for kv in range(2):
+        part = slice(kv * LANES, (kv + 1) * LANES)
+        turned = rotate_back(dq_ref[:, part], cosine, up, down)
+        back_ref[:, part] = (turned * HEAD_DIM**-0.5).astype(bf16)
+
+
+def attend_back(sel, saved, tables, seg_col, seg_row, low_grad, wo):
+    query, key, value, _, logs = saved
+    rows, width = low_grad.shape
+
+    def fixed(shape):
+        return pl.BlockSpec(shape, lambda i, s: (0,) * len(shape))
+
+    table = fixed((rows, LANES))
+    wide = pl.BlockSpec((rows, GROUP), lambda i, s: (0, s[0]))
+    thin = pl.BlockSpec((rows, LANES), lambda i, s: (0, s[0]))
+    return pl.pallas_call(
+        attend_back_kernel,
+        grid_spec=pltpu.PrefetchScalarGridSpec(
+            num_scalar_prefetch=1,
+            grid=(1,),
+            in_specs=[
+                wide, thin, thin, pl.BlockSpec((1, 8, rows), lambda i, s: (s[0], 0, 0)),
+                table, table, table, fixed((rows, 1)), fixed((1, rows)),
+                fixed((rows, width)), pl.BlockSpec((GROUP, width), lambda i, s: (s[0], 0)),
+            ],
+            out_specs=fixed((rows, 2 * GROUP)),
+            scratch_shapes=[
+                pltpu.VMEM((rows, rows), f32),
+                pltpu.VMEM((rows, GROUP), f32),
+                pltpu.VMEM((2, rows, LANES), f32),
+                pltpu.VMEM((2, rows, LANES), f32),
+            ],
+        ),
+        out_shape=jax.ShapeDtypeStruct((rows, 2 * GROUP), bf16),
+        compiler_params=params(),
+        cost_estimate=cost(14),
+        name="attend_back",
+    )(sel, query, key, value, logs, *tables, seg_col, seg_row, low_grad, wo)
+
+
+def project_kernel(final, fresh, sel_ref, back_ref, att_ref, low_ref, first_t_ref, wq_ref, wk_ref, wv_ref, *rest):
+    if not fresh:
+        before_ref, *rest = rest
     if final:
-
-        @pl.when(g == pl.num_programs(0) - 1)
-        def _():
-            values = x_ref[...].astype(f32)
-            first_grad = sum_ref[...]
-            gain = gain_ref[...].astype(f32)
-            scale = lax.rsqrt(jnp.mean(values * values, axis=-1, keepdims=True) + EPS)
-            norm_ref[...] = jnp.broadcast_to(
-                jnp.sum(first_grad * values * scale, axis=0, keepdims=True), norm_ref.shape
-            )
-            inner = jnp.mean(gain * first_grad * values, axis=-1, keepdims=True)
-            grad = scale * gain * first_grad - values * (scale * scale * scale) * inner
-            token_ref[...] = (grad + grad_ref[...]).astype(bf16)
-
-
-def attend_back(saved, tables, seg_col, seg_row, low_grad, wo, first_t, wq, wk, wv, final=None):
-    query, key, value, att, logs = saved
-    rows = query.shape[0]
-    width = wq.shape[0]
-    groups = query.shape[1] // GROUP
-    table = whole((rows, LANES))
-    wide = pl.BlockSpec((rows, GROUP), lambda g: (0, g))
-    thin = pl.BlockSpec((rows, LANES), lambda g: (0, g))
-    wide_w = pl.BlockSpec((width, GROUP), lambda g: (0, g))
-    thin_w = pl.BlockSpec((width, LANES), lambda g: (0, g))
-    tall_w = pl.BlockSpec((GROUP, width), lambda g: (g, 0))
-    square = whole((rows, width))
+        x_ref, gain_ref, grad_ref, group_ref, token_ref, norm_ref = rest
+    else:
+        group_ref, sum_ref = rest
+    back = back_ref[...]
+    group_ref[:, : 2 * GROUP] = nn(first_t_ref[...], back).astype(bf16)
+    group_ref[:, 2 * GROUP :] = tn(low_ref[...], att_ref[...]).astype(bf16)
+    first_grad = nt(back[:, :GROUP], wq_ref[...])
+    first_grad = first_grad + nt(back[:, GROUP : GROUP + LANES], wk_ref[...])
+    first_grad = first_grad + nt(back[:, GROUP + LANES :], wv_ref[...])
+    if not fresh:
+        first_grad = before_ref[...] + first_grad
+    if final:
+        inputs = x_ref[...].astype(f32)
+        gain = gain_ref[...].astype(f32)
+        scale = lax.rsqrt(jnp.mean(inputs * inputs, axis=-1, keepdims=True) + EPS)
+        norm_ref[...] = jnp.broadcast_to(
+            jnp.sum(first_grad * inputs * scale, axis=0, keepdims=True), norm_ref.shape
+        )
+        inner = jnp.mean(gain * first_grad * inputs, axis=-1, keepdims=True)
+        grad = scale * gain * first_grad - inputs * (scale * scale * scale) * inner
+        token_ref[...] = (grad + grad_ref[...]).astype(bf16)
+    else:
+        sum_ref[...] = first_grad
+
+
+def project(sel, back, att, low_grad, first_t, wq, wk, wv, before=None, final=None):
+    rows, width = low_grad.shape
+
+    def fixed(shape):
+        return pl.BlockSpec(shape, lambda i, s: (0,) * len(shape))
+
+    wide_w = pl.BlockSpec((width, GROUP), lambda i, s: (0, s[0]))
+    thin_w = pl.BlockSpec((width, LANES), lambda i, s: (0, s[0]))
+    square = fixed((rows, width))
     in_specs = [
-        wide, thin, thin, wide, pl.BlockSpec((1, 8, rows), lambda g: (g, 0, 0)),
-        table, table, table, whole((rows, 1)), whole((1, rows)),
-        square, tall_w, whole((width, rows)), wide_w, thin_w, thin_w,
+        fixed((rows, 2 * GROUP)), pl.BlockSpec((rows, GROUP), lambda i, s: (0, s[0])),
+        square, fixed((width, rows)), wide_w, thin_w, thin_w,
     ]
-    out_specs = [wide_w, thin_w, thin_w, tall_w]
-    out_shape = [
-        jax.ShapeDtypeStruct((width, groups * GROUP), bf16),
-        jax.ShapeDtypeStruct((width, groups * LANES), bf16),
-        jax.ShapeDtypeStruct((width, groups * LANES), bf16),
-        jax.ShapeDtypeStruct((groups * GROUP, width), bf16),
-    ]
-    scratch = [pltpu.VMEM((rows, rows), f32)]
+    out_specs = [fixed((width, 3 * GROUP))]
+    out_shape = [jax.ShapeDtypeStruct((width, 3 * GROUP), bf16)]
     extra = ()
+    if before is not None:
+        in_specs.append(square)
+        extra = (before,)
     if final is None:
         out_specs.append(square)
         out_shape.append(jax.ShapeDtypeStruct((rows, width), f32))
     else:
-        extra = final
-        in_specs += [square, square, whole((1, width)), square]
-        out_specs += [square, whole((8, width))]
+        extra = (*extra, *final)
+        in_specs += [square, fixed((1, width)), square]
+        out_specs += [square, fixed((8, width))]
         out_shape += [
             jax.ShapeDtypeStruct((rows, width), bf16),
             jax.ShapeDtypeStruct((8, width), f32),
         ]
-        scratch.append(pltpu.VMEM((rows, width), f32))
-    scratch += [
-        pltpu.VMEM((rows, GROUP), f32),
-        pltpu.VMEM((2, rows, LANES), f32),
-        pltpu.VMEM((2, rows, LANES), f32),
-    ]
     return pl.pallas_call(
-        partial(attend_back_kernel, final is not None),
-        grid=(groups,),
-        in_specs=in_specs,
-        out_specs=out_specs,
+        partial(project_kernel, final is not None, before is None),
+        grid_spec=pltpu.PrefetchScalarGridSpec(
+            num_scalar_prefetch=1, grid=(1,), in_specs=in_specs, out_specs=out_specs
+        ),
         out_shape=tuple(out_shape),
-        scratch_shapes=scratch,
         compiler_params=params(),
-        name="attend_back_final" if final is not None else "attend_back",
-    )(query, key, value, att, logs, *tables, seg_col, seg_row, low_grad, wo, first_t, wq, wk, wv, *extra)
+        cost_estimate=cost(7),
+        name="project_final" if final is not None else "project",
+    )(sel, back, att, low_grad, first_t, wq, wk, wv, *extra)
+
+
+def plain_order(piece, place, count):
+    shape = piece.shape
+    bit = 1
+    while bit < count:
+        pairs = piece.reshape(-1, 2, bit * shape[0] // count, shape[1])
+        flipped = jnp.concatenate([pairs[:, 1:], pairs[:, :1]], axis=1)
+        piece = jnp.where((place // bit) % 2 == 1, flipped, pairs)
+        bit *= 2
+    return piece.reshape(shape)
+
+
+def reorder(piece, place, count):
+    rows, columns = piece.shape
+    block = rows // count
+    if block % 16:
+        return plain_order(piece, place, count).astype(f32)
+
+    def kernel(place_ref, in_ref, out_ref):
+        for i in range(count):
+            start = pl.multiple_of((i ^ place_ref[0]) * block, block)
+            out_ref[i * block : (i + 1) * block, :] = in_ref[pl.ds(start, block), :].astype(f32)
+
+    return pl.pallas_call(
+        kernel,
+        grid_spec=pltpu.PrefetchScalarGridSpec(
+            num_scalar_prefetch=1,
+            grid=(1,),
+            in_specs=[pl.BlockSpec((rows, columns), lambda i, s: (0, 0))],
+            out_specs=pl.BlockSpec((rows, columns), lambda i, s: (0, 0)),
+        ),
+        out_shape=jax.ShapeDtypeStruct((rows, columns), f32),
+        compiler_params=params(),
+        cost_estimate=cost(3),
+        name="reorder",
+    )(place[None], piece)
+
+
+def unpack(mine, other, place, core, count):
+    rows, columns = mine.shape
+    block = rows // count
+    shapes = (
+        jax.ShapeDtypeStruct((rows, 2 * GROUP), f32),
+        jax.ShapeDtypeStruct((rows, 2 * LANES), f32),
+        jax.ShapeDtypeStruct((rows, 2 * LANES), f32),
+        jax.ShapeDtypeStruct((2 * GROUP, rows), f32),
+    )
+    if block % 16:
+        one, two = (plain_order(p, place, count) for p in (mine, other))
+        zero, one = jnp.where(core == 0, one, two), jnp.where(core == 0, two, one)
+        parts = ((0, GROUP), (GROUP, GROUP + LANES), (GROUP + LANES, 2 * GROUP), (2 * GROUP, 3 * GROUP))
+        out = [jnp.concatenate([zero[:, a:b], one[:, a:b]], 1).astype(f32) for a, b in parts]
+        return (*out[:3], out[3].T)
+
+    def kernel(place_ref, mine_ref, other_ref, query_ref, key_ref, value_ref, output_ref):
+        for group in range(2):
+            for i in range(count):
+                start = pl.multiple_of((i ^ place_ref[0]) * block, block)
+                here = slice(i * block, (i + 1) * block)
+                one = mine_ref[pl.ds(start, block), :].astype(f32)
+                two = other_ref[pl.ds(start, block), :].astype(f32)
+                rows_of = jnp.where(place_ref[1] == group, one, two)
+                wide = slice(group * GROUP, (group + 1) * GROUP)
+                thin = slice(group * LANES, (group + 1) * LANES)
+                query_ref[here, wide] = rows_of[:, :GROUP]
+                key_ref[here, thin] = rows_of[:, GROUP : GROUP + LANES]
+                value_ref[here, thin] = rows_of[:, GROUP + LANES : 2 * GROUP]
+                output_ref[wide, here] = rows_of[:, 2 * GROUP :].T
+
+    return pl.pallas_call(
+        kernel,
+        grid_spec=pltpu.PrefetchScalarGridSpec(
+            num_scalar_prefetch=1,
+            grid=(1,),
+            in_specs=[pl.BlockSpec((rows, columns), lambda i, s: (0, 0))] * 2,
+            out_specs=[pl.BlockSpec(o.shape, lambda i, s: (0, 0)) for o in shapes],
+        ),
+        out_shape=shapes,
+        compiler_params=params(),
+        cost_estimate=cost(5),
+        name="unpack",
+    )(jnp.stack([place, core]), mine, other)
 
 
 def swap_tensor(values):
@@ -566,20 +678,113 @@
     return lax.optimization_barrier((values, earlier))[0]
 
 
-def fetch_half(weights, core):
-    pieces = [
-        lax.dynamic_slice_in_dim(w, core * (w.shape[0] // 2), w.shape[0] // 2, 0) for w in weights
-    ]
-    got = [swap_tensor(p) for p in pieces]
-    return got
-
-
-def join_cores(got, core):
-    other = [swap_dp(p, 1) for p in got]
-    return [
-        jnp.where(core == 0, jnp.concatenate([a, b], 0), jnp.concatenate([b, a], 0))
-        for a, b in zip(got, other)
-    ]
+def bit_of(bit):
+    return (lax.axis_index("dp") // bit) % 2
+
+
+def cut(values, index, axis, count=2):
+    size = values.shape[axis] // count
+    return lax.dynamic_slice_in_dim(values, index * size, size, axis)
+
+
+def total(terms, start=None, size=None):
+    if start is not None:
+        terms = [lax.dynamic_slice_in_dim(t, start, size, 0) for t in terms]
+    if len(terms) == 1:
+        return terms[0]
+    out = terms[0].astype(f32)
+    for term in terms[1:]:
+        out = out + term.astype(f32)
+    return out.astype(bf16)
+
+
+def swap(values, bit):
+    return swap_tensor(values) if bit == 0 else swap_dp(values, bit)
+
+
+def scatter_sum(mine, theirs, order):
+    for bit in order:
+        if bit == 0:
+            (got,) = yield [(total(theirs), 0)]
+            mine, theirs = [*mine, got], None
+            continue
+        side = bit_of(bit)
+        sides, requests = [], []
+        for terms in (mine, theirs):
+            if terms is None:
+                continue
+            half = terms[0].shape[0] // 2
+            requests.append((total(terms, (1 - side) * half, half), bit))
+            sides.append(total(terms, side * half, half))
+        got = yield requests
+        mine = [sides[0], got[0]]
+        theirs = [sides[1], got[1]] if theirs is not None else None
+    return total(mine)
+
+
+def place_of(order):
+    place = 0
+    for bit in order:
+        if bit:
+            place = 2 * place + bit_of(bit)
+    return place
+
+
+def gather_back(piece, order):
+    for bit in reversed(order):
+        if bit:
+            (got,) = yield [(piece, bit)]
+            piece = jnp.concatenate([piece, got], 0)
+    return piece
+
+
+def sum_all(values):
+    for bit in [0] + [1 << i for i in range(30) if (1 << i) < lax.axis_size("dp")]:
+        (got,) = yield [(values, bit)]
+        values = values + got
+    return values
+
+
+def full_sum(kept, sent, order):
+    got = yield [(s, 1) for s in sent]
+    piece = yield from scatter_sum([kept[0], got[0]], [kept[1], got[1]], order)
+    piece = yield from gather_back(piece, order)
+    (other,) = yield [(piece, 1)]
+    return piece, other
+
+
+class Chains:
+    def __init__(self):
+        self.live = {}
+        self.done = {}
+
+    def advance(self, names=None, fence=None):
+        names = [n for n in (names or list(self.live)) if n in self.live]
+        requests = {}
+        waiting = {n: self.live[n][1] for n in names}
+        if fence is not None:
+            fence, waiting = lax.optimization_barrier((fence, waiting))
+        for n in names:
+            chain = self.live[n][0]
+            try:
+                requests[n] = chain.send(waiting[n])
+            except StopIteration as stop:
+                self.done[n] = stop.value
+                del self.live[n]
+        sends = {n: [v for v, _ in r] for n, r in requests.items()}
+        if fence is not None:
+            fence, sends = lax.optimization_barrier((fence, sends))
+        for n, r in requests.items():
+            self.live[n] = (self.live[n][0], [swap(v, bit) for v, (_, bit) in zip(sends[n], r)])
+        return fence
+
+    def add(self, name, chain):
+        self.live[name] = (chain, None)
+
+    def finish(self):
+        self.advance([n for n in self.live if self.live[n][1] is None], fence=())
+        while self.live:
+            self.advance(fence=())
 
 
 def per_device(
@@ -588,18 +793,13 @@
 ):
     length, width = tokens.shape
     side = lax.axis_index("tensor")
+    dp_size = lax.axis_size("dp")
     core = lax.axis_index("dp") % 2
     rows = SEQ_LEN
+    far = [8 << i for i in range(20) if (8 << i) < dp_size]
 
     def own(values):
         return lax.dynamic_slice_in_dim(values, side * rows, rows, 0)
-
-    got_one = fetch_half((w_query, w_key, w_value), core)
-    r_query, r_key, r_value = join_cores(got_one, core)
-    got_two = fetch_half(after((w_output,), got_one[0]), core)
-    (r_output,) = join_cores(got_two, core)
-    got_three = fetch_half(after((w_gate, w_up, w_down), got_two[0]), core)
-    r_gate, r_up, r_down = join_cores(got_three, core)
 
     x = own(tokens)
     cot = own(cotangent)
@@ -613,57 +813,155 @@
     frequency = THETA ** (-(2.0 * jnp.arange(half_dim, dtype=f32)) / HEAD_DIM)
     freq = jnp.broadcast_to(frequency[:, None], (half_dim, LANES))
 
+    near_own = [cut(w, core, 1) for w in (w_query, w_key, w_value)]
+    order_index = lax.axis_index("dp") % 4
+    near = [swap_tensor(w) for w in near_own]
+    near_out = swap_tensor(after(cut(w_output, core, 0), near[0]))
+    last = near_out
+    got = []
+    for w in (w_gate, w_up, w_down):
+        last = swap_tensor(after(lax.dynamic_slice_in_dim(w, order_index, 1, 0), last))
+        got.append(last)
+
     first, first_t, *tables = prologue(x, gain_one, seg_row, freq)
     saved_a = attend(first, w_query, w_key, w_value, tables, seg_col, seg_row)
-    saved_b = attend(first, r_query, r_key, r_value, tables, seg_col, seg_row)
+    near, first = lax.optimization_barrier((near, (first, saved_a)))
+    first, saved_a = first
+    far_qkv = [swap_dp(w, 1) for w in near]
+    saved_b = attend(first, *near, tables, seg_col, seg_row)
+    (near_out, got[0]), (first, saved_b) = lax.optimization_barrier(((near_out, got[0]), (first, saved_b)))
+    far_out = swap_dp(near_out, 1)
+    across = [swap_dp(got[0], 2)]
+    beside = [swap_dp(got[0], 1)]
+    saved_c = attend(first, *far_qkv, tables, seg_col, seg_row)
+    (across[0], got[1]), saved_c = lax.optimization_barrier(((across[0], got[1]), saved_c))
+    across.append(swap_dp(got[1], 2))
+    beside.append(swap_dp(got[1], 1))
+    corner = [swap_dp(across[0], 1)]
     resid, second, gates, places = router(
-        x, saved_a[3], saved_b[3], w_output, r_output, gain_two, wr_t, routes_t, slots_t
-    )
+        x, (saved_a[3], saved_b[3], saved_c[3]), (w_output, near_out, far_out), gain_two, wr_t, routes_t, slots_t
+    )
+    (across[1], got[2]), second = lax.optimization_barrier(((across[1], got[2]), second))
+    across.append(swap_dp(got[2], 2))
+    beside.append(swap_dp(got[2], 1))
+    corner.append(swap_dp(across[1], 1))
+    corner.append(swap_dp(across[2], 1))
+    r_gate, r_up, r_down = (jnp.concatenate(parts, axis=0) for parts in zip(got, beside, across, corner))
     (out, low_grad, resid_grad, small, gg_a, gg_b, gu_a, gu_b, gd_a, gd_b) = experts_layer(
-        second, cot, resid, gates, places, gain_two, wr_t,
+        order_index[None], second, cot, resid, gates, places, gain_two, wr_t,
         (w_gate, r_gate, w_up, r_up, w_down, r_down),
     )
 
-    def finish(mine, theirs):
-        total = mine.astype(f32) + swap_tensor(theirs).astype(f32)
-        return lax.psum(total.astype(bf16), "dp").astype(f32)
-
-    grad_gate = finish(gg_a, gg_b)
-    grad_up = finish(gu_a, gu_b)
-    grad_down = finish(gd_a, gd_b)
-    out_other = swap_tensor(out)
-
-    gq_b, gk_b, gv_b, go_b, partial_sum = attend_back(
-        saved_b, tables, seg_col, seg_row, low_grad, r_output, first_t, r_query, r_key, r_value
-    )
-    gq_a, gk_a, gv_a, go_a, token, norm_one = attend_back(
-        saved_a, tables, seg_col, seg_row, low_grad, w_output, first_t, w_query, w_key, w_value,
-        final=(partial_sum, x, gain_one, resid_grad),
-    )
-    token_other = swap_tensor(token)
-    grad_query = finish(gq_a, gq_b)
-    grad_key = finish(gk_a, gk_b)
-    grad_value = finish(gv_a, gv_b)
-    grad_output = finish(go_a, go_b)
-    packed = lax.psum(jnp.concatenate([small, norm_one], 0), ("dp", "tensor"))
+    chains = Chains()
+    near_bits = ([2, 4], [4, 2])
+    orders = [[*bits, 0, *far] for bits in near_bits]
+    experts_orders = {"gate": orders[0], "up": orders[1], "down0": orders[0], "down1": orders[1]}
+
+    def experts_chain(name, mine, theirs):
+        flat = [g.reshape(-1, g.shape[-1]) for g in (mine, theirs)]
+        kept = [cut(g, core, 0) for g in flat]
+        sent = [cut(g, 1 - core, 0) for g in flat]
+        chains.add(name, full_sum(kept, sent, experts_orders[name]))
+
+    experts_chain("gate", gg_a, gg_b)
+    experts_chain("up", gu_a, gu_b)
+    experts_chain("down0", gd_a[:, : gd_a.shape[1] // 2], gd_b[:, : gd_a.shape[1] // 2])
+    experts_chain("down1", gd_a[:, gd_a.shape[1] // 2 :], gd_b[:, gd_a.shape[1] // 2 :])
+    chains.add("small", sum_all(small))
+    grads_names = list(experts_orders)
+
+    def one_swap(values, bit):
+        (got,) = yield [(values, bit)]
+        return got
+
+    def piece_swaps(values, count):
+        size = values.shape[0] // count
+        received = []
+        for i in range(count):
+            (got,) = yield [(values[i * size : (i + 1) * size], 0)]
+            received.append(got)
+        return jnp.concatenate(received, 0)
+
+    chains.add("out", piece_swaps(out, 4))
+    zero = jnp.zeros((1,), jnp.int32)
+    one_minus = 1 - core[None]
+    shared = (tables, seg_col, seg_row)
+
+    low_grad = chains.advance(fence=low_grad)
+    back = attend_back(zero, saved_c, *shared, low_grad, far_out)
+    back = chains.advance(grads_names + ["out", "small"], fence=back)
+    group_d, partial_sum = project(zero, back, saved_c[3], low_grad, first_t, *far_qkv)
+    chains.add("other", one_swap(group_d, 1))
+    low_grad, partial_sum = chains.advance(["other", "out"], fence=(low_grad, partial_sum))
+    back = attend_back(zero, saved_b, *shared, low_grad, near_out)
+    back = chains.advance(["other", "out", "small"], fence=back)
+    group_c, partial_sum = project(zero, back, saved_b[3], low_grad, first_t, *near, before=partial_sum)
+    chains.add("theirs", piece_swaps(total([group_c, chains.done["other"]]), 2))
+    low_grad, partial_sum = chains.advance(grads_names + ["theirs", "out"], fence=(low_grad, partial_sum))
+    back = attend_back(one_minus, saved_a, *shared, low_grad, w_output)
+    back = chains.advance(grads_names + ["small"], fence=back)
+    group_b, partial_sum = project(
+        one_minus, back, saved_a[3], low_grad, first_t, w_query, w_key, w_value, before=partial_sum
+    )
+    chains.add("mine", one_swap(group_b, 1))
+    low_grad, partial_sum = chains.advance(["mine", "theirs"], fence=(low_grad, partial_sum))
+    back = attend_back(core[None], saved_a, *shared, low_grad, w_output)
+    back = chains.advance(grads_names + ["mine", "theirs", "small"], fence=back)
+    group_a, token, norm_one = project(
+        core[None], back, saved_a[3], low_grad, first_t, w_query, w_key, w_value,
+        before=partial_sum, final=(x, gain_one, resid_grad),
+    )
+    chains.advance(["small"])
+    terms = (group_a, chains.done["mine"], chains.done["theirs"])
+    half = width // 2
+    tails = [[*bits, *far] for bits in near_bits]
+
+    def tail(index):
+        piece = yield from scatter_sum([t[index * half : (index + 1) * half] for t in terms], None, tails[index])
+        piece = yield from gather_back(piece, tails[index])
+        (other,) = yield [(piece, 1)]
+        return piece, other
+
+    chains.add("token", piece_swaps(token, 4))
+    chains.add("tail0", tail(0))
+    chains.add("tail1", tail(1))
+    chains.add("norm", sum_all(norm_one))
+    chains.finish()
+    done = chains.done
+
+    halves = [
+        unpack(*done[f"tail{i}"], place_of(tails[i]), core, dp_size // 2) for i in range(2)
+    ]
+    grad_query, grad_key, grad_value = (jnp.concatenate([a, b], 0) for a, b in zip(halves[0][:3], halves[1][:3]))
+    grad_output = jnp.concatenate([halves[0][3], halves[1][3]], 1)
+
+    def expert_grad(name):
+        piece, other = done[name]
+        place = place_of(experts_orders[name]) + core * (dp_size // 2)
+        return reorder(jnp.concatenate([piece, other], 0), place, dp_size)
+
+    grad_gate = expert_grad("gate").reshape(w_gate.shape)
+    grad_up = expert_grad("up").reshape(w_up.shape)
+    parts = [
+        expert_grad(name).reshape(w_down.shape[0], w_down.shape[1] // 2, width) for name in ("down0", "down1")
+    ]
+    grad_down = jnp.concatenate(parts, 1)
+    small = done["small"]
     experts = w_router.shape[1]
-    grad_router = packed[:experts].T
-    grad_norm_ffn = packed[experts]
-    grad_norm_attn = packed[experts + 8]
 
     def both(mine, other):
         return jnp.where(side == 0, jnp.concatenate([mine, other], 0), jnp.concatenate([other, mine], 0))
 
     return (
-        both(out, out_other),
-        both(token, token_other).astype(f32),
+        both(out, done["out"]),
+        both(token, done["token"]).astype(f32),
         grad_query,
         grad_key,
         grad_value,
         grad_output,
-        grad_norm_attn,
-        grad_norm_ffn,
-        grad_router,
+        done["norm"][0],
+        small[experts],
+        small[:experts].T,
         grad_gate,
         grad_up,
         grad_down,

time: 698 us -> 575 us (0.82)
  waiting for transfers between devices: 410 us -> 105 us
  starting transfers between devices: 21.8 us -> 107 us
  Pallas kernels: 166 us -> 214 us
  local copies, waits for them, and re-layouts: 18.6 us -> 56.1 us
  other arithmetic: 62.1 us -> 81.9 us
  between operations: 14.7 us -> 2.23 us
    ppermute x16 -> x23, waiting for transfers between devices: 263 us -> 29.5 us  [swap_tensor(): return lax.ppermute(values, 'tensor', [(0, 1), (1, 0)])]
    psum x2 -> x0, waiting for transfers between devices: 147 us -> none  [the longest x1 122 us: finish(): return lax.psum(total.astype(bf16), 'dp').astype(f32)]
    ppermute x7 -> x81, starting transfers between devices: 1.64 us -> 82.5 us  [swap_dp(): return lax.ppermute(values, 'dp', [(i, i ^ bit) for i in range(count)])]
    ppermute x7 -> x81, waiting for transfers between devices: 0.02 us -> 75.2 us  [swap_dp(): return lax.ppermute(values, 'dp', [(i, i ^ bit) for i in range(count)])]
    pallas_call x3 -> x15, Pallas kernels: 112 us -> 158 us  [the longest x4 54.6 us: attend_back(): pl.pallas_call(attend_back_kernel, grid_spec=pltpu.PrefetchScalarGridSpec...]
    unnamed x52 -> x210, local copies, waits for them, and re-layouts: 0.69 us -> 21.1 us
    select_n x7 -> x0, other arithmetic: 18 us -> none  [join_cores(): jnp.where(core == 0, jnp.concatenate([a, b], 0), jnp.concatenate([b, a], 0))]
    concatenate x1 -> x26, other arithmetic: 1.45 us -> 19.1 us  [the longest x3 8.1 us: per_device(): jnp.concatenate(parts, axis=0)]
  transfers between devices with their start and end apart: 25 -> 104, of which waited for: 13 -> 27; matrix products, arithmetic and copies ran while one was open for 9% -> 12% of each run, Pallas kernels for 18% -> 27%
where the time goes in v2:
time: 575 us; the launch traced here: 566 us
  Pallas kernels  214 us (37%)
  starting transfers between devices  107 us (19%)
  waiting for transfers between devices  105 us (18%)
  other arithmetic  81.9 us (14%)
  local copies, waits for them, and re-layouts  56.1 us (10%)
    ppermute x81, starting transfers between devices, swap_dp(): return lax.ppermute(values, 'dp', [(i, i ^ bit) for i in range(count)])  82.5 us
    ppermute x81, waiting for transfers between devices, swap_dp(): return lax.ppermute(values, 'dp', [(i, i ^ bit) for i in range(count)])  75.2 us
    pallas_call x4, Pallas kernels, attend_back(): pl.pallas_call(attend_back_kernel, grid_spec=pltpu.PrefetchScalarGridSpec...  54.6 us
    convert_element_type x33, other arithmetic, total(): return out.astype(bf16)  44.3 us
    pallas_call x3, Pallas kernels, attend(): pl.pallas_call(attend_kernel, grid=(groups,), in_specs=[whole((rows, widt...  43.1 us
    pallas_call x4, Pallas kernels, project(): pl.pallas_call(partial(project_kernel, final is not None, before is None)...  42 us
    pallas_call x1, Pallas kernels, experts_layer(): pl.pallas_call(experts_kernel, grid_spec=pltpu.PrefetchScalarGridSpec(num...  39.5 us
    ppermute x23, waiting for transfers between devices, swap_tensor(): return lax.ppermute(values, 'tensor', [(0, 1), (1, 0)])  29.5 us
  transfers between devices with their start and end apart: 104, of which 27 were waited for; matrix products, arithmetic and copies ran while one was open for 12% of the time, Pallas kernels for 27%

profile of v2, /device:TPU:0, one launch (start us, length us, event | category | flops | bytes accessed | tf_op | source)
XLA Modules:
  0.0 565.8 jit_solution(5777976411854185013)
XLA Ops:
  1.8 3.0 collective-permute-start
  6.9 2.1 collective-permute-start.4
  9.0 3.1 constant_dynamic-slice_fusion.13.x_ref.rest_1_
  14.5 5.2 prologue.1
  19.8 20.2 %attend.3 = (bf16[1024,512]{1,0:T(8,128)(2,1)}, bf16[1024,256]{1,0:T(8,128)(2,1)}, bf16[1024,256]{1,0:T(8,128)(2,1)}, bf16[1024,512]{1,0:T(8,128)(2,1)}, f32[2,8,1024]{2,1,0:T(8,128)}) custom-call(bf16[1024,1024]{1,0:T(8,128)(2,1)} %get-tuple-element.304.first_ref, bf16[1024,512]{1,0:T(8,128)(2,1)} %wq_ref.5, bf16[1024,256]{1,0:T(8,128)(2,1)} %wk_ref.5, ...), custom_call_target="tpu_custom_call" | custom-call | flops 22000001024 | bytes 1048576 | tf_op jit(solution)/shard_map/attend/pallas_call | solution.py:180
  47.1 11.4 %attend.4 = (bf16[1024,256]{1,0:T(8,128)(2,1)}, bf16[1024,128]{1,0:T(8,128)(2,1)}, bf16[1024,128]{1,0:T(8,128)(2,1)}, bf16[1024,256]{1,0:T(8,128)(2,1)}, f32[1,8,1024]{2,1,0:T(8,128)}) custom-call(bf16[1024,1024]{1,0:T(8,128)(2,1)} %get-tuple-element.304.first_ref, bf16[1024,256]{1,0:T(8,128)(2,1)} %copy-done.86, bf16[1024,128]{1,0:T(8,128)(2,1)} %copy-done.89, ...), custom_call_target="tpu_custom_call" | custom-call | flops 11000000512 | bytes 1048576 | tf_op jit(solution)/shard_map/attend/pallas_call | solution.py:180
  64.5 11.5 %attend.5 = (bf16[1024,256]{1,0:T(8,128)(2,1)}, bf16[1024,128]{1,0:T(8,128)(2,1)}, bf16[1024,128]{1,0:T(8,128)(2,1)}, bf16[1024,256]{1,0:T(8,128)(2,1)}, f32[1,8,1024]{2,1,0:T(8,128)}) custom-call(bf16[1024,1024]{1,0:T(8,128)(2,1)} %get-tuple-element.304.first_ref, bf16[1024,256]{1,0:T(8,128)(2,1)} %copy-done.87, bf16[1024,128]{1,0:T(8,128)(2,1)} %copy-done.90, ...), custom_call_target="tpu_custom_call" | custom-call | flops 11000000512 | bytes 1048576 | tf_op jit(solution)/shard_map/attend/pallas_call | solution.py:180
  78.6 8.1 %router.1 = (f32[1024,1024]{1,0:T(8,128)}, bf16[1024,1024]{1,0:T(8,128)(2,1)}, f32[32,1024]{1,0:T(8,128)}, s32[8,1024]{1,0:T(8,128)}) custom-call(bf16[1024,1024]{1,0:T(8,128)(2,1)} %constant_dynamic-slice_fusion.13.x_ref.rest_1_, bf16[1024,512]{1,0:T(8,128)(2,1)} %get-tuple-element.312.att_a_ref.att_ref, ...), custom_call_target="tpu_custom_call" | custom-call | flops 8800000000 | bytes 1048576 | tf_op jit(solution)/shard_map/router/pallas_call | solution.py:248
  86.7 3.4 collective-permute-done.10
  92.9 10.5 %collective-permute-done.18 = bf16[1,256,1024]{2,1,0:T(8,128)(2,1)} collective-permute-done((bf16[1,256,1024]{2,1,0:T(8,128)(2,1)S(1)}, bf16[1,256,1024]{2,1,0:T(8,128)(2,1)}, u32[]{:S(2)}, u32[]{:S(2)}) %collective-permute-start.18) | collective-permute-done | bytes 524320 | tf_op jit(solution)/shard_map/ppermute | solution.py:674
  103.4 3.1 constant_dynamic-slice_fusion.8.cot_ref
  106.5 2.6 pad_maximum_fusion.1.wg_b_ref
  109.1 2.9 pad_maximum_fusion.2.wu_b_ref
  112.0 2.6 pad_maximum_fusion.3.wd_b_ref
  114.6 39.5 %experts.1 = (bf16[1024,1024]{1,0:T(8,128)(2,1)}, bf16[1024,1024]{1,0:T(8,128)(2,1)}, f32[1024,1024]{1,0:T(8,128)}, f32[40,1024]{1,0:T(8,128)}, bf16[4,1024,256]...) custom-call(s32[1]{0:T(128)} %bitcast.order_ref, ...), custom_call_target="tpu_custom_call" | custom-call | flops 42900000768 | bytes 1048576 | tf_op jit(solution)/shard_map/experts/pallas_call | solution.py:365
  168.0 6.4 %collective-permute-done.27 = f32[40,1024]{1,0:T(8,128)S(1)} collective-permute-done((f32[40,1024]{1,0:T(8,128)S(1)}, f32[40,1024]{1,0:T(8,128)S(1)}, u32[]{:S(2)}, u32[]{:S(2)}) %collective-permute-start.27) | collective-permute-done | bytes 163872 | tf_op jit(solution)/shard_map/ppermute | solution.py:669
  175.7 13.4 %attend_back.4.back_ref = bf16[1024,512]{1,0:T(8,128)(2,1)} custom-call(s32[1]{0:T(128)} %constant.370.clone.1.sel_ref, bf16[1024,256]{1,0:T(8,128)(2,1)} %get-tuple-element.325.q_ref, bf16[1024,128]{1,0:T(8,128)(2,1)} %get-tuple-element.326.k_ref, bf16[1024,128]{1,0:T(8,128)(2,1)} %get-tuple-element.327.v_ref, f32[1,8,1024]{2,1,0:T(8,128)} %get-tuple-element.328.lse_ref, ...), custom_call_target="tpu_custom_call" | custom-call | flops 15399999488 | bytes 1048576 | tf_op jit(solution)/shard_map/attend_back/pallas_call | solution.py:489
  192.0 2.4 add_convert_fusion.25
  196.4 2.1 add_convert_fusion.23
  198.5 2.6 add_convert_fusion.4
  203.3 2.7 add_convert_fusion.2
  206.0 2.7 add_convert_fusion.1
  210.4 8.9 %project.3 = (bf16[1024,768]{1,0:T(8,128)(2,1)}, f32[1024,1024]{1,0:T(8,128)}) custom-call(s32[1]{0:T(128)} %constant.370.clone.1.sel_ref, bf16[1024,512]{1,0:T(8,128)(2,1)} %attend_back.4.back_ref, bf16[1024,256]{1,0:T(8,128)(2,1)} %get-tuple-element.314.att_c_ref.att_ref, bf16[1024,1024]{1,0:T(8,128)(2,1)} %get-tuple-element.430.low_ref, ...), custom_call_target="tpu_custom_call" | custom-call | flops 7699999744 | bytes 1048576 | tf_op jit(solution)/shard_map/project/pallas_call | solution.py:573
  219.3 3.3 collective-permute-done.30
  227.5 13.8 %attend_back.5.back_ref = bf16[1024,512]{1,0:T(8,128)(2,1)} custom-call(s32[1]{0:T(128)} %constant.370.clone.1.sel_ref, bf16[1024,256]{1,0:T(8,128)(2,1)} %get-tuple-element.364.q_ref, bf16[1024,128]{1,0:T(8,128)(2,1)} %get-tuple-element.365.k_ref, bf16[1024,128]{1,0:T(8,128)(2,1)} %get-tuple-element.366.v_ref, f32[1,8,1024]{2,1,0:T(8,128)} %get-tuple-element.367.lse_ref, ...), custom_call_target="tpu_custom_call" | custom-call | flops 15399999488 | bytes 1048576 | tf_op jit(solution)/shard_map/attend_back/pallas_call | solution.py:489
  246.4 10.3 %project.4 = (bf16[1024,768]{1,0:T(8,128)(2,1)}, f32[1024,1024]{1,0:T(8,128)}) custom-call(s32[1]{0:T(128)} %constant.370.clone.1.sel_ref, bf16[1024,512]{1,0:T(8,128)(2,1)} %attend_back.5.back_ref, bf16[1024,256]{1,0:T(8,128)(2,1)} %get-tuple-element.313.att_b_ref.att_ref, bf16[1024,1024]{1,0:T(8,128)(2,1)} %get-tuple-element.430.low_ref, ...), custom_call_target="tpu_custom_call" | custom-call | flops 7699999744 | bytes 1048576 | tf_op jit(solution)/shard_map/project/pallas_call | solution.py:573
  260.0 2.3 add_convert_fusion
  265.1 5.7 collective-permute-done.39
  272.3 8.3 %collective-permute-done.42 = bf16[1024,256]{1,0:T(8,128)(2,1)S(1)} collective-permute-done((bf16[1024,256]{1,0:T(8,128)(2,1)S(1)}, bf16[1024,256]{1,0:T(8,128)(2,1)S(1)}, u32[]{:S(2)}, u32[]{:S(2)}) %collective-permute-start.42) | collective-permute-done | bytes 524320 | tf_op jit(solution)/shard_map/ppermute | solution.py:674
  299.1 13.6 %attend_back.6.back_ref = bf16[1024,512]{1,0:T(8,128)(2,1)} custom-call(s32[1]{0:T(128)S(6)} %sub.93.sel_ref, bf16[1024,512]{1,0:T(8,128)(2,1)} %get-tuple-element.391.q_ref, bf16[1024,256]{1,0:T(8,128)(2,1)} %get-tuple-element.392.k_ref, bf16[1024,256]{1,0:T(8,128)(2,1)} %get-tuple-element.393.v_ref, f32[2,8,1024]{2,1,0:T(8,128)} %get-tuple-element.394.lse_ref, ...), custom_call_target="tpu_custom_call" | custom-call | flops 15399999488 | bytes 1048576 | tf_op jit(solution)/shard_map/attend_back/pallas_call | solution.py:489
  323.3 10.2 %project.5 = (bf16[1024,768]{1,0:T(8,128)(2,1)}, f32[1024,1024]{1,0:T(8,128)}) custom-call(s32[1]{0:T(128)S(6)} %sub.93.sel_ref, bf16[1024,512]{1,0:T(8,128)(2,1)} %attend_back.6.back_ref, bf16[1024,512]{1,0:T(8,128)(2,1)} %get-tuple-element.312.att_a_ref.att_ref, bf16[1024,1024]{1,0:T(8,128)(2,1)} %get-tuple-element.430.low_ref, ...), custom_call_target="tpu_custom_call" | custom-call | flops 7699999744 | bytes 1048576 | tf_op jit(solution)/shard_map/project/pallas_call | solution.py:573
  340.1 13.8 %attend_back.7.back_ref = bf16[1024,512]{1,0:T(8,128)(2,1)} custom-call(s32[1]{0:T(128)} %bitcast.14.sel_ref, bf16[1024,512]{1,0:T(8,128)(2,1)} %get-tuple-element.391.q_ref, bf16[1024,256]{1,0:T(8,128)(2,1)} %get-tuple-element.392.k_ref, bf16[1024,256]{1,0:T(8,128)(2,1)} %get-tuple-element.393.v_ref, f32[2,8,1024]{2,1,0:T(8,128)} %get-tuple-element.394.lse_ref, ...), custom_call_target="tpu_custom_call" | custom-call | flops 15399999488 | bytes 1048576 | tf_op jit(solution)/shard_map/attend_back/pallas_call | solution.py:489
  353.9 12.3 %collective-permute-done.58 = bf16[512,768]{1,0:T(8,128)(2,1)} collective-permute-done((bf16[512,768]{1,0:T(8,128)(2,1)}, bf16[512,768]{1,0:T(8,128)(2,1)}, u32[]{:S(2)}, u32[]{:S(2)}) %collective-permute-start.58) | collective-permute-done | bytes 786464 | tf_op jit(solution)/shard_map/ppermute | solution.py:669
  374.3 2.4 fusion.7
  376.6 12.6 %project_final.1 = (bf16[1024,768]{1,0:T(8,128)(2,1)}, bf16[1024,1024]{1,0:T(8,128)(2,1)}, f32[8,1024]{1,0:T(8,128)}) custom-call(s32[1]{0:T(128)} %bitcast.14.sel_ref, bf16[1024,512]{1,0:T(8,128)(2,1)} %attend_back.7.back_ref, bf16[1024,512]{1,0:T(8,128)(2,1)} %get-tuple-element.312.att_a_ref.att_ref, bf16[1024,1024]{1,0:T(8,128)(2,1)} %get-tuple-element.430.low_ref, ...), custom_call_target="tpu_custom_call" | custom-call | flops 7699999744 | bytes 1048576 | tf_op jit(solution)/shard_map/project_final/pallas_call | solution.py:573
  401.0 2.7 collective-permute-start.60
  403.7 6.0 %collective-permute-done.63 = f32[8,1024]{1,0:T(8,128)S(1)} collective-permute-done((f32[8,1024]{1,0:T(8,128)S(1)}, f32[8,1024]{1,0:T(8,128)S(1)}, u32[]{:S(2)}, u32[]{:S(2)}) %collective-permute-start.63) | collective-permute-done | bytes 32800 | tf_op jit(solution)/shard_map/ppermute | solution.py:669
  409.7 2.6 collective-permute-start.61
  415.2 2.2 collective-permute-start.67
  417.6 4.0 collective-permute-done.62
  421.6 5.6 collective-permute-done.67
  433.3 2.9 collective-permute-start.69
  438.0 2.6 broadcast_select_fusion
  440.7 6.3 %collective-permute-start.72 = (bf16[128,768]{1,0:T(8,128)(2,1)S(1)}, bf16[128,768]{1,0:T(8,128)(2,1)S(1)}, u32[]{:S(2)}, u32[]{:S(2)}) collective-permute-start(bf16[128,768]{1,0:T(8,128)(2,1)S(1)} %get-tuple-element.477), channel_id=1, source_target_pairs={{0,8},{2,10},{4,12},{6,14},{8,0},{10,2},{12,4},{14,6},{16,24},{18,... | collective-permute-start | bytes 589832 | tf_op jit(solution)/shard_map/ppermute | solution.py:674
  450.0 4.8 collective-permute-done.75
  455.1 3.2 collective-permute-start.78
  464.8 4.7 collective-permute-done.80
  471.9 2.6 collective-permute-done.76
  477.8 2.8 collective-permute-start.88
  482.1 2.3 collective-permute-start.89
  486.2 6.6 %collective-permute-done.89 = bf16[64,768]{1,0:T(8,128)(2,1)S(1)} collective-permute-done((bf16[64,768]{1,0:T(8,128)(2,1)S(1)}, bf16[64,768]{1,0:T(8,128)(2,1)S(1)}, u32[]{:S(2)}, u32[]{:S(2)}) %collective-permute-start.89) | collective-permute-done | bytes 98336 | tf_op jit(solution)/shard_map/ppermute | solution.py:674
  492.8 5.2 collective-permute-start.85
  499.5 2.9 collective-permute-done.85
  504.7 3.9 select_convert_fusion
  511.8 4.0 collective-permute-done.96
  518.2 3.7 collective-permute-done.97
  529.0 2.7 reorder.7
  532.7 2.7 reorder.6
  537.5 4.1 pad_maximum_fusion
  541.7 3.9 reorder.4
  545.6 3.9 reorder.5
  550.4 4.1 unpack.3
  554.5 4.2 unpack.2
  558.7 2.8 pad_maximum_fusion.4
  (491 shorter events, 174.8 us)
Async XLA Ops:
  1.8 17.9 %collective-permute-start = (bf16[1024,256]{1,0:T(8,128)(2,1)S(1)}, bf16[1024,256]{1,0:T(8,128)(2,1)S(1)}, u32[]{:S(2)}, u32[]{:S(2)}) collective-permute-start(bf16[1024,256]{1,0:T(8,128)(2,1)S(1)} %constant_dynamic-slice_fusion.17), channel_id=1, source_target_pairs={{0,1},{1,0},{2,3},{3,2},{4,5},{5,4},{6,7},{7,6},{8,9},{9,8},{10,11... | collective-permute-start | bytes 1572872 | tf_op jit(solution)/shard_map/ppermute | solution.py:669
  5.8 38.7 %collective-permute-start.3 = (bf16[1024,128]{1,0:T(8,128)(2,1)S(1)}, bf16[1024,128]{1,0:T(8,128)(2,1)S(1)}, u32[]{:S(2)}, u32[]{:S(2)}) collective-permute-start(bf16[1024,128]{1,0:T(8,128)(2,1)S(1)} %constant_dynamic-slice_fusion.15), channel_id=1, source_target_pairs={{0,1},{1,0},{2,3},{3,2},{4,5},{5,4},{6,7},{7,6},{8,9},{9,8},{10,11... | collective-permute-start | bytes 786440 | tf_op jit(solution)/shard_map/ppermute | solution.py:669
  6.9 37.7 %collective-permute-start.4 = (bf16[1024,128]{1,0:T(8,128)(2,1)S(1)}, bf16[1024,128]{1,0:T(8,128)(2,1)}, u32[]{:S(2)}, u32[]{:S(2)}) collective-permute-start(bf16[1024,128]{1,0:T(8,128)(2,1)S(1)} %constant_dynamic-slice_fusion.14), channel_id=1, source_target_pairs={{0,1},{1,0},{2,3},{3,2},{4,5},{5,4},{6,7},{7,6},{8,9},{9,8},{10,11... | collective-permute-start | bytes 786440 | tf_op jit(solution)/shard_map/ppermute | solution.py:669
  19.7 25.5 %collective-permute-start.1 = (bf16[256,1024]{1,0:T(8,128)(2,1)S(1)}, bf16[256,1024]{1,0:T(8,128)(2,1)}, u32[]{:S(2)}, u32[]{:S(2)}) collective-permute-start(bf16[256,1024]{1,0:T(8,128)(2,1)S(1)} %constant_dynamic-slice_fusion.18), channel_id=1, source_target_pairs={{0,1},{1,0},{2,3},{3,2},{4,5},{5,4},{6,7},{7,6},{8,9},{9,8},{10,11... | collective-permute-start | bytes 1572872 | tf_op jit(solution)/shard_map/ppermute | solution.py:669
  44.6 18.6 %collective-permute-start.7 = (bf16[1024,256]{1,0:T(8,128)(2,1)S(1)}, bf16[1024,256]{1,0:T(8,128)(2,1)S(1)}, u32[]{:S(2)}, u32[]{:S(2)}) collective-permute-start(bf16[1024,256]{1,0:T(8,128)(2,1)S(1)} %collective-permute-done.wq_ref), channel_id=1, source_target_pairs={{0,2},{2,0},{4,6},{6,4},{8,10},{10,8},{12,14},{14,12},{16,18},{18,... | collective-permute-start | bytes 1572872 | tf_op jit(solution)/shard_map/ppermute | solution.py:674
  44.7 16.8 %collective-permute-start.8 = (bf16[1024,128]{1,0:T(8,128)(2,1)S(1)}, bf16[1024,128]{1,0:T(8,128)(2,1)S(1)}, u32[]{:S(2)}, u32[]{:S(2)}) collective-permute-start(bf16[1024,128]{1,0:T(8,128)(2,1)S(1)} %collective-permute-done.3.wk_ref), channel_id=1, source_target_pairs={{0,2},{2,0},{4,6},{6,4},{8,10},{10,8},{12,14},{14,12},{16,18},{18,... | collective-permute-start | bytes 786440 | tf_op jit(solution)/shard_map/ppermute | solution.py:674
  45.1 17.8 %collective-permute-start.9 = (bf16[1024,128]{1,0:T(8,128)(2,1)}, bf16[1024,128]{1,0:T(8,128)(2,1)S(1)}, u32[]{:S(2)}, u32[]{:S(2)}) collective-permute-start(bf16[1024,128]{1,0:T(8,128)(2,1)} %collective-permute-done.4.wv_ref), channel_id=1, source_target_pairs={{0,2},{2,0},{4,6},{6,4},{8,10},{10,8},{12,14},{14,12},{16,18},{18,... | collective-permute-start | bytes 786440 | tf_op jit(solution)/shard_map/ppermute | solution.py:674
  45.2 14.4 %collective-permute-start.2 = (bf16[1,1024,256]{2,1,0:T(8,128)(2,1)S(1)}, bf16[1,1024,256]{2,1,0:T(8,128)(2,1)S(1)}, u32[]{:S(2)}, u32[]{:S(2)}) collective-permute-start(bf16[1,1024,256]{2,1,0:T(8,128)(2,1)S(1)} %constant_dynamic-slice_fusion.16), channel_id=1, source_target_pairs={{0,1},{1,0},{2,3},{3,2},{4,5},{5,4},{6,7},{7,6},{8,9},{9,8},{10,11... | collective-permute-start | bytes 1572872 | tf_op jit(solution)/shard_map/ppermute | solution.py:669
  59.6 16.4 %collective-permute-start.5 = (bf16[1,1024,256]{2,1,0:T(8,128)(2,1)S(1)}, bf16[1,1024,256]{2,1,0:T(8,128)(2,1)S(1)}, u32[]{:S(2)}, u32[]{:S(2)}) collective-permute-start(bf16[1,1024,256]{2,1,0:T(8,128)(2,1)S(1)} %collective-permute-done.2), channel_id=1, source_target_pairs={{0,4},{2,6},{4,0},{6,2},{8,12},{10,14},{12,8},{14,10},{16,20},{18,... | collective-permute-start | bytes 1572872 | tf_op jit(solution)/shard_map/ppermute | solution.py:674
  61.4 31.0 %collective-permute-start.13 = (bf16[1,1024,256]{2,1,0:T(8,128)(2,1)S(1)}, bf16[1,1024,256]{2,1,0:T(8,128)(2,1)S(1)}, u32[]{:S(2)}, u32[]{:S(2)}) collective-permute-start(bf16[1,1024,256]{2,1,0:T(8,128)(2,1)S(1)} %collective-permute-done.2), channel_id=1, source_target_pairs={{0,2},{2,0},{4,6},{6,4},{8,10},{10,8},{12,14},{14,12},{16,18},{18,... | collective-permute-start | bytes 1572872 | tf_op jit(solution)/shard_map/ppermute | solution.py:674
  61.4 14.6 %collective-permute-start.6 = (bf16[1,1024,256]{2,1,0:T(8,128)(2,1)S(1)}, bf16[1,1024,256]{2,1,0:T(8,128)(2,1)S(1)}, u32[]{:S(2)}, u32[]{:S(2)}) collective-permute-start(bf16[1,1024,256]{2,1,0:T(8,128)(2,1)S(1)} %constant_dynamic-slice_fusion.12), channel_id=1, source_target_pairs={{0,1},{1,0},{2,3},{3,2},{4,5},{5,4},{6,7},{7,6},{8,9},{9,8},{10,11... | collective-permute-start | bytes 1572872 | tf_op jit(solution)/shard_map/ppermute | solution.py:669
  63.0 14.8 %collective-permute-start.12 = (bf16[256,1024]{1,0:T(8,128)(2,1)}, bf16[256,1024]{1,0:T(8,128)(2,1)S(1)}, u32[]{:S(2)}, u32[]{:S(2)}) collective-permute-start(bf16[256,1024]{1,0:T(8,128)(2,1)} %collective-permute-done.1.wo_b_ref.wo_ref), channel_id=1, source_target_pairs={{0,2},{2,0},{4,6},{6,4},{8,10},{10,8},{12,14},{14,12},{16,18},{18,... | collective-permute-start | bytes 1572872 | tf_op jit(solution)/shard_map/ppermute | solution.py:674
  76.1 14.0 %collective-permute-start.10 = (bf16[1,1024,256]{2,1,0:T(8,128)(2,1)S(1)}, bf16[1,1024,256]{2,1,0:T(8,128)(2,1)S(1)}, u32[]{:S(2)}, u32[]{:S(2)}) collective-permute-start(bf16[1,1024,256]{2,1,0:T(8,128)(2,1)S(1)} %collective-permute-done.6), channel_id=1, source_target_pairs={{0,4},{2,6},{4,0},{6,2},{8,12},{10,14},{12,8},{14,10},{16,20},{18,... | collective-permute-start | bytes 1572872 | tf_op jit(solution)/shard_map/ppermute | solution.py:674
  91.9 14.6 %collective-permute-start.14 = (bf16[1,1024,256]{2,1,0:T(8,128)(2,1)S(1)}, bf16[1,1024,256]{2,1,0:T(8,128)(2,1)}, u32[]{:S(2)}, u32[]{:S(2)}) collective-permute-start(bf16[1,1024,256]{2,1,0:T(8,128)(2,1)S(1)} %collective-permute-done.5), channel_id=1, source_target_pairs={{0,2},{2,0},{4,6},{6,4},{8,10},{10,8},{12,14},{14,12},{16,18},{18,... | collective-permute-start | bytes 1572872 | tf_op jit(solution)/shard_map/ppermute | solution.py:674
  91.9 17.2 %collective-permute-start.15 = (bf16[1,1024,256]{2,1,0:T(8,128)(2,1)S(1)}, bf16[1,1024,256]{2,1,0:T(8,128)(2,1)}, u32[]{:S(2)}, u32[]{:S(2)}) collective-permute-start(bf16[1,1024,256]{2,1,0:T(8,128)(2,1)S(1)} %collective-permute-done.6), channel_id=1, source_target_pairs={{0,2},{2,0},{4,6},{6,4},{8,10},{10,8},{12,14},{14,12},{16,18},{18,... | collective-permute-start | bytes 1572872 | tf_op jit(solution)/shard_map/ppermute | solution.py:674
  92.4 16.7 %collective-permute-start.16 = (bf16[1,1024,256]{2,1,0:T(8,128)(2,1)S(1)}, bf16[1,1024,256]{2,1,0:T(8,128)(2,1)}, u32[]{:S(2)}, u32[]{:S(2)}) collective-permute-start(bf16[1,1024,256]{2,1,0:T(8,128)(2,1)S(1)} %collective-permute-done.10), channel_id=1, source_target_pairs={{0,2},{2,0},{4,6},{6,4},{8,10},{10,8},{12,14},{14,12},{16,18},{18,... | collective-permute-start | bytes 1572872 | tf_op jit(solution)/shard_map/ppermute | solution.py:674
  92.4 19.6 %collective-permute-start.17 = (bf16[1,256,1024]{2,1,0:T(8,128)(2,1)S(1)}, bf16[1,256,1024]{2,1,0:T(8,128)(2,1)S(1)}, u32[]{:S(2)}, u32[]{:S(2)}) collective-permute-start(bf16[1,256,1024]{2,1,0:T(8,128)(2,1)S(1)} %collective-permute-done.11), channel_id=1, source_target_pairs={{0,2},{2,0},{4,6},{6,4},{8,10},{10,8},{12,14},{14,12},{16,18},{18,... | collective-permute-start | bytes 1572872 | tf_op jit(solution)/shard_map/ppermute | solution.py:674
  174.4 14.7 %collective-permute-start.24 = (bf16[2048,256]{1,0:T(8,128)(2,1)}, bf16[2048,256]{1,0:T(8,128)(2,1)}, u32[]{:S(2)}, u32[]{:S(2)}) collective-permute-start(bf16[2048,256]{1,0:T(8,128)(2,1)} %constant_dynamic-slice_fusion.3), channel_id=1, source_target_pairs={{0,2},{2,0},{4,6},{6,4},{8,10},{10,8},{12,14},{14,12},{16,18},{18,... | collective-permute-start | bytes 3145736 | tf_op jit(solution)/shard_map/ppermute | solution.py:674
  174.4 14.7 %collective-permute-start.25 = (bf16[2048,256]{1,0:T(8,128)(2,1)}, bf16[2048,256]{1,0:T(8,128)(2,1)S(1)}, u32[]{:S(2)}, u32[]{:S(2)}) collective-permute-start(bf16[2048,256]{1,0:T(8,128)(2,1)} %constant_dynamic-slice_fusion.2), channel_id=1, source_target_pairs={{0,2},{2,0},{4,6},{6,4},{8,10},{10,8},{12,14},{14,12},{16,18},{18,... | collective-permute-start | bytes 3145736 | tf_op jit(solution)/shard_map/ppermute | solution.py:674
  174.9 14.2 %collective-permute-start.26 = (bf16[256,1024]{1,0:T(8,128)(2,1)}, bf16[256,1024]{1,0:T(8,128)(2,1)S(1)}, u32[]{:S(2)}, u32[]{:S(2)}) collective-permute-start(bf16[256,1024]{1,0:T(8,128)(2,1)} %get-tuple-element.344), channel_id=1, source_target_pairs={{0,1},{1,0},{2,3},{3,2},{4,5},{5,4},{6,7},{7,6},{8,9},{9,8},{10,11... | collective-permute-start | bytes 1572872 | tf_op jit(solution)/shard_map/ppermute | solution.py:669
  175.2 13.9 %collective-permute-start.28 = (bf16[2048,256]{1,0:T(8,128)(2,1)}, bf16[2048,256]{1,0:T(8,128)(2,1)}, u32[]{:S(2)}, u32[]{:S(2)}) collective-permute-start(bf16[2048,256]{1,0:T(8,128)(2,1)} %constant_dynamic-slice_fusion.1), channel_id=1, source_target_pairs={{0,2},{2,0},{4,6},{6,4},{8,10},{10,8},{12,14},{14,12},{16,18},{18,... | collective-permute-start | bytes 3145736 | tf_op jit(solution)/shard_map/ppermute | solution.py:674
  175.2 13.9 %collective-permute-start.29 = (bf16[2048,256]{1,0:T(8,128)(2,1)}, bf16[2048,256]{1,0:T(8,128)(2,1)}, u32[]{:S(2)}, u32[]{:S(2)}) collective-permute-start(bf16[2048,256]{1,0:T(8,128)(2,1)} %constant_dynamic-slice_fusion), channel_id=1, source_target_pairs={{0,2},{2,0},{4,6},{6,4},{8,10},{10,8},{12,14},{14,12},{16,18},{18,... | collective-permute-start | bytes 3145736 | tf_op jit(solution)/shard_map/ppermute | solution.py:674
  222.6 20.7 %collective-permute-start.31 = (bf16[1024,768]{1,0:T(8,128)(2,1)}, bf16[1024,768]{1,0:T(8,128)(2,1)}, u32[]{:S(2)}, u32[]{:S(2)}) collective-permute-start(bf16[1024,768]{1,0:T(8,128)(2,1)} %get-tuple-element.372), channel_id=1, source_target_pairs={{0,2},{2,0},{4,6},{6,4},{8,10},{10,8},{12,14},{14,12},{16,18},{18,... | collective-permute-start | bytes 4718600 | tf_op jit(solution)/shard_map/ppermute | solution.py:674
  223.2 18.1 %collective-permute-start.33 = (f32[40,1024]{1,0:T(8,128)}, f32[40,1024]{1,0:T(8,128)S(1)}, u32[]{:S(2)}, u32[]{:S(2)}) collective-permute-start(f32[40,1024]{1,0:T(8,128)} %add.597), channel_id=1, source_target_pairs={{0,2},{2,0},{4,6},{6,4},{8,10},{10,8},{12,14},{14,12},{16,18},{18,... | collective-permute-start | bytes 491528 | tf_op jit(solution)/shard_map/ppermute | solution.py:674
  223.7 33.0 %collective-permute-start.34 = (bf16[128,1024]{1,0:T(8,128)(2,1)}, bf16[128,1024]{1,0:T(8,128)(2,1)S(1)}, u32[]{:S(2)}, u32[]{:S(2)}) collective-permute-start(bf16[128,1024]{1,0:T(8,128)(2,1)} %get-tuple-element.381), channel_id=1, source_target_pairs={{0,4},{2,6},{4,0},{6,2},{8,12},{10,14},{12,8},{14,10},{16,20},{18,... | collective-permute-start | bytes 786440 | tf_op jit(solution)/shard_map/ppermute | solution.py:674
  225.2 32.2 %collective-permute-start.35 = (bf16[128,1024]{1,0:T(8,128)(2,1)}, bf16[128,1024]{1,0:T(8,128)(2,1)S(1)}, u32[]{:S(2)}, u32[]{:S(2)}) collective-permute-start(bf16[128,1024]{1,0:T(8,128)(2,1)} %get-tuple-element.382), channel_id=1, source_target_pairs={{0,4},{2,6},{4,0},{6,2},{8,12},{10,14},{12,8},{14,10},{16,20},{18,... | collective-permute-start | bytes 786440 | tf_op jit(solution)/shard_map/ppermute | solution.py:674
  225.7 17.2 %collective-permute-start.32 = (bf16[256,1024]{1,0:T(8,128)(2,1)}, bf16[256,1024]{1,0:T(8,128)(2,1)S(1)}, u32[]{:S(2)}, u32[]{:S(2)}) collective-permute-start(bf16[256,1024]{1,0:T(8,128)(2,1)} %get-tuple-element.373), channel_id=1, source_target_pairs={{0,1},{1,0},{2,3},{3,2},{4,5},{5,4},{6,7},{7,6},{8,9},{9,8},{10,11... | collective-permute-start | bytes 1572872 | tf_op jit(solution)/shard_map/ppermute | solution.py:669
  241.3 17.7 %collective-permute-start.36 = (bf16[128,1024]{1,0:T(8,128)(2,1)}, bf16[128,1024]{1,0:T(8,128)(2,1)}, u32[]{:S(2)}, u32[]{:S(2)}) collective-permute-start(bf16[128,1024]{1,0:T(8,128)(2,1)} %get-tuple-element.383), channel_id=1, source_target_pairs={{0,8},{2,10},{4,12},{6,14},{8,0},{10,2},{12,4},{14,6},{16,24},{18,... | collective-permute-start | bytes 786440 | tf_op jit(solution)/shard_map/ppermute | solution.py:674
  242.9 16.8 %collective-permute-start.37 = (bf16[128,1024]{1,0:T(8,128)(2,1)}, bf16[128,1024]{1,0:T(8,128)(2,1)}, u32[]{:S(2)}, u32[]{:S(2)}) collective-permute-start(bf16[128,1024]{1,0:T(8,128)(2,1)} %get-tuple-element.384), channel_id=1, source_target_pairs={{0,8},{2,10},{4,12},{6,14},{8,0},{10,2},{12,4},{14,6},{16,24},{18,... | collective-permute-start | bytes 786440 | tf_op jit(solution)/shard_map/ppermute | solution.py:674
  243.3 20.3 %collective-permute-start.38 = (bf16[1024,256]{1,0:T(8,128)(2,1)S(1)}, bf16[1024,256]{1,0:T(8,128)(2,1)S(1)}, u32[]{:S(2)}, u32[]{:S(2)}) collective-permute-start(bf16[1024,256]{1,0:T(8,128)(2,1)S(1)} %copy-done.43), channel_id=1, source_target_pairs={{0,4},{2,6},{4,0},{6,2},{8,12},{10,14},{12,8},{14,10},{16,20},{18,... | collective-permute-start | bytes 1572872 | tf_op jit(solution)/shard_map/ppermute | solution.py:674
  256.7 14.0 %collective-permute-start.39 = (bf16[1024,256]{1,0:T(8,128)(2,1)S(1)}, bf16[1024,256]{1,0:T(8,128)(2,1)S(1)}, u32[]{:S(2)}, u32[]{:S(2)}) collective-permute-start(bf16[1024,256]{1,0:T(8,128)(2,1)S(1)} %copy-done.42), channel_id=1, source_target_pairs={{0,4},{2,6},{4,0},{6,2},{8,12},{10,14},{12,8},{14,10},{16,20},{18,... | collective-permute-start | bytes 1572872 | tf_op jit(solution)/shard_map/ppermute | solution.py:674
  257.4 14.9 %collective-permute-start.41 = (bf16[1024,256]{1,0:T(8,128)(2,1)S(1)}, bf16[1024,256]{1,0:T(8,128)(2,1)S(1)}, u32[]{:S(2)}, u32[]{:S(2)}) collective-permute-start(bf16[1024,256]{1,0:T(8,128)(2,1)S(1)} %copy-done.44), channel_id=1, source_target_pairs={{0,8},{2,10},{4,12},{6,14},{8,0},{10,2},{12,4},{14,6},{16,24},{18,... | collective-permute-start | bytes 1572872 | tf_op jit(solution)/shard_map/ppermute | solution.py:674
  259.1 21.5 %collective-permute-start.42 = (bf16[1024,256]{1,0:T(8,128)(2,1)S(1)}, bf16[1024,256]{1,0:T(8,128)(2,1)S(1)}, u32[]{:S(2)}, u32[]{:S(2)}) collective-permute-start(bf16[1024,256]{1,0:T(8,128)(2,1)S(1)} %copy-done.45), channel_id=1, source_target_pairs={{0,8},{2,10},{4,12},{6,14},{8,0},{10,2},{12,4},{14,6},{16,24},{18,... | collective-permute-start | bytes 1572872 | tf_op jit(solution)/shard_map/ppermute | solution.py:674
  259.7 20.9 %collective-permute-start.40 = (bf16[256,1024]{1,0:T(8,128)(2,1)S(1)}, bf16[256,1024]{1,0:T(8,128)(2,1)S(1)}, u32[]{:S(2)}, u32[]{:S(2)}) collective-permute-start(bf16[256,1024]{1,0:T(8,128)(2,1)S(1)} %copy-done.53), channel_id=1, source_target_pairs={{0,1},{1,0},{2,3},{3,2},{4,5},{5,4},{6,7},{7,6},{8,9},{9,8},{10,11... | collective-permute-start | bytes 1572872 | tf_op jit(solution)/shard_map/ppermute | solution.py:669
  263.6 28.4 %collective-permute-start.49 = (f32[40,1024]{1,0:T(8,128)}, f32[40,1024]{1,0:T(8,128)}, u32[]{:S(2)}, u32[]{:S(2)}) collective-permute-start(f32[40,1024]{1,0:T(8,128)} %add.601), channel_id=1, source_target_pairs={{0,4},{2,6},{4,0},{6,2},{8,12},{10,14},{12,8},{14,10},{16,20},{18,... | collective-permute-start | bytes 491528 | tf_op jit(solution)/shard_map/ppermute | solution.py:674
  291.4 21.3 %collective-permute-start.46 = (bf16[64,1024]{1,0:T(8,128)(2,1)}, bf16[64,1024]{1,0:T(8,128)(2,1)}, u32[]{:S(2)}, u32[]{:S(2)}) collective-permute-start(bf16[64,1024]{1,0:T(8,128)(2,1)} %add_convert_fusion.47), channel_id=1, source_target_pairs={{0,4},{2,6},{4,0},{6,2},{8,12},{10,14},{12,8},{14,10},{16,20},{18,... | collective-permute-start | bytes 393224 | tf_op jit(solution)/shard_map/ppermute | solution.py:674
  292.0 20.9 %collective-permute-start.47 = (bf16[512,256]{1,0:T(8,128)(2,1)}, bf16[512,256]{1,0:T(8,128)(2,1)}, u32[]{:S(2)}, u32[]{:S(2)}) collective-permute-start(bf16[512,256]{1,0:T(8,128)(2,1)} %get-tuple-element.412), channel_id=1, source_target_pairs={{0,8},{2,10},{4,12},{6,14},{8,0},{10,2},{12,4},{14,6},{16,24},{18,... | collective-permute-start | bytes 786440 | tf_op jit(solution)/shard_map/ppermute | solution.py:674
  294.1 18.8 %collective-permute-start.48 = (bf16[512,256]{1,0:T(8,128)(2,1)}, bf16[512,256]{1,0:T(8,128)(2,1)}, u32[]{:S(2)}, u32[]{:S(2)}) collective-permute-start(bf16[512,256]{1,0:T(8,128)(2,1)} %add_convert_fusion.21), channel_id=1, source_target_pairs={{0,8},{2,10},{4,12},{6,14},{8,0},{10,2},{12,4},{14,6},{16,24},{18,... | collective-permute-start | bytes 786440 | tf_op jit(solution)/shard_map/ppermute | solution.py:674
  297.0 15.9 %collective-permute-start.50 = (bf16[512,256]{1,0:T(8,128)(2,1)}, bf16[512,256]{1,0:T(8,128)(2,1)}, u32[]{:S(2)}, u32[]{:S(2)}) collective-permute-start(bf16[512,256]{1,0:T(8,128)(2,1)} %get-tuple-element.415), channel_id=1, source_target_pairs={{0,4},{2,6},{4,0},{6,2},{8,12},{10,14},{12,8},{14,10},{16,20},{18,... | collective-permute-start | bytes 786440 | tf_op jit(solution)/shard_map/ppermute | solution.py:674
  298.5 14.5 %collective-permute-start.51 = (bf16[512,256]{1,0:T(8,128)(2,1)}, bf16[512,256]{1,0:T(8,128)(2,1)}, u32[]{:S(2)}, u32[]{:S(2)}) collective-permute-start(bf16[512,256]{1,0:T(8,128)(2,1)} %add_convert_fusion.19), channel_id=1, source_target_pairs={{0,4},{2,6},{4,0},{6,2},{8,12},{10,14},{12,8},{14,10},{16,20},{18,... | collective-permute-start | bytes 786440 | tf_op jit(solution)/shard_map/ppermute | solution.py:674
  312.7 20.9 %collective-permute-start.52 = (bf16[512,768]{1,0:T(8,128)(2,1)}, bf16[512,768]{1,0:T(8,128)(2,1)}, u32[]{:S(2)}, u32[]{:S(2)}) collective-permute-start(bf16[512,768]{1,0:T(8,128)(2,1)} %get-tuple-element.426), channel_id=1, source_target_pairs={{0,1},{1,0},{2,3},{3,2},{4,5},{5,4},{6,7},{7,6},{8,9},{9,8},{10,11... | collective-permute-start | bytes 2359304 | tf_op jit(solution)/shard_map/ppermute | solution.py:669
  321.2 16.9 %collective-permute-start.53 = (bf16[64,1024]{1,0:T(8,128)(2,1)}, bf16[64,1024]{1,0:T(8,128)(2,1)}, u32[]{:S(2)}, u32[]{:S(2)}) collective-permute-start(bf16[64,1024]{1,0:T(8,128)(2,1)} %add_convert_fusion.45), channel_id=1, source_target_pairs={{0,1},{1,0},{2,3},{3,2},{4,5},{5,4},{6,7},{7,6},{8,9},{9,8},{10,11... | collective-permute-start | bytes 393224 | tf_op jit(solution)/shard_map/ppermute | solution.py:669
  323.0 15.3 %collective-permute-start.54 = (bf16[64,1024]{1,0:T(8,128)(2,1)}, bf16[64,1024]{1,0:T(8,128)(2,1)}, u32[]{:S(2)}, u32[]{:S(2)}) collective-permute-start(bf16[64,1024]{1,0:T(8,128)(2,1)} %add_convert_fusion.43), channel_id=1, source_target_pairs={{0,1},{1,0},{2,3},{3,2},{4,5},{5,4},{6,7},{7,6},{8,9},{9,8},{10,11... | collective-permute-start | bytes 393224 | tf_op jit(solution)/shard_map/ppermute | solution.py:669
  333.5 32.7 %collective-permute-start.56 = (bf16[1024,768]{1,0:T(8,128)(2,1)}, bf16[1024,768]{1,0:T(8,128)(2,1)}, u32[]{:S(2)}, u32[]{:S(2)}) collective-permute-start(bf16[1024,768]{1,0:T(8,128)(2,1)} %get-tuple-element.434), channel_id=1, source_target_pairs={{0,2},{2,0},{4,6},{6,4},{8,10},{10,8},{12,14},{14,12},{16,18},{18,... | collective-permute-start | bytes 4718600 | tf_op jit(solution)/shard_map/ppermute | solution.py:674
  334.7 19.2 %collective-permute-start.55 = (bf16[512,256]{1,0:T(8,128)(2,1)}, bf16[512,256]{1,0:T(8,128)(2,1)}, u32[]{:S(2)}, u32[]{:S(2)}) collective-permute-start(bf16[512,256]{1,0:T(8,128)(2,1)} %add_convert_fusion.17), channel_id=1, source_target_pairs={{0,1},{1,0},{2,3},{3,2},{4,5},{5,4},{6,7},{7,6},{8,9},{9,8},{10,11... | collective-permute-start | bytes 786440 | tf_op jit(solution)/shard_map/ppermute | solution.py:669
  336.5 17.4 %collective-permute-start.57 = (f32[40,1024]{1,0:T(8,128)S(1)}, f32[40,1024]{1,0:T(8,128)}, u32[]{:S(2)}, u32[]{:S(2)}) collective-permute-start(f32[40,1024]{1,0:T(8,128)S(1)} %add.636), channel_id=1, source_target_pairs={{0,8},{2,10},{4,12},{6,14},{8,0},{10,2},{12,4},{14,6},{16,24},{18,... | collective-permute-start | bytes 491528 | tf_op jit(solution)/shard_map/ppermute | solution.py:674
  338.1 15.8 %collective-permute-start.59 = (bf16[512,256]{1,0:T(8,128)(2,1)}, bf16[512,256]{1,0:T(8,128)(2,1)}, u32[]{:S(2)}, u32[]{:S(2)}) collective-permute-start(bf16[512,256]{1,0:T(8,128)(2,1)} %add_convert_fusion.15), channel_id=1, source_target_pairs={{0,1},{1,0},{2,3},{3,2},{4,5},{5,4},{6,7},{7,6},{8,9},{9,8},{10,11... | collective-permute-start | bytes 786440 | tf_op jit(solution)/shard_map/ppermute | solution.py:669
  338.4 27.9 %collective-permute-start.58 = (bf16[512,768]{1,0:T(8,128)(2,1)}, bf16[512,768]{1,0:T(8,128)(2,1)}, u32[]{:S(2)}, u32[]{:S(2)}) collective-permute-start(bf16[512,768]{1,0:T(8,128)(2,1)} %get-tuple-element.436), channel_id=1, source_target_pairs={{0,1},{1,0},{2,3},{3,2},{4,5},{5,4},{6,7},{7,6},{8,9},{9,8},{10,11... | collective-permute-start | bytes 2359304 | tf_op jit(solution)/shard_map/ppermute | solution.py:669
  395.4 31.8 %collective-permute-start.66 = (bf16[256,1024]{1,0:T(8,128)(2,1)S(1)}, bf16[256,1024]{1,0:T(8,128)(2,1)S(1)}, u32[]{:S(2)}, u32[]{:S(2)}) collective-permute-start(bf16[256,1024]{1,0:T(8,128)(2,1)S(1)} %get-tuple-element.463), channel_id=1, source_target_pairs={{0,1},{1,0},{2,3},{3,2},{4,5},{5,4},{6,7},{7,6},{8,9},{9,8},{10,11... | collective-permute-start | bytes 1572872 | tf_op jit(solution)/shard_map/ppermute | solution.py:669
  397.9 29.3 %collective-permute-start.64 = (bf16[256,768]{1,0:T(8,128)(2,1)S(1)}, bf16[256,768]{1,0:T(8,128)(2,1)S(1)}, u32[]{:S(2)}, u32[]{:S(2)}) collective-permute-start(bf16[256,768]{1,0:T(8,128)(2,1)S(1)} %get-tuple-element.461), channel_id=1, source_target_pairs={{0,4},{2,6},{4,0},{6,2},{8,12},{10,14},{12,8},{14,10},{16,20},{18,... | collective-permute-start | bytes 1179656 | tf_op jit(solution)/shard_map/ppermute | solution.py:674
  399.4 27.8 %collective-permute-start.65 = (bf16[256,768]{1,0:T(8,128)(2,1)S(1)}, bf16[256,768]{1,0:T(8,128)(2,1)S(1)}, u32[]{:S(2)}, u32[]{:S(2)}) collective-permute-start(bf16[256,768]{1,0:T(8,128)(2,1)S(1)} %get-tuple-element.462), channel_id=1, source_target_pairs={{0,8},{2,10},{4,12},{6,14},{8,0},{10,2},{12,4},{14,6},{16,24},{18,... | collective-permute-start | bytes 1179656 | tf_op jit(solution)/shard_map/ppermute | solution.py:674
  421.6 18.9 %collective-permute-start.103 = (f32[40,1024]{1,0:T(8,128)S(1)}, f32[40,1024]{1,0:T(8,128)S(1)}, u32[]{:S(2)}, u32[]{:S(2)}) collective-permute-start(f32[40,1024]{1,0:T(8,128)S(1)} %copy-done.41), channel_id=1, source_target_pairs={{0,16},{2,18},{4,20},{6,22},{8,24},{10,26},{12,28},{14,30},{16,0},... | collective-permute-start | bytes 491528 | tf_op jit(solution)/shard_map/ppermute | solution.py:674
  433.3 15.2 %collective-permute-start.69 = (bf16[32,1024]{1,0:T(8,128)(2,1)S(1)}, bf16[32,1024]{1,0:T(8,128)(2,1)S(1)}, u32[]{:S(2)}, u32[]{:S(2)}) collective-permute-start(bf16[32,1024]{1,0:T(8,128)(2,1)S(1)} %get-tuple-element.474), channel_id=1, source_target_pairs={{0,16},{2,18},{4,20},{6,22},{8,24},{10,26},{12,28},{14,30},{16,0},... | collective-permute-start | bytes 196616 | tf_op jit(solution)/shard_map/ppermute | solution.py:674
  436.2 18.6 %collective-permute-start.74 = (bf16[256,1024]{1,0:T(8,128)(2,1)S(1)}, bf16[256,1024]{1,0:T(8,128)(2,1)S(1)}, u32[]{:S(2)}, u32[]{:S(2)}) collective-permute-start(bf16[256,1024]{1,0:T(8,128)(2,1)S(1)} %get-tuple-element.479), channel_id=1, source_target_pairs={{0,1},{1,0},{2,3},{3,2},{4,5},{5,4},{6,7},{7,6},{8,9},{9,8},{10,11... | collective-permute-start | bytes 1572872 | tf_op jit(solution)/shard_map/ppermute | solution.py:669
  440.7 14.1 %collective-permute-start.72 = (bf16[128,768]{1,0:T(8,128)(2,1)S(1)}, bf16[128,768]{1,0:T(8,128)(2,1)S(1)}, u32[]{:S(2)}, u32[]{:S(2)}) collective-permute-start(bf16[128,768]{1,0:T(8,128)(2,1)S(1)} %get-tuple-element.477), channel_id=1, source_target_pairs={{0,8},{2,10},{4,12},{6,14},{8,0},{10,2},{12,4},{14,6},{16,24},{18,... | collective-permute-start | bytes 589832 | tf_op jit(solution)/shard_map/ppermute | solution.py:674
  455.1 21.0 %collective-permute-start.78 = (bf16[512,256]{1,0:T(8,128)(2,1)S(1)}, bf16[512,256]{1,0:T(8,128)(2,1)S(1)}, u32[]{:S(2)}, u32[]{:S(2)}) collective-permute-start(bf16[512,256]{1,0:T(8,128)(2,1)S(1)} %pad_maximum_fusion.18), channel_id=1, source_target_pairs={{0,8},{2,10},{4,12},{6,14},{8,0},{10,2},{12,4},{14,6},{16,24},{18,... | collective-permute-start | bytes 786440 | tf_op jit(solution)/shard_map/ppermute | solution.py:674
  476.3 26.1 %collective-permute-start.86 = (bf16[1024,256]{1,0:T(8,128)(2,1)S(1)}, bf16[1024,256]{1,0:T(8,128)(2,1)S(1)}, u32[]{:S(2)}, u32[]{:S(2)}) collective-permute-start(bf16[1024,256]{1,0:T(8,128)(2,1)S(1)} %pad_maximum_fusion.12), channel_id=1, source_target_pairs={{0,4},{2,6},{4,0},{6,2},{8,12},{10,14},{12,8},{14,10},{16,20},{18,... | collective-permute-start | bytes 1572872 | tf_op jit(solution)/shard_map/ppermute | solution.py:674
  480.6 21.8 %collective-permute-start.90 = (bf16[256,1024]{1,0:T(8,128)(2,1)S(1)}, bf16[256,1024]{1,0:T(8,128)(2,1)S(1)}, u32[]{:S(2)}, u32[]{:S(2)}) collective-permute-start(bf16[256,1024]{1,0:T(8,128)(2,1)S(1)} %get-tuple-element.511), channel_id=1, source_target_pairs={{0,1},{1,0},{2,3},{3,2},{4,5},{5,4},{6,7},{7,6},{8,9},{9,8},{10,11... | collective-permute-start | bytes 1572872 | tf_op jit(solution)/shard_map/ppermute | solution.py:669
  480.6 21.8 %collective-permute-start.91 = (bf16[1024,256]{1,0:T(8,128)(2,1)S(1)}, bf16[1024,256]{1,0:T(8,128)(2,1)S(1)}, u32[]{:S(2)}, u32[]{:S(2)}) collective-permute-start(bf16[1024,256]{1,0:T(8,128)(2,1)S(1)} %pad_maximum_fusion.13), channel_id=1, source_target_pairs={{0,8},{2,10},{4,12},{6,14},{8,0},{10,2},{12,4},{14,6},{16,24},{18,... | collective-permute-start | bytes 1572872 | tf_op jit(solution)/shard_map/ppermute | solution.py:674
  485.0 14.5 %collective-permute-start.84 = (bf16[128,1024]{1,0:T(8,128)(2,1)S(1)}, bf16[128,1024]{1,0:T(8,128)(2,1)S(1)}, u32[]{:S(2)}, u32[]{:S(2)}) collective-permute-start(bf16[128,1024]{1,0:T(8,128)(2,1)S(1)} %pad_maximum_fusion.20), channel_id=1, source_target_pairs={{0,4},{2,6},{4,0},{6,2},{8,12},{10,14},{12,8},{14,10},{16,20},{18,... | collective-permute-start | bytes 786440 | tf_op jit(solution)/shard_map/ppermute | solution.py:674
  503.6 18.4 %collective-permute-start.92 = (bf16[256,1024]{1,0:T(8,128)(2,1)S(1)}, bf16[256,1024]{1,0:T(8,128)(2,1)S(1)}, u32[]{:S(2)}, u32[]{:S(2)}) collective-permute-start(bf16[256,1024]{1,0:T(8,128)(2,1)S(1)} %pad_maximum_fusion.14), channel_id=1, source_target_pairs={{0,2},{2,0},{4,6},{6,4},{8,10},{10,8},{12,14},{14,12},{16,18},{18,... | collective-permute-start | bytes 1572872 | tf_op jit(solution)/shard_map/ppermute | solution.py:674
  503.7 18.3 %collective-permute-start.93 = (bf16[256,1024]{1,0:T(8,128)(2,1)S(1)}, bf16[256,1024]{1,0:T(8,128)(2,1)S(1)}, u32[]{:S(2)}, u32[]{:S(2)}) collective-permute-start(bf16[256,1024]{1,0:T(8,128)(2,1)S(1)} %pad_maximum_fusion.15), channel_id=1, source_target_pairs={{0,2},{2,0},{4,6},{6,4},{8,10},{10,8},{12,14},{14,12},{16,18},{18,... | collective-permute-start | bytes 1572872 | tf_op jit(solution)/shard_map/ppermute | solution.py:674
  504.2 17.8 %collective-permute-start.94 = (bf16[2048,256]{1,0:T(8,128)(2,1)S(1)}, bf16[2048,256]{1,0:T(8,128)(2,1)S(1)}, u32[]{:S(2)}, u32[]{:S(2)}) collective-permute-start(bf16[2048,256]{1,0:T(8,128)(2,1)S(1)} %pad_maximum_fusion.6), channel_id=1, source_target_pairs={{0,2},{2,0},{4,6},{6,4},{8,10},{10,8},{12,14},{14,12},{16,18},{18,... | collective-permute-start | bytes 3145736 | tf_op jit(solution)/shard_map/ppermute | solution.py:674
  504.4 17.6 %collective-permute-start.98 = (bf16[2048,256]{1,0:T(8,128)(2,1)S(1)}, bf16[2048,256]{1,0:T(8,128)(2,1)S(1)}, u32[]{:S(2)}, u32[]{:S(2)}) collective-permute-start(bf16[2048,256]{1,0:T(8,128)(2,1)S(1)} %pad_maximum_fusion.7), channel_id=1, source_target_pairs={{0,2},{2,0},{4,6},{6,4},{8,10},{10,8},{12,14},{14,12},{16,18},{18,... | collective-permute-start | bytes 3145736 | tf_op jit(solution)/shard_map/ppermute | solution.py:674
  (132 other events, 1303.0 us)

commit v3 on v2

--- a/solution.py
+++ b/solution.py
@@ -36,7 +36,7 @@
 def params(count=1):
     return pltpu.CompilerParams(
         dimension_semantics=("arbitrary",) * count if count else None,
-        vmem_limit_bytes=56 * 1024 * 1024,
+        vmem_limit_bytes=59 * 1024 * 1024,
     )
 
 
@@ -46,6 +46,10 @@
 
 def whole(shape):
     return pl.BlockSpec(shape, lambda *_: (0,) * len(shape))
+
+
+def once(shape):
+    return pl.BlockSpec(shape, lambda *_: (0,) * len(shape), pipeline_mode=pl.Buffered(1))
 
 
 def lane_iota(rows, lanes=LANES):
@@ -269,9 +273,8 @@
 def experts_kernel(
     order_ref, second_ref, cot_ref, resid_ref, gates_ref, places_ref, gain_ref, wr_ref,
     wg_a_ref, wg_b_ref, wu_a_ref, wu_b_ref, wd_a_ref, wd_b_ref,
-    out_ref, low_ref, grad_ref, small_ref,
-    gg_a_ref, gg_b_ref, gu_a_ref, gu_b_ref, gd_a_ref, gd_b_ref,
-    moe_ref, back_ref, slot_grads_ref,
+    out_ref, low_ref, grad_ref, small_ref, kept_ref, sent_ref,
+    moe_ref, slot_grads_ref,
 ):
     step = pl.program_id(0)
     e = step ^ order_ref[0]
@@ -286,10 +289,8 @@
     out_grad = (gate_slot * slot_grad).astype(bf16)
     expert_out = None
     back = None
-    for wg_ref, wu_ref, wd_ref, gg_ref, gu_ref, gd_ref in (
-        (wg_a_ref, wu_a_ref, wd_a_ref, gg_a_ref, gu_a_ref, gd_a_ref),
-        (wg_b_ref, wu_b_ref, wd_b_ref, gg_b_ref, gu_b_ref, gd_b_ref),
-    ):
+    factors = []
+    for wg_ref, wu_ref, wd_ref in ((wg_a_ref, wu_a_ref, wd_a_ref), (wg_b_ref, wu_b_ref, wd_b_ref)):
         wg, wu, wd = wg_ref[0], wu_ref[0], wd_ref[0]
         gate_pre = nn(expert_in, wg)
         up_pre = nn(expert_in, wu)
@@ -299,13 +300,27 @@
         part = nn(hidden, wd)
         expert_out = part if expert_out is None else expert_out + part
         hidden_grad = nt(out_grad, wd)
-        gd_ref[0] = tn(hidden, out_grad).astype(bf16)
         gate_low = (hidden_grad * up_pre * sig * (1.0 + gate_pre * (1.0 - sig))).astype(bf16)
         up_low = (hidden_grad * silu).astype(bf16)
-        gg_ref[0] = tn(expert_in, gate_low).astype(bf16)
-        gu_ref[0] = tn(expert_in, up_low).astype(bf16)
+        factors.append((gate_low, up_low, hidden))
         part = nt(gate_low, wg) + nt(up_low, wu)
         back = part if back is None else back + part
+
+    def weight_grads(ref):
+        size = hidden.shape[1]
+        for half, (gate_low, up_low, mixed) in enumerate(factors):
+            ref[0, half, :size, :] = tn(gate_low, expert_in).astype(bf16)
+            ref[0, half, size : 2 * size, :] = tn(up_low, expert_in).astype(bf16)
+            ref[0, half, 2 * size :, :] = tn(mixed, out_grad).astype(bf16)
+
+    @pl.when(step % 2 == 0)
+    def _():
+        weight_grads(kept_ref)
+
+    @pl.when(step % 2 == 1)
+    def _():
+        weight_grads(sent_ref)
+
     slot_gate = jnp.sum(expert_out * slot_grad, axis=1, keepdims=True)
     gate_row = jnp.sum(jnp.where(hit, slot_gate, 0.0), axis=0, keepdims=True)
     moe = tn(onehot, (gate_slot * expert_out).astype(bf16))
@@ -314,13 +329,13 @@
     @pl.when(step == 0)
     def _():
         moe_ref[...] = moe
-        back_ref[...] = second_back
+        grad_ref[...] = second_back
         slot_grads_ref[...] = jnp.zeros_like(slot_grads_ref)
 
     @pl.when(step > 0)
     def _():
         moe_ref[...] += moe
-        back_ref[...] += second_back
+        grad_ref[...] += second_back
 
     slot_grads_ref[pl.ds(e, 1), :] = gate_row
 
@@ -332,7 +347,7 @@
         gate_grad = slot_grads_ref[...]
         logit_grad = gates * (gate_grad - jnp.sum(gates * gate_grad, axis=0, keepdims=True))
         router_grad = None
-        second_grad = back_ref[...]
+        second_grad = grad_ref[...]
         for piece in split_three(logit_grad):
             part = nn(piece, second)
             router_grad = part if router_grad is None else router_grad + part
@@ -360,17 +375,17 @@
     tall = pl.BlockSpec((1, hidden, width), lambda i, o: (i ^ o[0], 0, 0))
     wide_rel = pl.BlockSpec((1, width, hidden), lambda i, o: (i, 0, 0))
     tall_rel = pl.BlockSpec((1, hidden, width), lambda i, o: (i, 0, 0))
-    wide_out = jax.ShapeDtypeStruct((window, width, hidden), bf16)
-    tall_out = jax.ShapeDtypeStruct((window, hidden, width), bf16)
+    grads_out = jax.ShapeDtypeStruct((window // 2, 2, 3 * hidden, width), bf16)
+    grads = pl.BlockSpec((1, 2, 3 * hidden, width), lambda i, o: ((i // 2) ^ (o[0] // 2), 0, 0, 0))
     return pl.pallas_call(
         experts_kernel,
         grid_spec=pltpu.PrefetchScalarGridSpec(
         num_scalar_prefetch=1,
         grid=(window,),
         in_specs=[
-            whole((rows, width)),
-            whole((rows, width)),
-            whole((rows, width)),
+            once((rows, width)),
+            once((rows, width)),
+            once((rows, width)),
             whole((experts, rows)),
             whole((8, rows)),
             whole((1, width)),
@@ -383,19 +398,14 @@
             tall_rel,
         ],
         out_specs=[
-            whole((rows, width)),
-            whole((rows, width)),
-            whole((rows, width)),
+            once((rows, width)),
+            once((rows, width)),
+            once((rows, width)),
             whole((experts + 8, width)),
-            wide,
-            wide,
-            wide,
-            wide,
-            tall,
-            tall,
+            grads,
+            grads,
         ],
         scratch_shapes=[
-            pltpu.VMEM((rows, width), f32),
             pltpu.VMEM((rows, width), f32),
             pltpu.VMEM((experts, rows), f32),
         ],
@@ -405,12 +415,8 @@
             jax.ShapeDtypeStruct((rows, width), bf16),
             jax.ShapeDtypeStruct((rows, width), f32),
             jax.ShapeDtypeStruct((experts + 8, width), f32),
-            wide_out,
-            wide_out,
-            wide_out,
-            wide_out,
-            tall_out,
-            tall_out,
+            grads_out,
+            grads_out,
         ),
         compiler_params=params(),
         cost_estimate=cost(39),
@@ -593,76 +599,176 @@
     return piece.reshape(shape)
 
 
-def reorder(piece, place, count):
-    rows, columns = piece.shape
+def add_split(colors, sides):
+    rows = [terms[0][0].shape[1] for terms in colors]
+    half = rows[0] // 2
+    if half % 16:
+        out = []
+        for terms, side in zip(colors, sides):
+            cutouts = [lax.slice_in_dim(t, i * n, (i + 1) * n, axis=0) for t, n, i in terms]
+            both = []
+            for at in (side, 1 - side):
+                pieces = [lax.dynamic_slice_in_dim(t, at * half, half, 1).astype(f32) for t in cutouts]
+                both.append(sum(pieces[1:], pieces[0]).astype(bf16))
+            out.append(tuple(both))
+        return out
+    steps = 4 if half % 64 == 0 else (2 if half % 32 == 0 else 1)
+    block = half // steps
+    in_specs, operands, out_specs, shapes, counts = [], [], [], [], []
+    for number, terms in enumerate(colors):
+        counts.append(len(terms))
+        for other in (0, 1):
+            for array, lead, index in terms:
+
+                def place(j, s, number=number, index=index, other=other):
+                    return (index, (s[number] ^ other) * steps + j, 0)
+
+                in_specs.append(pl.BlockSpec((lead, block, array.shape[2]), place))
+                operands.append(array)
+        array, lead, _ = terms[0]
+        for _ in range(2):
+            out_specs.append(pl.BlockSpec((lead, block, array.shape[2]), lambda j, s: (0, j, 0)))
+            shapes.append(jax.ShapeDtypeStruct((lead, half, array.shape[2]), bf16))
+
+    def kernel(side_ref, *refs):
+        ins, outs = refs[: len(operands)], refs[len(operands) :]
+        at = 0
+        for number, count in enumerate(counts):
+            for other in range(2):
+                value = ins[at][...].astype(f32)
+                for term in range(1, count):
+                    value = value + ins[at + term][...].astype(f32)
+                outs[2 * number + other][...] = value.astype(bf16)
+                at += count
+
+    out = pl.pallas_call(
+        kernel,
+        grid_spec=pltpu.PrefetchScalarGridSpec(
+            num_scalar_prefetch=1, grid=(steps,), in_specs=in_specs, out_specs=out_specs
+        ),
+        out_shape=tuple(shapes),
+        compiler_params=params(),
+        cost_estimate=cost(4),
+        name="add_split",
+    )(jnp.stack(sides), *operands)
+    return [(out[2 * i], out[2 * i + 1]) for i in range(len(colors))]
+
+
+def add_halves(colors):
+    count = len(colors)
+    _, rows, columns = colors[0][0].shape
+
+    def kernel(*refs):
+        ins, (mine_ref, theirs_ref) = refs[:-2], refs[-2:]
+        for i in range(count):
+            value = (ins[2 * i][...].astype(f32) + ins[2 * i + 1][...].astype(f32)).astype(bf16)
+            mine_ref[i] = value[0]
+            theirs_ref[i] = value[1]
+
+    shape = jax.ShapeDtypeStruct((count, rows, columns), bf16)
+    return pl.pallas_call(
+        kernel,
+        out_shape=(shape, shape),
+        compiler_params=params(0),
+        cost_estimate=cost(3),
+        name="add_halves",
+    )(*[a for pair in colors for a in pair])
+
+
+def straighten(pieces, places, count):
+    if (pieces[0].shape[0] // count) % 16:
+        return [plain_order(p, at, count) for p, at in zip(pieces, places)], [jnp.int32(0)] * len(places), 1
+    return pieces, places, count
+
+
+def unpack_experts(own, other, places, core, count):
+    pairs = len(own)
+    flat, places, count = straighten([*own, *other], [*places, *places], count)
+    rows, width = flat[0].shape
+    block, hidden = rows // count, rows // 3
+
+    def kernel(place_ref, *refs):
+        ins, (gate_ref, up_ref, down_ref, plain_ref) = refs[: 2 * pairs], refs[2 * pairs :]
+        e = pl.program_id(0)
+        for pair in range(pairs):
+            for far in range(2):
+                ref = ins[far * pairs + pair]
+
+                @pl.when(e == 2 * pair + (place_ref[pairs] ^ far))
+                def _(ref=ref, pair=pair):
+                    for i in range(count):
+                        start = pl.multiple_of((i ^ place_ref[pair]) * block, block)
+                        plain_ref[i * block : (i + 1) * block, :] = ref[pl.ds(start, block), :].astype(f32)
+
+        gate_ref[0] = plain_ref[:hidden, :].T
+        up_ref[0] = plain_ref[hidden : 2 * hidden, :].T
+        down_ref[0] = plain_ref[2 * hidden :, :]
+
+    wide = jax.ShapeDtypeStruct((2 * pairs, width, hidden), f32)
+    tall = jax.ShapeDtypeStruct((2 * pairs, hidden, width), f32)
+    return pl.pallas_call(
+        kernel,
+        grid_spec=pltpu.PrefetchScalarGridSpec(
+            num_scalar_prefetch=1,
+            grid=(2 * pairs,),
+            in_specs=[pl.BlockSpec((rows, width), lambda e, s: (0, 0))] * (2 * pairs),
+            out_specs=[
+                pl.BlockSpec((1, width, hidden), lambda e, s: (e, 0, 0)),
+                pl.BlockSpec((1, width, hidden), lambda e, s: (e, 0, 0)),
+                pl.BlockSpec((1, hidden, width), lambda e, s: (e, 0, 0)),
+            ],
+            scratch_shapes=[pltpu.VMEM((rows, width), f32)],
+        ),
+        out_shape=(wide, wide, tall),
+        compiler_params=params(),
+        cost_estimate=cost(10),
+        name="unpack_experts",
+    )(jnp.stack([*places[:pairs], core]), *flat)
+
+
+def unpack(own, other, places, core, count):
+    colors = len(own)
+    flat, places, count = straighten([*own, *other], [*places, *places], count)
+    rows, columns = flat[0].shape
     block = rows // count
-    if block % 16:
-        return plain_order(piece, place, count).astype(f32)
-
-    def kernel(place_ref, in_ref, out_ref):
-        for i in range(count):
-            start = pl.multiple_of((i ^ place_ref[0]) * block, block)
-            out_ref[i * block : (i + 1) * block, :] = in_ref[pl.ds(start, block), :].astype(f32)
+    shapes = (
+        jax.ShapeDtypeStruct((colors * rows, 2 * GROUP), f32),
+        jax.ShapeDtypeStruct((colors * rows, 2 * LANES), f32),
+        jax.ShapeDtypeStruct((colors * rows, 2 * LANES), f32),
+        jax.ShapeDtypeStruct((2 * GROUP, colors * rows), f32),
+    )
+
+    def kernel(place_ref, *refs):
+        ins, (query_ref, key_ref, value_ref, output_ref, plain_ref) = refs[: 2 * colors], refs[2 * colors :]
+        for group in range(2):
+            for color in range(colors):
+                for i in range(count):
+                    start = pl.multiple_of((i ^ place_ref[color]) * block, block)
+                    one = ins[color][pl.ds(start, block), :].astype(f32)
+                    two = ins[colors + color][pl.ds(start, block), :].astype(f32)
+                    plain_ref[i * block : (i + 1) * block, :] = jnp.where(place_ref[colors] == group, one, two)
+                here = slice(color * rows, (color + 1) * rows)
+                wide = slice(group * GROUP, (group + 1) * GROUP)
+                thin = slice(group * LANES, (group + 1) * LANES)
+                query_ref[here, wide] = plain_ref[:, :GROUP]
+                key_ref[here, thin] = plain_ref[:, GROUP : GROUP + LANES]
+                value_ref[here, thin] = plain_ref[:, GROUP + LANES : 2 * GROUP]
+                output_ref[wide, here] = plain_ref[:, 2 * GROUP :].T
 
     return pl.pallas_call(
         kernel,
         grid_spec=pltpu.PrefetchScalarGridSpec(
             num_scalar_prefetch=1,
             grid=(1,),
-            in_specs=[pl.BlockSpec((rows, columns), lambda i, s: (0, 0))],
-            out_specs=pl.BlockSpec((rows, columns), lambda i, s: (0, 0)),
-        ),
-        out_shape=jax.ShapeDtypeStruct((rows, columns), f32),
-        compiler_params=params(),
-        cost_estimate=cost(3),
-        name="reorder",
-    )(place[None], piece)
-
-
-def unpack(mine, other, place, core, count):
-    rows, columns = mine.shape
-    block = rows // count
-    shapes = (
-        jax.ShapeDtypeStruct((rows, 2 * GROUP), f32),
-        jax.ShapeDtypeStruct((rows, 2 * LANES), f32),
-        jax.ShapeDtypeStruct((rows, 2 * LANES), f32),
-        jax.ShapeDtypeStruct((2 * GROUP, rows), f32),
-    )
-    if block % 16:
-        one, two = (plain_order(p, place, count) for p in (mine, other))
-        zero, one = jnp.where(core == 0, one, two), jnp.where(core == 0, two, one)
-        parts = ((0, GROUP), (GROUP, GROUP + LANES), (GROUP + LANES, 2 * GROUP), (2 * GROUP, 3 * GROUP))
-        out = [jnp.concatenate([zero[:, a:b], one[:, a:b]], 1).astype(f32) for a, b in parts]
-        return (*out[:3], out[3].T)
-
-    def kernel(place_ref, mine_ref, other_ref, query_ref, key_ref, value_ref, output_ref):
-        for group in range(2):
-            for i in range(count):
-                start = pl.multiple_of((i ^ place_ref[0]) * block, block)
-                here = slice(i * block, (i + 1) * block)
-                one = mine_ref[pl.ds(start, block), :].astype(f32)
-                two = other_ref[pl.ds(start, block), :].astype(f32)
-                rows_of = jnp.where(place_ref[1] == group, one, two)
-                wide = slice(group * GROUP, (group + 1) * GROUP)
-                thin = slice(group * LANES, (group + 1) * LANES)
-                query_ref[here, wide] = rows_of[:, :GROUP]
-                key_ref[here, thin] = rows_of[:, GROUP : GROUP + LANES]
-                value_ref[here, thin] = rows_of[:, GROUP + LANES : 2 * GROUP]
-                output_ref[wide, here] = rows_of[:, 2 * GROUP :].T
-
-    return pl.pallas_call(
-        kernel,
-        grid_spec=pltpu.PrefetchScalarGridSpec(
-            num_scalar_prefetch=1,
-            grid=(1,),
-            in_specs=[pl.BlockSpec((rows, columns), lambda i, s: (0, 0))] * 2,
+            in_specs=[pl.BlockSpec((rows, columns), lambda i, s: (0, 0))] * (2 * colors),
             out_specs=[pl.BlockSpec(o.shape, lambda i, s: (0, 0)) for o in shapes],
+            scratch_shapes=[pltpu.VMEM((rows, columns), f32)],
         ),
         out_shape=shapes,
         compiler_params=params(),
-        cost_estimate=cost(5),
+        cost_estimate=cost(6),
         name="unpack",
-    )(jnp.stack([place, core]), mine, other)
+    )(jnp.stack([*places[:colors], core]), *flat)
 
 
 def swap_tensor(values):
@@ -687,11 +793,7 @@
     return lax.dynamic_slice_in_dim(values, index * size, size, axis)
 
 
-def total(terms, start=None, size=None):
-    if start is not None:
-        terms = [lax.dynamic_slice_in_dim(t, start, size, 0) for t in terms]
-    if len(terms) == 1:
-        return terms[0]
+def total(terms):
     out = terms[0].astype(f32)
     for term in terms[1:]:
         out = out + term.astype(f32)
@@ -700,26 +802,6 @@
 
 def swap(values, bit):
     return swap_tensor(values) if bit == 0 else swap_dp(values, bit)
-
-
-def scatter_sum(mine, theirs, order):
-    for bit in order:
-        if bit == 0:
-            (got,) = yield [(total(theirs), 0)]
-            mine, theirs = [*mine, got], None
-            continue
-        side = bit_of(bit)
-        sides, requests = [], []
-        for terms in (mine, theirs):
-            if terms is None:
-                continue
-            half = terms[0].shape[0] // 2
-            requests.append((total(terms, (1 - side) * half, half), bit))
-            sides.append(total(terms, side * half, half))
-        got = yield requests
-        mine = [sides[0], got[0]]
-        theirs = [sides[1], got[1]] if theirs is not None else None
-    return total(mine)
 
 
 def place_of(order):
@@ -730,12 +812,12 @@
     return place
 
 
-def gather_back(piece, order):
-    for bit in reversed(order):
-        if bit:
-            (got,) = yield [(piece, bit)]
-            piece = jnp.concatenate([piece, got], 0)
-    return piece
+def gather_back(pieces, orders):
+    for bits in zip(*(reversed(order) for order in orders)):
+        got = yield list(zip(pieces, bits))
+        pieces = [jnp.concatenate([p, g], 0) for p, g in zip(pieces, got)]
+    got = yield [(p, 1) for p in pieces]
+    return pieces, got
 
 
 def sum_all(values):
@@ -745,12 +827,37 @@
     return values
 
 
-def full_sum(kept, sent, order):
-    got = yield [(s, 1) for s in sent]
-    piece = yield from scatter_sum([kept[0], got[0]], [kept[1], got[1]], order)
-    piece = yield from gather_back(piece, order)
-    (other,) = yield [(piece, 1)]
-    return piece, other
+def experts_sum(kept, sent, orders, far):
+    flat = kept.reshape(-1, *kept.shape[2:])
+    (got,) = yield [(sent.reshape(flat.shape), 1)]
+    colors = [[(flat, 2, i), (got, 2, i)] for i in range(len(orders))]
+    for bits in zip(*orders):
+        split = add_split(colors, [bit_of(b) for b in bits])
+        got = yield [(s, b) for (_, s), b in zip(split, bits)]
+        colors = [[(k, 2, 0), (g, 2, 0)] for (k, _), g in zip(split, got)]
+    mine, theirs = add_halves([[t for t, _, _ in terms] for terms in colors])
+    (got,) = yield [(theirs, 0)]
+    count = len(orders)
+    for bit in far:
+        ((mine, theirs),) = add_split([[(mine, count, 0), (got, count, 0)]], [bit_of(bit)])
+        (got,) = yield [(theirs, bit)]
+    piece = total([mine, got])
+    for bit in reversed(far):
+        (got,) = yield [(piece, bit)]
+        piece = jnp.concatenate([piece, got], 1)
+    return (yield from gather_back([piece[i] for i in range(count)], orders))
+
+
+def attention_sum(terms, orders, far):
+    count = len(orders)
+    parts = [t.reshape(count, t.shape[0] // count, t.shape[1]) for t in terms]
+    colors = [[(p, 1, i) for p in parts] for i in range(count)]
+    for bits in [*zip(*orders), *[(b,) * count for b in far]]:
+        split = add_split(colors, [bit_of(b) for b in bits])
+        got = yield [(s, b) for (_, s), b in zip(split, bits)]
+        colors = [[(k, 1, 0), (g, 1, 0)] for (k, _), g in zip(split, got)]
+    pieces = [total([k[0], g[0]]) for (k, _, _), (g, _, _) in colors]
+    return (yield from gather_back(pieces, [[*order, *far] for order in orders]))
 
 
 class Chains:
@@ -847,106 +954,66 @@
     corner.append(swap_dp(across[1], 1))
     corner.append(swap_dp(across[2], 1))
     r_gate, r_up, r_down = (jnp.concatenate(parts, axis=0) for parts in zip(got, beside, across, corner))
-    (out, low_grad, resid_grad, small, gg_a, gg_b, gu_a, gu_b, gd_a, gd_b) = experts_layer(
+    out, low_grad, resid_grad, small, kept, sent = experts_layer(
         order_index[None], second, cot, resid, gates, places, gain_two, wr_t,
         (w_gate, r_gate, w_up, r_up, w_down, r_down),
     )
+    small = lax.psum(small, ("dp", "tensor"))
 
     chains = Chains()
-    near_bits = ([2, 4], [4, 2])
-    orders = [[*bits, 0, *far] for bits in near_bits]
-    experts_orders = {"gate": orders[0], "up": orders[1], "down0": orders[0], "down1": orders[1]}
-
-    def experts_chain(name, mine, theirs):
-        flat = [g.reshape(-1, g.shape[-1]) for g in (mine, theirs)]
-        kept = [cut(g, core, 0) for g in flat]
-        sent = [cut(g, 1 - core, 0) for g in flat]
-        chains.add(name, full_sum(kept, sent, experts_orders[name]))
-
-    experts_chain("gate", gg_a, gg_b)
-    experts_chain("up", gu_a, gu_b)
-    experts_chain("down0", gd_a[:, : gd_a.shape[1] // 2], gd_b[:, : gd_a.shape[1] // 2])
-    experts_chain("down1", gd_a[:, gd_a.shape[1] // 2 :], gd_b[:, gd_a.shape[1] // 2 :])
-    chains.add("small", sum_all(small))
-    grads_names = list(experts_orders)
-
-    def one_swap(values, bit):
-        (got,) = yield [(values, bit)]
-        return got
-
-    def piece_swaps(values, count):
+    orders = ([2, 4], [4, 2])
+
+    def piece_swaps(values, count, bit=0):
         size = values.shape[0] // count
         received = []
         for i in range(count):
-            (got,) = yield [(values[i * size : (i + 1) * size], 0)]
+            (got,) = yield [(values[i * size : (i + 1) * size], bit)]
             received.append(got)
-        return jnp.concatenate(received, 0)
-
-    chains.add("out", piece_swaps(out, 4))
+        return received[0] if count == 1 else jnp.concatenate(received, 0)
+
+    chains.add("grads", experts_sum(kept, sent, orders, far))
+    chains.add("out", piece_swaps(out, 2))
     zero = jnp.zeros((1,), jnp.int32)
     one_minus = 1 - core[None]
     shared = (tables, seg_col, seg_row)
 
     low_grad = chains.advance(fence=low_grad)
     back = attend_back(zero, saved_c, *shared, low_grad, far_out)
-    back = chains.advance(grads_names + ["out", "small"], fence=back)
+    back = chains.advance(["grads"], fence=back)
     group_d, partial_sum = project(zero, back, saved_c[3], low_grad, first_t, *far_qkv)
-    chains.add("other", one_swap(group_d, 1))
+    chains.add("other", piece_swaps(group_d, 1, 1))
     low_grad, partial_sum = chains.advance(["other", "out"], fence=(low_grad, partial_sum))
     back = attend_back(zero, saved_b, *shared, low_grad, near_out)
-    back = chains.advance(["other", "out", "small"], fence=back)
+    back = chains.advance(["other"], fence=back)
     group_c, partial_sum = project(zero, back, saved_b[3], low_grad, first_t, *near, before=partial_sum)
-    chains.add("theirs", piece_swaps(total([group_c, chains.done["other"]]), 2))
-    low_grad, partial_sum = chains.advance(grads_names + ["theirs", "out"], fence=(low_grad, partial_sum))
+    chains.add("theirs", piece_swaps(total([group_c, chains.done["other"]]), 1))
+    low_grad, partial_sum = chains.advance(["grads", "out", "theirs"], fence=(low_grad, partial_sum))
     back = attend_back(one_minus, saved_a, *shared, low_grad, w_output)
-    back = chains.advance(grads_names + ["small"], fence=back)
+    back = chains.advance(["grads"], fence=back)
     group_b, partial_sum = project(
         one_minus, back, saved_a[3], low_grad, first_t, w_query, w_key, w_value, before=partial_sum
     )
-    chains.add("mine", one_swap(group_b, 1))
-    low_grad, partial_sum = chains.advance(["mine", "theirs"], fence=(low_grad, partial_sum))
+    chains.add("mine", piece_swaps(group_b, 1, 1))
+    low_grad, partial_sum = chains.advance(["mine"], fence=(low_grad, partial_sum))
     back = attend_back(core[None], saved_a, *shared, low_grad, w_output)
-    back = chains.advance(grads_names + ["mine", "theirs", "small"], fence=back)
+    back = chains.advance(["grads", "mine", "theirs"], fence=back)
     group_a, token, norm_one = project(
         core[None], back, saved_a[3], low_grad, first_t, w_query, w_key, w_value,
         before=partial_sum, final=(x, gain_one, resid_grad),
     )
-    chains.advance(["small"])
-    terms = (group_a, chains.done["mine"], chains.done["theirs"])
-    half = width // 2
-    tails = [[*bits, *far] for bits in near_bits]
-
-    def tail(index):
-        piece = yield from scatter_sum([t[index * half : (index + 1) * half] for t in terms], None, tails[index])
-        piece = yield from gather_back(piece, tails[index])
-        (other,) = yield [(piece, 1)]
-        return piece, other
-
     chains.add("token", piece_swaps(token, 4))
-    chains.add("tail0", tail(0))
-    chains.add("tail1", tail(1))
+    chains.add("tail", attention_sum((group_a, chains.done["mine"], chains.done["theirs"]), orders, far))
     chains.add("norm", sum_all(norm_one))
     chains.finish()
     done = chains.done
 
-    halves = [
-        unpack(*done[f"tail{i}"], place_of(tails[i]), core, dp_size // 2) for i in range(2)
-    ]
-    grad_query, grad_key, grad_value = (jnp.concatenate([a, b], 0) for a, b in zip(halves[0][:3], halves[1][:3]))
-    grad_output = jnp.concatenate([halves[0][3], halves[1][3]], 1)
-
-    def expert_grad(name):
-        piece, other = done[name]
-        place = place_of(experts_orders[name]) + core * (dp_size // 2)
-        return reorder(jnp.concatenate([piece, other], 0), place, dp_size)
-
-    grad_gate = expert_grad("gate").reshape(w_gate.shape)
-    grad_up = expert_grad("up").reshape(w_up.shape)
-    parts = [
-        expert_grad(name).reshape(w_down.shape[0], w_down.shape[1] // 2, width) for name in ("down0", "down1")
-    ]
-    grad_down = jnp.concatenate(parts, 1)
-    small = done["small"]
+    place_far = place_of(far)
+    size_far = 2 ** len(far)
+    own_grads, other_grads = done["grads"]
+    places = [place_of(order) * size_far + place_far for order in orders]
+    grad_gate, grad_up, grad_down = unpack_experts(own_grads, other_grads, places, core, dp_size // 2)
+    own_tail, other_tail = done["tail"]
+    grad_query, grad_key, grad_value, grad_output = unpack(own_tail, other_tail, places, core, dp_size // 2)
     experts = w_router.shape[1]
 
     def both(mine, other):

time: 575 us -> 593 us (1.031)
  waiting for transfers between devices: 105 us -> 200 us
  other arithmetic: 81.9 us -> 32.5 us
  starting transfers between devices: 107 us -> 61.4 us
  Pallas kernels: 214 us -> 245 us
  local copies, waits for them, and re-layouts: 56.1 us -> 29.9 us
  between operations: 2.23 us -> 14.9 us
    psum x0 -> x1, waiting for transfers between devices: none -> 103 us  [per_device(): small = lax.psum(small, ('dp', 'tensor'))]
    convert_element_type x33 -> x4, other arithmetic: 44.3 us -> 3.12 us  [total(): return out.astype(bf16)]
    ppermute x81 -> x46, starting transfers between devices: 82.5 us -> 42.8 us  [swap_dp(): return lax.ppermute(values, 'dp', [(i, i ^ bit) for i in range(count)])]
    pallas_call x4 -> x8, Pallas kernels: 13.1 us -> 42.8 us  [the longest x6 30.6 us: add_split(): pl.pallas_call(kernel, grid_spec=pltpu.PrefetchScalarGridSpec(num_scalar_...]
    ppermute x23 -> x16, waiting for transfers between devices: 29.5 us -> 16 us  [swap_tensor(): return lax.ppermute(values, 'tensor', [(0, 1), (1, 0)])]
    unnamed x210 -> x97, local copies, waits for them, and re-layouts: 21.1 us -> 7.72 us
    dynamic_slice x12 -> x4, local copies, waits for them, and re-layouts: 10.6 us -> 3.12 us  [cut(): return lax.dynamic_slice_in_dim(values, index * size, size, axis)]
    ppermute x23 -> x16, starting transfers between devices: 24.4 us -> 18.6 us  [swap_tensor(): return lax.ppermute(values, 'tensor', [(0, 1), (1, 0)])]
  transfers between devices with their start and end apart: 104 -> 63, of which waited for: 27 -> 20; matrix products, arithmetic and copies ran while one was open for 12% -> 6% of each run, Pallas kernels for 27% -> 28%
where the time goes in v3:
time: 593 us; the launch traced here: 584 us
  Pallas kernels  245 us (41%)
  waiting for transfers between devices  200 us (34%)
  starting transfers between devices  61.4 us (10%)
  other arithmetic  32.5 us (5%)
  local copies, waits for them, and re-layouts  29.9 us (5%)
  between operations  14.9 us (3%)
    psum x1, waiting for transfers between devices, per_device(): small = lax.psum(small, ('dp', 'tensor'))  103 us
    ppermute x46, waiting for transfers between devices, swap_dp(): return lax.ppermute(values, 'dp', [(i, i ^ bit) for i in range(count)])  80.7 us
    pallas_call x4, Pallas kernels, attend_back(): pl.pallas_call(attend_back_kernel, grid_spec=pltpu.PrefetchScalarGridSpec...  53.7 us
    pallas_call x1, Pallas kernels, experts_layer(): pl.pallas_call(experts_kernel, grid_spec=pltpu.PrefetchScalarGridSpec(num...  44 us
    pallas_call x3, Pallas kernels, attend(): pl.pallas_call(attend_kernel, grid=(groups,), in_specs=[whole((rows, widt...  43 us
    ppermute x46, starting transfers between devices, swap_dp(): return lax.ppermute(values, 'dp', [(i, i ^ bit) for i in range(count)])  42.8 us
    pallas_call x4, Pallas kernels, project(): pl.pallas_call(partial(project_kernel, final is not None, before is None)...  42.2 us
    pallas_call x6, Pallas kernels, add_split(): pl.pallas_call(kernel, grid_spec=pltpu.PrefetchScalarGridSpec(num_scalar_...  30.6 us
  transfers between devices with their start and end apart: 63, of which 20 were waited for; matrix products, arithmetic and copies ran while one was open for 6% of the time, Pallas kernels for 28%

profile of v3, /device:TPU:0, one launch (start us, length us, event | category | flops | bytes accessed | tf_op | source)
XLA Modules:
  0.0 583.7 jit_solution(14195260401434368279)
XLA Ops:
  8.4 3.0 collective-permute-start
  13.5 2.1 collective-permute-start.4
  15.6 3.1 constant_dynamic-slice_fusion.3.x_ref.rest_1_
  21.0 5.2 prologue.1
  26.3 20.1 %attend.3 = (bf16[1024,512]{1,0:T(8,128)(2,1)}, bf16[1024,256]{1,0:T(8,128)(2,1)}, bf16[1024,256]{1,0:T(8,128)(2,1)}, bf16[1024,512]{1,0:T(8,128)(2,1)}, f32[2,8,1024]{2,1,0:T(8,128)}) custom-call(bf16[1024,1024]{1,0:T(8,128)(2,1)} %get-tuple-element.239.first_ref, bf16[1024,512]{1,0:T(8,128)(2,1)} %wq_ref.5, bf16[1024,256]{1,0:T(8,128)(2,1)} %wk_ref.5, ...), custom_call_target="tpu_custom_call" | custom-call | flops 22000001024 | bytes 1048576 | tf_op jit(solution)/shard_map/attend/pallas_call | solution.py:184
  51.7 1.9 collective-permute-start.2
  53.6 11.3 %attend.4 = (bf16[1024,256]{1,0:T(8,128)(2,1)}, bf16[1024,128]{1,0:T(8,128)(2,1)}, bf16[1024,128]{1,0:T(8,128)(2,1)}, bf16[1024,256]{1,0:T(8,128)(2,1)}, f32[1,8,1024]{2,1,0:T(8,128)}) custom-call(bf16[1024,1024]{1,0:T(8,128)(2,1)} %get-tuple-element.239.first_ref, bf16[1024,256]{1,0:T(8,128)(2,1)} %collective-permute-done.wq_ref, ...), custom_call_target="tpu_custom_call" | custom-call | flops 11000000512 | bytes 1048576 | tf_op jit(solution)/shard_map/attend/pallas_call | solution.py:184
  66.2 1.8 collective-permute-start.5
  71.1 11.6 %attend.5 = (bf16[1024,256]{1,0:T(8,128)(2,1)}, bf16[1024,128]{1,0:T(8,128)(2,1)}, bf16[1024,128]{1,0:T(8,128)(2,1)}, bf16[1024,256]{1,0:T(8,128)(2,1)}, f32[1,8,1024]{2,1,0:T(8,128)}) custom-call(bf16[1024,1024]{1,0:T(8,128)(2,1)} %get-tuple-element.239.first_ref, bf16[1024,256]{1,0:T(8,128)(2,1)} %copy-done.34, bf16[1024,128]{1,0:T(8,128)(2,1)} %copy-done.41, ...), custom_call_target="tpu_custom_call" | custom-call | flops 11000000512 | bytes 1048576 | tf_op jit(solution)/shard_map/attend/pallas_call | solution.py:184
  85.3 8.3 %router.1 = (f32[1024,1024]{1,0:T(8,128)}, bf16[1024,1024]{1,0:T(8,128)(2,1)}, f32[32,1024]{1,0:T(8,128)}, s32[8,1024]{1,0:T(8,128)}) custom-call(bf16[1024,1024]{1,0:T(8,128)(2,1)} %constant_dynamic-slice_fusion.3.x_ref.rest_1_, bf16[1024,512]{1,0:T(8,128)(2,1)} %get-tuple-element.247.att_a_ref.att_ref, ...), custom_call_target="tpu_custom_call" | custom-call | flops 8800000000 | bytes 1048576 | tf_op jit(solution)/shard_map/router/pallas_call | solution.py:252
  93.6 3.4 collective-permute-done.10
  99.6 10.8 %collective-permute-done.18 = bf16[1,256,1024]{2,1,0:T(8,128)(2,1)S(1)} collective-permute-done((bf16[1,256,1024]{2,1,0:T(8,128)(2,1)}, bf16[1,256,1024]{2,1,0:T(8,128)(2,1)S(1)}, u32[]{:S(2)}, u32[]{:S(2)}) %collective-permute-start.18) | collective-permute-done | bytes 524320 | tf_op jit(solution)/shard_map/ppermute | solution.py:780
  111.9 2.8 pad_maximum_fusion.wg_b_ref
  114.7 2.8 pad_maximum_fusion.1.wu_b_ref
  117.5 2.6 pad_maximum_fusion.2.wd_b_ref
  120.1 44.0 %experts.1 = (bf16[1024,1024]{1,0:T(8,128)(2,1)}, bf16[1024,1024]{1,0:T(8,128)(2,1)}, f32[1024,1024]{1,0:T(8,128)}, f32[40,1024]{1,0:T(8,128)}, bf16[2,2,768,102...) custom-call(s32[1]{0:T(128)} %bitcast.order_ref, bf16[1024,1024]{1,0:T(8,128)(2,1)} %get-tuple-element.252.second_ref, ...), custom_call_target="tpu_custom_call" | custom-call | flops 42900000768 | bytes 1048576 | tf_op jit(solution)/shard_map/experts/pallas_call | solution.py:380
  164.2 1.7 fusion.6
  167.3 13.4 %attend_back.4.back_ref = bf16[1024,512]{1,0:T(8,128)(2,1)} custom-call(s32[1]{0:T(128)} %constant.142.clone.1.sel_ref, bf16[1024,256]{1,0:T(8,128)(2,1)} %get-tuple-element.263.q_ref, bf16[1024,128]{1,0:T(8,128)(2,1)} %get-tuple-element.264.k_ref, bf16[1024,128]{1,0:T(8,128)(2,1)} %get-tuple-element.265.v_ref, f32[1,8,1024]{2,1,0:T(8,128)} %get-tuple-element.266.lse_ref, ...), custom_call_target="tpu_custom_call" | custom-call | flops 15399999488 | bytes 1048576 | tf_op jit(solution)/shard_map/attend_back/pallas_call | solution.py:495
  180.6 8.9 %add_split.6 = (bf16[2,384,1024]{2,1,0:T(8,128)(2,1)}, bf16[2,384,1024]{2,1,0:T(8,128)(2,1)}, bf16[2,384,1024]{2,1,0:T(8,128)(2,1)}, bf16[2,384,1024]{2,1,0:T(8,128)(2,1)}) custom-call(s32[2]{0:T(128)} %get-tuple-element.432.side_ref, bf16[4,768,1024]{2,1,0:T(8,128)(2,1)} %bitcast.31, ...), custom_call_target="tpu_custom_call" | custom-call | flops 4400000000 | bytes 1048576 | tf_op jit(solution)/shard_map/add_split/pallas_call | solution.py:644
  189.5 8.9 %project.3 = (bf16[1024,768]{1,0:T(8,128)(2,1)}, f32[1024,1024]{1,0:T(8,128)}) custom-call(s32[1]{0:T(128)} %constant.142.clone.1.sel_ref, bf16[1024,512]{1,0:T(8,128)(2,1)} %attend_back.4.back_ref, bf16[1024,256]{1,0:T(8,128)(2,1)} %get-tuple-element.249.att_c_ref.att_ref, bf16[1024,1024]{1,0:T(8,128)(2,1)} %get-tuple-element.323.low_ref, ...), custom_call_target="tpu_custom_call" | custom-call | flops 7699999744 | bytes 1048576 | tf_op jit(solution)/shard_map/project/pallas_call | solution.py:579
  199.4 1.9 collective-permute-start.25
  202.5 1.6 collective-permute-start.24
  204.1 13.6 %attend_back.5.back_ref = bf16[1024,512]{1,0:T(8,128)(2,1)} custom-call(s32[1]{0:T(128)} %constant.142.clone.1.sel_ref, bf16[1024,256]{1,0:T(8,128)(2,1)} %get-tuple-element.282.q_ref, bf16[1024,128]{1,0:T(8,128)(2,1)} %get-tuple-element.283.k_ref, bf16[1024,128]{1,0:T(8,128)(2,1)} %get-tuple-element.284.v_ref, f32[1,8,1024]{2,1,0:T(8,128)} %get-tuple-element.285.lse_ref, ...), custom_call_target="tpu_custom_call" | custom-call | flops 15399999488 | bytes 1048576 | tf_op jit(solution)/shard_map/attend_back/pallas_call | solution.py:495
  217.7 10.2 %project.4 = (bf16[1024,768]{1,0:T(8,128)(2,1)}, f32[1024,1024]{1,0:T(8,128)}) custom-call(s32[1]{0:T(128)} %constant.142.clone.1.sel_ref, bf16[1024,512]{1,0:T(8,128)(2,1)} %attend_back.5.back_ref, bf16[1024,256]{1,0:T(8,128)(2,1)} %get-tuple-element.248.att_b_ref.att_ref, bf16[1024,1024]{1,0:T(8,128)(2,1)} %get-tuple-element.323.low_ref, ...), custom_call_target="tpu_custom_call" | custom-call | flops 7699999744 | bytes 1048576 | tf_op jit(solution)/shard_map/project/pallas_call | solution.py:579
  227.9 10.2 %collective-permute-done.23.refs_1_.refs_3_ = bf16[2,384,1024]{2,1,0:T(8,128)(2,1)} collective-permute-done((bf16[2,384,1024]{2,1,0:T(8,128)(2,1)}, bf16[2,384,1024]{2,1,0:T(8,128)(2,1)}, u32[]{:S(2)}, u32[]{:S(2)}) %collective-permute-start.23) | collective-permute-done | bytes 1572896 | tf_op jit(solution)/shard_map/ppermute | solution.py:780
  239.1 2.9 add_convert_fusion
  242.0 5.9 %add_split.7 = (bf16[2,192,1024]{2,1,0:T(8,128)(2,1)}, bf16[2,192,1024]{2,1,0:T(8,128)(2,1)}, bf16[2,192,1024]{2,1,0:T(8,128)(2,1)}, bf16[2,192,1024]{2,1,0:T(8,128)(2,1)}) custom-call(s32[2]{0:T(128)} %get-tuple-element.433.side_ref, bf16[2,384,1024]{2,1,0:T(8,128)(2,1)} %get-tuple-element.300.refs_0_.refs_2_, ...), custom_call_target="tpu_custom_call" | custom-call | flops 4400000000 | bytes 1048576 | tf_op jit(solution)/shard_map/add_split/pallas_call | solution.py:644
  247.9 1.6 collective-permute-start.26
  250.6 13.4 %attend_back.6.back_ref = bf16[1024,512]{1,0:T(8,128)(2,1)} custom-call(s32[1]{0:T(128)S(6)} %sub.28.sel_ref, bf16[1024,512]{1,0:T(8,128)(2,1)} %get-tuple-element.294.q_ref, bf16[1024,256]{1,0:T(8,128)(2,1)} %get-tuple-element.295.k_ref, bf16[1024,256]{1,0:T(8,128)(2,1)} %get-tuple-element.296.v_ref, f32[2,8,1024]{2,1,0:T(8,128)} %get-tuple-element.297.lse_ref, ...), custom_call_target="tpu_custom_call" | custom-call | flops 15399999488 | bytes 1048576 | tf_op jit(solution)/shard_map/attend_back/pallas_call | solution.py:495
  264.0 2.7 collective-permute-done.26.refs_1_
  268.9 3.2 add_halves.1
  272.2 10.6 %project.5 = (bf16[1024,768]{1,0:T(8,128)(2,1)}, f32[1024,1024]{1,0:T(8,128)}) custom-call(s32[1]{0:T(128)S(6)} %sub.28.sel_ref, bf16[1024,512]{1,0:T(8,128)(2,1)} %attend_back.6.back_ref, bf16[1024,512]{1,0:T(8,128)(2,1)} %get-tuple-element.247.att_a_ref.att_ref, bf16[1024,1024]{1,0:T(8,128)(2,1)} %get-tuple-element.323.low_ref, ...), custom_call_target="tpu_custom_call" | custom-call | flops 7699999744 | bytes 1048576 | tf_op jit(solution)/shard_map/project/pallas_call | solution.py:579
  283.2 13.4 %attend_back.7.back_ref = bf16[1024,512]{1,0:T(8,128)(2,1)} custom-call(s32[1]{0:T(128)} %bitcast.10.sel_ref, bf16[1024,512]{1,0:T(8,128)(2,1)} %get-tuple-element.294.q_ref, bf16[1024,256]{1,0:T(8,128)(2,1)} %get-tuple-element.295.k_ref, bf16[1024,256]{1,0:T(8,128)(2,1)} %get-tuple-element.296.v_ref, f32[2,8,1024]{2,1,0:T(8,128)} %get-tuple-element.297.lse_ref, ...), custom_call_target="tpu_custom_call" | custom-call | flops 15399999488 | bytes 1048576 | tf_op jit(solution)/shard_map/attend_back/pallas_call | solution.py:495
  296.6 6.3 %collective-permute-done.28.refs_1_.refs_3_ = bf16[2,192,1024]{2,1,0:T(8,128)(2,1)S(1)} collective-permute-done((bf16[2,192,1024]{2,1,0:T(8,128)(2,1)}, bf16[2,192,1024]{2,1,0:T(8,128)(2,1)S(1)}, u32[]{:S(2)}, u32[]{:S(2)}) %collective-permute-start.28) | collective-permute-done | bytes 786464 | tf_op jit(solution)/shard_map/ppermute | solution.py:775
  303.8 2.9 add_split.8
  306.8 12.5 %project_final.1 = (bf16[1024,768]{1,0:T(8,128)(2,1)}, bf16[1024,1024]{1,0:T(8,128)(2,1)}, f32[8,1024]{1,0:T(8,128)}) custom-call(s32[1]{0:T(128)} %bitcast.10.sel_ref, bf16[1024,512]{1,0:T(8,128)(2,1)} %attend_back.7.back_ref, bf16[1024,512]{1,0:T(8,128)(2,1)} %get-tuple-element.247.att_a_ref.att_ref, bf16[1024,1024]{1,0:T(8,128)(2,1)} %get-tuple-element.323.low_ref, ...), custom_call_target="tpu_custom_call" | custom-call | flops 7699999744 | bytes 1048576 | tf_op jit(solution)/shard_map/project_final/pallas_call | solution.py:579
  319.3 2.5 fusion.5
  321.8 5.2 add_split.9
  328.8 2.6 collective-permute-start.31
  331.4 1.6 collective-permute-start.32
  333.0 8.3 %collective-permute-done.32 = f32[8,1024]{1,0:T(8,128)S(1)} collective-permute-done((f32[8,1024]{1,0:T(8,128)S(1)}, f32[8,1024]{1,0:T(8,128)S(1)}, u32[]{:S(2)}, u32[]{:S(2)}) %collective-permute-start.32) | collective-permute-done | bytes 32800 | tf_op jit(solution)/shard_map/ppermute | solution.py:775
  341.3 5.8 collective-permute-done.34.refs_5_.refs_7_
  347.8 4.0 add_split.10
  351.8 1.7 collective-permute-start.40
  354.5 3.5 collective-permute-start.38
  360.4 5.0 collective-permute-done.38.refs_1_.refs_3_
  365.4 7.2 %collective-permute-done.36 = bf16[2,96,1024]{2,1,0:T(8,128)(2,1)S(1)} collective-permute-done((bf16[2,96,1024]{2,1,0:T(8,128)(2,1)S(1)}, bf16[2,96,1024]{2,1,0:T(8,128)(2,1)S(1)}, u32[]{:S(2)}, u32[]{:S(2)}) %collective-permute-start.36) | collective-permute-done | bytes 393248 | tf_op jit(solution)/shard_map/ppermute | solution.py:780
  372.6 3.7 add_split.11
  380.5 7.1 %collective-permute-done.43 = f32[8,1024]{1,0:T(8,128)S(1)} collective-permute-done((f32[8,1024]{1,0:T(8,128)S(1)}, f32[8,1024]{1,0:T(8,128)S(1)}, u32[]{:S(2)}, u32[]{:S(2)}) %collective-permute-start.43) | collective-permute-done | bytes 32800 | tf_op jit(solution)/shard_map/ppermute | solution.py:780
  387.6 1.9 collective-permute-start.45
  389.4 3.9 collective-permute-done.45
  396.6 1.7 collective-permute-start.48
  398.3 1.6 collective-permute-start.52
  401.0 1.9 collective-permute-start.50
  402.8 14.6 %collective-permute-done.49 = f32[8,1024]{1,0:T(8,128)S(1)} collective-permute-done((f32[8,1024]{1,0:T(8,128)S(1)}, f32[8,1024]{1,0:T(8,128)S(1)}, u32[]{:S(2)}, u32[]{:S(2)}) %collective-permute-start.49) | collective-permute-done | bytes 32800 | tf_op jit(solution)/shard_map/ppermute | solution.py:780
  417.7 103.2 %all-reduce.2.cloned.1.call-done = f32[40,1024]{1,0:T(8,128)} async-done(((f32[40,1024]{1,0:T(8,128)}), f32[40,1024]{1,0:T(8,128)}) %all-reduce.2.cloned.1.call-update) | async-done | bytes 163856 | tf_op jit(solution)/shard_map/psum | solution.py:961
  527.1 1.9 pad_maximum_fusion.3.refs_0_
  529.8 3.7 maximum_select_fusion
  533.6 4.5 collective-permute-start.56
  541.8 2.9 collective-permute-done.55
  548.8 3.9 select_convert_fusion
  553.3 2.9 collective-permute-done.58
  560.1 8.9 %unpack_experts.1 = (f32[4,1024,256]{2,1,0:T(8,128)}, f32[4,1024,256]{2,1,0:T(8,128)}, f32[4,256,1024]{2,1,0:T(8,128)}) custom-call(s32[3]{0:T(128)} %pad_add_fusion.3.place_ref, bf16[768,1024]{1,0:T(8,128)(2,1)} %copy-done.5, bf16[768,1024]{1,0:T(8,128)(2,1)} %copy-done.4, bf16[768,1024]{1,0:T(8,128)(2,1)} %copy-done.27, ...), custom_call_target="tpu_custom_call" | custom-call | flops 11000000512 | bytes 1048576 | tf_op jit(solution)/shard_map/unpack_experts/pallas_call | solution.py:709
  570.7 5.9 %unpack.1 = (f32[1024,512]{1,0:T(8,128)}, f32[1024,256]{1,0:T(8,128)}, f32[1024,256]{1,0:T(8,128)}, f32[512,1024]{1,0:T(8,128)}) custom-call(s32[3]{0:T(128)} %pad_add_fusion.3.place_ref, bf16[512,768]{1,0:T(8,128)(2,1)} %copy-done.13, bf16[512,768]{1,0:T(8,128)(2,1)} %copy-done.12, bf16[512,768]{1,0:T(8,128)(2,1)} %copy-done.29, bf16[512,768]{1,0:T(8,128)(2,1)} %copy-done.31), custom_call_target="tpu_custom_call" | custom-call | flops 6600000000 | bytes 1048576 | tf_op jit(solution)/shard_map/unpack/pallas_call | solution.py:758
  (233 shorter events, 66.6 us)
Async XLA Ops:
  7.2 513.7 %all-reduce.2.cloned.1.call-start = ((), (), s32[]{:S(2)}) async-start(), calls=%async_computation | async-start | bytes 327680 | tf_op jit(solution)/shard_map/psum | solution.py:961
  8.4 17.8 %collective-permute-start = (bf16[1024,256]{1,0:T(8,128)(2,1)S(1)}, bf16[1024,256]{1,0:T(8,128)(2,1)}, u32[]{:S(2)}, u32[]{:S(2)}) collective-permute-start(bf16[1024,256]{1,0:T(8,128)(2,1)S(1)} %constant_dynamic-slice_fusion.7), channel_id=1, source_target_pairs={{0,1},{1,0},{2,3},{3,2},{4,5},{5,4},{6,7},{7,6},{8,9},{9,8},{10,11... | collective-permute-start | bytes 1572872 | tf_op jit(solution)/shard_map/ppermute | solution.py:775
  12.4 38.6 %collective-permute-start.3 = (bf16[1024,128]{1,0:T(8,128)(2,1)S(1)}, bf16[1024,128]{1,0:T(8,128)(2,1)S(1)}, u32[]{:S(2)}, u32[]{:S(2)}) collective-permute-start(bf16[1024,128]{1,0:T(8,128)(2,1)S(1)} %constant_dynamic-slice_fusion.5), channel_id=1, source_target_pairs={{0,1},{1,0},{2,3},{3,2},{4,5},{5,4},{6,7},{7,6},{8,9},{9,8},{10,11... | collective-permute-start | bytes 786440 | tf_op jit(solution)/shard_map/ppermute | solution.py:775
  13.5 37.5 %collective-permute-start.4 = (bf16[1024,128]{1,0:T(8,128)(2,1)S(1)}, bf16[1024,128]{1,0:T(8,128)(2,1)S(1)}, u32[]{:S(2)}, u32[]{:S(2)}) collective-permute-start(bf16[1024,128]{1,0:T(8,128)(2,1)S(1)} %constant_dynamic-slice_fusion.4), channel_id=1, source_target_pairs={{0,1},{1,0},{2,3},{3,2},{4,5},{5,4},{6,7},{7,6},{8,9},{9,8},{10,11... | collective-permute-start | bytes 786440 | tf_op jit(solution)/shard_map/ppermute | solution.py:775
  26.2 25.4 %collective-permute-start.1 = (bf16[256,1024]{1,0:T(8,128)(2,1)S(1)}, bf16[256,1024]{1,0:T(8,128)(2,1)S(1)}, u32[]{:S(2)}, u32[]{:S(2)}) collective-permute-start(bf16[256,1024]{1,0:T(8,128)(2,1)S(1)} %constant_dynamic-slice_fusion.8), channel_id=1, source_target_pairs={{0,1},{1,0},{2,3},{3,2},{4,5},{5,4},{6,7},{7,6},{8,9},{9,8},{10,11... | collective-permute-start | bytes 1572872 | tf_op jit(solution)/shard_map/ppermute | solution.py:775
  51.0 18.8 %collective-permute-start.7 = (bf16[1024,256]{1,0:T(8,128)(2,1)}, bf16[1024,256]{1,0:T(8,128)(2,1)S(1)}, u32[]{:S(2)}, u32[]{:S(2)}) collective-permute-start(bf16[1024,256]{1,0:T(8,128)(2,1)} %collective-permute-done.wq_ref), channel_id=1, source_target_pairs={{0,2},{2,0},{4,6},{6,4},{8,10},{10,8},{12,14},{14,12},{16,18},{18,... | collective-permute-start | bytes 1572872 | tf_op jit(solution)/shard_map/ppermute | solution.py:780
  51.1 16.9 %collective-permute-start.8 = (bf16[1024,128]{1,0:T(8,128)(2,1)S(1)}, bf16[1024,128]{1,0:T(8,128)(2,1)S(1)}, u32[]{:S(2)}, u32[]{:S(2)}) collective-permute-start(bf16[1024,128]{1,0:T(8,128)(2,1)S(1)} %collective-permute-done.3.wk_ref), channel_id=1, source_target_pairs={{0,2},{2,0},{4,6},{6,4},{8,10},{10,8},{12,14},{14,12},{16,18},{18,... | collective-permute-start | bytes 786440 | tf_op jit(solution)/shard_map/ppermute | solution.py:780
  51.6 18.0 %collective-permute-start.9 = (bf16[1024,128]{1,0:T(8,128)(2,1)S(1)}, bf16[1024,128]{1,0:T(8,128)(2,1)S(1)}, u32[]{:S(2)}, u32[]{:S(2)}) collective-permute-start(bf16[1024,128]{1,0:T(8,128)(2,1)S(1)} %collective-permute-done.4.wv_ref), channel_id=1, source_target_pairs={{0,2},{2,0},{4,6},{6,4},{8,10},{10,8},{12,14},{14,12},{16,18},{18,... | collective-permute-start | bytes 786440 | tf_op jit(solution)/shard_map/ppermute | solution.py:780
  51.7 14.6 %collective-permute-start.2 = (bf16[1,1024,256]{2,1,0:T(8,128)(2,1)S(1)}, bf16[1,1024,256]{2,1,0:T(8,128)(2,1)}, u32[]{:S(2)}, u32[]{:S(2)}) collective-permute-start(bf16[1,1024,256]{2,1,0:T(8,128)(2,1)S(1)} %constant_dynamic-slice_fusion.6), channel_id=1, source_target_pairs={{0,1},{1,0},{2,3},{3,2},{4,5},{5,4},{6,7},{7,6},{8,9},{9,8},{10,11... | collective-permute-start | bytes 1572872 | tf_op jit(solution)/shard_map/ppermute | solution.py:775
  66.2 16.4 %collective-permute-start.5 = (bf16[1,1024,256]{2,1,0:T(8,128)(2,1)}, bf16[1,1024,256]{2,1,0:T(8,128)(2,1)S(1)}, u32[]{:S(2)}, u32[]{:S(2)}) collective-permute-start(bf16[1,1024,256]{2,1,0:T(8,128)(2,1)} %collective-permute-done.2), channel_id=1, source_target_pairs={{0,4},{2,6},{4,0},{6,2},{8,12},{10,14},{12,8},{14,10},{16,20},{18,... | collective-permute-start | bytes 1572872 | tf_op jit(solution)/shard_map/ppermute | solution.py:780
  68.0 31.1 %collective-permute-start.13 = (bf16[1,1024,256]{2,1,0:T(8,128)(2,1)}, bf16[1,1024,256]{2,1,0:T(8,128)(2,1)}, u32[]{:S(2)}, u32[]{:S(2)}) collective-permute-start(bf16[1,1024,256]{2,1,0:T(8,128)(2,1)} %collective-permute-done.2), channel_id=1, source_target_pairs={{0,2},{2,0},{4,6},{6,4},{8,10},{10,8},{12,14},{14,12},{16,18},{18,... | collective-permute-start | bytes 1572872 | tf_op jit(solution)/shard_map/ppermute | solution.py:780
  68.0 14.6 %collective-permute-start.6 = (bf16[1,1024,256]{2,1,0:T(8,128)(2,1)S(1)}, bf16[1,1024,256]{2,1,0:T(8,128)(2,1)}, u32[]{:S(2)}, u32[]{:S(2)}) collective-permute-start(bf16[1,1024,256]{2,1,0:T(8,128)(2,1)S(1)} %constant_dynamic-slice_fusion.2), channel_id=1, source_target_pairs={{0,1},{1,0},{2,3},{3,2},{4,5},{5,4},{6,7},{7,6},{8,9},{9,8},{10,11... | collective-permute-start | bytes 1572872 | tf_op jit(solution)/shard_map/ppermute | solution.py:775
  69.6 14.9 %collective-permute-start.12 = (bf16[256,1024]{1,0:T(8,128)(2,1)S(1)}, bf16[256,1024]{1,0:T(8,128)(2,1)S(1)}, u32[]{:S(2)}, u32[]{:S(2)}) collective-permute-start(bf16[256,1024]{1,0:T(8,128)(2,1)S(1)} %collective-permute-done.1.wo_b_ref.wo_ref), channel_id=1, source_target_pairs={{0,2},{2,0},{4,6},{6,4},{8,10},{10,8},{12,14},{14,12},{16,18},{18,... | collective-permute-start | bytes 1572872 | tf_op jit(solution)/shard_map/ppermute | solution.py:780
  82.6 14.4 %collective-permute-start.10 = (bf16[1,1024,256]{2,1,0:T(8,128)(2,1)}, bf16[1,1024,256]{2,1,0:T(8,128)(2,1)}, u32[]{:S(2)}, u32[]{:S(2)}) collective-permute-start(bf16[1,1024,256]{2,1,0:T(8,128)(2,1)} %collective-permute-done.6), channel_id=1, source_target_pairs={{0,4},{2,6},{4,0},{6,2},{8,12},{10,14},{12,8},{14,10},{16,20},{18,... | collective-permute-start | bytes 1572872 | tf_op jit(solution)/shard_map/ppermute | solution.py:780
  83.2 13.8 %collective-permute-start.11 = (bf16[1,256,1024]{2,1,0:T(8,128)(2,1)S(1)}, bf16[1,256,1024]{2,1,0:T(8,128)(2,1)}, u32[]{:S(2)}, u32[]{:S(2)}) collective-permute-start(bf16[1,256,1024]{2,1,0:T(8,128)(2,1)S(1)} %constant_dynamic-slice_fusion.1), channel_id=1, source_target_pairs={{0,1},{1,0},{2,3},{3,2},{4,5},{5,4},{6,7},{7,6},{8,9},{9,8},{10,11... | collective-permute-start | bytes 1572872 | tf_op jit(solution)/shard_map/ppermute | solution.py:775
  97.0 13.4 %collective-permute-start.18 = (bf16[1,256,1024]{2,1,0:T(8,128)(2,1)}, bf16[1,256,1024]{2,1,0:T(8,128)(2,1)S(1)}, u32[]{:S(2)}, u32[]{:S(2)}) collective-permute-start(bf16[1,256,1024]{2,1,0:T(8,128)(2,1)} %collective-permute-done.11), channel_id=1, source_target_pairs={{0,4},{2,6},{4,0},{6,2},{8,12},{10,14},{12,8},{14,10},{16,20},{18,... | collective-permute-start | bytes 1572872 | tf_op jit(solution)/shard_map/ppermute | solution.py:780
  98.5 13.3 %collective-permute-start.14 = (bf16[1,1024,256]{2,1,0:T(8,128)(2,1)}, bf16[1,1024,256]{2,1,0:T(8,128)(2,1)S(1)}, u32[]{:S(2)}, u32[]{:S(2)}) collective-permute-start(bf16[1,1024,256]{2,1,0:T(8,128)(2,1)} %copy-done.14), channel_id=1, source_target_pairs={{0,2},{2,0},{4,6},{6,4},{8,10},{10,8},{12,14},{14,12},{16,18},{18,... | collective-permute-start | bytes 1572872 | tf_op jit(solution)/shard_map/ppermute | solution.py:780
  98.6 16.2 %collective-permute-start.15 = (bf16[1,1024,256]{2,1,0:T(8,128)(2,1)}, bf16[1,1024,256]{2,1,0:T(8,128)(2,1)S(1)}, u32[]{:S(2)}, u32[]{:S(2)}) collective-permute-start(bf16[1,1024,256]{2,1,0:T(8,128)(2,1)} %collective-permute-done.6), channel_id=1, source_target_pairs={{0,2},{2,0},{4,6},{6,4},{8,10},{10,8},{12,14},{14,12},{16,18},{18,... | collective-permute-start | bytes 1572872 | tf_op jit(solution)/shard_map/ppermute | solution.py:780
  99.1 15.7 %collective-permute-start.16 = (bf16[1,1024,256]{2,1,0:T(8,128)(2,1)}, bf16[1,1024,256]{2,1,0:T(8,128)(2,1)S(1)}, u32[]{:S(2)}, u32[]{:S(2)}) collective-permute-start(bf16[1,1024,256]{2,1,0:T(8,128)(2,1)} %collective-permute-done.10), channel_id=1, source_target_pairs={{0,2},{2,0},{4,6},{6,4},{8,10},{10,8},{12,14},{14,12},{16,18},{18,... | collective-permute-start | bytes 1572872 | tf_op jit(solution)/shard_map/ppermute | solution.py:780
  99.1 18.4 %collective-permute-start.17 = (bf16[1,256,1024]{2,1,0:T(8,128)(2,1)}, bf16[1,256,1024]{2,1,0:T(8,128)(2,1)S(1)}, u32[]{:S(2)}, u32[]{:S(2)}) collective-permute-start(bf16[1,256,1024]{2,1,0:T(8,128)(2,1)} %collective-permute-done.11), channel_id=1, source_target_pairs={{0,2},{2,0},{4,6},{6,4},{8,10},{10,8},{12,14},{14,12},{16,18},{18,... | collective-permute-start | bytes 1572872 | tf_op jit(solution)/shard_map/ppermute | solution.py:780
  110.4 7.1 %collective-permute-start.19 = (bf16[1,256,1024]{2,1,0:T(8,128)(2,1)S(1)}, bf16[1,256,1024]{2,1,0:T(8,128)(2,1)S(1)}, u32[]{:S(2)}, u32[]{:S(2)}) collective-permute-start(bf16[1,256,1024]{2,1,0:T(8,128)(2,1)S(1)} %collective-permute-done.18), channel_id=1, source_target_pairs={{0,2},{2,0},{4,6},{6,4},{8,10},{10,8},{12,14},{14,12},{16,18},{18,... | collective-permute-start | bytes 1572872 | tf_op jit(solution)/shard_map/ppermute | solution.py:780
  165.9 14.7 %collective-permute-start.20 = (bf16[4,768,1024]{2,1,0:T(8,128)(2,1)}, bf16[4,768,1024]{2,1,0:T(8,128)(2,1)}, u32[]{:S(2)}, u32[]{:S(2)}) collective-permute-start(bf16[4,768,1024]{2,1,0:T(8,128)(2,1)} %bitcast.58), channel_id=1, source_target_pairs={{0,2},{2,0},{4,6},{6,4},{8,10},{10,8},{12,14},{14,12},{16,18},{18,... | collective-permute-start | bytes 18874376 | tf_op jit(solution)/shard_map/ppermute | solution.py:780
  167.1 31.3 %collective-permute-start.21 = (bf16[512,1024]{1,0:T(8,128)(2,1)S(1)}, bf16[512,1024]{1,0:T(8,128)(2,1)S(1)}, u32[]{:S(2)}, u32[]{:S(2)}) collective-permute-start(bf16[512,1024]{1,0:T(8,128)(2,1)S(1)} %get-tuple-element.276), channel_id=1, source_target_pairs={{0,1},{1,0},{2,3},{3,2},{4,5},{5,4},{6,7},{7,6},{8,9},{9,8},{10,11... | collective-permute-start | bytes 3145736 | tf_op jit(solution)/shard_map/ppermute | solution.py:775
  199.4 18.3 %collective-permute-start.22 = (bf16[1024,768]{1,0:T(8,128)(2,1)}, bf16[1024,768]{1,0:T(8,128)(2,1)S(1)}, u32[]{:S(2)}, u32[]{:S(2)}) collective-permute-start(bf16[1024,768]{1,0:T(8,128)(2,1)} %get-tuple-element.286), channel_id=1, source_target_pairs={{0,2},{2,0},{4,6},{6,4},{8,10},{10,8},{12,14},{14,12},{16,18},{18,... | collective-permute-start | bytes 4718600 | tf_op jit(solution)/shard_map/ppermute | solution.py:780
  199.4 28.5 %collective-permute-start.25 = (bf16[512,1024]{1,0:T(8,128)(2,1)S(1)}, bf16[512,1024]{1,0:T(8,128)(2,1)S(1)}, u32[]{:S(2)}, u32[]{:S(2)}) collective-permute-start(bf16[512,1024]{1,0:T(8,128)(2,1)S(1)} %get-tuple-element.292), channel_id=1, source_target_pairs={{0,1},{1,0},{2,3},{3,2},{4,5},{5,4},{6,7},{7,6},{8,9},{9,8},{10,11... | collective-permute-start | bytes 3145736 | tf_op jit(solution)/shard_map/ppermute | solution.py:775
  201.3 36.8 %collective-permute-start.23 = (bf16[2,384,1024]{2,1,0:T(8,128)(2,1)}, bf16[2,384,1024]{2,1,0:T(8,128)(2,1)}, u32[]{:S(2)}, u32[]{:S(2)}) collective-permute-start(bf16[2,384,1024]{2,1,0:T(8,128)(2,1)} %get-tuple-element.290), channel_id=1, source_target_pairs={{0,4},{2,6},{4,0},{6,2},{8,12},{10,14},{12,8},{14,10},{16,20},{18,... | collective-permute-start | bytes 4718600 | tf_op jit(solution)/shard_map/ppermute | solution.py:780
  202.5 36.6 %collective-permute-start.24 = (bf16[2,384,1024]{2,1,0:T(8,128)(2,1)}, bf16[2,384,1024]{2,1,0:T(8,128)(2,1)}, u32[]{:S(2)}, u32[]{:S(2)}) collective-permute-start(bf16[2,384,1024]{2,1,0:T(8,128)(2,1)} %get-tuple-element.291), channel_id=1, source_target_pairs={{0,8},{2,10},{4,12},{6,14},{8,0},{10,2},{12,4},{14,6},{16,24},{18,... | collective-permute-start | bytes 4718600 | tf_op jit(solution)/shard_map/ppermute | solution.py:780
  247.9 18.8 %collective-permute-start.26 = (bf16[2,192,1024]{2,1,0:T(8,128)(2,1)}, bf16[2,192,1024]{2,1,0:T(8,128)(2,1)S(1)}, u32[]{:S(2)}, u32[]{:S(2)}) collective-permute-start(bf16[2,192,1024]{2,1,0:T(8,128)(2,1)} %get-tuple-element.309), channel_id=1, source_target_pairs={{0,8},{2,10},{4,12},{6,14},{8,0},{10,2},{12,4},{14,6},{16,24},{18,... | collective-permute-start | bytes 2359304 | tf_op jit(solution)/shard_map/ppermute | solution.py:780
  249.6 18.5 %collective-permute-start.27 = (bf16[2,192,1024]{2,1,0:T(8,128)(2,1)}, bf16[2,192,1024]{2,1,0:T(8,128)(2,1)S(1)}, u32[]{:S(2)}, u32[]{:S(2)}) collective-permute-start(bf16[2,192,1024]{2,1,0:T(8,128)(2,1)} %get-tuple-element.310), channel_id=1, source_target_pairs={{0,4},{2,6},{4,0},{6,2},{8,12},{10,14},{12,8},{14,10},{16,20},{18,... | collective-permute-start | bytes 2359304 | tf_op jit(solution)/shard_map/ppermute | solution.py:780
  250.4 52.6 %collective-permute-start.30 = (bf16[1024,768]{1,0:T(8,128)(2,1)}, bf16[1024,768]{1,0:T(8,128)(2,1)S(1)}, u32[]{:S(2)}, u32[]{:S(2)}) collective-permute-start(bf16[1024,768]{1,0:T(8,128)(2,1)} %add_convert_fusion), channel_id=1, source_target_pairs={{0,1},{1,0},{2,3},{3,2},{4,5},{5,4},{6,7},{7,6},{8,9},{9,8},{10,11... | collective-permute-start | bytes 4718600 | tf_op jit(solution)/shard_map/ppermute | solution.py:775
  282.8 20.2 %collective-permute-start.29 = (bf16[1024,768]{1,0:T(8,128)(2,1)}, bf16[1024,768]{1,0:T(8,128)(2,1)S(1)}, u32[]{:S(2)}, u32[]{:S(2)}) collective-permute-start(bf16[1024,768]{1,0:T(8,128)(2,1)} %get-tuple-element.325), channel_id=1, source_target_pairs={{0,2},{2,0},{4,6},{6,4},{8,10},{10,8},{12,14},{14,12},{16,18},{18,... | collective-permute-start | bytes 4718600 | tf_op jit(solution)/shard_map/ppermute | solution.py:780
  282.8 20.2 %collective-permute-start.28 = (bf16[2,192,1024]{2,1,0:T(8,128)(2,1)}, bf16[2,192,1024]{2,1,0:T(8,128)(2,1)S(1)}, u32[]{:S(2)}, u32[]{:S(2)}) collective-permute-start(bf16[2,192,1024]{2,1,0:T(8,128)(2,1)} %get-tuple-element.324), channel_id=1, source_target_pairs={{0,1},{1,0},{2,3},{3,2},{4,5},{5,4},{6,7},{7,6},{8,9},{9,8},{10,11... | collective-permute-start | bytes 2359304 | tf_op jit(solution)/shard_map/ppermute | solution.py:775
  321.8 25.3 %copy-start.16 = (bf16[2,96,1024]{2,1,0:T(8,128)(2,1)S(1)}, bf16[2,96,1024]{2,1,0:T(8,128)(2,1)}, u32[]{:S(2)}) copy-start(bf16[2,96,1024]{2,1,0:T(8,128)(2,1)} %get-tuple-element.347) | copy-start | bytes 1179652
  326.9 20.1 %collective-permute-start.35 = (bf16[256,1024]{1,0:T(8,128)(2,1)S(1)}, bf16[256,1024]{1,0:T(8,128)(2,1)S(1)}, u32[]{:S(2)}, u32[]{:S(2)}) collective-permute-start(bf16[256,1024]{1,0:T(8,128)(2,1)S(1)} %get-tuple-element.345), channel_id=1, source_target_pairs={{0,1},{1,0},{2,3},{3,2},{4,5},{5,4},{6,7},{7,6},{8,9},{9,8},{10,11... | collective-permute-start | bytes 1572872 | tf_op jit(solution)/shard_map/ppermute | solution.py:775
  327.4 13.8 %collective-permute-start.33 = (bf16[1,256,768]{2,1,0:T(8,128)(2,1)}, bf16[1,256,768]{2,1,0:T(8,128)(2,1)S(1)}, u32[]{:S(2)}, u32[]{:S(2)}) collective-permute-start(bf16[1,256,768]{2,1,0:T(8,128)(2,1)} %get-tuple-element.343), channel_id=1, source_target_pairs={{0,4},{2,6},{4,0},{6,2},{8,12},{10,14},{12,8},{14,10},{16,20},{18,... | collective-permute-start | bytes 1179656 | tf_op jit(solution)/shard_map/ppermute | solution.py:780
  328.2 18.8 %collective-permute-start.34 = (bf16[1,256,768]{2,1,0:T(8,128)(2,1)}, bf16[1,256,768]{2,1,0:T(8,128)(2,1)S(1)}, u32[]{:S(2)}, u32[]{:S(2)}) collective-permute-start(bf16[1,256,768]{2,1,0:T(8,128)(2,1)} %get-tuple-element.344), channel_id=1, source_target_pairs={{0,8},{2,10},{4,12},{6,14},{8,0},{10,2},{12,4},{14,6},{16,24},{18,... | collective-permute-start | bytes 1179656 | tf_op jit(solution)/shard_map/ppermute | solution.py:780
  328.8 18.3 %collective-permute-start.31 = (bf16[2,96,1024]{2,1,0:T(8,128)(2,1)S(1)}, bf16[2,96,1024]{2,1,0:T(8,128)(2,1)S(1)}, u32[]{:S(2)}, u32[]{:S(2)}) collective-permute-start(bf16[2,96,1024]{2,1,0:T(8,128)(2,1)S(1)} %copy-done.36), channel_id=1, source_target_pairs={{0,16},{2,18},{4,20},{6,22},{8,24},{10,26},{12,28},{14,30},{16,0},... | collective-permute-start | bytes 1179656 | tf_op jit(solution)/shard_map/ppermute | solution.py:780
  331.4 9.9 %collective-permute-start.32 = (f32[8,1024]{1,0:T(8,128)S(1)}, f32[8,1024]{1,0:T(8,128)S(1)}, u32[]{:S(2)}, u32[]{:S(2)}) collective-permute-start(f32[8,1024]{1,0:T(8,128)S(1)} %copy-done.20), channel_id=1, source_target_pairs={{0,1},{1,0},{2,3},{3,2},{4,5},{5,4},{6,7},{7,6},{8,9},{9,8},{10,11... | collective-permute-start | bytes 98312 | tf_op jit(solution)/shard_map/ppermute | solution.py:775
  351.8 20.7 %collective-permute-start.40 = (bf16[256,1024]{1,0:T(8,128)(2,1)S(1)}, bf16[256,1024]{1,0:T(8,128)(2,1)S(1)}, u32[]{:S(2)}, u32[]{:S(2)}) collective-permute-start(bf16[256,1024]{1,0:T(8,128)(2,1)S(1)} %get-tuple-element.360), channel_id=1, source_target_pairs={{0,1},{1,0},{2,3},{3,2},{4,5},{5,4},{6,7},{7,6},{8,9},{9,8},{10,11... | collective-permute-start | bytes 1572872 | tf_op jit(solution)/shard_map/ppermute | solution.py:775
  353.5 19.1 %collective-permute-start.36 = (bf16[2,96,1024]{2,1,0:T(8,128)(2,1)S(1)}, bf16[2,96,1024]{2,1,0:T(8,128)(2,1)S(1)}, u32[]{:S(2)}, u32[]{:S(2)}) collective-permute-start(bf16[2,96,1024]{2,1,0:T(8,128)(2,1)S(1)} %add_convert_fusion.1), channel_id=1, source_target_pairs={{0,16},{2,18},{4,20},{6,22},{8,24},{10,26},{12,28},{14,30},{16,0},... | collective-permute-start | bytes 1179656 | tf_op jit(solution)/shard_map/ppermute | solution.py:780
  354.5 10.9 %collective-permute-start.38 = (bf16[1,128,768]{2,1,0:T(8,128)(2,1)}, bf16[1,128,768]{2,1,0:T(8,128)(2,1)S(1)}, u32[]{:S(2)}, u32[]{:S(2)}) collective-permute-start(bf16[1,128,768]{2,1,0:T(8,128)(2,1)} %get-tuple-element.358), channel_id=1, source_target_pairs={{0,8},{2,10},{4,12},{6,14},{8,0},{10,2},{12,4},{14,6},{16,24},{18,... | collective-permute-start | bytes 589832 | tf_op jit(solution)/shard_map/ppermute | solution.py:780
  358.0 7.4 %collective-permute-start.39 = (bf16[1,128,768]{2,1,0:T(8,128)(2,1)}, bf16[1,128,768]{2,1,0:T(8,128)(2,1)S(1)}, u32[]{:S(2)}, u32[]{:S(2)}) collective-permute-start(bf16[1,128,768]{2,1,0:T(8,128)(2,1)} %get-tuple-element.359), channel_id=1, source_target_pairs={{0,4},{2,6},{4,0},{6,2},{8,12},{10,14},{12,8},{14,10},{16,20},{18,... | collective-permute-start | bytes 589832 | tf_op jit(solution)/shard_map/ppermute | solution.py:780
  359.2 1.2 collective-permute-start.37
  376.4 16.9 %collective-permute-start.46 = (bf16[256,1024]{1,0:T(8,128)(2,1)S(1)}, bf16[256,1024]{1,0:T(8,128)(2,1)S(1)}, u32[]{:S(2)}, u32[]{:S(2)}) collective-permute-start(bf16[256,1024]{1,0:T(8,128)(2,1)S(1)} %get-tuple-element.375), channel_id=1, source_target_pairs={{0,1},{1,0},{2,3},{3,2},{4,5},{5,4},{6,7},{7,6},{8,9},{9,8},{10,11... | collective-permute-start | bytes 1572872 | tf_op jit(solution)/shard_map/ppermute | solution.py:775
  376.9 16.4 %collective-permute-start.41 = (bf16[192,1024]{1,0:T(8,128)(2,1)S(1)}, bf16[192,1024]{1,0:T(8,128)(2,1)S(1)}, u32[]{:S(2)}, u32[]{:S(2)}) collective-permute-start(bf16[192,1024]{1,0:T(8,128)(2,1)S(1)} %get-tuple-element.370), channel_id=1, source_target_pairs={{0,8},{2,10},{4,12},{6,14},{8,0},{10,2},{12,4},{14,6},{16,24},{18,... | collective-permute-start | bytes 1179656 | tf_op jit(solution)/shard_map/ppermute | solution.py:780
  376.9 16.4 %collective-permute-start.42 = (bf16[192,1024]{1,0:T(8,128)(2,1)S(1)}, bf16[192,1024]{1,0:T(8,128)(2,1)S(1)}, u32[]{:S(2)}, u32[]{:S(2)}) collective-permute-start(bf16[192,1024]{1,0:T(8,128)(2,1)S(1)} %get-tuple-element.371), channel_id=1, source_target_pairs={{0,4},{2,6},{4,0},{6,2},{8,12},{10,14},{12,8},{14,10},{16,20},{18,... | collective-permute-start | bytes 1179656 | tf_op jit(solution)/shard_map/ppermute | solution.py:780
  378.1 9.5 %collective-permute-start.43 = (f32[8,1024]{1,0:T(8,128)S(1)}, f32[8,1024]{1,0:T(8,128)S(1)}, u32[]{:S(2)}, u32[]{:S(2)}) collective-permute-start(f32[8,1024]{1,0:T(8,128)S(1)} %add.107), channel_id=1, source_target_pairs={{0,4},{2,6},{4,0},{6,2},{8,12},{10,14},{12,8},{14,10},{16,20},{18,... | collective-permute-start | bytes 98312 | tf_op jit(solution)/shard_map/ppermute | solution.py:780
  378.9 10.5 %collective-permute-start.44 = (bf16[1,64,768]{2,1,0:T(8,128)(2,1)}, bf16[1,64,768]{2,1,0:T(8,128)(2,1)S(1)}, u32[]{:S(2)}, u32[]{:S(2)}) collective-permute-start(bf16[1,64,768]{2,1,0:T(8,128)(2,1)} %get-tuple-element.373), channel_id=1, source_target_pairs={{0,16},{2,18},{4,20},{6,22},{8,24},{10,26},{12,28},{14,30},{16,0},... | collective-permute-start | bytes 294920 | tf_op jit(solution)/shard_map/ppermute | solution.py:780
  387.6 5.7 collective-permute-start.45
  395.3 128.5 %collective-permute-start.47 = (bf16[384,1024]{1,0:T(8,128)(2,1)}, bf16[384,1024]{1,0:T(8,128)(2,1)}, u32[]{:S(2)}, u32[]{:S(2)}) collective-permute-start(bf16[384,1024]{1,0:T(8,128)(2,1)} %pad_maximum_fusion.5), channel_id=1, source_target_pairs={{0,4},{2,6},{4,0},{6,2},{8,12},{10,14},{12,8},{14,10},{16,20},{18,... | collective-permute-start | bytes 2359304 | tf_op jit(solution)/shard_map/ppermute | solution.py:780
  396.6 127.2 %collective-permute-start.48 = (bf16[384,1024]{1,0:T(8,128)(2,1)}, bf16[384,1024]{1,0:T(8,128)(2,1)}, u32[]{:S(2)}, u32[]{:S(2)}) collective-permute-start(bf16[384,1024]{1,0:T(8,128)(2,1)} %pad_maximum_fusion.6), channel_id=1, source_target_pairs={{0,8},{2,10},{4,12},{6,14},{8,0},{10,2},{12,4},{14,6},{16,24},{18,... | collective-permute-start | bytes 2359304 | tf_op jit(solution)/shard_map/ppermute | solution.py:780
  398.3 125.5 %collective-permute-start.52 = (bf16[256,1024]{1,0:T(8,128)(2,1)}, bf16[256,1024]{1,0:T(8,128)(2,1)S(1)}, u32[]{:S(2)}, u32[]{:S(2)}) collective-permute-start(bf16[256,1024]{1,0:T(8,128)(2,1)} %get-tuple-element.389), channel_id=1, source_target_pairs={{0,1},{1,0},{2,3},{3,2},{4,5},{5,4},{6,7},{7,6},{8,9},{9,8},{10,11... | collective-permute-start | bytes 1572872 | tf_op jit(solution)/shard_map/ppermute | solution.py:775
  400.0 17.5 %collective-permute-start.49 = (f32[8,1024]{1,0:T(8,128)S(1)}, f32[8,1024]{1,0:T(8,128)S(1)}, u32[]{:S(2)}, u32[]{:S(2)}) collective-permute-start(f32[8,1024]{1,0:T(8,128)S(1)} %add.108), channel_id=1, source_target_pairs={{0,8},{2,10},{4,12},{6,14},{8,0},{10,2},{12,4},{14,6},{16,24},{18,... | collective-permute-start | bytes 98312 | tf_op jit(solution)/shard_map/ppermute | solution.py:780
  401.0 122.8 %collective-permute-start.50 = (bf16[64,768]{1,0:T(8,128)(2,1)S(1)}, bf16[64,768]{1,0:T(8,128)(2,1)}, u32[]{:S(2)}, u32[]{:S(2)}) collective-permute-start(bf16[64,768]{1,0:T(8,128)(2,1)S(1)} %fusion.3), channel_id=1, source_target_pairs={{0,16},{2,18},{4,20},{6,22},{8,24},{10,26},{12,28},{14,30},{16,0},... | collective-permute-start | bytes 294920 | tf_op jit(solution)/shard_map/ppermute | solution.py:780
  417.4 106.4 %collective-permute-start.51 = (bf16[64,768]{1,0:T(8,128)(2,1)S(1)}, bf16[64,768]{1,0:T(8,128)(2,1)}, u32[]{:S(2)}, u32[]{:S(2)}) collective-permute-start(bf16[64,768]{1,0:T(8,128)(2,1)S(1)} %fusion.4), channel_id=1, source_target_pairs={{0,16},{2,18},{4,20},{6,22},{8,24},{10,26},{12,28},{14,30},{16,0},... | collective-permute-start | bytes 294920 | tf_op jit(solution)/shard_map/ppermute | solution.py:780
  529.0 15.8 %collective-permute-start.53 = (bf16[768,1024]{1,0:T(8,128)(2,1)S(1)}, bf16[768,1024]{1,0:T(8,128)(2,1)S(1)}, u32[]{:S(2)}, u32[]{:S(2)}) collective-permute-start(bf16[768,1024]{1,0:T(8,128)(2,1)S(1)} %pad_maximum_fusion.3.refs_0_), channel_id=1, source_target_pairs={{0,2},{2,0},{4,6},{6,4},{8,10},{10,8},{12,14},{14,12},{16,18},{18,... | collective-permute-start | bytes 4718600 | tf_op jit(solution)/shard_map/ppermute | solution.py:780
  529.5 15.3 %collective-permute-start.54 = (bf16[768,1024]{1,0:T(8,128)(2,1)S(1)}, bf16[768,1024]{1,0:T(8,128)(2,1)}, u32[]{:S(2)}, u32[]{:S(2)}) collective-permute-start(bf16[768,1024]{1,0:T(8,128)(2,1)S(1)} %pad_maximum_fusion.4.refs_1_), channel_id=1, source_target_pairs={{0,2},{2,0},{4,6},{6,4},{8,10},{10,8},{12,14},{14,12},{16,18},{18,... | collective-permute-start | bytes 4718600 | tf_op jit(solution)/shard_map/ppermute | solution.py:780
  533.6 11.1 %collective-permute-start.56 = (bf16[128,768]{1,0:T(8,128)(2,1)S(1)}, bf16[128,768]{1,0:T(8,128)(2,1)S(1)}, u32[]{:S(2)}, u32[]{:S(2)}) collective-permute-start(bf16[128,768]{1,0:T(8,128)(2,1)S(1)} %pad_maximum_fusion.12), channel_id=1, source_target_pairs={{0,8},{2,10},{4,12},{6,14},{8,0},{10,2},{12,4},{14,6},{16,24},{18,... | collective-permute-start | bytes 589832 | tf_op jit(solution)/shard_map/ppermute | solution.py:780
  538.1 6.7 %collective-permute-start.57 = (bf16[128,768]{1,0:T(8,128)(2,1)S(1)}, bf16[128,768]{1,0:T(8,128)(2,1)S(1)}, u32[]{:S(2)}, u32[]{:S(2)}) collective-permute-start(bf16[128,768]{1,0:T(8,128)(2,1)S(1)} %pad_maximum_fusion.13), channel_id=1, source_target_pairs={{0,4},{2,6},{4,0},{6,2},{8,12},{10,14},{12,8},{14,10},{16,20},{18,... | collective-permute-start | bytes 589832 | tf_op jit(solution)/shard_map/ppermute | solution.py:780
  539.6 5.2 collective-permute-start.55
  546.7 9.5 %collective-permute-start.58 = (bf16[256,768]{1,0:T(8,128)(2,1)S(1)}, bf16[256,768]{1,0:T(8,128)(2,1)S(1)}, u32[]{:S(2)}, u32[]{:S(2)}) collective-permute-start(bf16[256,768]{1,0:T(8,128)(2,1)S(1)} %pad_maximum_fusion.10), channel_id=1, source_target_pairs={{0,4},{2,6},{4,0},{6,2},{8,12},{10,14},{12,8},{14,10},{16,20},{18,... | collective-permute-start | bytes 1179656 | tf_op jit(solution)/shard_map/ppermute | solution.py:780
  548.0 9.4 %collective-permute-start.59 = (bf16[256,768]{1,0:T(8,128)(2,1)S(1)}, bf16[256,768]{1,0:T(8,128)(2,1)S(1)}, u32[]{:S(2)}, u32[]{:S(2)}) collective-permute-start(bf16[256,768]{1,0:T(8,128)(2,1)S(1)} %pad_maximum_fusion.11), channel_id=1, source_target_pairs={{0,8},{2,10},{4,12},{6,14},{8,0},{10,2},{12,4},{14,6},{16,24},{18,... | collective-permute-start | bytes 1179656 | tf_op jit(solution)/shard_map/ppermute | solution.py:780
  559.5 9.5 %collective-permute-start.60 = (bf16[512,768]{1,0:T(8,128)(2,1)S(1)}, bf16[512,768]{1,0:T(8,128)(2,1)S(1)}, u32[]{:S(2)}, u32[]{:S(2)}) collective-permute-start(bf16[512,768]{1,0:T(8,128)(2,1)S(1)} %pad_maximum_fusion.7.refs_0_), channel_id=1, source_target_pairs={{0,2},{2,0},{4,6},{6,4},{8,10},{10,8},{12,14},{14,12},{16,18},{18,... | collective-permute-start | bytes 2359304 | tf_op jit(solution)/shard_map/ppermute | solution.py:780
  559.6 9.4 %collective-permute-start.61 = (bf16[512,768]{1,0:T(8,128)(2,1)S(1)}, bf16[512,768]{1,0:T(8,128)(2,1)S(1)}, u32[]{:S(2)}, u32[]{:S(2)}) collective-permute-start(bf16[512,768]{1,0:T(8,128)(2,1)S(1)} %pad_maximum_fusion.8.refs_1_), channel_id=1, source_target_pairs={{0,2},{2,0},{4,6},{6,4},{8,10},{10,8},{12,14},{14,12},{16,18},{18,... | collective-permute-start | bytes 2359304 | tf_op jit(solution)/shard_map/ppermute | solution.py:780
  (44 other events, 308.3 us)
Sparse Core Ops, SparseCore 0:
  400.1 120.7 all-reduce.1

commit v4 on v3

--- a/solution.py
+++ b/solution.py
@@ -36,12 +36,12 @@
 def params(count=1):
     return pltpu.CompilerParams(
         dimension_semantics=("arbitrary",) * count if count else None,
-        vmem_limit_bytes=59 * 1024 * 1024,
+        vmem_limit_bytes=60 * 1024 * 1024,
     )
 
 
 def cost(micros):
-    return pl.CostEstimate(flops=int(micros * 1.1e9), bytes_accessed=1 << 20, transcendentals=0)
+    return pl.CostEstimate(flops=int(micros * 0.5e9), bytes_accessed=1 << 20, transcendentals=0)
 
 
 def whole(shape):
@@ -56,7 +56,7 @@
     return lax.broadcasted_iota(jnp.int32, (rows, lanes), 1)
 
 
-def prologue_kernel(x_ref, gain_ref, seg_ref, freq_ref, first_ref, first_t_ref, cos_ref, up_ref, down_ref):
+def prologue_kernel(side_ref, x_ref, gain_ref, seg_ref, freq_ref, first_ref, first_t_ref, cos_ref, up_ref, down_ref):
     rows = x_ref.shape[0]
     values = x_ref[...].astype(f32)
     scale = lax.rsqrt(jnp.mean(values * values, axis=-1, keepdims=True) + EPS)
@@ -79,22 +79,33 @@
     down_ref[...] = jnp.where(lower, 0.0, sine)
 
 
-def prologue(x, gain, seg_row, freq):
-    rows, width = x.shape
+def own_rows(shape):
+    return pl.BlockSpec(shape, lambda i, s: (s[0], 0), pipeline_mode=pl.Buffered(1))
+
+
+def prologue(side, tokens, gain, seg_row, freq):
+    rows, width = seg_row.shape[1], tokens.shape[1]
     table = jax.ShapeDtypeStruct((rows, LANES), f32)
+    shapes = (
+        jax.ShapeDtypeStruct((rows, width), bf16),
+        jax.ShapeDtypeStruct((width, rows), bf16),
+        table,
+        table,
+        table,
+    )
     return pl.pallas_call(
         prologue_kernel,
-        out_shape=(
-            jax.ShapeDtypeStruct((rows, width), bf16),
-            jax.ShapeDtypeStruct((width, rows), bf16),
-            table,
-            table,
-            table,
+        grid_spec=pltpu.PrefetchScalarGridSpec(
+            num_scalar_prefetch=1,
+            grid=(1,),
+            in_specs=[own_rows((rows, width)), once(gain.shape), once(seg_row.shape), once(freq.shape)],
+            out_specs=[whole(o.shape) for o in shapes],
         ),
-        compiler_params=params(0),
+        out_shape=shapes,
+        compiler_params=params(),
         cost_estimate=cost(5),
         name="prologue",
-    )(x, gain, seg_row, freq)
+    )(side, tokens, gain, seg_row, freq)
 
 
 def rotate(values, cosine, up, down):
@@ -217,7 +228,7 @@
 
 
 def router_kernel(
-    x_ref, att_a_ref, att_b_ref, att_c_ref, wo_a_ref, wo_b_ref, wo_c_ref, gain_ref, wr_ref, routes_ref, slots_ref,
+    side_ref, x_ref, att_a_ref, att_b_ref, att_c_ref, wo_a_ref, wo_b_ref, wo_c_ref, gain_ref, wr_ref, routes_ref, slots_ref,
     resid_ref, second_ref, gates_ref, places_ref,
 ):
     mixed = nn(att_a_ref[...], wo_a_ref[...])
@@ -247,20 +258,28 @@
     gates_ref[...] = weights / jnp.sum(weights, axis=0, keepdims=True)
 
 
-def router(x, attended, outputs, gain, wr_t, routes_t, slots_t):
-    rows, width = x.shape
+def router(side, tokens, attended, outputs, gain, wr_t, routes_t, slots_t):
+    rows, width = routes_t.shape[1], tokens.shape[1]
+    rest = (*attended, *outputs, gain, wr_t, routes_t, slots_t)
+    shapes = (
+        jax.ShapeDtypeStruct((rows, width), f32),
+        jax.ShapeDtypeStruct((rows, width), bf16),
+        jax.ShapeDtypeStruct((wr_t.shape[0], rows), f32),
+        jax.ShapeDtypeStruct((8, rows), jnp.int32),
+    )
     return pl.pallas_call(
         router_kernel,
-        out_shape=(
-            jax.ShapeDtypeStruct((rows, width), f32),
-            jax.ShapeDtypeStruct((rows, width), bf16),
-            jax.ShapeDtypeStruct((wr_t.shape[0], rows), f32),
-            jax.ShapeDtypeStruct((8, rows), jnp.int32),
+        grid_spec=pltpu.PrefetchScalarGridSpec(
+            num_scalar_prefetch=1,
+            grid=(1,),
+            in_specs=[own_rows((rows, width)), *[once(a.shape) for a in rest]],
+            out_specs=[whole(o.shape) for o in shapes],
         ),
-        compiler_params=params(0),
+        out_shape=shapes,
+        compiler_params=params(),
         cost_estimate=cost(8),
         name="router",
-    )(x, *attended, *outputs, gain, wr_t, routes_t, slots_t)
+    )(side, tokens, *rest)
 
 
 def split_three(values):
@@ -273,7 +292,7 @@
 def experts_kernel(
     order_ref, second_ref, cot_ref, resid_ref, gates_ref, places_ref, gain_ref, wr_ref,
     wg_a_ref, wg_b_ref, wu_a_ref, wu_b_ref, wd_a_ref, wd_b_ref,
-    out_ref, low_ref, grad_ref, small_ref, kept_ref, sent_ref,
+    out_ref, low_t_ref, low_ref, grad_ref, small_ref, kept_ref, sent_ref,
     moe_ref, slot_grads_ref,
 ):
     step = pl.program_id(0)
@@ -365,10 +384,12 @@
         grad = grad + cot_ref[...].astype(f32)
         grad_ref[...] = grad
         low_ref[...] = grad.astype(bf16)
+        low_t_ref[...] = grad.astype(bf16).T
 
 
 def experts_layer(order, second, cot, resid, gates, places, gain, wr_t, weights):
     rows, width = second.shape
+    own_cot = pl.BlockSpec((rows, width), lambda i, o: (o[1], 0), pipeline_mode=pl.Buffered(1))
     experts = gates.shape[0]
     window, _, hidden = weights[0].shape
     wide = pl.BlockSpec((1, width, hidden), lambda i, o: (i ^ o[0], 0, 0))
@@ -384,7 +405,7 @@
         grid=(window,),
         in_specs=[
             once((rows, width)),
-            once((rows, width)),
+            own_cot,
             once((rows, width)),
             whole((experts, rows)),
             whole((8, rows)),
@@ -399,6 +420,7 @@
         ],
         out_specs=[
             once((rows, width)),
+            once((width, rows)),
             once((rows, width)),
             once((rows, width)),
             whole((experts + 8, width)),
@@ -412,6 +434,7 @@
         ),
         out_shape=(
             jax.ShapeDtypeStruct((rows, width), bf16),
+            jax.ShapeDtypeStruct((width, rows), bf16),
             jax.ShapeDtypeStruct((rows, width), bf16),
             jax.ShapeDtypeStruct((rows, width), f32),
             jax.ShapeDtypeStruct((experts + 8, width), f32),
@@ -517,7 +540,7 @@
     )(sel, query, key, value, logs, *tables, seg_col, seg_row, low_grad, wo)
 
 
-def project_kernel(final, fresh, sel_ref, back_ref, att_ref, low_ref, first_t_ref, wq_ref, wk_ref, wv_ref, *rest):
+def project_kernel(final, fresh, sel_ref, back_ref, att_ref, low_t_ref, first_t_ref, wq_ref, wk_ref, wv_ref, *rest):
     if not fresh:
         before_ref, *rest = rest
     if final:
@@ -526,7 +549,7 @@
         group_ref, sum_ref = rest
     back = back_ref[...]
     group_ref[:, : 2 * GROUP] = nn(first_t_ref[...], back).astype(bf16)
-    group_ref[:, 2 * GROUP :] = tn(low_ref[...], att_ref[...]).astype(bf16)
+    group_ref[:, 2 * GROUP :] = nn(low_t_ref[...], att_ref[...]).astype(bf16)
     first_grad = nt(back[:, :GROUP], wq_ref[...])
     first_grad = first_grad + nt(back[:, GROUP : GROUP + LANES], wk_ref[...])
     first_grad = first_grad + nt(back[:, GROUP + LANES :], wv_ref[...])
@@ -546,8 +569,8 @@
         sum_ref[...] = first_grad
 
 
-def project(sel, back, att, low_grad, first_t, wq, wk, wv, before=None, final=None):
-    rows, width = low_grad.shape
+def project(sel, back, att, low_t, first_t, wq, wk, wv, before=None, final=None):
+    width, rows = low_t.shape
 
     def fixed(shape):
         return pl.BlockSpec(shape, lambda i, s: (0,) * len(shape))
@@ -557,7 +580,7 @@
     square = fixed((rows, width))
     in_specs = [
         fixed((rows, 2 * GROUP)), pl.BlockSpec((rows, GROUP), lambda i, s: (0, s[0])),
-        square, fixed((width, rows)), wide_w, thin_w, thin_w,
+        fixed((width, rows)), fixed((width, rows)), wide_w, thin_w, thin_w,
     ]
     out_specs = [fixed((width, 3 * GROUP))]
     out_shape = [jax.ShapeDtypeStruct((width, 3 * GROUP), bf16)]
@@ -570,7 +593,7 @@
         out_shape.append(jax.ShapeDtypeStruct((rows, width), f32))
     else:
         extra = (*extra, *final)
-        in_specs += [square, fixed((1, width)), square]
+        in_specs += [pl.BlockSpec((rows, width), lambda i, s: (s[1], 0)), fixed((1, width)), square]
         out_specs += [square, fixed((8, width))]
         out_shape += [
             jax.ShapeDtypeStruct((rows, width), bf16),
@@ -585,7 +608,7 @@
         compiler_params=params(),
         cost_estimate=cost(7),
         name="project_final" if final is not None else "project",
-    )(sel, back, att, low_grad, first_t, wq, wk, wv, *extra)
+    )(sel, back, att, low_t, first_t, wq, wk, wv, *extra)
 
 
 def plain_order(piece, place, count):
@@ -908,8 +931,6 @@
     def own(values):
         return lax.dynamic_slice_in_dim(values, side * rows, rows, 0)
 
-    x = own(tokens)
-    cot = own(cotangent)
     seg = own(segments)
     seg_row, seg_col = seg[None, :], seg[:, None]
     routes_t = own(routes).T
@@ -922,43 +943,42 @@
 
     near_own = [cut(w, core, 1) for w in (w_query, w_key, w_value)]
     order_index = lax.axis_index("dp") % 4
+    experts_own = [lax.dynamic_slice_in_dim(w, order_index, 1, 0) for w in (w_gate, w_up, w_down)]
     near = [swap_tensor(w) for w in near_own]
+    got = [swap_tensor(after(experts_own[0], near[1]))]
+
+    first, first_t, *tables = prologue(side[None], tokens, gain_one, seg_row, freq)
+    saved_a = attend(first, w_query, w_key, w_value, tables, seg_col, seg_row)
+    (near, got[0]), (first, saved_a) = lax.optimization_barrier(((near, got[0]), (first, saved_a)))
+    far_qkv = [swap_dp(w, 1) for w in near]
     near_out = swap_tensor(after(cut(w_output, core, 0), near[0]))
-    last = near_out
-    got = []
-    for w in (w_gate, w_up, w_down):
-        last = swap_tensor(after(lax.dynamic_slice_in_dim(w, order_index, 1, 0), last))
-        got.append(last)
-
-    first, first_t, *tables = prologue(x, gain_one, seg_row, freq)
-    saved_a = attend(first, w_query, w_key, w_value, tables, seg_col, seg_row)
-    near, first = lax.optimization_barrier((near, (first, saved_a)))
-    first, saved_a = first
-    far_qkv = [swap_dp(w, 1) for w in near]
-    saved_b = attend(first, *near, tables, seg_col, seg_row)
-    (near_out, got[0]), (first, saved_b) = lax.optimization_barrier(((near_out, got[0]), (first, saved_b)))
-    far_out = swap_dp(near_out, 1)
+    got.append(swap_tensor(after(experts_own[1], near[0])))
     across = [swap_dp(got[0], 2)]
     beside = [swap_dp(got[0], 1)]
-    saved_c = attend(first, *far_qkv, tables, seg_col, seg_row)
-    (across[0], got[1]), saved_c = lax.optimization_barrier(((across[0], got[1]), saved_c))
+    saved_b = attend(first, *near, tables, seg_col, seg_row)
+    (near_out, got[1], across[0]), (first, saved_b) = lax.optimization_barrier(
+        ((near_out, got[1], across[0]), (first, saved_b))
+    )
+    far_out = swap_dp(near_out, 1)
+    got.append(swap_tensor(after(experts_own[2], near_out)))
     across.append(swap_dp(got[1], 2))
     beside.append(swap_dp(got[1], 1))
     corner = [swap_dp(across[0], 1)]
-    resid, second, gates, places = router(
-        x, (saved_a[3], saved_b[3], saved_c[3]), (w_output, near_out, far_out), gain_two, wr_t, routes_t, slots_t
-    )
-    (across[1], got[2]), second = lax.optimization_barrier(((across[1], got[2]), second))
+    saved_c = attend(first, *far_qkv, tables, seg_col, seg_row)
+    (across[1], got[2]), saved_c = lax.optimization_barrier(((across[1], got[2]), saved_c))
     across.append(swap_dp(got[2], 2))
     beside.append(swap_dp(got[2], 1))
     corner.append(swap_dp(across[1], 1))
+    resid, second, gates, places = router(
+        side[None], tokens, (saved_a[3], saved_b[3], saved_c[3]), (w_output, near_out, far_out), gain_two, wr_t, routes_t, slots_t
+    )
+    across[2], second = lax.optimization_barrier((across[2], second))
     corner.append(swap_dp(across[2], 1))
     r_gate, r_up, r_down = (jnp.concatenate(parts, axis=0) for parts in zip(got, beside, across, corner))
-    out, low_grad, resid_grad, small, kept, sent = experts_layer(
-        order_index[None], second, cot, resid, gates, places, gain_two, wr_t,
+    out, low_t, low_grad, resid_grad, small, kept, sent = experts_layer(
+        jnp.stack([order_index, side]), second, cotangent, resid, gates, places, gain_two, wr_t,
         (w_gate, r_gate, w_up, r_up, w_down, r_down),
     )
-    small = lax.psum(small, ("dp", "tensor"))
 
     chains = Chains()
     orders = ([2, 4], [4, 2])
@@ -980,30 +1000,30 @@
     low_grad = chains.advance(fence=low_grad)
     back = attend_back(zero, saved_c, *shared, low_grad, far_out)
     back = chains.advance(["grads"], fence=back)
-    group_d, partial_sum = project(zero, back, saved_c[3], low_grad, first_t, *far_qkv)
+    group_d, partial_sum = project(zero, back, saved_c[3], low_t, first_t, *far_qkv)
     chains.add("other", piece_swaps(group_d, 1, 1))
     low_grad, partial_sum = chains.advance(["other", "out"], fence=(low_grad, partial_sum))
     back = attend_back(zero, saved_b, *shared, low_grad, near_out)
     back = chains.advance(["other"], fence=back)
-    group_c, partial_sum = project(zero, back, saved_b[3], low_grad, first_t, *near, before=partial_sum)
+    group_c, partial_sum = project(zero, back, saved_b[3], low_t, first_t, *near, before=partial_sum)
     chains.add("theirs", piece_swaps(total([group_c, chains.done["other"]]), 1))
     low_grad, partial_sum = chains.advance(["grads", "out", "theirs"], fence=(low_grad, partial_sum))
     back = attend_back(one_minus, saved_a, *shared, low_grad, w_output)
     back = chains.advance(["grads"], fence=back)
     group_b, partial_sum = project(
-        one_minus, back, saved_a[3], low_grad, first_t, w_query, w_key, w_value, before=partial_sum
+        one_minus, back, saved_a[3], low_t, first_t, w_query, w_key, w_value, before=partial_sum
     )
     chains.add("mine", piece_swaps(group_b, 1, 1))
     low_grad, partial_sum = chains.advance(["mine"], fence=(low_grad, partial_sum))
     back = attend_back(core[None], saved_a, *shared, low_grad, w_output)
     back = chains.advance(["grads", "mine", "theirs"], fence=back)
     group_a, token, norm_one = project(
-        core[None], back, saved_a[3], low_grad, first_t, w_query, w_key, w_value,
-        before=partial_sum, final=(x, gain_one, resid_grad),
+        jnp.stack([core, side]), back, saved_a[3], low_t, first_t, w_query, w_key, w_value,
+        before=partial_sum, final=(tokens, gain_one, resid_grad),
     )
     chains.add("token", piece_swaps(token, 4))
     chains.add("tail", attention_sum((group_a, chains.done["mine"], chains.done["theirs"]), orders, far))
-    chains.add("norm", sum_all(norm_one))
+    chains.add("small", sum_all(jnp.concatenate([small, norm_one], 0)))
     chains.finish()
     done = chains.done
 
@@ -1014,6 +1034,7 @@
     grad_gate, grad_up, grad_down = unpack_experts(own_grads, other_grads, places, core, dp_size // 2)
     own_tail, other_tail = done["tail"]
     grad_query, grad_key, grad_value, grad_output = unpack(own_tail, other_tail, places, core, dp_size // 2)
+    small = done["small"]
     experts = w_router.shape[1]
 
     def both(mine, other):
@@ -1026,7 +1047,7 @@
         grad_key,
         grad_value,
         grad_output,
-        done["norm"][0],
+        small[experts + 8],
         small[experts],
         small[:experts].T,
         grad_gate,

time: 593 us -> 475 us (0.80)
  waiting for transfers between devices: 200 us -> 95.8 us
  between operations: 14.9 us -> 1.52 us
  local copies, waits for them, and re-layouts: 29.9 us -> 22.9 us
    psum x1 -> x0, waiting for transfers between devices: 103 us -> none  [per_device(): small = lax.psum(small, ('dp', 'tensor'))]
    ppermute x46, waiting for transfers between devices: 80.7 us -> 70 us  [swap_dp(): return lax.ppermute(values, 'dp', [(i, i ^ bit) for i in range(count)])]
    ppermute x16, waiting for transfers between devices: 16 us -> 25.7 us  [swap_tensor(): return lax.ppermute(values, 'tensor', [(0, 1), (1, 0)])]
  transfers between devices with their start and end apart: 63 -> 62, of which waited for: 20 -> 20; matrix products, arithmetic and copies ran while one was open for 6% -> 6% of each run, Pallas kernels for 28% -> 35%
where the time goes in v4:
time: 475 us; the launch traced here: 466 us
  Pallas kernels  248 us (52%)
  waiting for transfers between devices  95.8 us (20%)
  starting transfers between devices  64.5 us (14%)
  other arithmetic  33.3 us (7%)
  local copies, waits for them, and re-layouts  22.9 us (5%)
    ppermute x46, waiting for transfers between devices, swap_dp(): return lax.ppermute(values, 'dp', [(i, i ^ bit) for i in range(count)])  70 us
    pallas_call x4, Pallas kernels, attend_back(): pl.pallas_call(attend_back_kernel, grid_spec=pltpu.PrefetchScalarGridSpec...  53.8 us
    pallas_call x1, Pallas kernels, experts_layer(): pl.pallas_call(experts_kernel, grid_spec=pltpu.PrefetchScalarGridSpec(num...  45.8 us
    ppermute x46, starting transfers between devices, swap_dp(): return lax.ppermute(values, 'dp', [(i, i ^ bit) for i in range(count)])  45.3 us
    pallas_call x3, Pallas kernels, attend(): pl.pallas_call(attend_kernel, grid=(groups,), in_specs=[whole((rows, widt...  43.1 us
    pallas_call x4, Pallas kernels, project(): pl.pallas_call(partial(project_kernel, final is not None, before is None)...  42.9 us
    pallas_call x6, Pallas kernels, add_split(): pl.pallas_call(kernel, grid_spec=pltpu.PrefetchScalarGridSpec(num_scalar_...  30.7 us
    ppermute x16, waiting for transfers between devices, swap_tensor(): return lax.ppermute(values, 'tensor', [(0, 1), (1, 0)])  25.7 us
  transfers between devices with their start and end apart: 62, of which 20 were waited for; matrix products, arithmetic and copies ran while one was open for 6% of the time, Pallas kernels for 35%

profile of v4, /device:TPU:0, one launch (start us, length us, event | category | flops | bytes accessed | tf_op | source)
XLA Modules:
  0.0 466.2 jit_solution(16038962353261047592)
XLA Ops:
  1.7 3.0 collective-permute-start.1
  6.8 2.1 collective-permute-start.2
  12.3 5.2 %prologue.1 = (bf16[1024,1024]{1,0:T(8,128)(2,1)}, bf16[1024,1024]{1,0:T(8,128)(2,1)}, f32[1024,128]{1,0:T(8,128)}, f32[1024,128]{1,0:T(8,128)}, f32[1024,128]{1,0:T(8,128)}) custom-call(s32[1]{0:T(128)} %bitcast.1.side_ref, bf16[2048,1024]{1,0:T(8,128)(2,1)} %rest_1_.1, bf16[1,1024]{1,0:T(2,128)(2,1)} %broadcast_in_dim.10.gain_ref.rest_2_, ...), custom_call_target="tpu_custom_call" | custom-call | flops 2500000000 | bytes 1048576 | tf_op jit(solution)/shard_map/prologue/pallas_call | solution.py:96
  17.7 20.1 %attend.3 = (bf16[1024,512]{1,0:T(8,128)(2,1)}, bf16[1024,256]{1,0:T(8,128)(2,1)}, bf16[1024,256]{1,0:T(8,128)(2,1)}, bf16[1024,512]{1,0:T(8,128)(2,1)}, f32[2,8,1024]{2,1,0:T(8,128)}) custom-call(bf16[1024,1024]{1,0:T(8,128)(2,1)} %get-tuple-element.244.first_ref, bf16[1024,512]{1,0:T(8,128)(2,1)} %wq_ref.5, bf16[1024,256]{1,0:T(8,128)(2,1)} %wk_ref.5, ...), custom_call_target="tpu_custom_call" | custom-call | flops 10000000000 | bytes 1048576 | tf_op jit(solution)/shard_map/attend/pallas_call | solution.py:195
  39.1 1.9 collective-permute-start.5
  41.2 1.9 collective-permute-start.6
  44.8 9.1 %collective-permute-done.5 = bf16[1,1024,256]{2,1,0:T(8,128)(2,1)S(1)} collective-permute-done((bf16[1,1024,256]{2,1,0:T(8,128)(2,1)S(1)}, bf16[1,1024,256]{2,1,0:T(8,128)(2,1)S(1)}, u32[]{:S(2)}, u32[]{:S(2)}) %collective-permute-start.5) | collective-permute-done | bytes 524320 | tf_op jit(solution)/shard_map/ppermute | solution.py:798
  53.9 11.4 %attend.4 = (bf16[1024,256]{1,0:T(8,128)(2,1)}, bf16[1024,128]{1,0:T(8,128)(2,1)}, bf16[1024,128]{1,0:T(8,128)(2,1)}, bf16[1024,256]{1,0:T(8,128)(2,1)}, f32[1,8,1024]{2,1,0:T(8,128)}) custom-call(bf16[1024,1024]{1,0:T(8,128)(2,1)} %get-tuple-element.244.first_ref, bf16[1024,256]{1,0:T(8,128)(2,1)} %collective-permute-done.wq_ref, ...), custom_call_target="tpu_custom_call" | custom-call | flops 5000000000 | bytes 1048576 | tf_op jit(solution)/shard_map/attend/pallas_call | solution.py:195
  65.4 2.0 collective-permute-start.8
  67.4 1.5 collective-permute-start.7
  69.7 11.6 %attend.5 = (bf16[1024,256]{1,0:T(8,128)(2,1)}, bf16[1024,128]{1,0:T(8,128)(2,1)}, bf16[1024,128]{1,0:T(8,128)(2,1)}, bf16[1024,256]{1,0:T(8,128)(2,1)}, f32[1,8,1024]{2,1,0:T(8,128)}) custom-call(bf16[1024,1024]{1,0:T(8,128)(2,1)} %get-tuple-element.244.first_ref, bf16[1024,256]{1,0:T(8,128)(2,1)} %copy-done.30, ...), custom_call_target="tpu_custom_call" | custom-call | flops 5000000000 | bytes 1048576 | tf_op jit(solution)/shard_map/attend/pallas_call | solution.py:195
  81.4 1.5 collective-permute-start.12
  85.2 8.7 %router.1 = (f32[1024,1024]{1,0:T(8,128)}, bf16[1024,1024]{1,0:T(8,128)(2,1)}, f32[32,1024]{1,0:T(8,128)}, s32[8,1024]{1,0:T(8,128)}) custom-call(s32[1]{0:T(128)} %bitcast.1.side_ref, bf16[2048,1024]{1,0:T(8,128)(2,1)} %rest_1_.1, bf16[1024,512]{1,0:T(8,128)(2,1)} %get-tuple-element.251.att_a_ref.att_ref, ...), custom_call_target="tpu_custom_call" | custom-call | flops 4000000000 | bytes 1048576 | tf_op jit(solution)/shard_map/router/pallas_call | solution.py:270
  93.9 1.8 collective-permute-done.12
  96.8 2.6 pad_maximum_fusion.wg_b_ref
  99.4 2.8 pad_maximum_fusion.1.wu_b_ref
  102.2 1.7 pad_maximum_fusion.2.wd_b_ref
  103.9 45.8 %experts.1 = (bf16[1024,1024]{1,0:T(8,128)(2,1)}, bf16[1024,1024]{1,0:T(8,128)(2,1)}, bf16[1024,1024]{1,0:T(8,128)(2,1)}, f32[1024,1024]{1,0:T(8,128)}, f32[40,1...) custom-call(s32[2]{0:T(128)} %pad_add_fusion.order_ref, ...), custom_call_target="tpu_custom_call" | custom-call | flops 19499999232 | bytes 1048576 | tf_op jit(solution)/shard_map/experts/pallas_call | solution.py:401
  149.7 2.7 fusion.6
  153.6 13.4 %attend_back.4.back_ref = bf16[1024,512]{1,0:T(8,128)(2,1)} custom-call(s32[1]{0:T(128)} %constant.142.clone.1.sel_ref, bf16[1024,256]{1,0:T(8,128)(2,1)} %get-tuple-element.266.q_ref, bf16[1024,128]{1,0:T(8,128)(2,1)} %get-tuple-element.267.k_ref, bf16[1024,128]{1,0:T(8,128)(2,1)} %get-tuple-element.268.v_ref, f32[1,8,1024]{2,1,0:T(8,128)} %get-tuple-element.269.lse_ref, ...), custom_call_target="tpu_custom_call" | custom-call | flops 7000000000 | bytes 1048576 | tf_op jit(solution)/shard_map/attend_back/pallas_call | solution.py:518
  166.9 8.8 %add_split.6 = (bf16[2,384,1024]{2,1,0:T(8,128)(2,1)}, bf16[2,384,1024]{2,1,0:T(8,128)(2,1)}, bf16[2,384,1024]{2,1,0:T(8,128)(2,1)}, bf16[2,384,1024]{2,1,0:T(8,128)(2,1)}) custom-call(s32[2]{0:T(128)} %get-tuple-element.438.side_ref, bf16[4,768,1024]{2,1,0:T(8,128)(2,1)} %bitcast.32, ...), custom_call_target="tpu_custom_call" | custom-call | flops 2000000000 | bytes 1048576 | tf_op jit(solution)/shard_map/add_split/pallas_call | solution.py:667
  175.8 8.9 %project.3 = (bf16[1024,768]{1,0:T(8,128)(2,1)}, f32[1024,1024]{1,0:T(8,128)}) custom-call(s32[1]{0:T(128)} %constant.142.clone.1.sel_ref, bf16[1024,512]{1,0:T(8,128)(2,1)} %attend_back.4.back_ref, bf16[1024,256]{1,0:T(8,128)(2,1)} %get-tuple-element.253.att_c_ref.att_ref, bf16[1024,1024]{1,0:T(8,128)(2,1)} %get-tuple-element.277.low_t_ref, ...), custom_call_target="tpu_custom_call" | custom-call | flops 3500000000 | bytes 1048576 | tf_op jit(solution)/shard_map/project/pallas_call | solution.py:602
  186.5 1.6 collective-permute-start.24
  189.6 13.6 %attend_back.5.back_ref = bf16[1024,512]{1,0:T(8,128)(2,1)} custom-call(s32[1]{0:T(128)} %constant.142.clone.1.sel_ref, bf16[1024,256]{1,0:T(8,128)(2,1)} %get-tuple-element.286.q_ref, bf16[1024,128]{1,0:T(8,128)(2,1)} %get-tuple-element.287.k_ref, bf16[1024,128]{1,0:T(8,128)(2,1)} %get-tuple-element.288.v_ref, f32[1,8,1024]{2,1,0:T(8,128)} %get-tuple-element.289.lse_ref, ...), custom_call_target="tpu_custom_call" | custom-call | flops 7000000000 | bytes 1048576 | tf_op jit(solution)/shard_map/attend_back/pallas_call | solution.py:518
  203.2 10.2 %project.4 = (bf16[1024,768]{1,0:T(8,128)(2,1)}, f32[1024,1024]{1,0:T(8,128)}) custom-call(s32[1]{0:T(128)} %constant.142.clone.1.sel_ref, bf16[1024,512]{1,0:T(8,128)(2,1)} %attend_back.5.back_ref, bf16[1024,256]{1,0:T(8,128)(2,1)} %get-tuple-element.252.att_b_ref.att_ref, bf16[1024,1024]{1,0:T(8,128)(2,1)} %get-tuple-element.277.low_t_ref, ...), custom_call_target="tpu_custom_call" | custom-call | flops 3500000000 | bytes 1048576 | tf_op jit(solution)/shard_map/project/pallas_call | solution.py:602
  213.4 9.4 %collective-permute-done.23.refs_1_.refs_3_ = bf16[2,384,1024]{2,1,0:T(8,128)(2,1)S(1)} collective-permute-done((bf16[2,384,1024]{2,1,0:T(8,128)(2,1)}, bf16[2,384,1024]{2,1,0:T(8,128)(2,1)S(1)}, u32[]{:S(2)}, u32[]{:S(2)}) %collective-permute-start.23) | collective-permute-done | bytes 1572896 | tf_op jit(solution)/shard_map/ppermute | solution.py:803
  223.0 4.3 add_convert_fusion
  227.3 5.9 %add_split.7 = (bf16[2,192,1024]{2,1,0:T(8,128)(2,1)}, bf16[2,192,1024]{2,1,0:T(8,128)(2,1)}, bf16[2,192,1024]{2,1,0:T(8,128)(2,1)}, bf16[2,192,1024]{2,1,0:T(8,128)(2,1)}) custom-call(s32[2]{0:T(128)} %get-tuple-element.439.side_ref, bf16[2,384,1024]{2,1,0:T(8,128)(2,1)} %get-tuple-element.304.refs_0_.refs_2_, bf16[2,384,1024]{2,1,0:T(8,128)(2,1)} %copy-done.4, ...), custom_call_target="tpu_custom_call" | custom-call | flops 2000000000 | bytes 1048576 | tf_op jit(solution)/shard_map/add_split/pallas_call | solution.py:667
  233.2 1.6 collective-permute-start.26
  237.5 13.4 %attend_back.6.back_ref = bf16[1024,512]{1,0:T(8,128)(2,1)} custom-call(s32[1]{0:T(128)S(6)} %sub.28.sel_ref, bf16[1024,512]{1,0:T(8,128)(2,1)} %get-tuple-element.298.q_ref, bf16[1024,256]{1,0:T(8,128)(2,1)} %get-tuple-element.299.k_ref, bf16[1024,256]{1,0:T(8,128)(2,1)} %get-tuple-element.300.v_ref, f32[2,8,1024]{2,1,0:T(8,128)} %get-tuple-element.301.lse_ref, ...), custom_call_target="tpu_custom_call" | custom-call | flops 7000000000 | bytes 1048576 | tf_op jit(solution)/shard_map/attend_back/pallas_call | solution.py:518
  254.7 3.3 add_halves.1
  257.9 10.7 %project.5 = (bf16[1024,768]{1,0:T(8,128)(2,1)}, f32[1024,1024]{1,0:T(8,128)}) custom-call(s32[1]{0:T(128)S(6)} %sub.28.sel_ref, bf16[1024,512]{1,0:T(8,128)(2,1)} %attend_back.6.back_ref, bf16[1024,512]{1,0:T(8,128)(2,1)} %get-tuple-element.251.att_a_ref.att_ref, bf16[1024,1024]{1,0:T(8,128)(2,1)} %get-tuple-element.277.low_t_ref, ...), custom_call_target="tpu_custom_call" | custom-call | flops 3500000000 | bytes 1048576 | tf_op jit(solution)/shard_map/project/pallas_call | solution.py:602
  270.8 13.4 %attend_back.7.back_ref = bf16[1024,512]{1,0:T(8,128)(2,1)} custom-call(s32[1]{0:T(128)} %bitcast.11.sel_ref, bf16[1024,512]{1,0:T(8,128)(2,1)} %get-tuple-element.298.q_ref, bf16[1024,256]{1,0:T(8,128)(2,1)} %get-tuple-element.299.k_ref, bf16[1024,256]{1,0:T(8,128)(2,1)} %get-tuple-element.300.v_ref, f32[2,8,1024]{2,1,0:T(8,128)} %get-tuple-element.301.lse_ref, ...), custom_call_target="tpu_custom_call" | custom-call | flops 7000000000 | bytes 1048576 | tf_op jit(solution)/shard_map/attend_back/pallas_call | solution.py:518
  284.2 4.7 %collective-permute-done.28.refs_1_.refs_3_ = bf16[2,192,1024]{2,1,0:T(8,128)(2,1)} collective-permute-done((bf16[2,192,1024]{2,1,0:T(8,128)(2,1)}, bf16[2,192,1024]{2,1,0:T(8,128)(2,1)}, u32[]{:S(2)}, u32[]{:S(2)}) %collective-permute-start.28) | collective-permute-done | bytes 786464 | tf_op jit(solution)/shard_map/ppermute | solution.py:798
  288.9 3.1 add_split.8
  292.0 13.2 %project_final.1 = (bf16[1024,768]{1,0:T(8,128)(2,1)}, bf16[1024,1024]{1,0:T(8,128)(2,1)}, f32[8,1024]{1,0:T(8,128)}) custom-call(s32[2]{0:T(128)} %pad_add_fusion.2.sel_ref, bf16[1024,512]{1,0:T(8,128)(2,1)} %attend_back.7.back_ref, bf16[1024,512]{1,0:T(8,128)(2,1)} %get-tuple-element.251.att_a_ref.att_ref, ...), custom_call_target="tpu_custom_call" | custom-call | flops 3500000000 | bytes 1048576 | tf_op jit(solution)/shard_map/project_final/pallas_call | solution.py:602
  305.2 2.6 fusion.5
  307.8 5.2 %add_split.9 = (bf16[1,256,768]{2,1,0:T(8,128)(2,1)}, bf16[1,256,768]{2,1,0:T(8,128)(2,1)}, bf16[1,256,768]{2,1,0:T(8,128)(2,1)}, bf16[1,256,768]{2,1,0:T(8,128)(2,1)}) custom-call(s32[2]{0:T(128)} %get-tuple-element.438.side_ref, bf16[2,512,768]{2,1,0:T(8,128)(2,1)} %bitcast.44, bf16[2,512,768]{2,1,0:T(8,128)(2,1)} %bitcast.40, ...), custom_call_target="tpu_custom_call" | custom-call | flops 2000000000 | bytes 1048576 | tf_op jit(solution)/shard_map/add_split/pallas_call | solution.py:667
  312.9 1.6 collective-permute-start.35
  315.9 2.6 collective-permute-start.31
  319.0 11.8 %collective-permute-done.32 = f32[48,1024]{1,0:T(8,128)S(1)} collective-permute-done((f32[48,1024]{1,0:T(8,128)S(1)}, f32[48,1024]{1,0:T(8,128)S(1)}, u32[]{:S(2)}, u32[]{:S(2)}) %collective-permute-start.32) | collective-permute-done | bytes 196640 | tf_op jit(solution)/shard_map/ppermute | solution.py:798
  330.8 3.4 collective-permute-done.34.refs_5_.refs_7_
  335.1 4.0 add_split.10
  340.5 3.5 collective-permute-start.38
  345.8 5.8 %collective-permute-done.38.refs_1_.refs_3_ = bf16[1,128,768]{2,1,0:T(8,128)(2,1)S(1)} collective-permute-done((bf16[1,128,768]{2,1,0:T(8,128)(2,1)}, bf16[1,128,768]{2,1,0:T(8,128)(2,1)S(1)}, u32[]{:S(2)}, u32[]{:S(2)}) %collective-permute-start.38) | collective-permute-done | bytes 196640 | tf_op jit(solution)/shard_map/ppermute | solution.py:803
  351.7 7.1 %collective-permute-done.36 = bf16[2,96,1024]{2,1,0:T(8,128)(2,1)S(1)} collective-permute-done((bf16[2,96,1024]{2,1,0:T(8,128)(2,1)S(1)}, bf16[2,96,1024]{2,1,0:T(8,128)(2,1)S(1)}, u32[]{:S(2)}, u32[]{:S(2)}) %collective-permute-start.36) | collective-permute-done | bytes 393248 | tf_op jit(solution)/shard_map/ppermute | solution.py:803
  358.9 3.7 add_split.11
  362.6 1.6 collective-permute-start.46
  367.6 6.8 %collective-permute-done.44 = bf16[1,64,768]{2,1,0:T(8,128)(2,1)S(1)} collective-permute-done((bf16[1,64,768]{2,1,0:T(8,128)(2,1)}, bf16[1,64,768]{2,1,0:T(8,128)(2,1)S(1)}, u32[]{:S(2)}, u32[]{:S(2)}) %collective-permute-start.44) | collective-permute-done | bytes 98336 | tf_op jit(solution)/shard_map/ppermute | solution.py:803
  374.4 3.4 collective-permute-start.45
  377.8 3.9 collective-permute-done.45
  388.0 2.0 collective-permute-start.49
  390.0 15.3 %collective-permute-done.50 = bf16[64,768]{1,0:T(8,128)(2,1)} collective-permute-done((bf16[64,768]{1,0:T(8,128)(2,1)S(1)}, bf16[64,768]{1,0:T(8,128)(2,1)}, u32[]{:S(2)}, u32[]{:S(2)}) %collective-permute-start.50) | collective-permute-done | bytes 98336 | tf_op jit(solution)/shard_map/ppermute | solution.py:803
  405.3 3.5 collective-permute-start.51
  409.4 2.0 collective-permute-done.51
  414.8 1.9 pad_maximum_fusion.3.refs_0_
  417.4 4.6 maximum_select_fusion
  422.2 3.1 collective-permute-start.55
  427.4 7.1 %collective-permute-done.55 = f32[48,1024]{1,0:T(8,128)S(1)} collective-permute-done((f32[48,1024]{1,0:T(8,128)S(1)}, f32[48,1024]{1,0:T(8,128)S(1)}, u32[]{:S(2)}, u32[]{:S(2)}) %collective-permute-start.55) | collective-permute-done | bytes 196640 | tf_op jit(solution)/shard_map/ppermute | solution.py:803
  436.5 1.8 collective-permute-start.59
  438.3 3.9 select_convert_fusion
  442.3 3.6 collective-permute-done.58
  449.4 8.9 %unpack_experts.1 = (f32[4,1024,256]{2,1,0:T(8,128)}, f32[4,1024,256]{2,1,0:T(8,128)}, f32[4,256,1024]{2,1,0:T(8,128)}) custom-call(s32[3]{0:T(128)} %pad_add_fusion.5.place_ref, bf16[768,1024]{1,0:T(8,128)(2,1)} %copy-done.7, bf16[768,1024]{1,0:T(8,128)(2,1)} %copy-done.6, bf16[768,1024]{1,0:T(8,128)(2,1)} %copy-done.25, ...), custom_call_target="tpu_custom_call" | custom-call | flops 5000000000 | bytes 1048576 | tf_op jit(solution)/shard_map/unpack_experts/pallas_call | solution.py:732
  460.1 5.9 %unpack.1 = (f32[1024,512]{1,0:T(8,128)}, f32[1024,256]{1,0:T(8,128)}, f32[1024,256]{1,0:T(8,128)}, f32[512,1024]{1,0:T(8,128)}) custom-call(s32[3]{0:T(128)} %pad_add_fusion.5.place_ref, bf16[512,768]{1,0:T(8,128)(2,1)} %copy-done.12, bf16[512,768]{1,0:T(8,128)(2,1)} %copy-done.11, bf16[512,768]{1,0:T(8,128)(2,1)} %copy-done.26, bf16[512,768]{1,0:T(8,128)(2,1)} %copy-done.27), custom_call_target="tpu_custom_call" | custom-call | flops 3000000000 | bytes 1048576 | tf_op jit(solution)/shard_map/unpack/pallas_call | solution.py:781
  (218 shorter events, 57.5 us)
Async XLA Ops:
  1.7 15.9 %collective-permute-start.1 = (bf16[1024,128]{1,0:T(8,128)(2,1)S(1)}, bf16[1024,128]{1,0:T(8,128)(2,1)S(1)}, u32[]{:S(2)}, u32[]{:S(2)}) collective-permute-start(bf16[1024,128]{1,0:T(8,128)(2,1)S(1)} %constant_dynamic-slice_fusion.4), channel_id=1, source_target_pairs={{0,1},{1,0},{2,3},{3,2},{4,5},{5,4},{6,7},{7,6},{8,9},{9,8},{10,11... | collective-permute-start | bytes 786440 | tf_op jit(solution)/shard_map/ppermute | solution.py:798
  5.7 33.2 %collective-permute-start = (bf16[1024,256]{1,0:T(8,128)(2,1)S(1)}, bf16[1024,256]{1,0:T(8,128)(2,1)}, u32[]{:S(2)}, u32[]{:S(2)}) collective-permute-start(bf16[1024,256]{1,0:T(8,128)(2,1)S(1)} %constant_dynamic-slice_fusion.5), channel_id=1, source_target_pairs={{0,1},{1,0},{2,3},{3,2},{4,5},{5,4},{6,7},{7,6},{8,9},{9,8},{10,11... | collective-permute-start | bytes 1572872 | tf_op jit(solution)/shard_map/ppermute | solution.py:798
  6.8 32.1 %collective-permute-start.2 = (bf16[1024,128]{1,0:T(8,128)(2,1)S(1)}, bf16[1024,128]{1,0:T(8,128)(2,1)S(1)}, u32[]{:S(2)}, u32[]{:S(2)}) collective-permute-start(bf16[1024,128]{1,0:T(8,128)(2,1)S(1)} %constant_dynamic-slice_fusion.3), channel_id=1, source_target_pairs={{0,1},{1,0},{2,3},{3,2},{4,5},{5,4},{6,7},{7,6},{8,9},{9,8},{10,11... | collective-permute-start | bytes 786440 | tf_op jit(solution)/shard_map/ppermute | solution.py:798
  17.6 26.8 %copy-start.34 = (bf16[1024,128]{1,0:T(8,128)(2,1)}, bf16[1024,128]{1,0:T(8,128)(2,1)S(1)}, u32[]{:S(2)}) copy-start(bf16[1024,128]{1,0:T(8,128)(2,1)S(1)} %collective-permute-done.1.wk_ref) | copy-start | bytes 786436
  17.6 21.5 %collective-permute-start.3 = (bf16[1,1024,256]{2,1,0:T(8,128)(2,1)S(1)}, bf16[1,1024,256]{2,1,0:T(8,128)(2,1)S(1)}, u32[]{:S(2)}, u32[]{:S(2)}) collective-permute-start(bf16[1,1024,256]{2,1,0:T(8,128)(2,1)S(1)} %constant_dynamic-slice_fusion.2), channel_id=1, source_target_pairs={{0,1},{1,0},{2,3},{3,2},{4,5},{5,4},{6,7},{7,6},{8,9},{9,8},{10,11... | collective-permute-start | bytes 1572872 | tf_op jit(solution)/shard_map/ppermute | solution.py:798
  39.1 14.9 %collective-permute-start.5 = (bf16[1,1024,256]{2,1,0:T(8,128)(2,1)S(1)}, bf16[1,1024,256]{2,1,0:T(8,128)(2,1)S(1)}, u32[]{:S(2)}, u32[]{:S(2)}) collective-permute-start(bf16[1,1024,256]{2,1,0:T(8,128)(2,1)S(1)} %constant_dynamic-slice_fusion.1), channel_id=1, source_target_pairs={{0,1},{1,0},{2,3},{3,2},{4,5},{5,4},{6,7},{7,6},{8,9},{9,8},{10,11... | collective-permute-start | bytes 1572872 | tf_op jit(solution)/shard_map/ppermute | solution.py:798
  41.0 24.3 %collective-permute-start.4 = (bf16[256,1024]{1,0:T(8,128)(2,1)S(1)}, bf16[256,1024]{1,0:T(8,128)(2,1)}, u32[]{:S(2)}, u32[]{:S(2)}) collective-permute-start(bf16[256,1024]{1,0:T(8,128)(2,1)S(1)} %constant_dynamic-slice_fusion.6), channel_id=1, source_target_pairs={{0,1},{1,0},{2,3},{3,2},{4,5},{5,4},{6,7},{7,6},{8,9},{9,8},{10,11... | collective-permute-start | bytes 1572872 | tf_op jit(solution)/shard_map/ppermute | solution.py:798
  41.2 24.1 %collective-permute-start.6 = (bf16[1,1024,256]{2,1,0:T(8,128)(2,1)S(1)}, bf16[1,1024,256]{2,1,0:T(8,128)(2,1)S(1)}, u32[]{:S(2)}, u32[]{:S(2)}) collective-permute-start(bf16[1,1024,256]{2,1,0:T(8,128)(2,1)S(1)} %collective-permute-done.3), channel_id=1, source_target_pairs={{0,4},{2,6},{4,0},{6,2},{8,12},{10,14},{12,8},{14,10},{16,20},{18,... | collective-permute-start | bytes 1572872 | tf_op jit(solution)/shard_map/ppermute | solution.py:803
  44.2 24.7 %collective-permute-start.9 = (bf16[1024,256]{1,0:T(8,128)(2,1)}, bf16[1024,256]{1,0:T(8,128)(2,1)S(1)}, u32[]{:S(2)}, u32[]{:S(2)}) collective-permute-start(bf16[1024,256]{1,0:T(8,128)(2,1)} %collective-permute-done.wq_ref), channel_id=1, source_target_pairs={{0,2},{2,0},{4,6},{6,4},{8,10},{10,8},{12,14},{14,12},{16,18},{18,... | collective-permute-start | bytes 1572872 | tf_op jit(solution)/shard_map/ppermute | solution.py:803
  44.3 24.6 %collective-permute-start.10 = (bf16[1024,128]{1,0:T(8,128)(2,1)S(1)}, bf16[1024,128]{1,0:T(8,128)(2,1)}, u32[]{:S(2)}, u32[]{:S(2)}) collective-permute-start(bf16[1024,128]{1,0:T(8,128)(2,1)S(1)} %collective-permute-done.1.wk_ref), channel_id=1, source_target_pairs={{0,2},{2,0},{4,6},{6,4},{8,10},{10,8},{12,14},{14,12},{16,18},{18,... | collective-permute-start | bytes 786440 | tf_op jit(solution)/shard_map/ppermute | solution.py:803
  53.9 15.0 %collective-permute-start.11 = (bf16[1024,128]{1,0:T(8,128)(2,1)}, bf16[1024,128]{1,0:T(8,128)(2,1)}, u32[]{:S(2)}, u32[]{:S(2)}) collective-permute-start(bf16[1024,128]{1,0:T(8,128)(2,1)} %copy-done.35), channel_id=1, source_target_pairs={{0,2},{2,0},{4,6},{6,4},{8,10},{10,8},{12,14},{14,12},{16,18},{18,... | collective-permute-start | bytes 786440 | tf_op jit(solution)/shard_map/ppermute | solution.py:803
  65.4 16.0 %collective-permute-start.8 = (bf16[1,256,1024]{2,1,0:T(8,128)(2,1)S(1)}, bf16[1,256,1024]{2,1,0:T(8,128)(2,1)S(1)}, u32[]{:S(2)}, u32[]{:S(2)}) collective-permute-start(bf16[1,256,1024]{2,1,0:T(8,128)(2,1)S(1)} %constant_dynamic-slice_fusion), channel_id=1, source_target_pairs={{0,1},{1,0},{2,3},{3,2},{4,5},{5,4},{6,7},{7,6},{8,9},{9,8},{10,11... | collective-permute-start | bytes 1572872 | tf_op jit(solution)/shard_map/ppermute | solution.py:798
  67.4 14.0 %collective-permute-start.7 = (bf16[1,1024,256]{2,1,0:T(8,128)(2,1)S(1)}, bf16[1,1024,256]{2,1,0:T(8,128)(2,1)S(1)}, u32[]{:S(2)}, u32[]{:S(2)}) collective-permute-start(bf16[1,1024,256]{2,1,0:T(8,128)(2,1)S(1)} %collective-permute-done.5), channel_id=1, source_target_pairs={{0,4},{2,6},{4,0},{6,2},{8,12},{10,14},{12,8},{14,10},{16,20},{18,... | collective-permute-start | bytes 1572872 | tf_op jit(solution)/shard_map/ppermute | solution.py:803
  68.9 15.8 %collective-permute-start.13 = (bf16[256,1024]{1,0:T(8,128)(2,1)}, bf16[256,1024]{1,0:T(8,128)(2,1)}, u32[]{:S(2)}, u32[]{:S(2)}) collective-permute-start(bf16[256,1024]{1,0:T(8,128)(2,1)} %collective-permute-done.4.wo_b_ref.wo_ref), channel_id=1, source_target_pairs={{0,2},{2,0},{4,6},{6,4},{8,10},{10,8},{12,14},{14,12},{16,18},{18,... | collective-permute-start | bytes 1572872 | tf_op jit(solution)/shard_map/ppermute | solution.py:803
  81.4 14.3 %collective-permute-start.12 = (bf16[1,256,1024]{2,1,0:T(8,128)(2,1)S(1)}, bf16[1,256,1024]{2,1,0:T(8,128)(2,1)S(1)}, u32[]{:S(2)}, u32[]{:S(2)}) collective-permute-start(bf16[1,256,1024]{2,1,0:T(8,128)(2,1)S(1)} %collective-permute-done.8), channel_id=1, source_target_pairs={{0,4},{2,6},{4,0},{6,2},{8,12},{10,14},{12,8},{14,10},{16,20},{18,... | collective-permute-start | bytes 1572872 | tf_op jit(solution)/shard_map/ppermute | solution.py:803
  82.9 12.8 %collective-permute-start.14 = (bf16[1,1024,256]{2,1,0:T(8,128)(2,1)S(1)}, bf16[1,1024,256]{2,1,0:T(8,128)(2,1)S(1)}, u32[]{:S(2)}, u32[]{:S(2)}) collective-permute-start(bf16[1,1024,256]{2,1,0:T(8,128)(2,1)S(1)} %collective-permute-done.3), channel_id=1, source_target_pairs={{0,2},{2,0},{4,6},{6,4},{8,10},{10,8},{12,14},{14,12},{16,18},{18,... | collective-permute-start | bytes 1572872 | tf_op jit(solution)/shard_map/ppermute | solution.py:803
  82.9 13.9 %collective-permute-start.15 = (bf16[1,1024,256]{2,1,0:T(8,128)(2,1)S(1)}, bf16[1,1024,256]{2,1,0:T(8,128)(2,1)}, u32[]{:S(2)}, u32[]{:S(2)}) collective-permute-start(bf16[1,1024,256]{2,1,0:T(8,128)(2,1)S(1)} %collective-permute-done.6), channel_id=1, source_target_pairs={{0,2},{2,0},{4,6},{6,4},{8,10},{10,8},{12,14},{14,12},{16,18},{18,... | collective-permute-start | bytes 1572872 | tf_op jit(solution)/shard_map/ppermute | solution.py:803
  84.7 14.8 %collective-permute-start.16 = (bf16[1,1024,256]{2,1,0:T(8,128)(2,1)S(1)}, bf16[1,1024,256]{2,1,0:T(8,128)(2,1)}, u32[]{:S(2)}, u32[]{:S(2)}) collective-permute-start(bf16[1,1024,256]{2,1,0:T(8,128)(2,1)S(1)} %collective-permute-done.5), channel_id=1, source_target_pairs={{0,2},{2,0},{4,6},{6,4},{8,10},{10,8},{12,14},{14,12},{16,18},{18,... | collective-permute-start | bytes 1572872 | tf_op jit(solution)/shard_map/ppermute | solution.py:803
  84.7 14.8 %collective-permute-start.17 = (bf16[1,1024,256]{2,1,0:T(8,128)(2,1)S(1)}, bf16[1,1024,256]{2,1,0:T(8,128)(2,1)}, u32[]{:S(2)}, u32[]{:S(2)}) collective-permute-start(bf16[1,1024,256]{2,1,0:T(8,128)(2,1)S(1)} %collective-permute-done.7), channel_id=1, source_target_pairs={{0,2},{2,0},{4,6},{6,4},{8,10},{10,8},{12,14},{14,12},{16,18},{18,... | collective-permute-start | bytes 1572872 | tf_op jit(solution)/shard_map/ppermute | solution.py:803
  95.7 6.5 %collective-permute-start.18 = (bf16[1,256,1024]{2,1,0:T(8,128)(2,1)S(1)}, bf16[1,256,1024]{2,1,0:T(8,128)(2,1)S(1)}, u32[]{:S(2)}, u32[]{:S(2)}) collective-permute-start(bf16[1,256,1024]{2,1,0:T(8,128)(2,1)S(1)} %collective-permute-done.8), channel_id=1, source_target_pairs={{0,2},{2,0},{4,6},{6,4},{8,10},{10,8},{12,14},{14,12},{16,18},{18,... | collective-permute-start | bytes 1572872 | tf_op jit(solution)/shard_map/ppermute | solution.py:803
  95.7 6.5 %collective-permute-start.19 = (bf16[1,256,1024]{2,1,0:T(8,128)(2,1)S(1)}, bf16[1,256,1024]{2,1,0:T(8,128)(2,1)S(1)}, u32[]{:S(2)}, u32[]{:S(2)}) collective-permute-start(bf16[1,256,1024]{2,1,0:T(8,128)(2,1)S(1)} %collective-permute-done.12), channel_id=1, source_target_pairs={{0,2},{2,0},{4,6},{6,4},{8,10},{10,8},{12,14},{14,12},{16,18},{18,... | collective-permute-start | bytes 1572872 | tf_op jit(solution)/shard_map/ppermute | solution.py:803
  152.4 14.6 %collective-permute-start.20 = (bf16[4,768,1024]{2,1,0:T(8,128)(2,1)}, bf16[4,768,1024]{2,1,0:T(8,128)(2,1)}, u32[]{:S(2)}, u32[]{:S(2)}) collective-permute-start(bf16[4,768,1024]{2,1,0:T(8,128)(2,1)} %bitcast.59), channel_id=1, source_target_pairs={{0,2},{2,0},{4,6},{6,4},{8,10},{10,8},{12,14},{14,12},{16,18},{18,... | collective-permute-start | bytes 18874376 | tf_op jit(solution)/shard_map/ppermute | solution.py:803
  153.0 31.6 %collective-permute-start.21 = (bf16[512,1024]{1,0:T(8,128)(2,1)S(1)}, bf16[512,1024]{1,0:T(8,128)(2,1)S(1)}, u32[]{:S(2)}, u32[]{:S(2)}) collective-permute-start(bf16[512,1024]{1,0:T(8,128)(2,1)S(1)} %get-tuple-element.280), channel_id=1, source_target_pairs={{0,1},{1,0},{2,3},{3,2},{4,5},{5,4},{6,7},{7,6},{8,9},{9,8},{10,11... | collective-permute-start | bytes 3145736 | tf_op jit(solution)/shard_map/ppermute | solution.py:798
  185.7 17.4 %collective-permute-start.22 = (bf16[1024,768]{1,0:T(8,128)(2,1)}, bf16[1024,768]{1,0:T(8,128)(2,1)}, u32[]{:S(2)}, u32[]{:S(2)}) collective-permute-start(bf16[1024,768]{1,0:T(8,128)(2,1)} %get-tuple-element.290), channel_id=1, source_target_pairs={{0,2},{2,0},{4,6},{6,4},{8,10},{10,8},{12,14},{14,12},{16,18},{18,... | collective-permute-start | bytes 4718600 | tf_op jit(solution)/shard_map/ppermute | solution.py:803
  186.0 36.8 %collective-permute-start.23 = (bf16[2,384,1024]{2,1,0:T(8,128)(2,1)}, bf16[2,384,1024]{2,1,0:T(8,128)(2,1)S(1)}, u32[]{:S(2)}, u32[]{:S(2)}) collective-permute-start(bf16[2,384,1024]{2,1,0:T(8,128)(2,1)} %get-tuple-element.294), channel_id=1, source_target_pairs={{0,4},{2,6},{4,0},{6,2},{8,12},{10,14},{12,8},{14,10},{16,20},{18,... | collective-permute-start | bytes 4718600 | tf_op jit(solution)/shard_map/ppermute | solution.py:803
  186.5 36.5 %collective-permute-start.24 = (bf16[2,384,1024]{2,1,0:T(8,128)(2,1)}, bf16[2,384,1024]{2,1,0:T(8,128)(2,1)S(1)}, u32[]{:S(2)}, u32[]{:S(2)}) collective-permute-start(bf16[2,384,1024]{2,1,0:T(8,128)(2,1)} %get-tuple-element.295), channel_id=1, source_target_pairs={{0,8},{2,10},{4,12},{6,14},{8,0},{10,2},{12,4},{14,6},{16,24},{18,... | collective-permute-start | bytes 4718600 | tf_op jit(solution)/shard_map/ppermute | solution.py:803
  188.1 25.3 %collective-permute-start.25 = (bf16[512,1024]{1,0:T(8,128)(2,1)}, bf16[512,1024]{1,0:T(8,128)(2,1)}, u32[]{:S(2)}, u32[]{:S(2)}) collective-permute-start(bf16[512,1024]{1,0:T(8,128)(2,1)} %get-tuple-element.296), channel_id=1, source_target_pairs={{0,1},{1,0},{2,3},{3,2},{4,5},{5,4},{6,7},{7,6},{8,9},{9,8},{10,11... | collective-permute-start | bytes 3145736 | tf_op jit(solution)/shard_map/ppermute | solution.py:798
  233.2 19.2 %collective-permute-start.26 = (bf16[2,192,1024]{2,1,0:T(8,128)(2,1)}, bf16[2,192,1024]{2,1,0:T(8,128)(2,1)S(1)}, u32[]{:S(2)}, u32[]{:S(2)}) collective-permute-start(bf16[2,192,1024]{2,1,0:T(8,128)(2,1)} %get-tuple-element.313), channel_id=1, source_target_pairs={{0,8},{2,10},{4,12},{6,14},{8,0},{10,2},{12,4},{14,6},{16,24},{18,... | collective-permute-start | bytes 2359304 | tf_op jit(solution)/shard_map/ppermute | solution.py:803
  234.8 18.9 %collective-permute-start.27 = (bf16[2,192,1024]{2,1,0:T(8,128)(2,1)}, bf16[2,192,1024]{2,1,0:T(8,128)(2,1)S(1)}, u32[]{:S(2)}, u32[]{:S(2)}) collective-permute-start(bf16[2,192,1024]{2,1,0:T(8,128)(2,1)} %get-tuple-element.314), channel_id=1, source_target_pairs={{0,4},{2,6},{4,0},{6,2},{8,12},{10,14},{12,8},{14,10},{16,20},{18,... | collective-permute-start | bytes 2359304 | tf_op jit(solution)/shard_map/ppermute | solution.py:803
  236.0 48.2 %collective-permute-start.30 = (bf16[1024,768]{1,0:T(8,128)(2,1)}, bf16[1024,768]{1,0:T(8,128)(2,1)S(1)}, u32[]{:S(2)}, u32[]{:S(2)}) collective-permute-start(bf16[1024,768]{1,0:T(8,128)(2,1)} %add_convert_fusion), channel_id=1, source_target_pairs={{0,1},{1,0},{2,3},{3,2},{4,5},{5,4},{6,7},{7,6},{8,9},{9,8},{10,11... | collective-permute-start | bytes 4718600 | tf_op jit(solution)/shard_map/ppermute | solution.py:798
  268.6 20.3 %collective-permute-start.29 = (bf16[1024,768]{1,0:T(8,128)(2,1)}, bf16[1024,768]{1,0:T(8,128)(2,1)S(1)}, u32[]{:S(2)}, u32[]{:S(2)}) collective-permute-start(bf16[1024,768]{1,0:T(8,128)(2,1)} %get-tuple-element.329), channel_id=1, source_target_pairs={{0,2},{2,0},{4,6},{6,4},{8,10},{10,8},{12,14},{14,12},{16,18},{18,... | collective-permute-start | bytes 4718600 | tf_op jit(solution)/shard_map/ppermute | solution.py:803
  268.6 20.3 %collective-permute-start.28 = (bf16[2,192,1024]{2,1,0:T(8,128)(2,1)}, bf16[2,192,1024]{2,1,0:T(8,128)(2,1)}, u32[]{:S(2)}, u32[]{:S(2)}) collective-permute-start(bf16[2,192,1024]{2,1,0:T(8,128)(2,1)} %get-tuple-element.328), channel_id=1, source_target_pairs={{0,1},{1,0},{2,3},{3,2},{4,5},{5,4},{6,7},{7,6},{8,9},{9,8},{10,11... | collective-permute-start | bytes 2359304 | tf_op jit(solution)/shard_map/ppermute | solution.py:798
  307.8 27.2 %copy-start.13 = (bf16[2,96,1024]{2,1,0:T(8,128)(2,1)S(1)}, bf16[2,96,1024]{2,1,0:T(8,128)(2,1)}, u32[]{:S(2)}) copy-start(bf16[2,96,1024]{2,1,0:T(8,128)(2,1)} %get-tuple-element.352) | copy-start | bytes 1179652
  312.9 22.0 %collective-permute-start.35 = (bf16[256,1024]{1,0:T(8,128)(2,1)S(1)}, bf16[256,1024]{1,0:T(8,128)(2,1)S(1)}, u32[]{:S(2)}, u32[]{:S(2)}) collective-permute-start(bf16[256,1024]{1,0:T(8,128)(2,1)S(1)} %get-tuple-element.350), channel_id=1, source_target_pairs={{0,1},{1,0},{2,3},{3,2},{4,5},{5,4},{6,7},{7,6},{8,9},{9,8},{10,11... | collective-permute-start | bytes 1572872 | tf_op jit(solution)/shard_map/ppermute | solution.py:798
  314.5 16.3 %collective-permute-start.33 = (bf16[1,256,768]{2,1,0:T(8,128)(2,1)}, bf16[1,256,768]{2,1,0:T(8,128)(2,1)S(1)}, u32[]{:S(2)}, u32[]{:S(2)}) collective-permute-start(bf16[1,256,768]{2,1,0:T(8,128)(2,1)} %get-tuple-element.348), channel_id=1, source_target_pairs={{0,4},{2,6},{4,0},{6,2},{8,12},{10,14},{12,8},{14,10},{16,20},{18,... | collective-permute-start | bytes 1179656 | tf_op jit(solution)/shard_map/ppermute | solution.py:803
  315.4 18.8 %collective-permute-start.34 = (bf16[1,256,768]{2,1,0:T(8,128)(2,1)}, bf16[1,256,768]{2,1,0:T(8,128)(2,1)S(1)}, u32[]{:S(2)}, u32[]{:S(2)}) collective-permute-start(bf16[1,256,768]{2,1,0:T(8,128)(2,1)} %get-tuple-element.349), channel_id=1, source_target_pairs={{0,8},{2,10},{4,12},{6,14},{8,0},{10,2},{12,4},{14,6},{16,24},{18,... | collective-permute-start | bytes 1179656 | tf_op jit(solution)/shard_map/ppermute | solution.py:803
  315.9 18.3 %collective-permute-start.31 = (bf16[2,96,1024]{2,1,0:T(8,128)(2,1)S(1)}, bf16[2,96,1024]{2,1,0:T(8,128)(2,1)S(1)}, u32[]{:S(2)}, u32[]{:S(2)}) collective-permute-start(bf16[2,96,1024]{2,1,0:T(8,128)(2,1)S(1)} %copy-done.31), channel_id=1, source_target_pairs={{0,16},{2,18},{4,20},{6,22},{8,24},{10,26},{12,28},{14,30},{16,0},... | collective-permute-start | bytes 1179656 | tf_op jit(solution)/shard_map/ppermute | solution.py:803
  318.5 12.3 %collective-permute-start.32 = (f32[48,1024]{1,0:T(8,128)S(1)}, f32[48,1024]{1,0:T(8,128)S(1)}, u32[]{:S(2)}, u32[]{:S(2)}) collective-permute-start(f32[48,1024]{1,0:T(8,128)S(1)} %constant_dynamic-update-slice_fusion), channel_id=1, source_target_pairs={{0,1},{1,0},{2,3},{3,2},{4,5},{5,4},{6,7},{7,6},{8,9},{9,8},{10,11... | collective-permute-start | bytes 589832 | tf_op jit(solution)/shard_map/ppermute | solution.py:798
  339.1 19.6 %collective-permute-start.40 = (bf16[256,1024]{1,0:T(8,128)(2,1)S(1)}, bf16[256,1024]{1,0:T(8,128)(2,1)S(1)}, u32[]{:S(2)}, u32[]{:S(2)}) collective-permute-start(bf16[256,1024]{1,0:T(8,128)(2,1)S(1)} %get-tuple-element.365), channel_id=1, source_target_pairs={{0,1},{1,0},{2,3},{3,2},{4,5},{5,4},{6,7},{7,6},{8,9},{9,8},{10,11... | collective-permute-start | bytes 1572872 | tf_op jit(solution)/shard_map/ppermute | solution.py:798
  339.7 19.1 %collective-permute-start.36 = (bf16[2,96,1024]{2,1,0:T(8,128)(2,1)S(1)}, bf16[2,96,1024]{2,1,0:T(8,128)(2,1)S(1)}, u32[]{:S(2)}, u32[]{:S(2)}) collective-permute-start(bf16[2,96,1024]{2,1,0:T(8,128)(2,1)S(1)} %add_convert_fusion.1), channel_id=1, source_target_pairs={{0,16},{2,18},{4,20},{6,22},{8,24},{10,26},{12,28},{14,30},{16,0},... | collective-permute-start | bytes 1179656 | tf_op jit(solution)/shard_map/ppermute | solution.py:803
  340.5 5.3 %collective-permute-start.37 = (f32[48,1024]{1,0:T(8,128)S(1)}, f32[48,1024]{1,0:T(8,128)S(1)}, u32[]{:S(2)}, u32[]{:S(2)}) collective-permute-start(f32[48,1024]{1,0:T(8,128)S(1)} %add.102), channel_id=1, source_target_pairs={{0,2},{2,0},{4,6},{6,4},{8,10},{10,8},{12,14},{14,12},{16,18},{18,... | collective-permute-start | bytes 589832 | tf_op jit(solution)/shard_map/ppermute | solution.py:803
  340.5 11.1 %collective-permute-start.38 = (bf16[1,128,768]{2,1,0:T(8,128)(2,1)}, bf16[1,128,768]{2,1,0:T(8,128)(2,1)S(1)}, u32[]{:S(2)}, u32[]{:S(2)}) collective-permute-start(bf16[1,128,768]{2,1,0:T(8,128)(2,1)} %get-tuple-element.363), channel_id=1, source_target_pairs={{0,8},{2,10},{4,12},{6,14},{8,0},{10,2},{12,4},{14,6},{16,24},{18,... | collective-permute-start | bytes 589832 | tf_op jit(solution)/shard_map/ppermute | solution.py:803
  344.0 7.6 %collective-permute-start.39 = (bf16[1,128,768]{2,1,0:T(8,128)(2,1)}, bf16[1,128,768]{2,1,0:T(8,128)(2,1)S(1)}, u32[]{:S(2)}, u32[]{:S(2)}) collective-permute-start(bf16[1,128,768]{2,1,0:T(8,128)(2,1)} %get-tuple-element.364), channel_id=1, source_target_pairs={{0,4},{2,6},{4,0},{6,2},{8,12},{10,14},{12,8},{14,10},{16,20},{18,... | collective-permute-start | bytes 589832 | tf_op jit(solution)/shard_map/ppermute | solution.py:803
  362.6 19.0 %collective-permute-start.46 = (bf16[256,1024]{1,0:T(8,128)(2,1)S(1)}, bf16[256,1024]{1,0:T(8,128)(2,1)S(1)}, u32[]{:S(2)}, u32[]{:S(2)}) collective-permute-start(bf16[256,1024]{1,0:T(8,128)(2,1)S(1)} %get-tuple-element.380), channel_id=1, source_target_pairs={{0,1},{1,0},{2,3},{3,2},{4,5},{5,4},{6,7},{7,6},{8,9},{9,8},{10,11... | collective-permute-start | bytes 1572872 | tf_op jit(solution)/shard_map/ppermute | solution.py:798
  364.2 17.4 %collective-permute-start.41 = (bf16[192,1024]{1,0:T(8,128)(2,1)S(1)}, bf16[192,1024]{1,0:T(8,128)(2,1)S(1)}, u32[]{:S(2)}, u32[]{:S(2)}) collective-permute-start(bf16[192,1024]{1,0:T(8,128)(2,1)S(1)} %get-tuple-element.375), channel_id=1, source_target_pairs={{0,8},{2,10},{4,12},{6,14},{8,0},{10,2},{12,4},{14,6},{16,24},{18,... | collective-permute-start | bytes 1179656 | tf_op jit(solution)/shard_map/ppermute | solution.py:803
  364.2 17.4 %collective-permute-start.42 = (bf16[192,1024]{1,0:T(8,128)(2,1)S(1)}, bf16[192,1024]{1,0:T(8,128)(2,1)S(1)}, u32[]{:S(2)}, u32[]{:S(2)}) collective-permute-start(bf16[192,1024]{1,0:T(8,128)(2,1)S(1)} %get-tuple-element.376), channel_id=1, source_target_pairs={{0,4},{2,6},{4,0},{6,2},{8,12},{10,14},{12,8},{14,10},{16,20},{18,... | collective-permute-start | bytes 1179656 | tf_op jit(solution)/shard_map/ppermute | solution.py:803
  365.4 9.0 %collective-permute-start.44 = (bf16[1,64,768]{2,1,0:T(8,128)(2,1)}, bf16[1,64,768]{2,1,0:T(8,128)(2,1)S(1)}, u32[]{:S(2)}, u32[]{:S(2)}) collective-permute-start(bf16[1,64,768]{2,1,0:T(8,128)(2,1)} %get-tuple-element.378), channel_id=1, source_target_pairs={{0,16},{2,18},{4,20},{6,22},{8,24},{10,26},{12,28},{14,30},{16,0},... | collective-permute-start | bytes 294920 | tf_op jit(solution)/shard_map/ppermute | solution.py:803
  366.7 14.9 %collective-permute-start.43 = (f32[48,1024]{1,0:T(8,128)S(1)}, f32[48,1024]{1,0:T(8,128)S(1)}, u32[]{:S(2)}, u32[]{:S(2)}) collective-permute-start(f32[48,1024]{1,0:T(8,128)S(1)} %add.103), channel_id=1, source_target_pairs={{0,4},{2,6},{4,0},{6,2},{8,12},{10,14},{12,8},{14,10},{16,20},{18,... | collective-permute-start | bytes 589832 | tf_op jit(solution)/shard_map/ppermute | solution.py:803
  374.4 7.2 %collective-permute-start.45 = (bf16[1,64,768]{2,1,0:T(8,128)(2,1)}, bf16[1,64,768]{2,1,0:T(8,128)(2,1)S(1)}, u32[]{:S(2)}, u32[]{:S(2)}) collective-permute-start(bf16[1,64,768]{2,1,0:T(8,128)(2,1)} %get-tuple-element.379), channel_id=1, source_target_pairs={{0,16},{2,18},{4,20},{6,22},{8,24},{10,26},{12,28},{14,30},{16,0},... | collective-permute-start | bytes 294920 | tf_op jit(solution)/shard_map/ppermute | solution.py:803
  384.4 27.0 %collective-permute-start.47 = (bf16[384,1024]{1,0:T(8,128)(2,1)}, bf16[384,1024]{1,0:T(8,128)(2,1)}, u32[]{:S(2)}, u32[]{:S(2)}) collective-permute-start(bf16[384,1024]{1,0:T(8,128)(2,1)} %pad_maximum_fusion.5), channel_id=1, source_target_pairs={{0,4},{2,6},{4,0},{6,2},{8,12},{10,14},{12,8},{14,10},{16,20},{18,... | collective-permute-start | bytes 2359304 | tf_op jit(solution)/shard_map/ppermute | solution.py:803
  385.6 25.8 %collective-permute-start.48 = (bf16[384,1024]{1,0:T(8,128)(2,1)}, bf16[384,1024]{1,0:T(8,128)(2,1)}, u32[]{:S(2)}, u32[]{:S(2)}) collective-permute-start(bf16[384,1024]{1,0:T(8,128)(2,1)} %pad_maximum_fusion.6), channel_id=1, source_target_pairs={{0,8},{2,10},{4,12},{6,14},{8,0},{10,2},{12,4},{14,6},{16,24},{18,... | collective-permute-start | bytes 2359304 | tf_op jit(solution)/shard_map/ppermute | solution.py:803
  386.1 25.3 %collective-permute-start.52 = (bf16[256,1024]{1,0:T(8,128)(2,1)}, bf16[256,1024]{1,0:T(8,128)(2,1)S(1)}, u32[]{:S(2)}, u32[]{:S(2)}) collective-permute-start(bf16[256,1024]{1,0:T(8,128)(2,1)} %get-tuple-element.394), channel_id=1, source_target_pairs={{0,1},{1,0},{2,3},{3,2},{4,5},{5,4},{6,7},{7,6},{8,9},{9,8},{10,11... | collective-permute-start | bytes 1572872 | tf_op jit(solution)/shard_map/ppermute | solution.py:798
  386.6 18.7 %collective-permute-start.50 = (bf16[64,768]{1,0:T(8,128)(2,1)S(1)}, bf16[64,768]{1,0:T(8,128)(2,1)}, u32[]{:S(2)}, u32[]{:S(2)}) collective-permute-start(bf16[64,768]{1,0:T(8,128)(2,1)S(1)} %fusion.3), channel_id=1, source_target_pairs={{0,16},{2,18},{4,20},{6,22},{8,24},{10,26},{12,28},{14,30},{16,0},... | collective-permute-start | bytes 294920 | tf_op jit(solution)/shard_map/ppermute | solution.py:803
  388.0 23.4 %collective-permute-start.49 = (f32[48,1024]{1,0:T(8,128)}, f32[48,1024]{1,0:T(8,128)}, u32[]{:S(2)}, u32[]{:S(2)}) collective-permute-start(f32[48,1024]{1,0:T(8,128)} %add.104), channel_id=1, source_target_pairs={{0,8},{2,10},{4,12},{6,14},{8,0},{10,2},{12,4},{14,6},{16,24},{18,... | collective-permute-start | bytes 589832 | tf_op jit(solution)/shard_map/ppermute | solution.py:803
  405.3 6.1 %collective-permute-start.51 = (bf16[64,768]{1,0:T(8,128)(2,1)S(1)}, bf16[64,768]{1,0:T(8,128)(2,1)S(1)}, u32[]{:S(2)}, u32[]{:S(2)}) collective-permute-start(bf16[64,768]{1,0:T(8,128)(2,1)S(1)} %fusion.4), channel_id=1, source_target_pairs={{0,16},{2,18},{4,20},{6,22},{8,24},{10,26},{12,28},{14,30},{16,0},... | collective-permute-start | bytes 294920 | tf_op jit(solution)/shard_map/ppermute | solution.py:803
  416.7 17.8 %collective-permute-start.53 = (bf16[768,1024]{1,0:T(8,128)(2,1)S(1)}, bf16[768,1024]{1,0:T(8,128)(2,1)S(1)}, u32[]{:S(2)}, u32[]{:S(2)}) collective-permute-start(bf16[768,1024]{1,0:T(8,128)(2,1)S(1)} %pad_maximum_fusion.3.refs_0_), channel_id=1, source_target_pairs={{0,2},{2,0},{4,6},{6,4},{8,10},{10,8},{12,14},{14,12},{16,18},{18,... | collective-permute-start | bytes 4718600 | tf_op jit(solution)/shard_map/ppermute | solution.py:803
  416.8 17.8 %collective-permute-start.54 = (bf16[768,1024]{1,0:T(8,128)(2,1)S(1)}, bf16[768,1024]{1,0:T(8,128)(2,1)}, u32[]{:S(2)}, u32[]{:S(2)}) collective-permute-start(bf16[768,1024]{1,0:T(8,128)(2,1)S(1)} %pad_maximum_fusion.4.refs_1_), channel_id=1, source_target_pairs={{0,2},{2,0},{4,6},{6,4},{8,10},{10,8},{12,14},{14,12},{16,18},{18,... | collective-permute-start | bytes 4718600 | tf_op jit(solution)/shard_map/ppermute | solution.py:803
  422.2 12.3 %collective-permute-start.55 = (f32[48,1024]{1,0:T(8,128)S(1)}, f32[48,1024]{1,0:T(8,128)S(1)}, u32[]{:S(2)}, u32[]{:S(2)}) collective-permute-start(f32[48,1024]{1,0:T(8,128)S(1)} %add.111), channel_id=1, source_target_pairs={{0,16},{2,18},{4,20},{6,22},{8,24},{10,26},{12,28},{14,30},{16,0},... | collective-permute-start | bytes 589832 | tf_op jit(solution)/shard_map/ppermute | solution.py:803
  425.3 9.2 %collective-permute-start.56 = (bf16[128,768]{1,0:T(8,128)(2,1)S(1)}, bf16[128,768]{1,0:T(8,128)(2,1)S(1)}, u32[]{:S(2)}, u32[]{:S(2)}) collective-permute-start(bf16[128,768]{1,0:T(8,128)(2,1)S(1)} %pad_maximum_fusion.12), channel_id=1, source_target_pairs={{0,8},{2,10},{4,12},{6,14},{8,0},{10,2},{12,4},{14,6},{16,24},{18,... | collective-permute-start | bytes 589832 | tf_op jit(solution)/shard_map/ppermute | solution.py:803
  425.8 8.7 %collective-permute-start.57 = (bf16[128,768]{1,0:T(8,128)(2,1)S(1)}, bf16[128,768]{1,0:T(8,128)(2,1)S(1)}, u32[]{:S(2)}, u32[]{:S(2)}) collective-permute-start(bf16[128,768]{1,0:T(8,128)(2,1)S(1)} %pad_maximum_fusion.13), channel_id=1, source_target_pairs={{0,4},{2,6},{4,0},{6,2},{8,12},{10,14},{12,8},{14,10},{16,20},{18,... | collective-permute-start | bytes 589832 | tf_op jit(solution)/shard_map/ppermute | solution.py:803
  435.6 10.3 %collective-permute-start.58 = (bf16[256,768]{1,0:T(8,128)(2,1)S(1)}, bf16[256,768]{1,0:T(8,128)(2,1)S(1)}, u32[]{:S(2)}, u32[]{:S(2)}) collective-permute-start(bf16[256,768]{1,0:T(8,128)(2,1)S(1)} %pad_maximum_fusion.10), channel_id=1, source_target_pairs={{0,4},{2,6},{4,0},{6,2},{8,12},{10,14},{12,8},{14,10},{16,20},{18,... | collective-permute-start | bytes 1179656 | tf_op jit(solution)/shard_map/ppermute | solution.py:803
  436.5 10.0 %collective-permute-start.59 = (bf16[256,768]{1,0:T(8,128)(2,1)S(1)}, bf16[256,768]{1,0:T(8,128)(2,1)S(1)}, u32[]{:S(2)}, u32[]{:S(2)}) collective-permute-start(bf16[256,768]{1,0:T(8,128)(2,1)S(1)} %pad_maximum_fusion.11), channel_id=1, source_target_pairs={{0,8},{2,10},{4,12},{6,14},{8,0},{10,2},{12,4},{14,6},{16,24},{18,... | collective-permute-start | bytes 1179656 | tf_op jit(solution)/shard_map/ppermute | solution.py:803
  447.6 10.7 %collective-permute-start.60 = (bf16[512,768]{1,0:T(8,128)(2,1)S(1)}, bf16[512,768]{1,0:T(8,128)(2,1)S(1)}, u32[]{:S(2)}, u32[]{:S(2)}) collective-permute-start(bf16[512,768]{1,0:T(8,128)(2,1)S(1)} %pad_maximum_fusion.7.refs_0_), channel_id=1, source_target_pairs={{0,2},{2,0},{4,6},{6,4},{8,10},{10,8},{12,14},{14,12},{16,18},{18,... | collective-permute-start | bytes 2359304 | tf_op jit(solution)/shard_map/ppermute | solution.py:803
  447.7 10.7 %collective-permute-start.61 = (bf16[512,768]{1,0:T(8,128)(2,1)S(1)}, bf16[512,768]{1,0:T(8,128)(2,1)S(1)}, u32[]{:S(2)}, u32[]{:S(2)}) collective-permute-start(bf16[512,768]{1,0:T(8,128)(2,1)S(1)} %pad_maximum_fusion.8.refs_1_), channel_id=1, source_target_pairs={{0,2},{2,0},{4,6},{6,4},{8,10},{10,8},{12,14},{14,12},{16,18},{18,... | collective-permute-start | bytes 2359304 | tf_op jit(solution)/shard_map/ppermute | solution.py:803
  (36 other events, 267.0 us)

commit v5 on v4

--- a/solution.py
+++ b/solution.py
@@ -41,7 +41,7 @@
 
 
 def cost(micros):
-    return pl.CostEstimate(flops=int(micros * 0.5e9), bytes_accessed=1 << 20, transcendentals=0)
+    return pl.CostEstimate(flops=int(micros * 1.1e9), bytes_accessed=1 << 20, transcendentals=0)
 
 
 def whole(shape):
@@ -540,16 +540,20 @@
     )(sel, query, key, value, logs, *tables, seg_col, seg_row, low_grad, wo)
 
 
-def project_kernel(final, fresh, sel_ref, back_ref, att_ref, low_t_ref, first_t_ref, wq_ref, wk_ref, wv_ref, *rest):
+def project_kernel(
+    final, fresh, sel_ref, back_ref, att_ref, low_t_ref, first_t_ref, wq_ref, wk_ref, wv_ref, *rest
+):
     if not fresh:
         before_ref, *rest = rest
     if final:
         x_ref, gain_ref, grad_ref, group_ref, token_ref, norm_ref = rest
     else:
         group_ref, sum_ref = rest
-    back = back_ref[...]
-    group_ref[:, : 2 * GROUP] = nn(first_t_ref[...], back).astype(bf16)
+    step = pl.program_id(0)
+    block = first_t_ref.shape[0]
+    group_ref[:, : 2 * GROUP] = nn(first_t_ref[...], back_ref[...]).astype(bf16)
     group_ref[:, 2 * GROUP :] = nn(low_t_ref[...], att_ref[...]).astype(bf16)
+    back = back_ref[pl.ds(pl.multiple_of(step * block, block), block), :]
     first_grad = nt(back[:, :GROUP], wq_ref[...])
     first_grad = first_grad + nt(back[:, GROUP : GROUP + LANES], wk_ref[...])
     first_grad = first_grad + nt(back[:, GROUP + LANES :], wv_ref[...])
@@ -559,9 +563,16 @@
         inputs = x_ref[...].astype(f32)
         gain = gain_ref[...].astype(f32)
         scale = lax.rsqrt(jnp.mean(inputs * inputs, axis=-1, keepdims=True) + EPS)
-        norm_ref[...] = jnp.broadcast_to(
-            jnp.sum(first_grad * inputs * scale, axis=0, keepdims=True), norm_ref.shape
-        )
+        norm = jnp.broadcast_to(jnp.sum(first_grad * inputs * scale, axis=0, keepdims=True), norm_ref.shape)
+
+        @pl.when(step == 0)
+        def _():
+            norm_ref[...] = norm
+
+        @pl.when(step > 0)
+        def _():
+            norm_ref[...] += norm
+
         inner = jnp.mean(gain * first_grad * inputs, axis=-1, keepdims=True)
         grad = scale * gain * first_grad - inputs * (scale * scale * scale) * inner
         token_ref[...] = (grad + grad_ref[...]).astype(bf16)
@@ -571,30 +582,33 @@
 
 def project(sel, back, att, low_t, first_t, wq, wk, wv, before=None, final=None):
     width, rows = low_t.shape
+    steps = 4
+    block = rows // steps
+    assert rows == width
 
     def fixed(shape):
         return pl.BlockSpec(shape, lambda i, s: (0,) * len(shape))
 
     wide_w = pl.BlockSpec((width, GROUP), lambda i, s: (0, s[0]))
     thin_w = pl.BlockSpec((width, LANES), lambda i, s: (0, s[0]))
-    square = fixed((rows, width))
+    strip = pl.BlockSpec((block, width), lambda i, s: (i, 0))
     in_specs = [
         fixed((rows, 2 * GROUP)), pl.BlockSpec((rows, GROUP), lambda i, s: (0, s[0])),
-        fixed((width, rows)), fixed((width, rows)), wide_w, thin_w, thin_w,
+        strip, strip, wide_w, thin_w, thin_w,
     ]
-    out_specs = [fixed((width, 3 * GROUP))]
+    out_specs = [pl.BlockSpec((block, 3 * GROUP), lambda i, s: (i, 0))]
     out_shape = [jax.ShapeDtypeStruct((width, 3 * GROUP), bf16)]
     extra = ()
     if before is not None:
-        in_specs.append(square)
+        in_specs.append(strip)
         extra = (before,)
     if final is None:
-        out_specs.append(square)
+        out_specs.append(strip)
         out_shape.append(jax.ShapeDtypeStruct((rows, width), f32))
     else:
         extra = (*extra, *final)
-        in_specs += [pl.BlockSpec((rows, width), lambda i, s: (s[1], 0)), fixed((1, width)), square]
-        out_specs += [square, fixed((8, width))]
+        in_specs += [pl.BlockSpec((block, width), lambda i, s: (s[1] * steps + i, 0)), fixed((1, width)), strip]
+        out_specs += [strip, fixed((8, width))]
         out_shape += [
             jax.ShapeDtypeStruct((rows, width), bf16),
             jax.ShapeDtypeStruct((8, width), f32),
@@ -602,7 +616,7 @@
     return pl.pallas_call(
         partial(project_kernel, final is not None, before is None),
         grid_spec=pltpu.PrefetchScalarGridSpec(
-            num_scalar_prefetch=1, grid=(1,), in_specs=in_specs, out_specs=out_specs
+            num_scalar_prefetch=1, grid=(steps,), in_specs=in_specs, out_specs=out_specs
         ),
         out_shape=tuple(out_shape),
         compiler_params=params(),
@@ -875,12 +889,21 @@
     count = len(orders)
     parts = [t.reshape(count, t.shape[0] // count, t.shape[1]) for t in terms]
     colors = [[(p, 1, i) for p in parts] for i in range(count)]
-    for bits in [*zip(*orders), *[(b,) * count for b in far]]:
+    for bits in zip(*orders):
         split = add_split(colors, [bit_of(b) for b in bits])
         got = yield [(s, b) for (_, s), b in zip(split, bits)]
         colors = [[(k, 1, 0), (g, 1, 0)] for (k, _), g in zip(split, got)]
-    pieces = [total([k[0], g[0]]) for (k, _, _), (g, _, _) in colors]
-    return (yield from gather_back(pieces, [[*order, *far] for order in orders]))
+    for bit in far:
+        split = add_split(colors, [bit_of(bit)] * count)
+        (got,) = yield [(jnp.concatenate([s for _, s in split], 0), bit)]
+        colors = [[(k, 1, 0), (got, 1, i)] for i, (k, _) in enumerate(split)]
+    piece = jnp.concatenate(
+        [total([lax.slice_in_dim(t, i, i + n, axis=0) for t, n, i in terms]) for terms in colors], 0
+    )
+    for bit in reversed(far):
+        (got,) = yield [(piece, bit)]
+        piece = jnp.concatenate([piece, got], 1)
+    return (yield from gather_back([piece[i] for i in range(count)], orders))
 
 
 class Chains:
@@ -911,11 +934,6 @@
     def add(self, name, chain):
         self.live[name] = (chain, None)
 
-    def finish(self):
-        self.advance([n for n in self.live if self.live[n][1] is None], fence=())
-        while self.live:
-            self.advance(fence=())
-
 
 def per_device(
     tokens, cotangent, segments, routes, slot_index,
@@ -1024,25 +1042,36 @@
     chains.add("token", piece_swaps(token, 4))
     chains.add("tail", attention_sum((group_a, chains.done["mine"], chains.done["theirs"]), orders, far))
     chains.add("small", sum_all(jnp.concatenate([small, norm_one], 0)))
-    chains.finish()
-    done = chains.done
+
+    def both(mine, other):
+        return jnp.where(side == 0, jnp.concatenate([mine, other], 0), jnp.concatenate([other, mine], 0))
 
     place_far = place_of(far)
     size_far = 2 ** len(far)
-    own_grads, other_grads = done["grads"]
     places = [place_of(order) * size_far + place_far for order in orders]
-    grad_gate, grad_up, grad_down = unpack_experts(own_grads, other_grads, places, core, dp_size // 2)
+    done = chains.done
+    finishers = {
+        "out": lambda got: both(out, got),
+        "token": lambda got: both(token, got).astype(f32),
+        "grads": lambda got: unpack_experts(*got, places, core, dp_size // 2),
+    }
+    results = {}
+    chains.advance(["token", "tail", "small"], fence=())
+    while chains.live:
+        ready = {n: f(done[n]) for n, f in finishers.items() if n in done and n not in results}
+        results.update(chains.advance(fence=ready))
+    for name, finisher in finishers.items():
+        if name not in results:
+            results[name] = finisher(done[name])
+    grad_gate, grad_up, grad_down = results["grads"]
     own_tail, other_tail = done["tail"]
     grad_query, grad_key, grad_value, grad_output = unpack(own_tail, other_tail, places, core, dp_size // 2)
     small = done["small"]
     experts = w_router.shape[1]
 
-    def both(mine, other):
-        return jnp.where(side == 0, jnp.concatenate([mine, other], 0), jnp.concatenate([other, mine], 0))
-
     return (
-        both(out, done["out"]),
-        both(token, done["token"]).astype(f32),
+        results["out"],
+        results["token"],
         grad_query,
         grad_key,
         grad_value,

time: 475 us -> 455 us (0.958)
  waiting for transfers between devices: 95.8 us -> 87.9 us
  Pallas kernels: 248 us -> 243 us
    pallas_call x4, Pallas kernels: 42.9 us -> 37.5 us  [project(): pl.pallas_call(partial(project_kernel, final is not None, before is None)...]
    ppermute x46 -> x44, waiting for transfers between devices: 70 us -> 65 us  [swap_dp(): return lax.ppermute(values, 'dp', [(i, i ^ bit) for i in range(count)])]
    ppermute x46 -> x44, starting transfers between devices: 45.3 us -> 40.4 us  [swap_dp(): return lax.ppermute(values, 'dp', [(i, i ^ bit) for i in range(count)])]
  transfers between devices with their start and end apart: 62 -> 60, of which waited for: 20 -> 18; matrix products, arithmetic and copies ran while one was open for 6% -> 6% of each run, Pallas kernels for 35% -> 35%
where the time goes in v5:
time: 455 us; the launch traced here: 446 us
  Pallas kernels  243 us (53%)
  waiting for transfers between devices  87.9 us (19%)
  starting transfers between devices  62.3 us (14%)
  other arithmetic  29.6 us (7%)
  local copies, waits for them, and re-layouts  21.4 us (5%)
    ppermute x44, waiting for transfers between devices, swap_dp(): return lax.ppermute(values, 'dp', [(i, i ^ bit) for i in range(count)])  65 us
    pallas_call x4, Pallas kernels, attend_back(): pl.pallas_call(attend_back_kernel, grid_spec=pltpu.PrefetchScalarGridSpec...  53.6 us
    pallas_call x1, Pallas kernels, experts_layer(): pl.pallas_call(experts_kernel, grid_spec=pltpu.PrefetchScalarGridSpec(num...  45.6 us
    pallas_call x3, Pallas kernels, attend(): pl.pallas_call(attend_kernel, grid=(groups,), in_specs=[whole((rows, widt...  43.3 us
    ppermute x44, starting transfers between devices, swap_dp(): return lax.ppermute(values, 'dp', [(i, i ^ bit) for i in range(count)])  40.4 us
    pallas_call x4, Pallas kernels, project(): pl.pallas_call(partial(project_kernel, final is not None, before is None)...  37.5 us
    pallas_call x6, Pallas kernels, add_split(): pl.pallas_call(kernel, grid_spec=pltpu.PrefetchScalarGridSpec(num_scalar_...  30.8 us
    ppermute x16, waiting for transfers between devices, swap_tensor(): return lax.ppermute(values, 'tensor', [(0, 1), (1, 0)])  22.9 us
  transfers between devices with their start and end apart: 60, of which 18 were waited for; matrix products, arithmetic and copies ran while one was open for 6% of the time, Pallas kernels for 35%

profile of v5, /device:TPU:0, one launch (start us, length us, event | category | flops | bytes accessed | tf_op | source)
XLA Modules:
  0.0 446.0 jit_solution(5838333136584342312)
XLA Ops:
  1.7 3.0 collective-permute-start.1
  6.8 2.1 collective-permute-start.2
  10.8 5.3 %prologue.1 = (bf16[1024,1024]{1,0:T(8,128)(2,1)}, bf16[1024,1024]{1,0:T(8,128)(2,1)}, f32[1024,128]{1,0:T(8,128)}, f32[1024,128]{1,0:T(8,128)}, f32[1024,128]{1,0:T(8,128)}) custom-call(s32[1]{0:T(128)} %bitcast.1.side_ref, bf16[2048,1024]{1,0:T(8,128)(2,1)} %rest_1_.1, bf16[1,1024]{1,0:T(2,128)(2,1)} %broadcast_in_dim.24.gain_ref.rest_2_, ...), custom_call_target="tpu_custom_call" | custom-call | flops 5500000256 | bytes 1048576 | tf_op jit(solution)/shard_map/prologue/pallas_call | solution.py:96
  18.3 20.2 %attend.3 = (bf16[1024,512]{1,0:T(8,128)(2,1)}, bf16[1024,256]{1,0:T(8,128)(2,1)}, bf16[1024,256]{1,0:T(8,128)(2,1)}, bf16[1024,512]{1,0:T(8,128)(2,1)}, f32[2,8,1024]{2,1,0:T(8,128)}) custom-call(bf16[1024,1024]{1,0:T(8,128)(2,1)} %get-tuple-element.250.first_ref, bf16[1024,512]{1,0:T(8,128)(2,1)} %wq_ref.5, bf16[1024,256]{1,0:T(8,128)(2,1)} %wk_ref.5, ...), custom_call_target="tpu_custom_call" | custom-call | flops 22000001024 | bytes 1048576 | tf_op jit(solution)/shard_map/attend/pallas_call | solution.py:195
  39.7 2.0 collective-permute-start.5
  44.3 2.0 collective-permute-start.6
  46.3 8.3 %collective-permute-done.5 = bf16[1,1024,256]{2,1,0:T(8,128)(2,1)S(1)} collective-permute-done((bf16[1,1024,256]{2,1,0:T(8,128)(2,1)S(1)}, bf16[1,1024,256]{2,1,0:T(8,128)(2,1)S(1)}, u32[]{:S(2)}, u32[]{:S(2)}) %collective-permute-start.5) | collective-permute-done | bytes 524320 | tf_op jit(solution)/shard_map/ppermute | solution.py:812
  54.6 11.4 %attend.4 = (bf16[1024,256]{1,0:T(8,128)(2,1)}, bf16[1024,128]{1,0:T(8,128)(2,1)}, bf16[1024,128]{1,0:T(8,128)(2,1)}, bf16[1024,256]{1,0:T(8,128)(2,1)}, f32[1,8,1024]{2,1,0:T(8,128)}) custom-call(bf16[1024,1024]{1,0:T(8,128)(2,1)} %get-tuple-element.250.first_ref, bf16[1024,256]{1,0:T(8,128)(2,1)} %copy-done.36, bf16[1024,128]{1,0:T(8,128)(2,1)} %copy-done.39, ...), custom_call_target="tpu_custom_call" | custom-call | flops 11000000512 | bytes 1048576 | tf_op jit(solution)/shard_map/attend/pallas_call | solution.py:195
  66.6 2.0 collective-permute-start.7
  70.3 11.7 %attend.5 = (bf16[1024,256]{1,0:T(8,128)(2,1)}, bf16[1024,128]{1,0:T(8,128)(2,1)}, bf16[1024,128]{1,0:T(8,128)(2,1)}, bf16[1024,256]{1,0:T(8,128)(2,1)}, f32[1,8,1024]{2,1,0:T(8,128)}) custom-call(bf16[1024,1024]{1,0:T(8,128)(2,1)} %get-tuple-element.250.first_ref, bf16[1024,256]{1,0:T(8,128)(2,1)} %collective-permute-done.9.wq_ref, ...), custom_call_target="tpu_custom_call" | custom-call | flops 11000000512 | bytes 1048576 | tf_op jit(solution)/shard_map/attend/pallas_call | solution.py:195
  83.5 8.7 %router.1 = (f32[1024,1024]{1,0:T(8,128)}, bf16[1024,1024]{1,0:T(8,128)(2,1)}, f32[32,1024]{1,0:T(8,128)}, s32[8,1024]{1,0:T(8,128)}) custom-call(s32[1]{0:T(128)} %bitcast.1.side_ref, bf16[2048,1024]{1,0:T(8,128)(2,1)} %rest_1_.1, bf16[1024,512]{1,0:T(8,128)(2,1)} %get-tuple-element.257.att_a_ref.att_ref, ...), custom_call_target="tpu_custom_call" | custom-call | flops 8800000000 | bytes 1048576 | tf_op jit(solution)/shard_map/router/pallas_call | solution.py:270
  92.2 5.1 %collective-permute-done.12 = bf16[1,256,1024]{2,1,0:T(8,128)(2,1)S(1)} collective-permute-done((bf16[1,256,1024]{2,1,0:T(8,128)(2,1)S(1)}, bf16[1,256,1024]{2,1,0:T(8,128)(2,1)S(1)}, u32[]{:S(2)}, u32[]{:S(2)}) %collective-permute-start.12) | collective-permute-done | bytes 524320 | tf_op jit(solution)/shard_map/ppermute | solution.py:817
  98.4 2.6 pad_maximum_fusion.wg_b_ref
  101.0 2.8 pad_maximum_fusion.1.wu_b_ref
  103.8 1.6 pad_maximum_fusion.2.wd_b_ref
  105.4 45.6 %experts.1 = (bf16[1024,1024]{1,0:T(8,128)(2,1)}, bf16[1024,1024]{1,0:T(8,128)(2,1)}, bf16[1024,1024]{1,0:T(8,128)(2,1)}, f32[1024,1024]{1,0:T(8,128)}, f32[40,1...) custom-call(s32[2]{0:T(128)} %pad_add_fusion.order_ref, ...), custom_call_target="tpu_custom_call" | custom-call | flops 42900000768 | bytes 1048576 | tf_op jit(solution)/shard_map/experts/pallas_call | solution.py:401
  151.0 1.7 fusion.4
  155.0 13.4 %attend_back.4.back_ref = bf16[1024,512]{1,0:T(8,128)(2,1)} custom-call(s32[1]{0:T(128)} %constant.138.clone.1.sel_ref, bf16[1024,256]{1,0:T(8,128)(2,1)} %get-tuple-element.272.q_ref, bf16[1024,128]{1,0:T(8,128)(2,1)} %get-tuple-element.273.k_ref, bf16[1024,128]{1,0:T(8,128)(2,1)} %get-tuple-element.274.v_ref, f32[1,8,1024]{2,1,0:T(8,128)} %get-tuple-element.275.lse_ref, ...), custom_call_target="tpu_custom_call" | custom-call | flops 15399999488 | bytes 1048576 | tf_op jit(solution)/shard_map/attend_back/pallas_call | solution.py:518
  168.4 8.4 %add_split.6 = (bf16[2,384,1024]{2,1,0:T(8,128)(2,1)}, bf16[2,384,1024]{2,1,0:T(8,128)(2,1)}, bf16[2,384,1024]{2,1,0:T(8,128)(2,1)}, bf16[2,384,1024]{2,1,0:T(8,128)(2,1)}) custom-call(s32[2]{0:T(128)} %get-tuple-element.454.side_ref, bf16[4,768,1024]{2,1,0:T(8,128)(2,1)} %bitcast.32, ...), custom_call_target="tpu_custom_call" | custom-call | flops 4400000000 | bytes 1048576 | tf_op jit(solution)/shard_map/add_split/pallas_call | solution.py:681
  176.8 8.3 %project.3 = (bf16[1024,768]{1,0:T(8,128)(2,1)}, f32[1024,1024]{1,0:T(8,128)}) custom-call(s32[1]{0:T(128)} %constant.138.clone.1.sel_ref, bf16[1024,512]{1,0:T(8,128)(2,1)} %attend_back.4.back_ref, bf16[1024,256]{1,0:T(8,128)(2,1)} %get-tuple-element.259.att_c_ref.att_ref, bf16[1024,1024]{1,0:T(8,128)(2,1)} %get-tuple-element.283.low_t_ref, ...), custom_call_target="tpu_custom_call" | custom-call | flops 7699999744 | bytes 1048576 | tf_op jit(solution)/shard_map/project/pallas_call | solution.py:616
  187.1 1.8 collective-permute-start.24
  188.9 13.4 %attend_back.5.back_ref = bf16[1024,512]{1,0:T(8,128)(2,1)} custom-call(s32[1]{0:T(128)} %constant.138.clone.1.sel_ref, bf16[1024,256]{1,0:T(8,128)(2,1)} %get-tuple-element.292.q_ref, bf16[1024,128]{1,0:T(8,128)(2,1)} %get-tuple-element.293.k_ref, bf16[1024,128]{1,0:T(8,128)(2,1)} %get-tuple-element.294.v_ref, f32[1,8,1024]{2,1,0:T(8,128)} %get-tuple-element.295.lse_ref, ...), custom_call_target="tpu_custom_call" | custom-call | flops 15399999488 | bytes 1048576 | tf_op jit(solution)/shard_map/attend_back/pallas_call | solution.py:518
  202.3 8.9 %project.4 = (bf16[1024,768]{1,0:T(8,128)(2,1)}, f32[1024,1024]{1,0:T(8,128)}) custom-call(s32[1]{0:T(128)} %constant.138.clone.1.sel_ref, bf16[1024,512]{1,0:T(8,128)(2,1)} %attend_back.5.back_ref, bf16[1024,256]{1,0:T(8,128)(2,1)} %get-tuple-element.258.att_b_ref.att_ref, bf16[1024,1024]{1,0:T(8,128)(2,1)} %get-tuple-element.283.low_t_ref, ...), custom_call_target="tpu_custom_call" | custom-call | flops 7699999744 | bytes 1048576 | tf_op jit(solution)/shard_map/project/pallas_call | solution.py:616
  211.7 11.8 %collective-permute-done.23.refs_1_.refs_3_ = bf16[2,384,1024]{2,1,0:T(8,128)(2,1)} collective-permute-done((bf16[2,384,1024]{2,1,0:T(8,128)(2,1)}, bf16[2,384,1024]{2,1,0:T(8,128)(2,1)}, u32[]{:S(2)}, u32[]{:S(2)}) %collective-permute-start.23) | collective-permute-done | bytes 1572896 | tf_op jit(solution)/shard_map/ppermute | solution.py:817
  223.6 2.9 add_convert_fusion
  226.5 6.1 %add_split.7 = (bf16[2,192,1024]{2,1,0:T(8,128)(2,1)}, bf16[2,192,1024]{2,1,0:T(8,128)(2,1)}, bf16[2,192,1024]{2,1,0:T(8,128)(2,1)}, bf16[2,192,1024]{2,1,0:T(8,128)(2,1)}) custom-call(s32[2]{0:T(128)} %get-tuple-element.455.side_ref, bf16[2,384,1024]{2,1,0:T(8,128)(2,1)} %get-tuple-element.310.refs_0_.refs_2_, ...), custom_call_target="tpu_custom_call" | custom-call | flops 4400000000 | bytes 1048576 | tf_op jit(solution)/shard_map/add_split/pallas_call | solution.py:681
  232.6 1.8 collective-permute-start.26
  234.4 1.5 collective-permute-start.27
  235.9 1.5 collective-permute-start.30
  237.4 13.4 %attend_back.6.back_ref = bf16[1024,512]{1,0:T(8,128)(2,1)} custom-call(s32[1]{0:T(128)S(6)} %sub.27.sel_ref, bf16[1024,512]{1,0:T(8,128)(2,1)} %get-tuple-element.304.q_ref, bf16[1024,256]{1,0:T(8,128)(2,1)} %get-tuple-element.305.k_ref, bf16[1024,256]{1,0:T(8,128)(2,1)} %get-tuple-element.306.v_ref, f32[2,8,1024]{2,1,0:T(8,128)} %get-tuple-element.307.lse_ref, ...), custom_call_target="tpu_custom_call" | custom-call | flops 15399999488 | bytes 1048576 | tf_op jit(solution)/shard_map/attend_back/pallas_call | solution.py:518
  253.7 3.3 add_halves.1
  257.0 9.2 %project.5 = (bf16[1024,768]{1,0:T(8,128)(2,1)}, f32[1024,1024]{1,0:T(8,128)}) custom-call(s32[1]{0:T(128)S(6)} %sub.27.sel_ref, bf16[1024,512]{1,0:T(8,128)(2,1)} %attend_back.6.back_ref, bf16[1024,512]{1,0:T(8,128)(2,1)} %get-tuple-element.257.att_a_ref.att_ref, bf16[1024,1024]{1,0:T(8,128)(2,1)} %get-tuple-element.283.low_t_ref, ...), custom_call_target="tpu_custom_call" | custom-call | flops 7699999744 | bytes 1048576 | tf_op jit(solution)/shard_map/project/pallas_call | solution.py:616
  266.8 1.6 collective-permute-start.28
  268.4 13.4 %attend_back.7.back_ref = bf16[1024,512]{1,0:T(8,128)(2,1)} custom-call(s32[1]{0:T(128)} %bitcast.11.sel_ref, bf16[1024,512]{1,0:T(8,128)(2,1)} %get-tuple-element.304.q_ref, bf16[1024,256]{1,0:T(8,128)(2,1)} %get-tuple-element.305.k_ref, bf16[1024,256]{1,0:T(8,128)(2,1)} %get-tuple-element.306.v_ref, f32[2,8,1024]{2,1,0:T(8,128)} %get-tuple-element.307.lse_ref, ...), custom_call_target="tpu_custom_call" | custom-call | flops 15399999488 | bytes 1048576 | tf_op jit(solution)/shard_map/attend_back/pallas_call | solution.py:518
  281.8 5.9 %collective-permute-done.28.refs_1_.refs_3_ = bf16[2,192,1024]{2,1,0:T(8,128)(2,1)} collective-permute-done((bf16[2,192,1024]{2,1,0:T(8,128)(2,1)}, bf16[2,192,1024]{2,1,0:T(8,128)(2,1)}, u32[]{:S(2)}, u32[]{:S(2)}) %collective-permute-start.28) | collective-permute-done | bytes 786464 | tf_op jit(solution)/shard_map/ppermute | solution.py:812
  287.8 2.9 add_split.8
  290.7 11.1 %project_final.1 = (bf16[1024,768]{1,0:T(8,128)(2,1)}, bf16[1024,1024]{1,0:T(8,128)(2,1)}, f32[8,1024]{1,0:T(8,128)}) custom-call(s32[2]{0:T(128)} %pad_add_fusion.3.sel_ref, bf16[1024,512]{1,0:T(8,128)(2,1)} %attend_back.7.back_ref, bf16[1024,512]{1,0:T(8,128)(2,1)} %get-tuple-element.257.att_a_ref.att_ref, ...), custom_call_target="tpu_custom_call" | custom-call | flops 7699999744 | bytes 1048576 | tf_op jit(solution)/shard_map/project_final/pallas_call | solution.py:616
  301.8 2.9 fusion.3
  304.7 5.4 %add_split.9 = (bf16[1,256,768]{2,1,0:T(8,128)(2,1)}, bf16[1,256,768]{2,1,0:T(8,128)(2,1)}, bf16[1,256,768]{2,1,0:T(8,128)(2,1)}, bf16[1,256,768]{2,1,0:T(8,128)(2,1)}) custom-call(s32[2]{0:T(128)} %get-tuple-element.454.side_ref, bf16[2,512,768]{2,1,0:T(8,128)(2,1)} %bitcast.44, bf16[2,512,768]{2,1,0:T(8,128)(2,1)} %bitcast.40, ...), custom_call_target="tpu_custom_call" | custom-call | flops 4400000000 | bytes 1048576 | tf_op jit(solution)/shard_map/add_split/pallas_call | solution.py:681
  310.1 1.6 collective-permute-start.35
  313.6 2.6 collective-permute-start.31
  316.1 4.6 %maximum_select_fusion = bf16[2048,1024]{1,0:T(8,128)(2,1)} fusion(bf16[512,1024]{1,0:T(8,128)(2,1)} %copy-done.10, bf16[512,1024]{1,0:T(8,128)(2,1)S(1)} %copy-done.9, bf16[1024,1024]{1,0:T(8,128)(2,1)S(1)} %copy-done.3, pred[]{:T(512)S(6)} %eq.22), kind=kLoop, calls=%fused_computation | loop fusion | flops 27262976 | bytes 8388609 | tf_op jit(solution)/shard_map/jit(_where)/select_n | solution.py:1047
  320.8 7.2 %collective-permute-done.32 = f32[48,1024]{1,0:T(8,128)S(1)} collective-permute-done((f32[48,1024]{1,0:T(8,128)S(1)}, f32[48,1024]{1,0:T(8,128)S(1)}, u32[]{:S(2)}, u32[]{:S(2)}) %collective-permute-start.32) | collective-permute-done | bytes 196640 | tf_op jit(solution)/shard_map/ppermute | solution.py:812
  328.0 3.3 collective-permute-done.34.refs_5_.refs_7_
  332.1 4.1 add_split.10
  336.2 2.5 collective-permute-start.40
  338.7 4.1 collective-permute-start.38
  344.4 6.2 %collective-permute-done.38.refs_1_.refs_3_ = bf16[1,128,768]{2,1,0:T(8,128)(2,1)S(1)} collective-permute-done((bf16[1,128,768]{2,1,0:T(8,128)(2,1)}, bf16[1,128,768]{2,1,0:T(8,128)(2,1)S(1)}, u32[]{:S(2)}, u32[]{:S(2)}) %collective-permute-start.38) | collective-permute-done | bytes 196640 | tf_op jit(solution)/shard_map/ppermute | solution.py:817
  350.6 4.6 %collective-permute-done.36 = bf16[2,96,1024]{2,1,0:T(8,128)(2,1)S(1)} collective-permute-done((bf16[2,96,1024]{2,1,0:T(8,128)(2,1)S(1)}, bf16[2,96,1024]{2,1,0:T(8,128)(2,1)S(1)}, u32[]{:S(2)}, u32[]{:S(2)}) %collective-permute-start.36) | collective-permute-done | bytes 393248 | tf_op jit(solution)/shard_map/ppermute | solution.py:817
  355.4 3.9 add_split.11
  360.3 1.7 collective-permute-start.45
  364.0 2.8 collective-permute-start.44
  366.9 8.9 %collective-permute-done.43 = f32[48,1024]{1,0:T(8,128)S(1)} collective-permute-done((f32[48,1024]{1,0:T(8,128)S(1)}, f32[48,1024]{1,0:T(8,128)S(1)}, u32[]{:S(2)}, u32[]{:S(2)}) %collective-permute-start.43) | collective-permute-done | bytes 196640 | tf_op jit(solution)/shard_map/ppermute | solution.py:817
  380.4 1.7 collective-permute-start.47
  382.1 1.6 collective-permute-start.50
  384.5 3.5 collective-permute-start.49
  388.0 18.7 %collective-permute-done.48 = f32[48,1024]{1,0:T(8,128)S(1)} collective-permute-done((f32[48,1024]{1,0:T(8,128)}, f32[48,1024]{1,0:T(8,128)S(1)}, u32[]{:S(2)}, u32[]{:S(2)}) %collective-permute-start.48) | collective-permute-done | bytes 196640 | tf_op jit(solution)/shard_map/ppermute | solution.py:817
  408.3 1.9 pad_maximum_fusion.3.refs_0_
  410.8 2.6 collective-permute-start.53
  415.9 4.0 select_convert_fusion
  419.8 2.9 collective-permute-done.53
  424.5 1.8 collective-permute-start.57
  426.2 8.9 %unpack_experts.1 = (f32[4,1024,256]{2,1,0:T(8,128)}, f32[4,1024,256]{2,1,0:T(8,128)}, f32[4,256,1024]{2,1,0:T(8,128)}) custom-call(s32[3]{0:T(128)} %pad_add_fusion.5.place_ref, bf16[768,1024]{1,0:T(8,128)(2,1)} %copy-done.5, bf16[768,1024]{1,0:T(8,128)(2,1)} %copy-done.4, bf16[768,1024]{1,0:T(8,128)(2,1)} %copy-done.30, bf16[768,1024]{1,0:T(8,128)(2,1)} %copy-done.31), custom_call_target="tpu_custom_call" | custom-call | flops 11000000512 | bytes 1048576 | tf_op jit(solution)/shard_map/unpack_experts/pallas_call | solution.py:746
  439.7 5.9 %unpack.1 = (f32[1024,512]{1,0:T(8,128)}, f32[1024,256]{1,0:T(8,128)}, f32[1024,256]{1,0:T(8,128)}, f32[512,1024]{1,0:T(8,128)}) custom-call(s32[3]{0:T(128)} %pad_add_fusion.5.place_ref, bf16[512,768]{1,0:T(8,128)(2,1)} %copy-done.12, bf16[512,768]{1,0:T(8,128)(2,1)} %copy-done.11, bf16[512,768]{1,0:T(8,128)(2,1)} %copy-done.32, bf16[512,768]{1,0:T(8,128)(2,1)} %copy-done.34), custom_call_target="tpu_custom_call" | custom-call | flops 6600000000 | bytes 1048576 | tf_op jit(solution)/shard_map/unpack/pallas_call | solution.py:795
  (225 shorter events, 47.4 us)
Async XLA Ops:
  1.7 16.5 %collective-permute-start.1 = (bf16[1024,128]{1,0:T(8,128)(2,1)S(1)}, bf16[1024,128]{1,0:T(8,128)(2,1)S(1)}, u32[]{:S(2)}, u32[]{:S(2)}) collective-permute-start(bf16[1024,128]{1,0:T(8,128)(2,1)S(1)} %constant_dynamic-slice_fusion.4), channel_id=1, source_target_pairs={{0,1},{1,0},{2,3},{3,2},{4,5},{5,4},{6,7},{7,6},{8,9},{9,8},{10,11... | collective-permute-start | bytes 786440 | tf_op jit(solution)/shard_map/ppermute | solution.py:812
  5.7 33.9 %collective-permute-start = (bf16[1024,256]{1,0:T(8,128)(2,1)S(1)}, bf16[1024,256]{1,0:T(8,128)(2,1)S(1)}, u32[]{:S(2)}, u32[]{:S(2)}) collective-permute-start(bf16[1024,256]{1,0:T(8,128)(2,1)S(1)} %constant_dynamic-slice_fusion.5), channel_id=1, source_target_pairs={{0,1},{1,0},{2,3},{3,2},{4,5},{5,4},{6,7},{7,6},{8,9},{9,8},{10,11... | collective-permute-start | bytes 1572872 | tf_op jit(solution)/shard_map/ppermute | solution.py:812
  6.8 32.8 %collective-permute-start.2 = (bf16[1024,128]{1,0:T(8,128)(2,1)S(1)}, bf16[1024,128]{1,0:T(8,128)(2,1)}, u32[]{:S(2)}, u32[]{:S(2)}) collective-permute-start(bf16[1024,128]{1,0:T(8,128)(2,1)S(1)} %constant_dynamic-slice_fusion.3), channel_id=1, source_target_pairs={{0,1},{1,0},{2,3},{3,2},{4,5},{5,4},{6,7},{7,6},{8,9},{9,8},{10,11... | collective-permute-start | bytes 786440 | tf_op jit(solution)/shard_map/ppermute | solution.py:812
  18.2 21.5 %collective-permute-start.3 = (bf16[1,1024,256]{2,1,0:T(8,128)(2,1)S(1)}, bf16[1,1024,256]{2,1,0:T(8,128)(2,1)S(1)}, u32[]{:S(2)}, u32[]{:S(2)}) collective-permute-start(bf16[1,1024,256]{2,1,0:T(8,128)(2,1)S(1)} %constant_dynamic-slice_fusion.2), channel_id=1, source_target_pairs={{0,1},{1,0},{2,3},{3,2},{4,5},{5,4},{6,7},{7,6},{8,9},{9,8},{10,11... | collective-permute-start | bytes 1572872 | tf_op jit(solution)/shard_map/ppermute | solution.py:812
  18.3 23.5 %copy-start.28 = (bf16[1024]{0:T(1024)(128)(2,1)S(1)}, bf16[1024]{0:T(1024)(128)(2,1)}, u32[]{:S(2)}) copy-start(bf16[1024]{0:T(1024)(128)(2,1)} %param.25) | copy-start | bytes 6148
  18.3 24.1 %copy-start.25 = (s32[2048,8]{0,1:T(8,128)S(1)}, s32[2048,8]{0,1:T(8,128)}, u32[]{:S(2)}) copy-start(s32[2048,8]{0,1:T(8,128)} %param.19) | copy-start | bytes 196612
  18.3 24.1 %copy-start.26 = (s32[2048,8]{0,1:T(8,128)S(1)}, s32[2048,8]{0,1:T(8,128)}, u32[]{:S(2)}) copy-start(s32[2048,8]{0,1:T(8,128)} %param.18) | copy-start | bytes 196612
  18.3 24.7 %copy-start.19 = (bf16[512,1024]{1,0:T(8,128)(2,1)S(1)}, bf16[512,1024]{1,0:T(8,128)(2,1)}, u32[]{:S(2)}) copy-start(bf16[512,1024]{1,0:T(8,128)(2,1)} %wo_ref.3) | copy-start | bytes 3145732
  39.7 14.9 %collective-permute-start.5 = (bf16[1,1024,256]{2,1,0:T(8,128)(2,1)S(1)}, bf16[1,1024,256]{2,1,0:T(8,128)(2,1)S(1)}, u32[]{:S(2)}, u32[]{:S(2)}) collective-permute-start(bf16[1,1024,256]{2,1,0:T(8,128)(2,1)S(1)} %constant_dynamic-slice_fusion.1), channel_id=1, source_target_pairs={{0,1},{1,0},{2,3},{3,2},{4,5},{5,4},{6,7},{7,6},{8,9},{9,8},{10,11... | collective-permute-start | bytes 1572872 | tf_op jit(solution)/shard_map/ppermute | solution.py:812
  44.1 24.7 %collective-permute-start.9 = (bf16[1024,256]{1,0:T(8,128)(2,1)S(1)}, bf16[1024,256]{1,0:T(8,128)(2,1)}, u32[]{:S(2)}, u32[]{:S(2)}) collective-permute-start(bf16[1024,256]{1,0:T(8,128)(2,1)S(1)} %collective-permute-done.wq_ref), channel_id=1, source_target_pairs={{0,2},{2,0},{4,6},{6,4},{8,10},{10,8},{12,14},{14,12},{16,18},{18,... | collective-permute-start | bytes 1572872 | tf_op jit(solution)/shard_map/ppermute | solution.py:817
  44.2 21.8 %collective-permute-start.4 = (bf16[256,1024]{1,0:T(8,128)(2,1)S(1)}, bf16[256,1024]{1,0:T(8,128)(2,1)}, u32[]{:S(2)}, u32[]{:S(2)}) collective-permute-start(bf16[256,1024]{1,0:T(8,128)(2,1)S(1)} %constant_dynamic-slice_fusion.6), channel_id=1, source_target_pairs={{0,1},{1,0},{2,3},{3,2},{4,5},{5,4},{6,7},{7,6},{8,9},{9,8},{10,11... | collective-permute-start | bytes 1572872 | tf_op jit(solution)/shard_map/ppermute | solution.py:812
  44.3 22.2 %collective-permute-start.6 = (bf16[1,1024,256]{2,1,0:T(8,128)(2,1)S(1)}, bf16[1,1024,256]{2,1,0:T(8,128)(2,1)S(1)}, u32[]{:S(2)}, u32[]{:S(2)}) collective-permute-start(bf16[1,1024,256]{2,1,0:T(8,128)(2,1)S(1)} %collective-permute-done.3), channel_id=1, source_target_pairs={{0,4},{2,6},{4,0},{6,2},{8,12},{10,14},{12,8},{14,10},{16,20},{18,... | collective-permute-start | bytes 1572872 | tf_op jit(solution)/shard_map/ppermute | solution.py:817
  46.3 20.3 %collective-permute-start.10 = (bf16[1024,128]{1,0:T(8,128)(2,1)S(1)}, bf16[1024,128]{1,0:T(8,128)(2,1)}, u32[]{:S(2)}, u32[]{:S(2)}) collective-permute-start(bf16[1024,128]{1,0:T(8,128)(2,1)S(1)} %copy-done.40), channel_id=1, source_target_pairs={{0,2},{2,0},{4,6},{6,4},{8,10},{10,8},{12,14},{14,12},{16,18},{18,... | collective-permute-start | bytes 786440 | tf_op jit(solution)/shard_map/ppermute | solution.py:817
  54.6 14.0 %collective-permute-start.11 = (bf16[1024,128]{1,0:T(8,128)(2,1)}, bf16[1024,128]{1,0:T(8,128)(2,1)}, u32[]{:S(2)}, u32[]{:S(2)}) collective-permute-start(bf16[1024,128]{1,0:T(8,128)(2,1)} %collective-permute-done.2.wv_ref), channel_id=1, source_target_pairs={{0,2},{2,0},{4,6},{6,4},{8,10},{10,8},{12,14},{14,12},{16,18},{18,... | collective-permute-start | bytes 786440 | tf_op jit(solution)/shard_map/ppermute | solution.py:817
  66.0 31.3 %collective-permute-start.14 = (bf16[1,1024,256]{2,1,0:T(8,128)(2,1)S(1)}, bf16[1,1024,256]{2,1,0:T(8,128)(2,1)S(1)}, u32[]{:S(2)}, u32[]{:S(2)}) collective-permute-start(bf16[1,1024,256]{2,1,0:T(8,128)(2,1)S(1)} %collective-permute-done.3), channel_id=1, source_target_pairs={{0,2},{2,0},{4,6},{6,4},{8,10},{10,8},{12,14},{14,12},{16,18},{18,... | collective-permute-start | bytes 1572872 | tf_op jit(solution)/shard_map/ppermute | solution.py:817
  66.5 16.7 %collective-permute-start.13 = (bf16[256,1024]{1,0:T(8,128)(2,1)}, bf16[256,1024]{1,0:T(8,128)(2,1)}, u32[]{:S(2)}, u32[]{:S(2)}) collective-permute-start(bf16[256,1024]{1,0:T(8,128)(2,1)} %collective-permute-done.4.wo_b_ref.wo_ref), channel_id=1, source_target_pairs={{0,2},{2,0},{4,6},{6,4},{8,10},{10,8},{12,14},{14,12},{16,18},{18,... | collective-permute-start | bytes 1572872 | tf_op jit(solution)/shard_map/ppermute | solution.py:817
  66.6 16.4 %collective-permute-start.7 = (bf16[1,1024,256]{2,1,0:T(8,128)(2,1)S(1)}, bf16[1,1024,256]{2,1,0:T(8,128)(2,1)S(1)}, u32[]{:S(2)}, u32[]{:S(2)}) collective-permute-start(bf16[1,1024,256]{2,1,0:T(8,128)(2,1)S(1)} %collective-permute-done.5), channel_id=1, source_target_pairs={{0,4},{2,6},{4,0},{6,2},{8,12},{10,14},{12,8},{14,10},{16,20},{18,... | collective-permute-start | bytes 1572872 | tf_op jit(solution)/shard_map/ppermute | solution.py:817
  68.6 32.4 %collective-permute-start.16 = (bf16[1,1024,256]{2,1,0:T(8,128)(2,1)S(1)}, bf16[1,1024,256]{2,1,0:T(8,128)(2,1)}, u32[]{:S(2)}, u32[]{:S(2)}) collective-permute-start(bf16[1,1024,256]{2,1,0:T(8,128)(2,1)S(1)} %collective-permute-done.5), channel_id=1, source_target_pairs={{0,2},{2,0},{4,6},{6,4},{8,10},{10,8},{12,14},{14,12},{16,18},{18,... | collective-permute-start | bytes 1572872 | tf_op jit(solution)/shard_map/ppermute | solution.py:817
  68.8 14.2 %collective-permute-start.8 = (bf16[1,256,1024]{2,1,0:T(8,128)(2,1)S(1)}, bf16[1,256,1024]{2,1,0:T(8,128)(2,1)S(1)}, u32[]{:S(2)}, u32[]{:S(2)}) collective-permute-start(bf16[1,256,1024]{2,1,0:T(8,128)(2,1)S(1)} %constant_dynamic-slice_fusion), channel_id=1, source_target_pairs={{0,1},{1,0},{2,3},{3,2},{4,5},{5,4},{6,7},{7,6},{8,9},{9,8},{10,11... | collective-permute-start | bytes 1572872 | tf_op jit(solution)/shard_map/ppermute | solution.py:812
  82.9 15.5 %collective-permute-start.15 = (bf16[1,1024,256]{2,1,0:T(8,128)(2,1)S(1)}, bf16[1,1024,256]{2,1,0:T(8,128)(2,1)}, u32[]{:S(2)}, u32[]{:S(2)}) collective-permute-start(bf16[1,1024,256]{2,1,0:T(8,128)(2,1)S(1)} %collective-permute-done.6), channel_id=1, source_target_pairs={{0,2},{2,0},{4,6},{6,4},{8,10},{10,8},{12,14},{14,12},{16,18},{18,... | collective-permute-start | bytes 1572872 | tf_op jit(solution)/shard_map/ppermute | solution.py:817
  82.9 14.3 %collective-permute-start.12 = (bf16[1,256,1024]{2,1,0:T(8,128)(2,1)S(1)}, bf16[1,256,1024]{2,1,0:T(8,128)(2,1)S(1)}, u32[]{:S(2)}, u32[]{:S(2)}) collective-permute-start(bf16[1,256,1024]{2,1,0:T(8,128)(2,1)S(1)} %collective-permute-done.8), channel_id=1, source_target_pairs={{0,4},{2,6},{4,0},{6,2},{8,12},{10,14},{12,8},{14,10},{16,20},{18,... | collective-permute-start | bytes 1572872 | tf_op jit(solution)/shard_map/ppermute | solution.py:817
  83.2 17.8 %collective-permute-start.17 = (bf16[1,1024,256]{2,1,0:T(8,128)(2,1)S(1)}, bf16[1,1024,256]{2,1,0:T(8,128)(2,1)}, u32[]{:S(2)}, u32[]{:S(2)}) collective-permute-start(bf16[1,1024,256]{2,1,0:T(8,128)(2,1)S(1)} %collective-permute-done.7), channel_id=1, source_target_pairs={{0,2},{2,0},{4,6},{6,4},{8,10},{10,8},{12,14},{14,12},{16,18},{18,... | collective-permute-start | bytes 1572872 | tf_op jit(solution)/shard_map/ppermute | solution.py:817
  97.3 6.5 %collective-permute-start.18 = (bf16[1,256,1024]{2,1,0:T(8,128)(2,1)S(1)}, bf16[1,256,1024]{2,1,0:T(8,128)(2,1)S(1)}, u32[]{:S(2)}, u32[]{:S(2)}) collective-permute-start(bf16[1,256,1024]{2,1,0:T(8,128)(2,1)S(1)} %collective-permute-done.8), channel_id=1, source_target_pairs={{0,2},{2,0},{4,6},{6,4},{8,10},{10,8},{12,14},{14,12},{16,18},{18,... | collective-permute-start | bytes 1572872 | tf_op jit(solution)/shard_map/ppermute | solution.py:817
  97.3 6.5 %collective-permute-start.19 = (bf16[1,256,1024]{2,1,0:T(8,128)(2,1)S(1)}, bf16[1,256,1024]{2,1,0:T(8,128)(2,1)S(1)}, u32[]{:S(2)}, u32[]{:S(2)}) collective-permute-start(bf16[1,256,1024]{2,1,0:T(8,128)(2,1)S(1)} %collective-permute-done.12), channel_id=1, source_target_pairs={{0,2},{2,0},{4,6},{6,4},{8,10},{10,8},{12,14},{14,12},{16,18},{18,... | collective-permute-start | bytes 1572872 | tf_op jit(solution)/shard_map/ppermute | solution.py:817
  152.8 15.6 %collective-permute-start.20 = (bf16[4,768,1024]{2,1,0:T(8,128)(2,1)}, bf16[4,768,1024]{2,1,0:T(8,128)(2,1)}, u32[]{:S(2)}, u32[]{:S(2)}) collective-permute-start(bf16[4,768,1024]{2,1,0:T(8,128)(2,1)} %bitcast.59), channel_id=1, source_target_pairs={{0,2},{2,0},{4,6},{6,4},{8,10},{10,8},{12,14},{14,12},{16,18},{18,... | collective-permute-start | bytes 18874376 | tf_op jit(solution)/shard_map/ppermute | solution.py:817
  153.5 31.6 %collective-permute-start.21 = (bf16[512,1024]{1,0:T(8,128)(2,1)S(1)}, bf16[512,1024]{1,0:T(8,128)(2,1)S(1)}, u32[]{:S(2)}, u32[]{:S(2)}) collective-permute-start(bf16[512,1024]{1,0:T(8,128)(2,1)S(1)} %get-tuple-element.286), channel_id=1, source_target_pairs={{0,1},{1,0},{2,3},{3,2},{4,5},{5,4},{6,7},{7,6},{8,9},{9,8},{10,11... | collective-permute-start | bytes 3145736 | tf_op jit(solution)/shard_map/ppermute | solution.py:812
  186.2 16.2 %collective-permute-start.22 = (bf16[1024,768]{1,0:T(8,128)(2,1)}, bf16[1024,768]{1,0:T(8,128)(2,1)S(1)}, u32[]{:S(2)}, u32[]{:S(2)}) collective-permute-start(bf16[1024,768]{1,0:T(8,128)(2,1)} %get-tuple-element.296), channel_id=1, source_target_pairs={{0,2},{2,0},{4,6},{6,4},{8,10},{10,8},{12,14},{14,12},{16,18},{18,... | collective-permute-start | bytes 4718600 | tf_op jit(solution)/shard_map/ppermute | solution.py:817
  186.3 25.4 %collective-permute-start.25 = (bf16[512,1024]{1,0:T(8,128)(2,1)S(1)}, bf16[512,1024]{1,0:T(8,128)(2,1)S(1)}, u32[]{:S(2)}, u32[]{:S(2)}) collective-permute-start(bf16[512,1024]{1,0:T(8,128)(2,1)S(1)} %get-tuple-element.302), channel_id=1, source_target_pairs={{0,1},{1,0},{2,3},{3,2},{4,5},{5,4},{6,7},{7,6},{8,9},{9,8},{10,11... | collective-permute-start | bytes 3145736 | tf_op jit(solution)/shard_map/ppermute | solution.py:812
  186.8 36.7 %collective-permute-start.23 = (bf16[2,384,1024]{2,1,0:T(8,128)(2,1)}, bf16[2,384,1024]{2,1,0:T(8,128)(2,1)}, u32[]{:S(2)}, u32[]{:S(2)}) collective-permute-start(bf16[2,384,1024]{2,1,0:T(8,128)(2,1)} %get-tuple-element.300), channel_id=1, source_target_pairs={{0,4},{2,6},{4,0},{6,2},{8,12},{10,14},{12,8},{14,10},{16,20},{18,... | collective-permute-start | bytes 4718600 | tf_op jit(solution)/shard_map/ppermute | solution.py:817
  187.1 36.5 %collective-permute-start.24 = (bf16[2,384,1024]{2,1,0:T(8,128)(2,1)}, bf16[2,384,1024]{2,1,0:T(8,128)(2,1)}, u32[]{:S(2)}, u32[]{:S(2)}) collective-permute-start(bf16[2,384,1024]{2,1,0:T(8,128)(2,1)} %get-tuple-element.301), channel_id=1, source_target_pairs={{0,8},{2,10},{4,12},{6,14},{8,0},{10,2},{12,4},{14,6},{16,24},{18,... | collective-permute-start | bytes 4718600 | tf_op jit(solution)/shard_map/ppermute | solution.py:817
  232.6 18.9 %collective-permute-start.26 = (bf16[2,192,1024]{2,1,0:T(8,128)(2,1)}, bf16[2,192,1024]{2,1,0:T(8,128)(2,1)S(1)}, u32[]{:S(2)}, u32[]{:S(2)}) collective-permute-start(bf16[2,192,1024]{2,1,0:T(8,128)(2,1)} %get-tuple-element.319), channel_id=1, source_target_pairs={{0,8},{2,10},{4,12},{6,14},{8,0},{10,2},{12,4},{14,6},{16,24},{18,... | collective-permute-start | bytes 2359304 | tf_op jit(solution)/shard_map/ppermute | solution.py:817
  234.4 18.4 %collective-permute-start.27 = (bf16[2,192,1024]{2,1,0:T(8,128)(2,1)}, bf16[2,192,1024]{2,1,0:T(8,128)(2,1)S(1)}, u32[]{:S(2)}, u32[]{:S(2)}) collective-permute-start(bf16[2,192,1024]{2,1,0:T(8,128)(2,1)} %get-tuple-element.320), channel_id=1, source_target_pairs={{0,4},{2,6},{4,0},{6,2},{8,12},{10,14},{12,8},{14,10},{16,20},{18,... | collective-permute-start | bytes 2359304 | tf_op jit(solution)/shard_map/ppermute | solution.py:817
  235.9 45.9 %collective-permute-start.30 = (bf16[1024,768]{1,0:T(8,128)(2,1)}, bf16[1024,768]{1,0:T(8,128)(2,1)S(1)}, u32[]{:S(2)}, u32[]{:S(2)}) collective-permute-start(bf16[1024,768]{1,0:T(8,128)(2,1)} %add_convert_fusion), channel_id=1, source_target_pairs={{0,1},{1,0},{2,3},{3,2},{4,5},{5,4},{6,7},{7,6},{8,9},{9,8},{10,11... | collective-permute-start | bytes 4718600 | tf_op jit(solution)/shard_map/ppermute | solution.py:812
  266.1 21.6 %collective-permute-start.29 = (bf16[1024,768]{1,0:T(8,128)(2,1)}, bf16[1024,768]{1,0:T(8,128)(2,1)S(1)}, u32[]{:S(2)}, u32[]{:S(2)}) collective-permute-start(bf16[1024,768]{1,0:T(8,128)(2,1)} %get-tuple-element.335), channel_id=1, source_target_pairs={{0,2},{2,0},{4,6},{6,4},{8,10},{10,8},{12,14},{14,12},{16,18},{18,... | collective-permute-start | bytes 4718600 | tf_op jit(solution)/shard_map/ppermute | solution.py:817
  266.8 20.9 %collective-permute-start.28 = (bf16[2,192,1024]{2,1,0:T(8,128)(2,1)}, bf16[2,192,1024]{2,1,0:T(8,128)(2,1)}, u32[]{:S(2)}, u32[]{:S(2)}) collective-permute-start(bf16[2,192,1024]{2,1,0:T(8,128)(2,1)} %get-tuple-element.334), channel_id=1, source_target_pairs={{0,1},{1,0},{2,3},{3,2},{4,5},{5,4},{6,7},{7,6},{8,9},{9,8},{10,11... | collective-permute-start | bytes 2359304 | tf_op jit(solution)/shard_map/ppermute | solution.py:812
  310.1 21.2 %collective-permute-start.35 = (bf16[256,1024]{1,0:T(8,128)(2,1)}, bf16[256,1024]{1,0:T(8,128)(2,1)S(1)}, u32[]{:S(2)}, u32[]{:S(2)}) collective-permute-start(bf16[256,1024]{1,0:T(8,128)(2,1)} %get-tuple-element.356), channel_id=1, source_target_pairs={{0,1},{1,0},{2,3},{3,2},{4,5},{5,4},{6,7},{7,6},{8,9},{9,8},{10,11... | collective-permute-start | bytes 1572872 | tf_op jit(solution)/shard_map/ppermute | solution.py:812
  311.7 16.3 %collective-permute-start.33 = (bf16[1,256,768]{2,1,0:T(8,128)(2,1)}, bf16[1,256,768]{2,1,0:T(8,128)(2,1)S(1)}, u32[]{:S(2)}, u32[]{:S(2)}) collective-permute-start(bf16[1,256,768]{2,1,0:T(8,128)(2,1)} %get-tuple-element.354), channel_id=1, source_target_pairs={{0,4},{2,6},{4,0},{6,2},{8,12},{10,14},{12,8},{14,10},{16,20},{18,... | collective-permute-start | bytes 1179656 | tf_op jit(solution)/shard_map/ppermute | solution.py:817
  312.5 18.8 %collective-permute-start.34 = (bf16[1,256,768]{2,1,0:T(8,128)(2,1)}, bf16[1,256,768]{2,1,0:T(8,128)(2,1)S(1)}, u32[]{:S(2)}, u32[]{:S(2)}) collective-permute-start(bf16[1,256,768]{2,1,0:T(8,128)(2,1)} %get-tuple-element.355), channel_id=1, source_target_pairs={{0,8},{2,10},{4,12},{6,14},{8,0},{10,2},{12,4},{14,6},{16,24},{18,... | collective-permute-start | bytes 1179656 | tf_op jit(solution)/shard_map/ppermute | solution.py:817
  313.0 15.0 %collective-permute-start.32 = (f32[48,1024]{1,0:T(8,128)S(1)}, f32[48,1024]{1,0:T(8,128)S(1)}, u32[]{:S(2)}, u32[]{:S(2)}) collective-permute-start(f32[48,1024]{1,0:T(8,128)S(1)} %constant_dynamic-update-slice_fusion), channel_id=1, source_target_pairs={{0,1},{1,0},{2,3},{3,2},{4,5},{5,4},{6,7},{7,6},{8,9},{9,8},{10,11... | collective-permute-start | bytes 589832 | tf_op jit(solution)/shard_map/ppermute | solution.py:812
  313.6 17.8 %collective-permute-start.31 = (bf16[2,96,1024]{2,1,0:T(8,128)(2,1)}, bf16[2,96,1024]{2,1,0:T(8,128)(2,1)S(1)}, u32[]{:S(2)}, u32[]{:S(2)}) collective-permute-start(bf16[2,96,1024]{2,1,0:T(8,128)(2,1)} %get-tuple-element.341), channel_id=1, source_target_pairs={{0,16},{2,18},{4,20},{6,22},{8,24},{10,26},{12,28},{14,30},{16,0},... | collective-permute-start | bytes 1179656 | tf_op jit(solution)/shard_map/ppermute | solution.py:817
  336.2 19.0 %collective-permute-start.40 = (bf16[256,1024]{1,0:T(8,128)(2,1)S(1)}, bf16[256,1024]{1,0:T(8,128)(2,1)S(1)}, u32[]{:S(2)}, u32[]{:S(2)}) collective-permute-start(bf16[256,1024]{1,0:T(8,128)(2,1)S(1)} %copy-done.17), channel_id=1, source_target_pairs={{0,1},{1,0},{2,3},{3,2},{4,5},{5,4},{6,7},{7,6},{8,9},{9,8},{10,11... | collective-permute-start | bytes 1572872 | tf_op jit(solution)/shard_map/ppermute | solution.py:812
  338.7 16.6 %collective-permute-start.36 = (bf16[2,96,1024]{2,1,0:T(8,128)(2,1)S(1)}, bf16[2,96,1024]{2,1,0:T(8,128)(2,1)S(1)}, u32[]{:S(2)}, u32[]{:S(2)}) collective-permute-start(bf16[2,96,1024]{2,1,0:T(8,128)(2,1)S(1)} %add_convert_fusion.1), channel_id=1, source_target_pairs={{0,16},{2,18},{4,20},{6,22},{8,24},{10,26},{12,28},{14,30},{16,0},... | collective-permute-start | bytes 1179656 | tf_op jit(solution)/shard_map/ppermute | solution.py:817
  338.7 5.7 %collective-permute-start.37 = (f32[48,1024]{1,0:T(8,128)S(1)}, f32[48,1024]{1,0:T(8,128)S(1)}, u32[]{:S(2)}, u32[]{:S(2)}) collective-permute-start(f32[48,1024]{1,0:T(8,128)S(1)} %add.99), channel_id=1, source_target_pairs={{0,2},{2,0},{4,6},{6,4},{8,10},{10,8},{12,14},{14,12},{16,18},{18,... | collective-permute-start | bytes 589832 | tf_op jit(solution)/shard_map/ppermute | solution.py:817
  338.7 11.9 %collective-permute-start.38 = (bf16[1,128,768]{2,1,0:T(8,128)(2,1)}, bf16[1,128,768]{2,1,0:T(8,128)(2,1)S(1)}, u32[]{:S(2)}, u32[]{:S(2)}) collective-permute-start(bf16[1,128,768]{2,1,0:T(8,128)(2,1)} %get-tuple-element.371), channel_id=1, source_target_pairs={{0,8},{2,10},{4,12},{6,14},{8,0},{10,2},{12,4},{14,6},{16,24},{18,... | collective-permute-start | bytes 589832 | tf_op jit(solution)/shard_map/ppermute | solution.py:817
  342.8 7.8 %collective-permute-start.39 = (bf16[1,128,768]{2,1,0:T(8,128)(2,1)}, bf16[1,128,768]{2,1,0:T(8,128)(2,1)S(1)}, u32[]{:S(2)}, u32[]{:S(2)}) collective-permute-start(bf16[1,128,768]{2,1,0:T(8,128)(2,1)} %get-tuple-element.372), channel_id=1, source_target_pairs={{0,4},{2,6},{4,0},{6,2},{8,12},{10,14},{12,8},{14,10},{16,20},{18,... | collective-permute-start | bytes 589832 | tf_op jit(solution)/shard_map/ppermute | solution.py:817
  360.3 15.5 %collective-permute-start.45 = (bf16[256,1024]{1,0:T(8,128)(2,1)S(1)}, bf16[256,1024]{1,0:T(8,128)(2,1)S(1)}, u32[]{:S(2)}, u32[]{:S(2)}) collective-permute-start(bf16[256,1024]{1,0:T(8,128)(2,1)S(1)} %copy-done.16), channel_id=1, source_target_pairs={{0,1},{1,0},{2,3},{3,2},{4,5},{5,4},{6,7},{7,6},{8,9},{9,8},{10,11... | collective-permute-start | bytes 1572872 | tf_op jit(solution)/shard_map/ppermute | solution.py:812
  362.0 13.7 %collective-permute-start.41 = (bf16[192,1024]{1,0:T(8,128)(2,1)S(1)}, bf16[192,1024]{1,0:T(8,128)(2,1)S(1)}, u32[]{:S(2)}, u32[]{:S(2)}) collective-permute-start(bf16[192,1024]{1,0:T(8,128)(2,1)S(1)} %get-tuple-element.383), channel_id=1, source_target_pairs={{0,8},{2,10},{4,12},{6,14},{8,0},{10,2},{12,4},{14,6},{16,24},{18,... | collective-permute-start | bytes 1179656 | tf_op jit(solution)/shard_map/ppermute | solution.py:817
  362.0 13.7 %collective-permute-start.42 = (bf16[192,1024]{1,0:T(8,128)(2,1)S(1)}, bf16[192,1024]{1,0:T(8,128)(2,1)S(1)}, u32[]{:S(2)}, u32[]{:S(2)}) collective-permute-start(bf16[192,1024]{1,0:T(8,128)(2,1)S(1)} %get-tuple-element.384), channel_id=1, source_target_pairs={{0,4},{2,6},{4,0},{6,2},{8,12},{10,14},{12,8},{14,10},{16,20},{18,... | collective-permute-start | bytes 1179656 | tf_op jit(solution)/shard_map/ppermute | solution.py:817
  363.1 12.7 %collective-permute-start.43 = (f32[48,1024]{1,0:T(8,128)S(1)}, f32[48,1024]{1,0:T(8,128)S(1)}, u32[]{:S(2)}, u32[]{:S(2)}) collective-permute-start(f32[48,1024]{1,0:T(8,128)S(1)} %add.100), channel_id=1, source_target_pairs={{0,4},{2,6},{4,0},{6,2},{8,12},{10,14},{12,8},{14,10},{16,20},{18,... | collective-permute-start | bytes 589832 | tf_op jit(solution)/shard_map/ppermute | solution.py:817
  364.0 11.7 %collective-permute-start.44 = (bf16[2,64,768]{2,1,0:T(8,128)(2,1)S(1)}, bf16[2,64,768]{2,1,0:T(8,128)(2,1)S(1)}, u32[]{:S(2)}, u32[]{:S(2)}) collective-permute-start(bf16[2,64,768]{2,1,0:T(8,128)(2,1)S(1)} %pad_maximum_fusion.13), channel_id=1, source_target_pairs={{0,16},{2,18},{4,20},{6,22},{8,24},{10,26},{12,28},{14,30},{16,0},... | collective-permute-start | bytes 589832 | tf_op jit(solution)/shard_map/ppermute | solution.py:817
  379.2 27.6 %collective-permute-start.46 = (bf16[384,1024]{1,0:T(8,128)(2,1)}, bf16[384,1024]{1,0:T(8,128)(2,1)}, u32[]{:S(2)}, u32[]{:S(2)}) collective-permute-start(bf16[384,1024]{1,0:T(8,128)(2,1)} %pad_maximum_fusion.5), channel_id=1, source_target_pairs={{0,4},{2,6},{4,0},{6,2},{8,12},{10,14},{12,8},{14,10},{16,20},{18,... | collective-permute-start | bytes 2359304 | tf_op jit(solution)/shard_map/ppermute | solution.py:817
  380.4 26.4 %collective-permute-start.47 = (bf16[384,1024]{1,0:T(8,128)(2,1)}, bf16[384,1024]{1,0:T(8,128)(2,1)}, u32[]{:S(2)}, u32[]{:S(2)}) collective-permute-start(bf16[384,1024]{1,0:T(8,128)(2,1)} %pad_maximum_fusion.6), channel_id=1, source_target_pairs={{0,8},{2,10},{4,12},{6,14},{8,0},{10,2},{12,4},{14,6},{16,24},{18,... | collective-permute-start | bytes 2359304 | tf_op jit(solution)/shard_map/ppermute | solution.py:817
  382.1 24.7 %collective-permute-start.50 = (bf16[256,1024]{1,0:T(8,128)(2,1)}, bf16[256,1024]{1,0:T(8,128)(2,1)S(1)}, u32[]{:S(2)}, u32[]{:S(2)}) collective-permute-start(bf16[256,1024]{1,0:T(8,128)(2,1)} %get-tuple-element.399), channel_id=1, source_target_pairs={{0,1},{1,0},{2,3},{3,2},{4,5},{5,4},{6,7},{7,6},{8,9},{9,8},{10,11... | collective-permute-start | bytes 1572872 | tf_op jit(solution)/shard_map/ppermute | solution.py:812
  384.4 22.4 %collective-permute-start.48 = (f32[48,1024]{1,0:T(8,128)}, f32[48,1024]{1,0:T(8,128)S(1)}, u32[]{:S(2)}, u32[]{:S(2)}) collective-permute-start(f32[48,1024]{1,0:T(8,128)} %add.101), channel_id=1, source_target_pairs={{0,8},{2,10},{4,12},{6,14},{8,0},{10,2},{12,4},{14,6},{16,24},{18,... | collective-permute-start | bytes 589832 | tf_op jit(solution)/shard_map/ppermute | solution.py:817
  384.5 22.3 %collective-permute-start.49 = (bf16[2,64,768]{2,1,0:T(8,128)(2,1)}, bf16[2,64,768]{2,1,0:T(8,128)(2,1)S(1)}, u32[]{:S(2)}, u32[]{:S(2)}) collective-permute-start(bf16[2,64,768]{2,1,0:T(8,128)(2,1)} %pad_maximum_fusion.14), channel_id=1, source_target_pairs={{0,16},{2,18},{4,20},{6,22},{8,24},{10,26},{12,28},{14,30},{16,0},... | collective-permute-start | bytes 589832 | tf_op jit(solution)/shard_map/ppermute | solution.py:817
  410.2 12.6 %collective-permute-start.51 = (bf16[768,1024]{1,0:T(8,128)(2,1)S(1)}, bf16[768,1024]{1,0:T(8,128)(2,1)S(1)}, u32[]{:S(2)}, u32[]{:S(2)}) collective-permute-start(bf16[768,1024]{1,0:T(8,128)(2,1)S(1)} %pad_maximum_fusion.3.refs_0_), channel_id=1, source_target_pairs={{0,2},{2,0},{4,6},{6,4},{8,10},{10,8},{12,14},{14,12},{16,18},{18,... | collective-permute-start | bytes 4718600 | tf_op jit(solution)/shard_map/ppermute | solution.py:817
  410.3 12.5 %collective-permute-start.52 = (bf16[768,1024]{1,0:T(8,128)(2,1)S(1)}, bf16[768,1024]{1,0:T(8,128)(2,1)S(1)}, u32[]{:S(2)}, u32[]{:S(2)}) collective-permute-start(bf16[768,1024]{1,0:T(8,128)(2,1)S(1)} %pad_maximum_fusion.4.refs_1_), channel_id=1, source_target_pairs={{0,2},{2,0},{4,6},{6,4},{8,10},{10,8},{12,14},{14,12},{16,18},{18,... | collective-permute-start | bytes 4718600 | tf_op jit(solution)/shard_map/ppermute | solution.py:817
  410.8 12.0 %collective-permute-start.53 = (f32[48,1024]{1,0:T(8,128)S(1)}, f32[48,1024]{1,0:T(8,128)S(1)}, u32[]{:S(2)}, u32[]{:S(2)}) collective-permute-start(f32[48,1024]{1,0:T(8,128)S(1)} %add.104), channel_id=1, source_target_pairs={{0,16},{2,18},{4,20},{6,22},{8,24},{10,26},{12,28},{14,30},{16,0},... | collective-permute-start | bytes 589832 | tf_op jit(solution)/shard_map/ppermute | solution.py:817
  413.4 9.4 %collective-permute-start.54 = (bf16[128,768]{1,0:T(8,128)(2,1)S(1)}, bf16[128,768]{1,0:T(8,128)(2,1)S(1)}, u32[]{:S(2)}, u32[]{:S(2)}) collective-permute-start(bf16[128,768]{1,0:T(8,128)(2,1)S(1)} %get-tuple-element.408), channel_id=1, source_target_pairs={{0,8},{2,10},{4,12},{6,14},{8,0},{10,2},{12,4},{14,6},{16,24},{18,... | collective-permute-start | bytes 589832 | tf_op jit(solution)/shard_map/ppermute | solution.py:817
  414.1 8.6 %collective-permute-start.55 = (bf16[128,768]{1,0:T(8,128)(2,1)S(1)}, bf16[128,768]{1,0:T(8,128)(2,1)S(1)}, u32[]{:S(2)}, u32[]{:S(2)}) collective-permute-start(bf16[128,768]{1,0:T(8,128)(2,1)S(1)} %get-tuple-element.409), channel_id=1, source_target_pairs={{0,4},{2,6},{4,0},{6,2},{8,12},{10,14},{12,8},{14,10},{16,20},{18,... | collective-permute-start | bytes 589832 | tf_op jit(solution)/shard_map/ppermute | solution.py:817
  422.9 12.2 %collective-permute-start.56 = (bf16[256,768]{1,0:T(8,128)(2,1)S(1)}, bf16[256,768]{1,0:T(8,128)(2,1)S(1)}, u32[]{:S(2)}, u32[]{:S(2)}) collective-permute-start(bf16[256,768]{1,0:T(8,128)(2,1)S(1)} %pad_maximum_fusion.11), channel_id=1, source_target_pairs={{0,4},{2,6},{4,0},{6,2},{8,12},{10,14},{12,8},{14,10},{16,20},{18,... | collective-permute-start | bytes 1179656 | tf_op jit(solution)/shard_map/ppermute | solution.py:817
  424.5 10.7 %collective-permute-start.57 = (bf16[256,768]{1,0:T(8,128)(2,1)S(1)}, bf16[256,768]{1,0:T(8,128)(2,1)S(1)}, u32[]{:S(2)}, u32[]{:S(2)}) collective-permute-start(bf16[256,768]{1,0:T(8,128)(2,1)S(1)} %pad_maximum_fusion.12), channel_id=1, source_target_pairs={{0,8},{2,10},{4,12},{6,14},{8,0},{10,2},{12,4},{14,6},{16,24},{18,... | collective-permute-start | bytes 1179656 | tf_op jit(solution)/shard_map/ppermute | solution.py:817
  435.3 2.4 collective-permute-start.58
  435.4 3.4 collective-permute-start.59
  (39 other events, 302.0 us)

commit v6 on v5

--- a/solution.py
+++ b/solution.py
@@ -188,9 +188,11 @@
         lse_ref[0, :, mine] = logs.T[:8]
 
 
-def attend(first, wq, wk, wv, tables, seg_col, seg_row):
+def attend(first, weights, tables, seg_col, seg_row):
     rows, width = first.shape
-    groups = wq.shape[1] // GROUP
+    packed = len(weights) == 1
+    wq, wk, wv = weights * 3 if packed else weights
+    groups = 1 if packed else wq.shape[1] // GROUP
     table = whole((rows, LANES))
     return pl.pallas_call(
         attend_kernel,
@@ -198,8 +200,8 @@
         in_specs=[
             whole((rows, width)),
             pl.BlockSpec((width, GROUP), lambda g: (0, g)),
-            pl.BlockSpec((width, LANES), lambda g: (0, g)),
-            pl.BlockSpec((width, LANES), lambda g: (0, g)),
+            pl.BlockSpec((width, LANES), lambda g: (0, 2 if packed else g)),
+            pl.BlockSpec((width, LANES), lambda g: (0, 3 if packed else g)),
             table,
             table,
             table,
@@ -580,8 +582,10 @@
         sum_ref[...] = first_grad
 
 
-def project(sel, back, att, low_t, first_t, wq, wk, wv, before=None, final=None):
+def project(sel, back, att, low_t, first_t, weights, before=None, final=None):
     width, rows = low_t.shape
+    packed = len(weights) == 1
+    wq, wk, wv = weights * 3 if packed else weights
     steps = 4
     block = rows // steps
     assert rows == width
@@ -590,11 +594,12 @@
         return pl.BlockSpec(shape, lambda i, s: (0,) * len(shape))
 
     wide_w = pl.BlockSpec((width, GROUP), lambda i, s: (0, s[0]))
-    thin_w = pl.BlockSpec((width, LANES), lambda i, s: (0, s[0]))
+    key_w = pl.BlockSpec((width, LANES), lambda i, s: (0, 2 if packed else s[0]))
+    value_w = pl.BlockSpec((width, LANES), lambda i, s: (0, 3 if packed else s[0]))
     strip = pl.BlockSpec((block, width), lambda i, s: (i, 0))
     in_specs = [
         fixed((rows, 2 * GROUP)), pl.BlockSpec((rows, GROUP), lambda i, s: (0, s[0])),
-        strip, strip, wide_w, thin_w, thin_w,
+        strip, strip, wide_w, key_w, value_w,
     ]
     out_specs = [pl.BlockSpec((block, 3 * GROUP), lambda i, s: (i, 0))]
     out_shape = [jax.ShapeDtypeStruct((width, 3 * GROUP), bf16)]
@@ -959,21 +964,20 @@
     frequency = THETA ** (-(2.0 * jnp.arange(half_dim, dtype=f32)) / HEAD_DIM)
     freq = jnp.broadcast_to(frequency[:, None], (half_dim, LANES))
 
-    near_own = [cut(w, core, 1) for w in (w_query, w_key, w_value)]
+    near = swap_tensor(jnp.concatenate([cut(w, core, 1) for w in (w_query, w_key, w_value)], 1))
     order_index = lax.axis_index("dp") % 4
     experts_own = [lax.dynamic_slice_in_dim(w, order_index, 1, 0) for w in (w_gate, w_up, w_down)]
-    near = [swap_tensor(w) for w in near_own]
-    got = [swap_tensor(after(experts_own[0], near[1]))]
+    got = [swap_tensor(experts_own[0])]
 
     first, first_t, *tables = prologue(side[None], tokens, gain_one, seg_row, freq)
-    saved_a = attend(first, w_query, w_key, w_value, tables, seg_col, seg_row)
+    saved_a = attend(first, (w_query, w_key, w_value), tables, seg_col, seg_row)
     (near, got[0]), (first, saved_a) = lax.optimization_barrier(((near, got[0]), (first, saved_a)))
-    far_qkv = [swap_dp(w, 1) for w in near]
-    near_out = swap_tensor(after(cut(w_output, core, 0), near[0]))
-    got.append(swap_tensor(after(experts_own[1], near[0])))
+    far_qkv = swap_dp(near, 1)
+    near_out = swap_tensor(after(cut(w_output, core, 0), near))
+    got.append(swap_tensor(after(experts_own[1], near)))
     across = [swap_dp(got[0], 2)]
     beside = [swap_dp(got[0], 1)]
-    saved_b = attend(first, *near, tables, seg_col, seg_row)
+    saved_b = attend(first, (near,), tables, seg_col, seg_row)
     (near_out, got[1], across[0]), (first, saved_b) = lax.optimization_barrier(
         ((near_out, got[1], across[0]), (first, saved_b))
     )
@@ -982,7 +986,7 @@
     across.append(swap_dp(got[1], 2))
     beside.append(swap_dp(got[1], 1))
     corner = [swap_dp(across[0], 1)]
-    saved_c = attend(first, *far_qkv, tables, seg_col, seg_row)
+    saved_c = attend(first, (far_qkv,), tables, seg_col, seg_row)
     (across[1], got[2]), saved_c = lax.optimization_barrier(((across[1], got[2]), saved_c))
     across.append(swap_dp(got[2], 2))
     beside.append(swap_dp(got[2], 1))
@@ -1018,25 +1022,25 @@
     low_grad = chains.advance(fence=low_grad)
     back = attend_back(zero, saved_c, *shared, low_grad, far_out)
     back = chains.advance(["grads"], fence=back)
-    group_d, partial_sum = project(zero, back, saved_c[3], low_t, first_t, *far_qkv)
+    group_d, partial_sum = project(zero, back, saved_c[3], low_t, first_t, (far_qkv,))
     chains.add("other", piece_swaps(group_d, 1, 1))
     low_grad, partial_sum = chains.advance(["other", "out"], fence=(low_grad, partial_sum))
     back = attend_back(zero, saved_b, *shared, low_grad, near_out)
     back = chains.advance(["other"], fence=back)
-    group_c, partial_sum = project(zero, back, saved_b[3], low_t, first_t, *near, before=partial_sum)
+    group_c, partial_sum = project(zero, back, saved_b[3], low_t, first_t, (near,), before=partial_sum)
     chains.add("theirs", piece_swaps(total([group_c, chains.done["other"]]), 1))
     low_grad, partial_sum = chains.advance(["grads", "out", "theirs"], fence=(low_grad, partial_sum))
     back = attend_back(one_minus, saved_a, *shared, low_grad, w_output)
     back = chains.advance(["grads"], fence=back)
     group_b, partial_sum = project(
-        one_minus, back, saved_a[3], low_t, first_t, w_query, w_key, w_value, before=partial_sum
+        one_minus, back, saved_a[3], low_t, first_t, (w_query, w_key, w_value), before=partial_sum
     )
     chains.add("mine", piece_swaps(group_b, 1, 1))
     low_grad, partial_sum = chains.advance(["mine"], fence=(low_grad, partial_sum))
     back = attend_back(core[None], saved_a, *shared, low_grad, w_output)
     back = chains.advance(["grads", "mine", "theirs"], fence=back)
     group_a, token, norm_one = project(
-        jnp.stack([core, side]), back, saved_a[3], low_t, first_t, w_query, w_key, w_value,
+        jnp.stack([core, side]), back, saved_a[3], low_t, first_t, (w_query, w_key, w_value),
         before=partial_sum, final=(tokens, gain_one, resid_grad),
     )
     chains.add("token", piece_swaps(token, 4))

time: 455 us -> 459 us (level)
  waiting for transfers between devices: 87.9 us -> 93 us
    ppermute x16 -> x14, waiting for transfers between devices: 22.9 us -> 27.1 us  [swap_tensor(): return lax.ppermute(values, 'tensor', [(0, 1), (1, 0)])]
    ppermute x16 -> x14, starting transfers between devices: 22 us -> 19.9 us  [swap_tensor(): return lax.ppermute(values, 'tensor', [(0, 1), (1, 0)])]
    ppermute x44 -> x42, waiting for transfers between devices: 65 us -> 65.8 us  [swap_dp(): return lax.ppermute(values, 'dp', [(i, i ^ bit) for i in range(count)])]
    ppermute x44 -> x42, starting transfers between devices: 40.4 us -> 40.4 us  [swap_dp(): return lax.ppermute(values, 'dp', [(i, i ^ bit) for i in range(count)])]
  transfers between devices with their start and end apart: 60 -> 56, of which waited for: 18 -> 19; matrix products, arithmetic and copies ran while one was open for 6% -> 6% of each run, Pallas kernels for 35% -> 35%
where the time goes in v6:
time: 459 us; the launch traced here: 450 us
  Pallas kernels  243 us (53%)
  waiting for transfers between devices  93 us (20%)
  starting transfers between devices  60.4 us (13%)
  other arithmetic  30.2 us (7%)
  local copies, waits for them, and re-layouts  21.5 us (5%)
    ppermute x42, waiting for transfers between devices, swap_dp(): return lax.ppermute(values, 'dp', [(i, i ^ bit) for i in range(count)])  65.8 us
    pallas_call x4, Pallas kernels, attend_back(): pl.pallas_call(attend_back_kernel, grid_spec=pltpu.PrefetchScalarGridSpec...  53.6 us
    pallas_call x1, Pallas kernels, experts_layer(): pl.pallas_call(experts_kernel, grid_spec=pltpu.PrefetchScalarGridSpec(num...  45.6 us
    pallas_call x3, Pallas kernels, attend(): pl.pallas_call(attend_kernel, grid=(groups,), in_specs=[whole((rows, widt...  43.2 us
    ppermute x42, starting transfers between devices, swap_dp(): return lax.ppermute(values, 'dp', [(i, i ^ bit) for i in range(count)])  40.4 us
    pallas_call x4, Pallas kernels, project(): pl.pallas_call(partial(project_kernel, final is not None, before is None)...  37.5 us
    pallas_call x6, Pallas kernels, add_split(): pl.pallas_call(kernel, grid_spec=pltpu.PrefetchScalarGridSpec(num_scalar_...  30.8 us
    ppermute x14, waiting for transfers between devices, swap_tensor(): return lax.ppermute(values, 'tensor', [(0, 1), (1, 0)])  27.1 us
  transfers between devices with their start and end apart: 56, of which 19 were waited for; matrix products, arithmetic and copies ran while one was open for 6% of the time, Pallas kernels for 35%

profile of v6, /device:TPU:0, one launch (start us, length us, event | category | flops | bytes accessed | tf_op | source)
XLA Modules:
  0.0 449.7 jit_solution(8441190285985868028)
XLA Ops:
  3.0 3.0 collective-permute-start
  9.5 5.3 %prologue.1 = (bf16[1024,1024]{1,0:T(8,128)(2,1)}, bf16[1024,1024]{1,0:T(8,128)(2,1)}, f32[1024,128]{1,0:T(8,128)}, f32[1024,128]{1,0:T(8,128)}, f32[1024,128]{1,0:T(8,128)}) custom-call(s32[1]{0:T(128)} %bitcast.1.side_ref, bf16[2048,1024]{1,0:T(8,128)(2,1)} %rest_1_.1, bf16[1,1024]{1,0:T(2,128)(2,1)} %broadcast_in_dim.24.gain_ref.rest_2_, ...), custom_call_target="tpu_custom_call" | custom-call | flops 5500000256 | bytes 1048576 | tf_op jit(solution)/shard_map/prologue/pallas_call | solution.py:96
  14.8 20.1 %attend.3 = (bf16[1024,512]{1,0:T(8,128)(2,1)}, bf16[1024,256]{1,0:T(8,128)(2,1)}, bf16[1024,256]{1,0:T(8,128)(2,1)}, bf16[1024,512]{1,0:T(8,128)(2,1)}, f32[2,8,1024]{2,1,0:T(8,128)}) custom-call(bf16[1024,1024]{1,0:T(8,128)(2,1)} %get-tuple-element.244.first_ref, bf16[1024,512]{1,0:T(8,128)(2,1)} %wq_ref.5, bf16[1024,256]{1,0:T(8,128)(2,1)} %wk_ref.5, ...), custom_call_target="tpu_custom_call" | custom-call | flops 22000001024 | bytes 1048576 | tf_op jit(solution)/shard_map/attend/pallas_call | solution.py:197
  38.3 2.1 collective-permute-done.1
  41.6 1.8 collective-permute-start.4
  45.6 11.4 %attend.4 = (bf16[1024,256]{1,0:T(8,128)(2,1)}, bf16[1024,128]{1,0:T(8,128)(2,1)}, bf16[1024,128]{1,0:T(8,128)(2,1)}, bf16[1024,256]{1,0:T(8,128)(2,1)}, f32[1,8,1024]{2,1,0:T(8,128)}) custom-call(bf16[1024,1024]{1,0:T(8,128)(2,1)} %get-tuple-element.244.first_ref, bf16[1024,512]{1,0:T(8,128)(2,1)} %collective-permute-done.wq_ref.wk_ref.wv_ref, ...), custom_call_target="tpu_custom_call" | custom-call | flops 11000000512 | bytes 1048576 | tf_op jit(solution)/shard_map/attend/pallas_call | solution.py:197
  58.3 10.7 %collective-permute-done.2.wo_b_ref.wo_ref = bf16[256,1024]{1,0:T(8,128)(2,1)} collective-permute-done((bf16[256,1024]{1,0:T(8,128)(2,1)S(1)}, bf16[256,1024]{1,0:T(8,128)(2,1)}, u32[]{:S(2)}, u32[]{:S(2)}) %collective-permute-start.2) | collective-permute-done | bytes 524320 | tf_op jit(solution)/shard_map/ppermute | solution.py:817
  69.8 1.7 collective-permute-start.6
  71.6 11.8 %attend.5 = (bf16[1024,256]{1,0:T(8,128)(2,1)}, bf16[1024,128]{1,0:T(8,128)(2,1)}, bf16[1024,128]{1,0:T(8,128)(2,1)}, bf16[1024,256]{1,0:T(8,128)(2,1)}, f32[1,8,1024]{2,1,0:T(8,128)}) custom-call(bf16[1024,1024]{1,0:T(8,128)(2,1)} %get-tuple-element.244.first_ref, bf16[1024,512]{1,0:T(8,128)(2,1)} %collective-permute-done.7.wq_ref.wk_ref.wv_ref, ...), custom_call_target="tpu_custom_call" | custom-call | flops 11000000512 | bytes 1048576 | tf_op jit(solution)/shard_map/attend/pallas_call | solution.py:197
  83.8 1.8 collective-permute-start.8
  85.8 8.7 %router.1 = (f32[1024,1024]{1,0:T(8,128)}, bf16[1024,1024]{1,0:T(8,128)(2,1)}, f32[32,1024]{1,0:T(8,128)}, s32[8,1024]{1,0:T(8,128)}) custom-call(s32[1]{0:T(128)} %bitcast.1.side_ref, bf16[2048,1024]{1,0:T(8,128)(2,1)} %rest_1_.1, bf16[1024,512]{1,0:T(8,128)(2,1)} %get-tuple-element.251.att_a_ref.att_ref, ...), custom_call_target="tpu_custom_call" | custom-call | flops 8800000000 | bytes 1048576 | tf_op jit(solution)/shard_map/router/pallas_call | solution.py:272
  94.5 3.9 collective-permute-done.8
  99.5 2.6 pad_maximum_fusion.wg_b_ref
  102.1 2.6 pad_maximum_fusion.1.wu_b_ref
  104.7 2.7 pad_maximum_fusion.2.wd_b_ref
  107.4 45.6 %experts.1 = (bf16[1024,1024]{1,0:T(8,128)(2,1)}, bf16[1024,1024]{1,0:T(8,128)(2,1)}, bf16[1024,1024]{1,0:T(8,128)(2,1)}, f32[1024,1024]{1,0:T(8,128)}, f32[40,1...) custom-call(s32[2]{0:T(128)} %pad_add_fusion.order_ref, ...), custom_call_target="tpu_custom_call" | custom-call | flops 42900000768 | bytes 1048576 | tf_op jit(solution)/shard_map/experts/pallas_call | solution.py:403
  153.0 2.7 fusion.4
  156.4 1.7 collective-permute-start.17
  158.1 13.4 %attend_back.4.back_ref = bf16[1024,512]{1,0:T(8,128)(2,1)} custom-call(s32[1]{0:T(128)} %constant.138.clone.1.sel_ref, bf16[1024,256]{1,0:T(8,128)(2,1)} %get-tuple-element.266.q_ref, bf16[1024,128]{1,0:T(8,128)(2,1)} %get-tuple-element.267.k_ref, bf16[1024,128]{1,0:T(8,128)(2,1)} %get-tuple-element.268.v_ref, f32[1,8,1024]{2,1,0:T(8,128)} %get-tuple-element.269.lse_ref, ...), custom_call_target="tpu_custom_call" | custom-call | flops 15399999488 | bytes 1048576 | tf_op jit(solution)/shard_map/attend_back/pallas_call | solution.py:520
  171.5 8.4 %add_split.6 = (bf16[2,384,1024]{2,1,0:T(8,128)(2,1)}, bf16[2,384,1024]{2,1,0:T(8,128)(2,1)}, bf16[2,384,1024]{2,1,0:T(8,128)(2,1)}, bf16[2,384,1024]{2,1,0:T(8,128)(2,1)}) custom-call(s32[2]{0:T(128)} %get-tuple-element.448.side_ref, bf16[4,768,1024]{2,1,0:T(8,128)(2,1)} %bitcast.32, ...), custom_call_target="tpu_custom_call" | custom-call | flops 4400000000 | bytes 1048576 | tf_op jit(solution)/shard_map/add_split/pallas_call | solution.py:686
  179.9 8.3 %project.3 = (bf16[1024,768]{1,0:T(8,128)(2,1)}, f32[1024,1024]{1,0:T(8,128)}) custom-call(s32[1]{0:T(128)} %constant.138.clone.1.sel_ref, bf16[1024,512]{1,0:T(8,128)(2,1)} %attend_back.4.back_ref, bf16[1024,256]{1,0:T(8,128)(2,1)} %get-tuple-element.253.att_c_ref.att_ref, bf16[1024,1024]{1,0:T(8,128)(2,1)} %get-tuple-element.277.low_t_ref, ...), custom_call_target="tpu_custom_call" | custom-call | flops 7699999744 | bytes 1048576 | tf_op jit(solution)/shard_map/project/pallas_call | solution.py:621
  189.8 1.8 collective-permute-start.19
  191.6 1.6 collective-permute-start.20
  193.1 13.4 %attend_back.5.back_ref = bf16[1024,512]{1,0:T(8,128)(2,1)} custom-call(s32[1]{0:T(128)} %constant.138.clone.1.sel_ref, bf16[1024,256]{1,0:T(8,128)(2,1)} %get-tuple-element.286.q_ref, bf16[1024,128]{1,0:T(8,128)(2,1)} %get-tuple-element.287.k_ref, bf16[1024,128]{1,0:T(8,128)(2,1)} %get-tuple-element.288.v_ref, f32[1,8,1024]{2,1,0:T(8,128)} %get-tuple-element.289.lse_ref, ...), custom_call_target="tpu_custom_call" | custom-call | flops 15399999488 | bytes 1048576 | tf_op jit(solution)/shard_map/attend_back/pallas_call | solution.py:520
  206.5 9.0 %project.4 = (bf16[1024,768]{1,0:T(8,128)(2,1)}, f32[1024,1024]{1,0:T(8,128)}) custom-call(s32[1]{0:T(128)} %constant.138.clone.1.sel_ref, bf16[1024,512]{1,0:T(8,128)(2,1)} %attend_back.5.back_ref, bf16[1024,256]{1,0:T(8,128)(2,1)} %get-tuple-element.252.att_b_ref.att_ref, bf16[1024,1024]{1,0:T(8,128)(2,1)} %get-tuple-element.277.low_t_ref, ...), custom_call_target="tpu_custom_call" | custom-call | flops 7699999744 | bytes 1048576 | tf_op jit(solution)/shard_map/project/pallas_call | solution.py:621
  215.5 10.9 %collective-permute-done.19.refs_1_.refs_3_ = bf16[2,384,1024]{2,1,0:T(8,128)(2,1)} collective-permute-done((bf16[2,384,1024]{2,1,0:T(8,128)(2,1)}, bf16[2,384,1024]{2,1,0:T(8,128)(2,1)}, u32[]{:S(2)}, u32[]{:S(2)}) %collective-permute-start.19) | collective-permute-done | bytes 1572896 | tf_op jit(solution)/shard_map/ppermute | solution.py:822
  227.9 2.9 add_convert_fusion
  230.8 6.1 %add_split.7 = (bf16[2,192,1024]{2,1,0:T(8,128)(2,1)}, bf16[2,192,1024]{2,1,0:T(8,128)(2,1)}, bf16[2,192,1024]{2,1,0:T(8,128)(2,1)}, bf16[2,192,1024]{2,1,0:T(8,128)(2,1)}) custom-call(s32[2]{0:T(128)} %get-tuple-element.449.side_ref, bf16[2,384,1024]{2,1,0:T(8,128)(2,1)} %get-tuple-element.304.refs_0_.refs_2_, ...), custom_call_target="tpu_custom_call" | custom-call | flops 4400000000 | bytes 1048576 | tf_op jit(solution)/shard_map/add_split/pallas_call | solution.py:686
  236.9 1.6 collective-permute-start.22
  240.5 13.4 %attend_back.6.back_ref = bf16[1024,512]{1,0:T(8,128)(2,1)} custom-call(s32[1]{0:T(128)S(6)} %sub.27.sel_ref, bf16[1024,512]{1,0:T(8,128)(2,1)} %get-tuple-element.298.q_ref, bf16[1024,256]{1,0:T(8,128)(2,1)} %get-tuple-element.299.k_ref, bf16[1024,256]{1,0:T(8,128)(2,1)} %get-tuple-element.300.v_ref, f32[2,8,1024]{2,1,0:T(8,128)} %get-tuple-element.301.lse_ref, ...), custom_call_target="tpu_custom_call" | custom-call | flops 15399999488 | bytes 1048576 | tf_op jit(solution)/shard_map/attend_back/pallas_call | solution.py:520
  253.9 1.6 collective-permute-done.22.refs_1_
  257.7 3.3 add_halves.1
  261.0 9.2 %project.5 = (bf16[1024,768]{1,0:T(8,128)(2,1)}, f32[1024,1024]{1,0:T(8,128)}) custom-call(s32[1]{0:T(128)S(6)} %sub.27.sel_ref, bf16[1024,512]{1,0:T(8,128)(2,1)} %attend_back.6.back_ref, bf16[1024,512]{1,0:T(8,128)(2,1)} %get-tuple-element.251.att_a_ref.att_ref, bf16[1024,1024]{1,0:T(8,128)(2,1)} %get-tuple-element.277.low_t_ref, ...), custom_call_target="tpu_custom_call" | custom-call | flops 7699999744 | bytes 1048576 | tf_op jit(solution)/shard_map/project/pallas_call | solution.py:621
  272.5 13.4 %attend_back.7.back_ref = bf16[1024,512]{1,0:T(8,128)(2,1)} custom-call(s32[1]{0:T(128)} %bitcast.11.sel_ref, bf16[1024,512]{1,0:T(8,128)(2,1)} %get-tuple-element.298.q_ref, bf16[1024,256]{1,0:T(8,128)(2,1)} %get-tuple-element.299.k_ref, bf16[1024,256]{1,0:T(8,128)(2,1)} %get-tuple-element.300.v_ref, f32[2,8,1024]{2,1,0:T(8,128)} %get-tuple-element.301.lse_ref, ...), custom_call_target="tpu_custom_call" | custom-call | flops 15399999488 | bytes 1048576 | tf_op jit(solution)/shard_map/attend_back/pallas_call | solution.py:520
  285.9 5.3 %collective-permute-done.24.refs_1_.refs_3_ = bf16[2,192,1024]{2,1,0:T(8,128)(2,1)} collective-permute-done((bf16[2,192,1024]{2,1,0:T(8,128)(2,1)}, bf16[2,192,1024]{2,1,0:T(8,128)(2,1)}, u32[]{:S(2)}, u32[]{:S(2)}) %collective-permute-start.24) | collective-permute-done | bytes 786464 | tf_op jit(solution)/shard_map/ppermute | solution.py:817
  291.2 2.9 add_split.8
  294.1 11.1 %project_final.1 = (bf16[1024,768]{1,0:T(8,128)(2,1)}, bf16[1024,1024]{1,0:T(8,128)(2,1)}, f32[8,1024]{1,0:T(8,128)}) custom-call(s32[2]{0:T(128)} %get-tuple-element.450.sel_ref, bf16[1024,512]{1,0:T(8,128)(2,1)} %attend_back.7.back_ref, bf16[1024,512]{1,0:T(8,128)(2,1)} %get-tuple-element.251.att_a_ref.att_ref, ...), custom_call_target="tpu_custom_call" | custom-call | flops 7699999744 | bytes 1048576 | tf_op jit(solution)/shard_map/project_final/pallas_call | solution.py:621
  305.2 2.9 fusion.3
  308.1 5.4 %add_split.9 = (bf16[1,256,768]{2,1,0:T(8,128)(2,1)}, bf16[1,256,768]{2,1,0:T(8,128)(2,1)}, bf16[1,256,768]{2,1,0:T(8,128)(2,1)}, bf16[1,256,768]{2,1,0:T(8,128)(2,1)}) custom-call(s32[2]{0:T(128)} %get-tuple-element.448.side_ref, bf16[2,512,768]{2,1,0:T(8,128)(2,1)} %bitcast.44, bf16[2,512,768]{2,1,0:T(8,128)(2,1)} %bitcast.40, ...), custom_call_target="tpu_custom_call" | custom-call | flops 4400000000 | bytes 1048576 | tf_op jit(solution)/shard_map/add_split/pallas_call | solution.py:686
  317.2 2.6 collective-permute-start.27
  319.8 4.6 %maximum_select_fusion = bf16[2048,1024]{1,0:T(8,128)(2,1)} fusion(bf16[512,1024]{1,0:T(8,128)(2,1)} %copy-done.10, bf16[512,1024]{1,0:T(8,128)(2,1)S(1)} %copy-done.9, bf16[1024,1024]{1,0:T(8,128)(2,1)S(1)} %copy-done.3, pred[]{:T(512)S(6)} %eq.22), kind=kLoop, calls=%fused_computation | loop fusion | flops 27262976 | bytes 8388609 | tf_op jit(solution)/shard_map/jit(_where)/select_n | solution.py:1051
  324.4 7.2 %collective-permute-done.28 = f32[48,1024]{1,0:T(8,128)S(1)} collective-permute-done((f32[48,1024]{1,0:T(8,128)S(1)}, f32[48,1024]{1,0:T(8,128)S(1)}, u32[]{:S(2)}, u32[]{:S(2)}) %collective-permute-start.28) | collective-permute-done | bytes 196640 | tf_op jit(solution)/shard_map/ppermute | solution.py:817
  331.6 3.4 collective-permute-done.30.refs_5_.refs_7_
  335.7 4.1 add_split.10
  339.9 2.5 collective-permute-start.36
  342.4 4.1 collective-permute-start.34
  347.4 6.9 %collective-permute-done.34.refs_1_.refs_3_ = bf16[1,128,768]{2,1,0:T(8,128)(2,1)S(1)} collective-permute-done((bf16[1,128,768]{2,1,0:T(8,128)(2,1)}, bf16[1,128,768]{2,1,0:T(8,128)(2,1)S(1)}, u32[]{:S(2)}, u32[]{:S(2)}) %collective-permute-start.34) | collective-permute-done | bytes 196640 | tf_op jit(solution)/shard_map/ppermute | solution.py:822
  354.3 4.6 %collective-permute-done.32 = bf16[2,96,1024]{2,1,0:T(8,128)(2,1)S(1)} collective-permute-done((bf16[2,96,1024]{2,1,0:T(8,128)(2,1)S(1)}, bf16[2,96,1024]{2,1,0:T(8,128)(2,1)S(1)}, u32[]{:S(2)}, u32[]{:S(2)}) %collective-permute-start.32) | collective-permute-done | bytes 393248 | tf_op jit(solution)/shard_map/ppermute | solution.py:822
  359.0 3.8 add_split.11
  363.9 1.7 collective-permute-start.41
  367.7 2.4 collective-permute-start.40
  370.1 9.3 %collective-permute-done.39 = f32[48,1024]{1,0:T(8,128)S(1)} collective-permute-done((f32[48,1024]{1,0:T(8,128)S(1)}, f32[48,1024]{1,0:T(8,128)S(1)}, u32[]{:S(2)}, u32[]{:S(2)}) %collective-permute-start.39) | collective-permute-done | bytes 196640 | tf_op jit(solution)/shard_map/ppermute | solution.py:822
  383.7 1.9 collective-permute-start.43
  385.7 1.7 collective-permute-start.46
  388.1 3.5 collective-permute-start.45
  391.7 18.7 %collective-permute-done.44 = f32[48,1024]{1,0:T(8,128)S(1)} collective-permute-done((f32[48,1024]{1,0:T(8,128)}, f32[48,1024]{1,0:T(8,128)S(1)}, u32[]{:S(2)}, u32[]{:S(2)}) %collective-permute-start.44) | collective-permute-done | bytes 196640 | tf_op jit(solution)/shard_map/ppermute | solution.py:822
  411.9 1.9 pad_maximum_fusion.3.refs_0_
  414.4 2.6 collective-permute-start.49
  420.0 4.0 select_convert_fusion
  424.0 2.4 collective-permute-done.49
  426.5 1.6 collective-permute-start.52
  428.1 1.8 collective-permute-start.53
  429.9 8.9 %unpack_experts.1 = (f32[4,1024,256]{2,1,0:T(8,128)}, f32[4,1024,256]{2,1,0:T(8,128)}, f32[4,256,1024]{2,1,0:T(8,128)}) custom-call(s32[3]{0:T(128)} %pad_add_fusion.5.place_ref, bf16[768,1024]{1,0:T(8,128)(2,1)} %copy-done.5, bf16[768,1024]{1,0:T(8,128)(2,1)} %copy-done.4, bf16[768,1024]{1,0:T(8,128)(2,1)} %copy-done.29, bf16[768,1024]{1,0:T(8,128)(2,1)} %copy-done.30), custom_call_target="tpu_custom_call" | custom-call | flops 11000000512 | bytes 1048576 | tf_op jit(solution)/shard_map/unpack_experts/pallas_call | solution.py:751
  443.3 5.9 %unpack.1 = (f32[1024,512]{1,0:T(8,128)}, f32[1024,256]{1,0:T(8,128)}, f32[1024,256]{1,0:T(8,128)}, f32[512,1024]{1,0:T(8,128)}) custom-call(s32[3]{0:T(128)} %pad_add_fusion.5.place_ref, bf16[512,768]{1,0:T(8,128)(2,1)} %copy-done.12, bf16[512,768]{1,0:T(8,128)(2,1)} %copy-done.11, bf16[512,768]{1,0:T(8,128)(2,1)} %copy-done.31, bf16[512,768]{1,0:T(8,128)(2,1)} %copy-done.33), custom_call_target="tpu_custom_call" | custom-call | flops 6600000000 | bytes 1048576 | tf_op jit(solution)/shard_map/unpack/pallas_call | solution.py:800
  (208 shorter events, 49.8 us)
Async XLA Ops:
  3.0 37.4 %collective-permute-start = (bf16[1024,512]{1,0:T(8,128)(2,1)S(1)}, bf16[1024,512]{1,0:T(8,128)(2,1)}, u32[]{:S(2)}, u32[]{:S(2)}) collective-permute-start(bf16[1024,512]{1,0:T(8,128)(2,1)S(1)} %pad_maximum_fusion.5), channel_id=1, source_target_pairs={{0,1},{1,0},{2,3},{3,2},{4,5},{5,4},{6,7},{7,6},{8,9},{9,8},{10,11... | collective-permute-start | bytes 3145736 | tf_op jit(solution)/shard_map/ppermute | solution.py:817
  7.0 33.3 %collective-permute-start.1 = (bf16[1,1024,256]{2,1,0:T(8,128)(2,1)S(1)}, bf16[1,1024,256]{2,1,0:T(8,128)(2,1)S(1)}, u32[]{:S(2)}, u32[]{:S(2)}) collective-permute-start(bf16[1,1024,256]{2,1,0:T(8,128)(2,1)S(1)} %constant_dynamic-slice_fusion.2), channel_id=1, source_target_pairs={{0,1},{1,0},{2,3},{3,2},{4,5},{5,4},{6,7},{7,6},{8,9},{9,8},{10,11... | collective-permute-start | bytes 1572872 | tf_op jit(solution)/shard_map/ppermute | solution.py:817
  40.4 29.5 %collective-permute-start.7 = (bf16[1024,512]{1,0:T(8,128)(2,1)}, bf16[1024,512]{1,0:T(8,128)(2,1)}, u32[]{:S(2)}, u32[]{:S(2)}) collective-permute-start(bf16[1024,512]{1,0:T(8,128)(2,1)} %collective-permute-done.wq_ref.wk_ref.wv_ref), channel_id=1, source_target_pairs={{0,2},{2,0},{4,6},{6,4},{8,10},{10,8},{12,14},{14,12},{16,18},{18,... | collective-permute-start | bytes 3145736 | tf_op jit(solution)/shard_map/ppermute | solution.py:822
  41.6 27.5 %collective-permute-start.4 = (bf16[1,1024,256]{2,1,0:T(8,128)(2,1)S(1)}, bf16[1,1024,256]{2,1,0:T(8,128)(2,1)S(1)}, u32[]{:S(2)}, u32[]{:S(2)}) collective-permute-start(bf16[1,1024,256]{2,1,0:T(8,128)(2,1)S(1)} %collective-permute-done.1), channel_id=1, source_target_pairs={{0,4},{2,6},{4,0},{6,2},{8,12},{10,14},{12,8},{14,10},{16,20},{18,... | collective-permute-start | bytes 1572872 | tf_op jit(solution)/shard_map/ppermute | solution.py:822
  43.4 55.0 %collective-permute-start.10 = (bf16[1,1024,256]{2,1,0:T(8,128)(2,1)S(1)}, bf16[1,1024,256]{2,1,0:T(8,128)(2,1)S(1)}, u32[]{:S(2)}, u32[]{:S(2)}) collective-permute-start(bf16[1,1024,256]{2,1,0:T(8,128)(2,1)S(1)} %collective-permute-done.1), channel_id=1, source_target_pairs={{0,2},{2,0},{4,6},{6,4},{8,10},{10,8},{12,14},{14,12},{16,18},{18,... | collective-permute-start | bytes 1572872 | tf_op jit(solution)/shard_map/ppermute | solution.py:822
  43.6 14.7 %collective-permute-start.3 = (bf16[1,1024,256]{2,1,0:T(8,128)(2,1)S(1)}, bf16[1,1024,256]{2,1,0:T(8,128)(2,1)S(1)}, u32[]{:S(2)}, u32[]{:S(2)}) collective-permute-start(bf16[1,1024,256]{2,1,0:T(8,128)(2,1)S(1)} %constant_dynamic-slice_fusion.1), channel_id=1, source_target_pairs={{0,1},{1,0},{2,3},{3,2},{4,5},{5,4},{6,7},{7,6},{8,9},{9,8},{10,11... | collective-permute-start | bytes 1572872 | tf_op jit(solution)/shard_map/ppermute | solution.py:817
  45.1 24.0 %collective-permute-start.2 = (bf16[256,1024]{1,0:T(8,128)(2,1)S(1)}, bf16[256,1024]{1,0:T(8,128)(2,1)}, u32[]{:S(2)}, u32[]{:S(2)}) collective-permute-start(bf16[256,1024]{1,0:T(8,128)(2,1)S(1)} %constant_dynamic-slice_fusion.6), channel_id=1, source_target_pairs={{0,1},{1,0},{2,3},{3,2},{4,5},{5,4},{6,7},{7,6},{8,9},{9,8},{10,11... | collective-permute-start | bytes 1572872 | tf_op jit(solution)/shard_map/ppermute | solution.py:817
  69.1 14.7 %collective-permute-start.5 = (bf16[1,1024,256]{2,1,0:T(8,128)(2,1)S(1)}, bf16[1,1024,256]{2,1,0:T(8,128)(2,1)S(1)}, u32[]{:S(2)}, u32[]{:S(2)}) collective-permute-start(bf16[1,1024,256]{2,1,0:T(8,128)(2,1)S(1)} %collective-permute-done.3), channel_id=1, source_target_pairs={{0,4},{2,6},{4,0},{6,2},{8,12},{10,14},{12,8},{14,10},{16,20},{18,... | collective-permute-start | bytes 1572872 | tf_op jit(solution)/shard_map/ppermute | solution.py:822
  69.3 32.8 %collective-permute-start.12 = (bf16[1,1024,256]{2,1,0:T(8,128)(2,1)S(1)}, bf16[1,1024,256]{2,1,0:T(8,128)(2,1)S(1)}, u32[]{:S(2)}, u32[]{:S(2)}) collective-permute-start(bf16[1,1024,256]{2,1,0:T(8,128)(2,1)S(1)} %collective-permute-done.3), channel_id=1, source_target_pairs={{0,2},{2,0},{4,6},{6,4},{8,10},{10,8},{12,14},{14,12},{16,18},{18,... | collective-permute-start | bytes 1572872 | tf_op jit(solution)/shard_map/ppermute | solution.py:822
  69.3 16.2 %collective-permute-start.9 = (bf16[256,1024]{1,0:T(8,128)(2,1)}, bf16[256,1024]{1,0:T(8,128)(2,1)}, u32[]{:S(2)}, u32[]{:S(2)}) collective-permute-start(bf16[256,1024]{1,0:T(8,128)(2,1)} %collective-permute-done.2.wo_b_ref.wo_ref), channel_id=1, source_target_pairs={{0,2},{2,0},{4,6},{6,4},{8,10},{10,8},{12,14},{14,12},{16,18},{18,... | collective-permute-start | bytes 1572872 | tf_op jit(solution)/shard_map/ppermute | solution.py:822
  69.8 13.9 %collective-permute-start.6 = (bf16[1,256,1024]{2,1,0:T(8,128)(2,1)S(1)}, bf16[1,256,1024]{2,1,0:T(8,128)(2,1)}, u32[]{:S(2)}, u32[]{:S(2)}) collective-permute-start(bf16[1,256,1024]{2,1,0:T(8,128)(2,1)S(1)} %constant_dynamic-slice_fusion), channel_id=1, source_target_pairs={{0,1},{1,0},{2,3},{3,2},{4,5},{5,4},{6,7},{7,6},{8,9},{9,8},{10,11... | collective-permute-start | bytes 1572872 | tf_op jit(solution)/shard_map/ppermute | solution.py:817
  83.8 15.7 %collective-permute-start.11 = (bf16[1,1024,256]{2,1,0:T(8,128)(2,1)S(1)}, bf16[1,1024,256]{2,1,0:T(8,128)(2,1)}, u32[]{:S(2)}, u32[]{:S(2)}) collective-permute-start(bf16[1,1024,256]{2,1,0:T(8,128)(2,1)S(1)} %collective-permute-done.4), channel_id=1, source_target_pairs={{0,2},{2,0},{4,6},{6,4},{8,10},{10,8},{12,14},{14,12},{16,18},{18,... | collective-permute-start | bytes 1572872 | tf_op jit(solution)/shard_map/ppermute | solution.py:822
  83.8 14.6 %collective-permute-start.8 = (bf16[1,256,1024]{2,1,0:T(8,128)(2,1)}, bf16[1,256,1024]{2,1,0:T(8,128)(2,1)S(1)}, u32[]{:S(2)}, u32[]{:S(2)}) collective-permute-start(bf16[1,256,1024]{2,1,0:T(8,128)(2,1)} %collective-permute-done.6), channel_id=1, source_target_pairs={{0,4},{2,6},{4,0},{6,2},{8,12},{10,14},{12,8},{14,10},{16,20},{18,... | collective-permute-start | bytes 1572872 | tf_op jit(solution)/shard_map/ppermute | solution.py:822
  85.6 16.5 %collective-permute-start.13 = (bf16[1,1024,256]{2,1,0:T(8,128)(2,1)S(1)}, bf16[1,1024,256]{2,1,0:T(8,128)(2,1)}, u32[]{:S(2)}, u32[]{:S(2)}) collective-permute-start(bf16[1,1024,256]{2,1,0:T(8,128)(2,1)S(1)} %collective-permute-done.5), channel_id=1, source_target_pairs={{0,2},{2,0},{4,6},{6,4},{8,10},{10,8},{12,14},{14,12},{16,18},{18,... | collective-permute-start | bytes 1572872 | tf_op jit(solution)/shard_map/ppermute | solution.py:822
  98.4 6.4 %collective-permute-start.14 = (bf16[1,256,1024]{2,1,0:T(8,128)(2,1)}, bf16[1,256,1024]{2,1,0:T(8,128)(2,1)S(1)}, u32[]{:S(2)}, u32[]{:S(2)}) collective-permute-start(bf16[1,256,1024]{2,1,0:T(8,128)(2,1)} %collective-permute-done.6), channel_id=1, source_target_pairs={{0,2},{2,0},{4,6},{6,4},{8,10},{10,8},{12,14},{14,12},{16,18},{18,... | collective-permute-start | bytes 1572872 | tf_op jit(solution)/shard_map/ppermute | solution.py:822
  98.4 6.4 %collective-permute-start.15 = (bf16[1,256,1024]{2,1,0:T(8,128)(2,1)S(1)}, bf16[1,256,1024]{2,1,0:T(8,128)(2,1)S(1)}, u32[]{:S(2)}, u32[]{:S(2)}) collective-permute-start(bf16[1,256,1024]{2,1,0:T(8,128)(2,1)S(1)} %collective-permute-done.8), channel_id=1, source_target_pairs={{0,2},{2,0},{4,6},{6,4},{8,10},{10,8},{12,14},{14,12},{16,18},{18,... | collective-permute-start | bytes 1572872 | tf_op jit(solution)/shard_map/ppermute | solution.py:822
  155.7 15.8 %collective-permute-start.16 = (bf16[4,768,1024]{2,1,0:T(8,128)(2,1)}, bf16[4,768,1024]{2,1,0:T(8,128)(2,1)}, u32[]{:S(2)}, u32[]{:S(2)}) collective-permute-start(bf16[4,768,1024]{2,1,0:T(8,128)(2,1)} %bitcast.59), channel_id=1, source_target_pairs={{0,2},{2,0},{4,6},{6,4},{8,10},{10,8},{12,14},{14,12},{16,18},{18,... | collective-permute-start | bytes 18874376 | tf_op jit(solution)/shard_map/ppermute | solution.py:822
  156.4 31.8 %collective-permute-start.17 = (bf16[512,1024]{1,0:T(8,128)(2,1)S(1)}, bf16[512,1024]{1,0:T(8,128)(2,1)S(1)}, u32[]{:S(2)}, u32[]{:S(2)}) collective-permute-start(bf16[512,1024]{1,0:T(8,128)(2,1)S(1)} %get-tuple-element.280), channel_id=1, source_target_pairs={{0,1},{1,0},{2,3},{3,2},{4,5},{5,4},{6,7},{7,6},{8,9},{9,8},{10,11... | collective-permute-start | bytes 3145736 | tf_op jit(solution)/shard_map/ppermute | solution.py:817
  189.2 17.3 %collective-permute-start.18 = (bf16[1024,768]{1,0:T(8,128)(2,1)}, bf16[1024,768]{1,0:T(8,128)(2,1)S(1)}, u32[]{:S(2)}, u32[]{:S(2)}) collective-permute-start(bf16[1024,768]{1,0:T(8,128)(2,1)} %get-tuple-element.290), channel_id=1, source_target_pairs={{0,2},{2,0},{4,6},{6,4},{8,10},{10,8},{12,14},{14,12},{16,18},{18,... | collective-permute-start | bytes 4718600 | tf_op jit(solution)/shard_map/ppermute | solution.py:822
  189.5 26.0 %collective-permute-start.21 = (bf16[512,1024]{1,0:T(8,128)(2,1)}, bf16[512,1024]{1,0:T(8,128)(2,1)S(1)}, u32[]{:S(2)}, u32[]{:S(2)}) collective-permute-start(bf16[512,1024]{1,0:T(8,128)(2,1)} %get-tuple-element.296), channel_id=1, source_target_pairs={{0,1},{1,0},{2,3},{3,2},{4,5},{5,4},{6,7},{7,6},{8,9},{9,8},{10,11... | collective-permute-start | bytes 3145736 | tf_op jit(solution)/shard_map/ppermute | solution.py:817
  189.8 36.7 %collective-permute-start.19 = (bf16[2,384,1024]{2,1,0:T(8,128)(2,1)}, bf16[2,384,1024]{2,1,0:T(8,128)(2,1)}, u32[]{:S(2)}, u32[]{:S(2)}) collective-permute-start(bf16[2,384,1024]{2,1,0:T(8,128)(2,1)} %get-tuple-element.294), channel_id=1, source_target_pairs={{0,4},{2,6},{4,0},{6,2},{8,12},{10,14},{12,8},{14,10},{16,20},{18,... | collective-permute-start | bytes 4718600 | tf_op jit(solution)/shard_map/ppermute | solution.py:822
  191.6 36.4 %collective-permute-start.20 = (bf16[2,384,1024]{2,1,0:T(8,128)(2,1)}, bf16[2,384,1024]{2,1,0:T(8,128)(2,1)}, u32[]{:S(2)}, u32[]{:S(2)}) collective-permute-start(bf16[2,384,1024]{2,1,0:T(8,128)(2,1)} %get-tuple-element.295), channel_id=1, source_target_pairs={{0,8},{2,10},{4,12},{6,14},{8,0},{10,2},{12,4},{14,6},{16,24},{18,... | collective-permute-start | bytes 4718600 | tf_op jit(solution)/shard_map/ppermute | solution.py:822
  215.5 21.4 %copy-start.10 = (bf16[512,1024]{1,0:T(8,128)(2,1)}, bf16[512,1024]{1,0:T(8,128)(2,1)S(1)}, u32[]{:S(2)}) copy-start(bf16[512,1024]{1,0:T(8,128)(2,1)S(1)} %collective-permute-done.21) | copy-start | bytes 3145732
  236.9 18.6 %collective-permute-start.22 = (bf16[2,192,1024]{2,1,0:T(8,128)(2,1)}, bf16[2,192,1024]{2,1,0:T(8,128)(2,1)S(1)}, u32[]{:S(2)}, u32[]{:S(2)}) collective-permute-start(bf16[2,192,1024]{2,1,0:T(8,128)(2,1)} %get-tuple-element.313), channel_id=1, source_target_pairs={{0,8},{2,10},{4,12},{6,14},{8,0},{10,2},{12,4},{14,6},{16,24},{18,... | collective-permute-start | bytes 2359304 | tf_op jit(solution)/shard_map/ppermute | solution.py:822
  238.6 18.2 %collective-permute-start.23 = (bf16[2,192,1024]{2,1,0:T(8,128)(2,1)}, bf16[2,192,1024]{2,1,0:T(8,128)(2,1)S(1)}, u32[]{:S(2)}, u32[]{:S(2)}) collective-permute-start(bf16[2,192,1024]{2,1,0:T(8,128)(2,1)} %get-tuple-element.314), channel_id=1, source_target_pairs={{0,4},{2,6},{4,0},{6,2},{8,12},{10,14},{12,8},{14,10},{16,20},{18,... | collective-permute-start | bytes 2359304 | tf_op jit(solution)/shard_map/ppermute | solution.py:822
  239.1 46.8 %collective-permute-start.26 = (bf16[1024,768]{1,0:T(8,128)(2,1)}, bf16[1024,768]{1,0:T(8,128)(2,1)S(1)}, u32[]{:S(2)}, u32[]{:S(2)}) collective-permute-start(bf16[1024,768]{1,0:T(8,128)(2,1)} %add_convert_fusion), channel_id=1, source_target_pairs={{0,1},{1,0},{2,3},{3,2},{4,5},{5,4},{6,7},{7,6},{8,9},{9,8},{10,11... | collective-permute-start | bytes 4718600 | tf_op jit(solution)/shard_map/ppermute | solution.py:817
  270.1 21.1 %collective-permute-start.25 = (bf16[1024,768]{1,0:T(8,128)(2,1)}, bf16[1024,768]{1,0:T(8,128)(2,1)S(1)}, u32[]{:S(2)}, u32[]{:S(2)}) collective-permute-start(bf16[1024,768]{1,0:T(8,128)(2,1)} %get-tuple-element.329), channel_id=1, source_target_pairs={{0,2},{2,0},{4,6},{6,4},{8,10},{10,8},{12,14},{14,12},{16,18},{18,... | collective-permute-start | bytes 4718600 | tf_op jit(solution)/shard_map/ppermute | solution.py:822
  270.9 20.3 %collective-permute-start.24 = (bf16[2,192,1024]{2,1,0:T(8,128)(2,1)}, bf16[2,192,1024]{2,1,0:T(8,128)(2,1)}, u32[]{:S(2)}, u32[]{:S(2)}) collective-permute-start(bf16[2,192,1024]{2,1,0:T(8,128)(2,1)} %get-tuple-element.328), channel_id=1, source_target_pairs={{0,1},{1,0},{2,3},{3,2},{4,5},{5,4},{6,7},{7,6},{8,9},{9,8},{10,11... | collective-permute-start | bytes 2359304 | tf_op jit(solution)/shard_map/ppermute | solution.py:817
  308.1 11.7 %copy-start.3 = (bf16[1024,1024]{1,0:T(8,128)(2,1)S(1)}, bf16[1024,1024]{1,0:T(8,128)(2,1)}, u32[]{:S(2)}) copy-start(bf16[1024,1024]{1,0:T(8,128)(2,1)} %get-tuple-element.262) | copy-start | bytes 6291460
  308.1 11.7 %copy-start.9 = (bf16[512,1024]{1,0:T(8,128)(2,1)S(1)}, bf16[512,1024]{1,0:T(8,128)(2,1)}, u32[]{:S(2)}) copy-start(bf16[512,1024]{1,0:T(8,128)(2,1)} %copy-done.8) | copy-start | bytes 3145732
  313.6 21.5 %copy-start.18 = (bf16[2,96,1024]{2,1,0:T(8,128)(2,1)S(1)}, bf16[2,96,1024]{2,1,0:T(8,128)(2,1)}, u32[]{:S(2)}) copy-start(bf16[2,96,1024]{2,1,0:T(8,128)(2,1)} %get-tuple-element.352) | copy-start | bytes 1179652
  313.6 21.4 %collective-permute-start.31 = (bf16[256,1024]{1,0:T(8,128)(2,1)}, bf16[256,1024]{1,0:T(8,128)(2,1)S(1)}, u32[]{:S(2)}, u32[]{:S(2)}) collective-permute-start(bf16[256,1024]{1,0:T(8,128)(2,1)} %get-tuple-element.350), channel_id=1, source_target_pairs={{0,1},{1,0},{2,3},{3,2},{4,5},{5,4},{6,7},{7,6},{8,9},{9,8},{10,11... | collective-permute-start | bytes 1572872 | tf_op jit(solution)/shard_map/ppermute | solution.py:817
  315.1 16.5 %collective-permute-start.29 = (bf16[1,256,768]{2,1,0:T(8,128)(2,1)}, bf16[1,256,768]{2,1,0:T(8,128)(2,1)S(1)}, u32[]{:S(2)}, u32[]{:S(2)}) collective-permute-start(bf16[1,256,768]{2,1,0:T(8,128)(2,1)} %get-tuple-element.348), channel_id=1, source_target_pairs={{0,4},{2,6},{4,0},{6,2},{8,12},{10,14},{12,8},{14,10},{16,20},{18,... | collective-permute-start | bytes 1179656 | tf_op jit(solution)/shard_map/ppermute | solution.py:822
  316.2 18.8 %collective-permute-start.30 = (bf16[1,256,768]{2,1,0:T(8,128)(2,1)}, bf16[1,256,768]{2,1,0:T(8,128)(2,1)S(1)}, u32[]{:S(2)}, u32[]{:S(2)}) collective-permute-start(bf16[1,256,768]{2,1,0:T(8,128)(2,1)} %get-tuple-element.349), channel_id=1, source_target_pairs={{0,8},{2,10},{4,12},{6,14},{8,0},{10,2},{12,4},{14,6},{16,24},{18,... | collective-permute-start | bytes 1179656 | tf_op jit(solution)/shard_map/ppermute | solution.py:822
  316.7 14.9 %collective-permute-start.28 = (f32[48,1024]{1,0:T(8,128)S(1)}, f32[48,1024]{1,0:T(8,128)S(1)}, u32[]{:S(2)}, u32[]{:S(2)}) collective-permute-start(f32[48,1024]{1,0:T(8,128)S(1)} %constant_dynamic-update-slice_fusion), channel_id=1, source_target_pairs={{0,1},{1,0},{2,3},{3,2},{4,5},{5,4},{6,7},{7,6},{8,9},{9,8},{10,11... | collective-permute-start | bytes 589832 | tf_op jit(solution)/shard_map/ppermute | solution.py:817
  317.2 17.8 %collective-permute-start.27 = (bf16[2,96,1024]{2,1,0:T(8,128)(2,1)}, bf16[2,96,1024]{2,1,0:T(8,128)(2,1)S(1)}, u32[]{:S(2)}, u32[]{:S(2)}) collective-permute-start(bf16[2,96,1024]{2,1,0:T(8,128)(2,1)} %get-tuple-element.335), channel_id=1, source_target_pairs={{0,16},{2,18},{4,20},{6,22},{8,24},{10,26},{12,28},{14,30},{16,0},... | collective-permute-start | bytes 1179656 | tf_op jit(solution)/shard_map/ppermute | solution.py:822
  339.9 19.0 %collective-permute-start.36 = (bf16[256,1024]{1,0:T(8,128)(2,1)S(1)}, bf16[256,1024]{1,0:T(8,128)(2,1)S(1)}, u32[]{:S(2)}, u32[]{:S(2)}) collective-permute-start(bf16[256,1024]{1,0:T(8,128)(2,1)S(1)} %copy-done.17), channel_id=1, source_target_pairs={{0,1},{1,0},{2,3},{3,2},{4,5},{5,4},{6,7},{7,6},{8,9},{9,8},{10,11... | collective-permute-start | bytes 1572872 | tf_op jit(solution)/shard_map/ppermute | solution.py:817
  342.4 16.5 %collective-permute-start.32 = (bf16[2,96,1024]{2,1,0:T(8,128)(2,1)S(1)}, bf16[2,96,1024]{2,1,0:T(8,128)(2,1)S(1)}, u32[]{:S(2)}, u32[]{:S(2)}) collective-permute-start(bf16[2,96,1024]{2,1,0:T(8,128)(2,1)S(1)} %add_convert_fusion.1), channel_id=1, source_target_pairs={{0,16},{2,18},{4,20},{6,22},{8,24},{10,26},{12,28},{14,30},{16,0},... | collective-permute-start | bytes 1179656 | tf_op jit(solution)/shard_map/ppermute | solution.py:822
  342.4 5.0 %collective-permute-start.33 = (f32[48,1024]{1,0:T(8,128)S(1)}, f32[48,1024]{1,0:T(8,128)S(1)}, u32[]{:S(2)}, u32[]{:S(2)}) collective-permute-start(f32[48,1024]{1,0:T(8,128)S(1)} %add.99), channel_id=1, source_target_pairs={{0,2},{2,0},{4,6},{6,4},{8,10},{10,8},{12,14},{14,12},{16,18},{18,... | collective-permute-start | bytes 589832 | tf_op jit(solution)/shard_map/ppermute | solution.py:822
  342.4 11.9 %collective-permute-start.34 = (bf16[1,128,768]{2,1,0:T(8,128)(2,1)}, bf16[1,128,768]{2,1,0:T(8,128)(2,1)S(1)}, u32[]{:S(2)}, u32[]{:S(2)}) collective-permute-start(bf16[1,128,768]{2,1,0:T(8,128)(2,1)} %get-tuple-element.365), channel_id=1, source_target_pairs={{0,8},{2,10},{4,12},{6,14},{8,0},{10,2},{12,4},{14,6},{16,24},{18,... | collective-permute-start | bytes 589832 | tf_op jit(solution)/shard_map/ppermute | solution.py:822
  346.5 7.8 %collective-permute-start.35 = (bf16[1,128,768]{2,1,0:T(8,128)(2,1)}, bf16[1,128,768]{2,1,0:T(8,128)(2,1)S(1)}, u32[]{:S(2)}, u32[]{:S(2)}) collective-permute-start(bf16[1,128,768]{2,1,0:T(8,128)(2,1)} %get-tuple-element.366), channel_id=1, source_target_pairs={{0,4},{2,6},{4,0},{6,2},{8,12},{10,14},{12,8},{14,10},{16,20},{18,... | collective-permute-start | bytes 589832 | tf_op jit(solution)/shard_map/ppermute | solution.py:822
  362.9 19.2 %copy-start.20 = (bf16[1,64,768]{2,1,0:T(8,128)(2,1)S(1)}, bf16[1,64,768]{2,1,0:T(8,128)(2,1)}, u32[]{:S(2)}) copy-start(bf16[1,64,768]{2,1,0:T(8,128)(2,1)} %get-tuple-element.386) | copy-start | bytes 294916
  362.9 19.2 %copy-start.21 = (bf16[1,64,768]{2,1,0:T(8,128)(2,1)S(1)}, bf16[1,64,768]{2,1,0:T(8,128)(2,1)}, u32[]{:S(2)}) copy-start(bf16[1,64,768]{2,1,0:T(8,128)(2,1)} %get-tuple-element.388) | copy-start | bytes 294916
  363.9 15.5 %collective-permute-start.41 = (bf16[256,1024]{1,0:T(8,128)(2,1)S(1)}, bf16[256,1024]{1,0:T(8,128)(2,1)S(1)}, u32[]{:S(2)}, u32[]{:S(2)}) collective-permute-start(bf16[256,1024]{1,0:T(8,128)(2,1)S(1)} %copy-done.16), channel_id=1, source_target_pairs={{0,1},{1,0},{2,3},{3,2},{4,5},{5,4},{6,7},{7,6},{8,9},{9,8},{10,11... | collective-permute-start | bytes 1572872 | tf_op jit(solution)/shard_map/ppermute | solution.py:817
  365.6 13.8 %collective-permute-start.37 = (bf16[192,1024]{1,0:T(8,128)(2,1)S(1)}, bf16[192,1024]{1,0:T(8,128)(2,1)S(1)}, u32[]{:S(2)}, u32[]{:S(2)}) collective-permute-start(bf16[192,1024]{1,0:T(8,128)(2,1)S(1)} %get-tuple-element.377), channel_id=1, source_target_pairs={{0,8},{2,10},{4,12},{6,14},{8,0},{10,2},{12,4},{14,6},{16,24},{18,... | collective-permute-start | bytes 1179656 | tf_op jit(solution)/shard_map/ppermute | solution.py:822
  365.7 13.8 %collective-permute-start.38 = (bf16[192,1024]{1,0:T(8,128)(2,1)S(1)}, bf16[192,1024]{1,0:T(8,128)(2,1)S(1)}, u32[]{:S(2)}, u32[]{:S(2)}) collective-permute-start(bf16[192,1024]{1,0:T(8,128)(2,1)S(1)} %get-tuple-element.378), channel_id=1, source_target_pairs={{0,4},{2,6},{4,0},{6,2},{8,12},{10,14},{12,8},{14,10},{16,20},{18,... | collective-permute-start | bytes 1179656 | tf_op jit(solution)/shard_map/ppermute | solution.py:822
  366.6 12.8 %collective-permute-start.39 = (f32[48,1024]{1,0:T(8,128)S(1)}, f32[48,1024]{1,0:T(8,128)S(1)}, u32[]{:S(2)}, u32[]{:S(2)}) collective-permute-start(f32[48,1024]{1,0:T(8,128)S(1)} %add.100), channel_id=1, source_target_pairs={{0,4},{2,6},{4,0},{6,2},{8,12},{10,14},{12,8},{14,10},{16,20},{18,... | collective-permute-start | bytes 589832 | tf_op jit(solution)/shard_map/ppermute | solution.py:822
  367.7 11.7 %collective-permute-start.40 = (bf16[2,64,768]{2,1,0:T(8,128)(2,1)S(1)}, bf16[2,64,768]{2,1,0:T(8,128)(2,1)S(1)}, u32[]{:S(2)}, u32[]{:S(2)}) collective-permute-start(bf16[2,64,768]{2,1,0:T(8,128)(2,1)S(1)} %pad_maximum_fusion.14), channel_id=1, source_target_pairs={{0,16},{2,18},{4,20},{6,22},{8,24},{10,26},{12,28},{14,30},{16,0},... | collective-permute-start | bytes 589832 | tf_op jit(solution)/shard_map/ppermute | solution.py:822
  382.8 27.5 %collective-permute-start.42 = (bf16[384,1024]{1,0:T(8,128)(2,1)}, bf16[384,1024]{1,0:T(8,128)(2,1)}, u32[]{:S(2)}, u32[]{:S(2)}) collective-permute-start(bf16[384,1024]{1,0:T(8,128)(2,1)} %pad_maximum_fusion.6), channel_id=1, source_target_pairs={{0,4},{2,6},{4,0},{6,2},{8,12},{10,14},{12,8},{14,10},{16,20},{18,... | collective-permute-start | bytes 2359304 | tf_op jit(solution)/shard_map/ppermute | solution.py:822
  383.7 26.7 %collective-permute-start.43 = (bf16[384,1024]{1,0:T(8,128)(2,1)}, bf16[384,1024]{1,0:T(8,128)(2,1)}, u32[]{:S(2)}, u32[]{:S(2)}) collective-permute-start(bf16[384,1024]{1,0:T(8,128)(2,1)} %pad_maximum_fusion.7), channel_id=1, source_target_pairs={{0,8},{2,10},{4,12},{6,14},{8,0},{10,2},{12,4},{14,6},{16,24},{18,... | collective-permute-start | bytes 2359304 | tf_op jit(solution)/shard_map/ppermute | solution.py:822
  385.7 24.7 %collective-permute-start.46 = (bf16[256,1024]{1,0:T(8,128)(2,1)}, bf16[256,1024]{1,0:T(8,128)(2,1)S(1)}, u32[]{:S(2)}, u32[]{:S(2)}) collective-permute-start(bf16[256,1024]{1,0:T(8,128)(2,1)} %get-tuple-element.393), channel_id=1, source_target_pairs={{0,1},{1,0},{2,3},{3,2},{4,5},{5,4},{6,7},{7,6},{8,9},{9,8},{10,11... | collective-permute-start | bytes 1572872 | tf_op jit(solution)/shard_map/ppermute | solution.py:817
  388.0 22.5 %copy-start.15 = (f32[48,1024]{1,0:T(8,128)S(1)}, f32[48,1024]{1,0:T(8,128)}, u32[]{:S(2)}) copy-start(f32[48,1024]{1,0:T(8,128)} %add.101) | copy-start | bytes 589828
  388.0 22.5 %copy-start.7 = (bf16[192,1024]{1,0:T(8,128)(2,1)S(1)}, bf16[192,1024]{1,0:T(8,128)(2,1)}, u32[]{:S(2)}) copy-start(bf16[192,1024]{1,0:T(8,128)(2,1)} %copy-done.6) | copy-start | bytes 1179652
  388.1 22.3 %collective-permute-start.44 = (f32[48,1024]{1,0:T(8,128)}, f32[48,1024]{1,0:T(8,128)S(1)}, u32[]{:S(2)}, u32[]{:S(2)}) collective-permute-start(f32[48,1024]{1,0:T(8,128)} %add.101), channel_id=1, source_target_pairs={{0,8},{2,10},{4,12},{6,14},{8,0},{10,2},{12,4},{14,6},{16,24},{18,... | collective-permute-start | bytes 589832 | tf_op jit(solution)/shard_map/ppermute | solution.py:822
  388.1 22.2 %collective-permute-start.45 = (bf16[2,64,768]{2,1,0:T(8,128)(2,1)}, bf16[2,64,768]{2,1,0:T(8,128)(2,1)S(1)}, u32[]{:S(2)}, u32[]{:S(2)}) collective-permute-start(bf16[2,64,768]{2,1,0:T(8,128)(2,1)} %pad_maximum_fusion.15), channel_id=1, source_target_pairs={{0,16},{2,18},{4,20},{6,22},{8,24},{10,26},{12,28},{14,30},{16,0},... | collective-permute-start | bytes 589832 | tf_op jit(solution)/shard_map/ppermute | solution.py:822
  413.8 12.6 %collective-permute-start.47 = (bf16[768,1024]{1,0:T(8,128)(2,1)S(1)}, bf16[768,1024]{1,0:T(8,128)(2,1)S(1)}, u32[]{:S(2)}, u32[]{:S(2)}) collective-permute-start(bf16[768,1024]{1,0:T(8,128)(2,1)S(1)} %pad_maximum_fusion.3.refs_0_), channel_id=1, source_target_pairs={{0,2},{2,0},{4,6},{6,4},{8,10},{10,8},{12,14},{14,12},{16,18},{18,... | collective-permute-start | bytes 4718600 | tf_op jit(solution)/shard_map/ppermute | solution.py:822
  413.9 12.5 %collective-permute-start.48 = (bf16[768,1024]{1,0:T(8,128)(2,1)S(1)}, bf16[768,1024]{1,0:T(8,128)(2,1)S(1)}, u32[]{:S(2)}, u32[]{:S(2)}) collective-permute-start(bf16[768,1024]{1,0:T(8,128)(2,1)S(1)} %pad_maximum_fusion.4.refs_1_), channel_id=1, source_target_pairs={{0,2},{2,0},{4,6},{6,4},{8,10},{10,8},{12,14},{14,12},{16,18},{18,... | collective-permute-start | bytes 4718600 | tf_op jit(solution)/shard_map/ppermute | solution.py:822
  414.4 12.0 %collective-permute-start.49 = (f32[48,1024]{1,0:T(8,128)S(1)}, f32[48,1024]{1,0:T(8,128)S(1)}, u32[]{:S(2)}, u32[]{:S(2)}) collective-permute-start(f32[48,1024]{1,0:T(8,128)S(1)} %add.104), channel_id=1, source_target_pairs={{0,16},{2,18},{4,20},{6,22},{8,24},{10,26},{12,28},{14,30},{16,0},... | collective-permute-start | bytes 589832 | tf_op jit(solution)/shard_map/ppermute | solution.py:822
  417.0 9.4 %collective-permute-start.50 = (bf16[128,768]{1,0:T(8,128)(2,1)S(1)}, bf16[128,768]{1,0:T(8,128)(2,1)S(1)}, u32[]{:S(2)}, u32[]{:S(2)}) collective-permute-start(bf16[128,768]{1,0:T(8,128)(2,1)S(1)} %get-tuple-element.402), channel_id=1, source_target_pairs={{0,8},{2,10},{4,12},{6,14},{8,0},{10,2},{12,4},{14,6},{16,24},{18,... | collective-permute-start | bytes 589832 | tf_op jit(solution)/shard_map/ppermute | solution.py:822
  417.7 8.6 %collective-permute-start.51 = (bf16[128,768]{1,0:T(8,128)(2,1)S(1)}, bf16[128,768]{1,0:T(8,128)(2,1)S(1)}, u32[]{:S(2)}, u32[]{:S(2)}) collective-permute-start(bf16[128,768]{1,0:T(8,128)(2,1)S(1)} %get-tuple-element.403), channel_id=1, source_target_pairs={{0,4},{2,6},{4,0},{6,2},{8,12},{10,14},{12,8},{14,10},{16,20},{18,... | collective-permute-start | bytes 589832 | tf_op jit(solution)/shard_map/ppermute | solution.py:822
  426.5 12.3 %collective-permute-start.52 = (bf16[256,768]{1,0:T(8,128)(2,1)S(1)}, bf16[256,768]{1,0:T(8,128)(2,1)S(1)}, u32[]{:S(2)}, u32[]{:S(2)}) collective-permute-start(bf16[256,768]{1,0:T(8,128)(2,1)S(1)} %pad_maximum_fusion.12), channel_id=1, source_target_pairs={{0,4},{2,6},{4,0},{6,2},{8,12},{10,14},{12,8},{14,10},{16,20},{18,... | collective-permute-start | bytes 1179656 | tf_op jit(solution)/shard_map/ppermute | solution.py:822
  428.1 10.7 %collective-permute-start.53 = (bf16[256,768]{1,0:T(8,128)(2,1)S(1)}, bf16[256,768]{1,0:T(8,128)(2,1)S(1)}, u32[]{:S(2)}, u32[]{:S(2)}) collective-permute-start(bf16[256,768]{1,0:T(8,128)(2,1)S(1)} %pad_maximum_fusion.13), channel_id=1, source_target_pairs={{0,8},{2,10},{4,12},{6,14},{8,0},{10,2},{12,4},{14,6},{16,24},{18,... | collective-permute-start | bytes 1179656 | tf_op jit(solution)/shard_map/ppermute | solution.py:822
  439.0 2.4 collective-permute-start.54
  439.0 3.4 collective-permute-start.55
  (31 other events, 120.8 us)
